TPU v7x, 32 devices: a whole 2x2x4 slice. The times are simulated.
32 devices in a mesh: rollout: 2 (over y), frame: 2 (over core), seq: 8 (over z, x).
Axes of the slice: x: 2, y: 2, z: 4, core: 2. Of those that a mesh axis runs over, the one named last changes fastest.
Arguments:
- queries: bfloat16 [4, 4, 64, 2048], P(('rollout', 'frame'), None, 'seq'), parts along dimension 0, may hold values from -13 to 13
- keys: bfloat16 [4, 4, 64, 2048], P(('rollout', 'frame'), None, 'seq'), parts along dimension 0, may hold values from -13 to 13
- values: bfloat16 [4, 4, 64, 2048], P(('rollout', 'frame'), None, 'seq'), parts along dimension 0, may hold values from -6 to 6
- slot_of: int32 [4, 4], P('rollout'), parts along dimension 0, may hold values from 0 to 7, as said below
- level_of: int32 [4, 4], P('rollout'), parts along dimension 0, may hold values from 0 to 7
- gate_table: float32 [8, 2048], replicated, may hold values from 0.25 to 2
Outputs:
- attended: bfloat16 [4, 4, 64, 2048], P(('rollout', 'frame'), None, 'seq'), parts along dimension 0
There are 2 independent parts, one for each index of `rollout`. A program takes and returns all parts, laid end to end along the dimension named above; an argument that names none is the same for every part. Nothing has to cross between parts.
Inputs may be any that keep to these rules, and one draw needn't show every extreme that they name: `slot_of`: each number 0 to 7 is the slot of exactly one frame.
All inputs are finite; a program needn't handle non-finite values.
Results may differ from a plain program's by a relative error of at most 0.0055.
Values may be sent and summed in bfloat16 or wider, within the bound.
No kernel may reach another device: no remote copies, remote signals or barrier semaphores. Data moves between devices by JAX's collectives and lax.ppermute only.
A program may use at most 64 MiB of HBM per device.

v0:
```python
import functools
import math

import jax
import jax.numpy as jnp
from jax import lax
from jax.experimental import pallas as pl
from jax.experimental.pallas import tpu as pltpu
from jax.sharding import PartitionSpec as P

H = 16
HEAD = 128
AXES = ("frame", "seq")
SMEM = pl.BlockSpec(memory_space=pltpu.SMEM)
VMEM = pl.BlockSpec(memory_space=pltpu.VMEM)
PARAMS = pltpu.CompilerParams(vmem_limit_bytes=32 * 1024 * 1024)


def pack(*refs):
    out_ref = refs[-1]
    width = out_ref.shape[-1]
    for place, ref in enumerate(refs[:-1]):
        for device in range(out_ref.shape[0]):
            out_ref[device, place] = ref[:, device * width : (device + 1) * width]


def unpack(held_ref, out_ref):
    width = held_ref.shape[-1]
    for device in range(held_ref.shape[0]):
        out_ref[:, device * width : (device + 1) * width] = held_ref[device]


def attend(slot_ref, level_ref, packed_ref, gate_ref, out_ref, *, group_devices, tokens):
    devices, _, rows, width = packed_ref.shape
    local_frames = rows // tokens
    group_count = devices // group_devices
    key_count = devices * rows
    index = lax.broadcasted_iota(jnp.int32, (1, key_count), 1)
    frame = index // (group_devices * rows) * local_frames + index // tokens % local_frames
    key_slots = jnp.zeros((1, key_count), jnp.int32)
    for one in range(group_count * local_frames):
        slot = slot_ref[one // local_frames, one % local_frames]
        key_slots = jnp.where(frame == one, slot, key_slots)
    scale = math.log2(math.e) / math.sqrt(HEAD)
    step = max(1, min(group_devices, 128 // rows))
    for column in range(0, width, HEAD):
        part = pl.ds(column, HEAD)
        keys = packed_ref[:, 1, :, part].reshape(key_count, HEAD)
        values = packed_ref[:, 2, :, part].reshape(key_count, HEAD)
        for group in range(group_count):
            shown = []
            gates = []
            for local in range(local_frames):
                visible = key_slots <= slot_ref[group, local]
                shown.append(jnp.where(visible, 0.0, -jnp.inf).reshape(1, 1, 1, key_count))
                level = level_ref[group, local]
                gates.append(gate_ref[pl.ds(level, 1), part].reshape(1, 1, 1, HEAD))
            shown = jnp.concatenate(shown, axis=1)
            gates = jnp.concatenate(gates, axis=1)
            for start in range(group * group_devices, (group + 1) * group_devices, step):
                queries = packed_ref[start : start + step, 0, :, part].reshape(step * rows, HEAD)
                scores = lax.dot_general(
                    queries, keys, (((1,), (1,)), ((), ())), preferred_element_type=jnp.float32
                )
                scores = scores.reshape(step, local_frames, tokens, key_count) * scale + shown
                scores = scores.reshape(step * rows, key_count)
                weights = jnp.exp2(scores - jnp.max(scores, axis=1, keepdims=True))
                weights = weights.astype(jnp.bfloat16)
                total = jnp.sum(weights.astype(jnp.float32), axis=1, keepdims=True)
                mixed = jnp.dot(weights, values, preferred_element_type=jnp.float32) / total
                mixed = mixed.reshape(step, local_frames, tokens, HEAD) * gates
                out_ref[start : start + step, :, part] = mixed.reshape(step, rows, HEAD).astype(
                    out_ref.dtype
                )


def one_head_each(queries, keys, values, slot_of, level_of, gate_table):
    seq_count = lax.axis_size("seq")
    devices = lax.axis_size("frame") * seq_count
    _, local_frames, tokens, all_width = queries.shape
    rows, width = local_frames * tokens, all_width // devices
    exchange = functools.partial(
        lax.all_to_all, axis_name=AXES, split_axis=0, concat_axis=0, tiled=True
    )
    packed = pl.pallas_call(
        pack,
        out_shape=jax.ShapeDtypeStruct((devices, 3, rows, width), queries.dtype),
        in_specs=[VMEM] * 3,
        out_specs=VMEM,
        compiler_params=PARAMS,
    )(*(taken.reshape(rows, all_width) for taken in (queries, keys, values)))
    packed = exchange(packed)
    device_index = lax.axis_index("frame") * seq_count + lax.axis_index("seq")
    gates = lax.dynamic_slice_in_dim(gate_table, device_index * width, width, 1)
    answer = pl.pallas_call(
        functools.partial(attend, group_devices=seq_count, tokens=tokens),
        out_shape=jax.ShapeDtypeStruct((devices, rows, width), queries.dtype),
        in_specs=[SMEM, SMEM, VMEM, VMEM],
        out_specs=VMEM,
        compiler_params=PARAMS,
    )(slot_of, level_of, packed, gates)
    answer = exchange(answer)
    answer = pl.pallas_call(
        unpack,
        out_shape=jax.ShapeDtypeStruct((rows, all_width), queries.dtype),
        in_specs=[VMEM],
        out_specs=VMEM,
        compiler_params=PARAMS,
    )(answer)
    return answer.reshape(queries.shape)


def shared_heads(queries, keys, values, slot_of, level_of, gate_table):
    devices = lax.axis_size("frame") * lax.axis_size("seq")
    _, local_frames, tokens, _ = queries.shape
    rows, blocks = local_frames * tokens, devices // H
    block_rows = rows // blocks
    exchange = functools.partial(
        lax.all_to_all, axis_name=AXES, split_axis=0, concat_axis=0, tiled=True
    )

    def by_head(taken):
        return taken.reshape(rows, H, HEAD).transpose(1, 0, 2)

    def key_pieces(taken):
        pieces = jnp.broadcast_to(by_head(taken)[:, None], (H, blocks, rows, HEAD))
        return exchange(pieces.reshape(devices, rows, HEAD)).reshape(devices * rows, HEAD)

    key_rows, value_rows = key_pieces(keys), key_pieces(values)
    query_rows = exchange(by_head(queries).reshape(devices, block_rows, HEAD))
    query_rows = query_rows.reshape(devices * block_rows, HEAD)
    device_index = lax.axis_index("frame") * lax.axis_size("seq") + lax.axis_index("seq")
    head, block = device_index // blocks, device_index % blocks

    def per_row(table):
        table = jnp.repeat(table, tokens, axis=1)[:, None]
        return jnp.broadcast_to(table, (table.shape[0], lax.axis_size("seq"), rows))

    row_slots, row_levels = per_row(slot_of), per_row(level_of)
    query_slots = lax.dynamic_slice_in_dim(row_slots, block * block_rows, block_rows, 2)
    levels = lax.dynamic_slice_in_dim(row_levels, block * block_rows, block_rows, 2).reshape(-1)
    scores = lax.dot_general(
        query_rows, key_rows, (((1,), (1,)), ((), ())), preferred_element_type=jnp.float32
    )
    visible = row_slots.reshape(1, -1) <= query_slots.reshape(-1, 1)
    scores = jnp.where(visible, scores * (1.0 / math.sqrt(HEAD)), -jnp.inf)
    weights = jnp.exp(scores - jnp.max(scores, axis=1, keepdims=True)).astype(jnp.bfloat16)
    total = jnp.sum(weights.astype(jnp.float32), axis=1, keepdims=True)
    mixed = jnp.dot(weights, value_rows, preferred_element_type=jnp.float32) / total
    gates = lax.dynamic_slice_in_dim(gate_table, head * HEAD, HEAD, 1)[levels]
    answer = exchange((mixed * gates).astype(queries.dtype).reshape(devices, block_rows, HEAD))
    return answer.reshape(H, rows, HEAD).transpose(1, 0, 2).reshape(queries.shape)


def body(queries, *others):
    devices = lax.axis_size("frame") * lax.axis_size("seq")
    if devices > H:
        return shared_heads(queries, *others)
    return one_head_each(queries, *others)


def solution(mesh):
    return jax.shard_map(
        body,
        mesh=mesh,
        in_specs=(
            P(("rollout", "frame"), None, "seq", None),
            P(("rollout", "frame"), None, "seq", None),
            P(("rollout", "frame"), None, "seq", None),
            P("rollout", None),
            P("rollout", None),
            P(),
        ),
        out_specs=P(("rollout", "frame"), None, "seq", None),
        check_vma=False,
    )
```

profile of v0, /device:TPU:0, one launch (start us, length us, event | category | flops | bytes accessed | tf_op | source)
XLA Modules:
  0.0 36.7 jit_solution(11198300047031449475)
XLA Ops:
  0.0 0.0 copy-start
  0.0 0.0 copy-start.1
  0.0 0.9 %copy-done.1 = bf16[1,4,8,2048]{3,2,1,0:T(8,128)(2,1)S(1)} copy-done((bf16[1,4,8,2048]{3,2,1,0:T(8,128)(2,1)S(1)}, bf16[1,4,8,2048]{3,2,1,0:T(8,128)(2,1)}, u32[]{:S(2)}) %copy-start.1) | copy-done | bytes 131096
  0.9 0.0 copy-start.2
  0.9 0.9 %copy-done.2 = bf16[1,4,8,2048]{3,2,1,0:T(8,128)(2,1)S(1)} copy-done((bf16[1,4,8,2048]{3,2,1,0:T(8,128)(2,1)S(1)}, bf16[1,4,8,2048]{3,2,1,0:T(8,128)(2,1)}, u32[]{:S(2)}) %copy-start.2) | copy-done | bytes 131096
  1.8 0.0 copy-start.3
  1.8 0.9 %copy-done.3 = bf16[1,4,8,2048]{3,2,1,0:T(8,128)(2,1)S(1)} copy-done((bf16[1,4,8,2048]{3,2,1,0:T(8,128)(2,1)S(1)}, bf16[1,4,8,2048]{3,2,1,0:T(8,128)(2,1)}, u32[]{:S(2)}) %copy-start.3) | copy-done | bytes 131096
  2.7 0.8 %shard_map.64 = bf16[16,3,32,128]{3,2,1,0:T(8,128)(2,1)} custom-call(bf16[32,2048]{1,0:T(8,128)(2,1)S(1)} %bitcast.4, bf16[32,2048]{1,0:T(8,128)(2,1)S(1)} %bitcast.5, bf16[32,2048]{1,0:T(8,128)(2,1)S(1)} %bitcast.6), custom_call_target="tpu_custom_call" | custom-call | tf_op jit(solution)/shard_map/pallas_call | solution.py:85
  3.6 7.4 %all-to-all-start = ((bf16[16,3,32,128]{3,2,1,0:T(8,128)(2,1)}), bf16[16,3,32,128]{3,2,1,0:T(8,128)(2,1)S(1)}, u32[]{:S(2)}, u32[]{:S(2)}) async-start(bf16[16,3,32,128]{3,2,1,0:T(8,128)(2,1)} %shard_map.64), calls=%async_computation | async-start | bytes 786432 | tf_op jit(solution)/shard_map/all_to_all | solution.py:92
  10.9 0.0 copy-done
  10.9 0.0 copy-start.4
  11.0 0.0 copy-start.5
  11.0 13.0 %all-to-all-done.packed_ref = bf16[16,3,32,128]{3,2,1,0:T(8,128)(2,1)S(1)} async-done(((bf16[16,3,32,128]{3,2,1,0:T(8,128)(2,1)}), bf16[16,3,32,128]{3,2,1,0:T(8,128)(2,1)S(1)}, u32[]{:S(2)}, u32[]{:S(2)}) %all-to-all-start) | async-done | bytes 393248 | tf_op jit(solution)/shard_map/all_to_all | solution.py:92
  24.0 0.0 copy-done.4
  24.0 0.0 copy-done.5
  24.0 1.7 %shard_map.65 = bf16[16,32,128]{2,1,0:T(8,128)(2,1)S(1)} custom-call(s32[2,4]{1,0:T(2,128)S(1)} %copy-done.4, s32[2,4]{1,0:T(2,128)S(1)} %copy-done.5, bf16[16,3,32,128]{3,2,1,0:T(8,128)(2,1)S(1)} %all-to-all-done.packed_ref, f32[8,128]{1,0:T(8,128)S(1)} %constant_dynamic-slice_fusion.gate_ref), custom_call_target="tpu_custom_call" | custom-call | tf_op jit(solution)/shard_map/pallas_call | solution.py:95
  25.8 10.2 %all_to_all.10.held_ref = bf16[16,32,128]{2,1,0:T(8,128)(2,1)S(1)} all-to-all(bf16[16,32,128]{2,1,0:T(8,128)(2,1)S(1)} %shard_map.65), channel_id=1, replica_groups=mesh['rollout'=2,'frame'=2,'seq'=8] {'frame','seq'}, dimensions={0} | all-to-all | bytes 262144 | tf_op jit(solution)/shard_map/all_to_all | solution.py:102
  36.0 0.7 %shard_map.66 = bf16[32,2048]{1,0:T(8,128)(2,1)} custom-call(bf16[16,32,128]{2,1,0:T(8,128)(2,1)S(1)} %all_to_all.10.held_ref), custom_call_target="tpu_custom_call" | custom-call | tf_op jit(solution)/shard_map/pallas_call | solution.py:103
  (1 shorter events, 0.0 us)
Async XLA Ops:
  0.0 10.9 %copy-start = (f32[8,2048]{1,0:T(8,128)S(1)}, f32[8,2048]{1,0:T(8,128)}, u32[]{:S(2)}) copy-start(f32[8,2048]{1,0:T(8,128)} %param.11) | copy-start | bytes 196612
  0.0 0.9 %copy-start.1 = (bf16[1,4,8,2048]{3,2,1,0:T(8,128)(2,1)S(1)}, bf16[1,4,8,2048]{3,2,1,0:T(8,128)(2,1)}, u32[]{:S(2)}) copy-start(bf16[1,4,8,2048]{3,2,1,0:T(8,128)(2,1)} %param.6) | copy-start | bytes 393220
  0.9 0.9 %copy-start.2 = (bf16[1,4,8,2048]{3,2,1,0:T(8,128)(2,1)S(1)}, bf16[1,4,8,2048]{3,2,1,0:T(8,128)(2,1)}, u32[]{:S(2)}) copy-start(bf16[1,4,8,2048]{3,2,1,0:T(8,128)(2,1)} %param.7) | copy-start | bytes 393220
  1.8 0.9 %copy-start.3 = (bf16[1,4,8,2048]{3,2,1,0:T(8,128)(2,1)S(1)}, bf16[1,4,8,2048]{3,2,1,0:T(8,128)(2,1)}, u32[]{:S(2)}) copy-start(bf16[1,4,8,2048]{3,2,1,0:T(8,128)(2,1)} %param.8) | copy-start | bytes 393220
  3.6 20.5 %all-to-all-start = ((bf16[16,3,32,128]{3,2,1,0:T(8,128)(2,1)}), bf16[16,3,32,128]{3,2,1,0:T(8,128)(2,1)S(1)}, u32[]{:S(2)}, u32[]{:S(2)}) async-start(bf16[16,3,32,128]{3,2,1,0:T(8,128)(2,1)} %shard_map.64), calls=%async_computation | async-start | bytes 786432 | tf_op jit(solution)/shard_map/all_to_all | solution.py:92
  10.9 13.1 %copy-start.4 = (s32[2,4]{1,0:T(2,128)S(1)}, s32[2,4]{1,0:T(2,128)}, u32[]{:S(2)}) copy-start(s32[2,4]{1,0:T(2,128)} %slot_ref.1) | copy-start | bytes 100
  11.0 13.1 %copy-start.5 = (s32[2,4]{1,0:T(2,128)S(1)}, s32[2,4]{1,0:T(2,128)}, u32[]{:S(2)}) copy-start(s32[2,4]{1,0:T(2,128)} %level_ref.1) | copy-start | bytes 100
where the time goes:
time: 37 us; the launch traced here: 36.7 us
  waiting for transfers between devices  13 us (35%)
  blocking collectives  10.2 us (28%)
  starting transfers between devices  7.36 us (20%)
  Pallas kernels  3.23 us (9%)
  local copies, waits for them, and re-layouts  2.77 us (7%)
    all_to_all x1, waiting for transfers between devices, one_head_each(): packed = exchange(packed)  13 us
    all_to_all x1, blocking collectives, one_head_each(): answer = exchange(answer)  10.2 us
    all_to_all x1, starting transfers between devices, one_head_each(): packed = exchange(packed)  7.36 us
    unnamed x12, local copies, waits for them, and re-layouts  2.76 us
    pallas_call x1, Pallas kernels, one_head_each(): pl.pallas_call(functools.partial(attend, group_devices=seq_count, tokens=...  1.74 us
    pallas_call x1, Pallas kernels, one_head_each(): pl.pallas_call(pack, out_shape=jax.ShapeDtypeStruct((devices, 3, rows, wi...  0.81 us
  transfers between devices with their start and end apart: 1, of which 1 were waited for; matrix products, arithmetic and copies ran while one was open for 0% of the time, Pallas kernels for 0%

commit v1 on v0

--- a/solution.py
+++ b/solution.py
@@ -16,49 +16,67 @@
 PARAMS = pltpu.CompilerParams(vmem_limit_bytes=32 * 1024 * 1024)
 
 
-def pack(*refs):
+def pack(index_ref, *refs):
+    operands, outs, held_ref, sems = refs[:3], refs[3:-2], refs[-2], refs[-1]
+    copies = [
+        pltpu.make_async_copy(ref, held_ref.at[place], sems.at[place])
+        for place, ref in enumerate(operands)
+    ]
+    for copy in copies:
+        copy.start()
+    width = outs[0].shape[-1]
+    for place, copy in enumerate(copies):
+        copy.wait()
+        for offset, out_ref in enumerate(outs):
+            column = pl.multiple_of((index_ref[0] ^ offset) * width, width)
+            out_ref[place] = held_ref[place, :, pl.ds(column, width)]
+
+
+def unpack(index_ref, *refs):
     out_ref = refs[-1]
-    width = out_ref.shape[-1]
-    for place, ref in enumerate(refs[:-1]):
-        for device in range(out_ref.shape[0]):
-            out_ref[device, place] = ref[:, device * width : (device + 1) * width]
-
-
-def unpack(held_ref, out_ref):
-    width = held_ref.shape[-1]
-    for device in range(held_ref.shape[0]):
-        out_ref[:, device * width : (device + 1) * width] = held_ref[device]
-
-
-def attend(slot_ref, level_ref, packed_ref, gate_ref, out_ref, *, group_devices, tokens):
-    devices, _, rows, width = packed_ref.shape
+    width = refs[0].shape[-1]
+    for offset, ref in enumerate(refs[:-1]):
+        column = pl.multiple_of((index_ref[0] ^ offset) * width, width)
+        out_ref[:, pl.ds(column, width)] = ref[...]
+
+
+def attend(index_ref, slot_ref, level_ref, gate_ref, *refs, group_devices, tokens):
+    devices = len(refs) // 2
+    packed, outs = refs[:devices], refs[devices:]
+    _, rows, width = packed[0].shape
     local_frames = rows // tokens
-    group_count = devices // group_devices
     key_count = devices * rows
+    device_index = index_ref[0]
     index = lax.broadcasted_iota(jnp.int32, (1, key_count), 1)
-    frame = index // (group_devices * rows) * local_frames + index // tokens % local_frames
+    frame = (device_index ^ (index // rows)) // group_devices * local_frames
+    frame = frame + index // tokens % local_frames
     key_slots = jnp.zeros((1, key_count), jnp.int32)
-    for one in range(group_count * local_frames):
+    for one in range(devices // group_devices * local_frames):
         slot = slot_ref[one // local_frames, one % local_frames]
         key_slots = jnp.where(frame == one, slot, key_slots)
     scale = math.log2(math.e) / math.sqrt(HEAD)
     step = max(1, min(group_devices, 128 // rows))
     for column in range(0, width, HEAD):
         part = pl.ds(column, HEAD)
-        keys = packed_ref[:, 1, :, part].reshape(key_count, HEAD)
-        values = packed_ref[:, 2, :, part].reshape(key_count, HEAD)
-        for group in range(group_count):
+        keys = jnp.concatenate([ref[1, :, part] for ref in packed], axis=0)
+        values = jnp.concatenate([ref[2, :, part] for ref in packed], axis=0)
+        gate_column = pl.ds(pl.multiple_of(device_index * width + column, HEAD), HEAD)
+        gate_block = gate_ref[:, gate_column]
+        level_rows = lax.broadcasted_iota(jnp.int32, gate_block.shape, 0)
+        for first in range(0, devices, group_devices):
+            group = (device_index ^ first) // group_devices
             shown = []
             gates = []
             for local in range(local_frames):
                 visible = key_slots <= slot_ref[group, local]
                 shown.append(jnp.where(visible, 0.0, -jnp.inf).reshape(1, 1, 1, key_count))
-                level = level_ref[group, local]
-                gates.append(gate_ref[pl.ds(level, 1), part].reshape(1, 1, 1, HEAD))
+                gate = jnp.where(level_rows == level_ref[group, local], gate_block, 0.0)
+                gates.append(jnp.sum(gate, axis=0).reshape(1, 1, 1, HEAD))
             shown = jnp.concatenate(shown, axis=1)
             gates = jnp.concatenate(gates, axis=1)
-            for start in range(group * group_devices, (group + 1) * group_devices, step):
-                queries = packed_ref[start : start + step, 0, :, part].reshape(step * rows, HEAD)
+            for start in range(first, first + group_devices, step):
+                taken = range(start, start + step)
+                queries = jnp.concatenate([packed[one][0, :, part] for one in taken], axis=0)
                 scores = lax.dot_general(
                     queries, keys, (((1,), (1,)), ((), ())), preferred_element_type=jnp.float32
                 )
@@ -69,9 +87,19 @@
                 total = jnp.sum(weights.astype(jnp.float32), axis=1, keepdims=True)
                 mixed = jnp.dot(weights, values, preferred_element_type=jnp.float32) / total
                 mixed = mixed.reshape(step, local_frames, tokens, HEAD) * gates
-                out_ref[start : start + step, :, part] = mixed.reshape(step, rows, HEAD).astype(
-                    out_ref.dtype
-                )
+                mixed = mixed.reshape(step, rows, HEAD).astype(jnp.bfloat16)
+                for place, one in enumerate(taken):
+                    outs[one][:, part] = mixed[place]
+
+
+def exchange(pieces):
+    devices = len(pieces)
+    return [
+        lax.ppermute(piece, AXES, [(one, one ^ offset) for one in range(devices)])
+        if offset
+        else piece
+        for offset, piece in enumerate(pieces)
+    ]
 
 
 def one_head_each(queries, keys, values, slot_of, level_of, gate_table):
@@ -79,34 +107,35 @@
     devices = lax.axis_size("frame") * seq_count
     _, local_frames, tokens, all_width = queries.shape
     rows, width = local_frames * tokens, all_width // devices
-    exchange = functools.partial(
-        lax.all_to_all, axis_name=AXES, split_axis=0, concat_axis=0, tiled=True
-    )
+    device_index = lax.axis_index("frame") * seq_count + lax.axis_index("seq")
+    device_index = device_index.reshape(1)
     packed = pl.pallas_call(
         pack,
-        out_shape=jax.ShapeDtypeStruct((devices, 3, rows, width), queries.dtype),
-        in_specs=[VMEM] * 3,
-        out_specs=VMEM,
+        out_shape=[jax.ShapeDtypeStruct((3, rows, width), queries.dtype)] * devices,
+        in_specs=[SMEM] + [pl.BlockSpec(memory_space=pltpu.HBM)] * 3,
+        out_specs=[VMEM] * devices,
+        scratch_shapes=[
+            pltpu.VMEM((3, rows, all_width), queries.dtype),
+            pltpu.SemaphoreType.DMA((3,)),
+        ],
         compiler_params=PARAMS,
-    )(*(taken.reshape(rows, all_width) for taken in (queries, keys, values)))
+    )(device_index, *(taken.reshape(rows, all_width) for taken in (queries, keys, values)))
     packed = exchange(packed)
-    device_index = lax.axis_index("frame") * seq_count + lax.axis_index("seq")
-    gates = lax.dynamic_slice_in_dim(gate_table, device_index * width, width, 1)
     answer = pl.pallas_call(
         functools.partial(attend, group_devices=seq_count, tokens=tokens),
-        out_shape=jax.ShapeDtypeStruct((devices, rows, width), queries.dtype),
-        in_specs=[SMEM, SMEM, VMEM, VMEM],
-        out_specs=VMEM,
+        out_shape=[jax.ShapeDtypeStruct((rows, width), queries.dtype)] * devices,
+        in_specs=[SMEM] * 3 + [VMEM] * (devices + 1),
+        out_specs=[VMEM] * devices,
         compiler_params=PARAMS,
-    )(slot_of, level_of, packed, gates)
+    )(device_index, slot_of, level_of, gate_table, *packed)
     answer = exchange(answer)
     answer = pl.pallas_call(
         unpack,
         out_shape=jax.ShapeDtypeStruct((rows, all_width), queries.dtype),
-        in_specs=[VMEM],
+        in_specs=[SMEM] + [VMEM] * devices,
         out_specs=VMEM,
         compiler_params=PARAMS,
-    )(answer)
+    )(device_index, *answer)
     return answer.reshape(queries.shape)
 
 

time: 37 us -> 60.6 us (1.64)
  the two profiles are of different devices: /device:TPU:0 before, /device:TPU:1 now
where the time goes in v1:
time: 60.6 us; the launch traced here: 60.4 us
  starting transfers between devices  44.1 us (73%)
  waiting for transfers between devices  10.4 us (17%)
  Pallas kernels  3.21 us (5%)
  local copies, waits for them, and re-layouts  2.72 us (4%)
    ppermute x30, starting transfers between devices, exchange(): lax.ppermute(piece, AXES, [(one, one ^ offset) for one in range(devices)])  44.1 us
    ppermute x30, waiting for transfers between devices, exchange(): lax.ppermute(piece, AXES, [(one, one ^ offset) for one in range(devices)])  10.4 us
    unnamed x12, local copies, waits for them, and re-layouts  2.72 us
    pallas_call x1, Pallas kernels, one_head_each(): pl.pallas_call(functools.partial(attend, group_devices=seq_count, tokens=...  1.8 us
  transfers between devices with their start and end apart: 30, of which 5 were waited for; matrix products, arithmetic and copies ran while one was open for 0% of the time, Pallas kernels for 0%

profile of v1, /device:TPU:1, one launch (start us, length us, event | category | flops | bytes accessed | tf_op | source)
XLA Modules:
  0.0 60.4 jit_solution(17007855325284498214)
XLA Ops:
  0.0 0.9 %copy-done = bf16[1,4,8,2048]{3,2,1,0:T(8,128)(2,1)S(1)} copy-done((bf16[1,4,8,2048]{3,2,1,0:T(8,128)(2,1)S(1)}, bf16[1,4,8,2048]{3,2,1,0:T(8,128)(2,1)}, u32[]{:S(2)}) %copy-start) | copy-done | bytes 131096
  0.9 0.9 %copy-done.1 = bf16[1,4,8,2048]{3,2,1,0:T(8,128)(2,1)S(1)} copy-done((bf16[1,4,8,2048]{3,2,1,0:T(8,128)(2,1)S(1)}, bf16[1,4,8,2048]{3,2,1,0:T(8,128)(2,1)}, u32[]{:S(2)}) %copy-start.1) | copy-done | bytes 131096
  1.8 0.9 %copy-done.2 = bf16[1,4,8,2048]{3,2,1,0:T(8,128)(2,1)S(1)} copy-done((bf16[1,4,8,2048]{3,2,1,0:T(8,128)(2,1)S(1)}, bf16[1,4,8,2048]{3,2,1,0:T(8,128)(2,1)}, u32[]{:S(2)}) %copy-start.2) | copy-done | bytes 131096
  2.7 0.7 %shard_map.64 = (bf16[3,32,128]{2,1,0:T(8,128)(2,1)S(1)}, bf16[3,32,128]{2,1,0:T(8,128)(2,1)S(1)}, bf16[3,32,128]{2,1,0:T(8,128)(2,1)S(1)}, bf16[3,32,128]{2,1,0...) custom-call(s32[1]{0:T(128)} %bitcast.index_ref, ...), custom_call_target="tpu_custom_call" | custom-call | tf_op jit(solution)/shard_map/pallas_call | solution.py:112
  3.4 2.1 %collective-permute-start = (bf16[3,32,128]{2,1,0:T(8,128)(2,1)S(1)}, bf16[3,32,128]{2,1,0:T(8,128)(2,1)S(1)}, u32[]{:S(2)}, u32[]{:S(2)}) collective-permute-start(bf16[3,32,128]{2,1,0:T(8,128)(2,1)S(1)} %get-tuple-element.38), channel_id=1, source_target_pairs={{0,1},{1,0},{2,3},{3,2},{4,5},{5,4},{6,7},{7,6},{8,9},{9,8},{10,11... | collective-permute-start | bytes 73736 | tf_op jit(solution)/shard_map/ppermute | solution.py:98
  5.6 1.3 %collective-permute-start.1 = (bf16[3,32,128]{2,1,0:T(8,128)(2,1)S(1)}, bf16[3,32,128]{2,1,0:T(8,128)(2,1)S(1)}, u32[]{:S(2)}, u32[]{:S(2)}) collective-permute-start(bf16[3,32,128]{2,1,0:T(8,128)(2,1)S(1)} %get-tuple-element.39), channel_id=1, source_target_pairs={{0,2},{1,3},{2,0},{3,1},{4,6},{5,7},{6,4},{7,5},{8,10},{9,11},{10,... | collective-permute-start | bytes 73736 | tf_op jit(solution)/shard_map/ppermute | solution.py:98
  6.9 0.0 collective-permute-start.2
  6.9 2.4 %collective-permute-start.3 = (bf16[3,32,128]{2,1,0:T(8,128)(2,1)S(1)}, bf16[3,32,128]{2,1,0:T(8,128)(2,1)S(1)}, u32[]{:S(2)}, u32[]{:S(2)}) collective-permute-start(bf16[3,32,128]{2,1,0:T(8,128)(2,1)S(1)} %get-tuple-element.41), channel_id=1, source_target_pairs={{0,4},{1,5},{2,6},{3,7},{4,0},{5,1},{6,2},{7,3},{8,12},{9,13},{10,... | collective-permute-start | bytes 73736 | tf_op jit(solution)/shard_map/ppermute | solution.py:98
  9.3 1.0 %collective-permute-start.4 = (bf16[3,32,128]{2,1,0:T(8,128)(2,1)S(1)}, bf16[3,32,128]{2,1,0:T(8,128)(2,1)S(1)}, u32[]{:S(2)}, u32[]{:S(2)}) collective-permute-start(bf16[3,32,128]{2,1,0:T(8,128)(2,1)S(1)} %get-tuple-element.42), channel_id=1, source_target_pairs={{0,5},{1,4},{2,7},{3,6},{4,1},{5,0},{6,3},{7,2},{8,13},{9,12},{10,... | collective-permute-start | bytes 73736 | tf_op jit(solution)/shard_map/ppermute | solution.py:98
  10.3 0.0 collective-permute-done.refs_1_
  10.3 3.3 %collective-permute-start.5 = (bf16[3,32,128]{2,1,0:T(8,128)(2,1)S(1)}, bf16[3,32,128]{2,1,0:T(8,128)(2,1)S(1)}, u32[]{:S(2)}, u32[]{:S(2)}) collective-permute-start(bf16[3,32,128]{2,1,0:T(8,128)(2,1)S(1)} %get-tuple-element.43), channel_id=1, source_target_pairs={{0,6},{1,7},{2,4},{3,5},{4,2},{5,3},{6,0},{7,1},{8,14},{9,15},{10,... | collective-permute-start | bytes 73736 | tf_op jit(solution)/shard_map/ppermute | solution.py:98
  13.6 0.0 collective-permute-done.1.refs_2_
  13.6 0.0 collective-permute-start.6
  13.7 0.0 collective-permute-done.2.refs_3_
  13.7 2.4 %collective-permute-start.7 = (bf16[3,32,128]{2,1,0:T(8,128)(2,1)S(1)}, bf16[3,32,128]{2,1,0:T(8,128)(2,1)S(1)}, u32[]{:S(2)}, u32[]{:S(2)}) collective-permute-start(bf16[3,32,128]{2,1,0:T(8,128)(2,1)S(1)} %get-tuple-element.45), channel_id=1, source_target_pairs={{0,8},{1,9},{2,10},{3,11},{4,12},{5,13},{6,14},{7,15},{8,0},{9,1},... | collective-permute-start | bytes 73736 | tf_op jit(solution)/shard_map/ppermute | solution.py:98
  16.0 0.0 collective-permute-done.3.refs_4_
  16.0 1.3 %collective-permute-start.8 = (bf16[3,32,128]{2,1,0:T(8,128)(2,1)S(1)}, bf16[3,32,128]{2,1,0:T(8,128)(2,1)S(1)}, u32[]{:S(2)}, u32[]{:S(2)}) collective-permute-start(bf16[3,32,128]{2,1,0:T(8,128)(2,1)S(1)} %get-tuple-element.46), channel_id=1, source_target_pairs={{0,9},{1,8},{2,11},{3,10},{4,13},{5,12},{6,15},{7,14},{8,1},{9,0},... | collective-permute-start | bytes 73736 | tf_op jit(solution)/shard_map/ppermute | solution.py:98
  17.3 0.0 collective-permute-done.4.refs_5_
  17.3 0.6 collective-permute-start.9
  17.9 0.0 collective-permute-done.5.refs_6_
  17.9 1.0 %collective-permute-start.10 = (bf16[3,32,128]{2,1,0:T(8,128)(2,1)S(1)}, bf16[3,32,128]{2,1,0:T(8,128)(2,1)S(1)}, u32[]{:S(2)}, u32[]{:S(2)}) collective-permute-start(bf16[3,32,128]{2,1,0:T(8,128)(2,1)S(1)} %get-tuple-element.48), channel_id=1, source_target_pairs={{0,11},{1,10},{2,9},{3,8},{4,15},{5,14},{6,13},{7,12},{8,3},{9,2},... | collective-permute-start | bytes 73736 | tf_op jit(solution)/shard_map/ppermute | solution.py:98
  19.0 0.1 collective-permute-done.6.refs_7_
  19.0 2.3 %collective-permute-start.11 = (bf16[3,32,128]{2,1,0:T(8,128)(2,1)S(1)}, bf16[3,32,128]{2,1,0:T(8,128)(2,1)S(1)}, u32[]{:S(2)}, u32[]{:S(2)}) collective-permute-start(bf16[3,32,128]{2,1,0:T(8,128)(2,1)S(1)} %get-tuple-element.49), channel_id=1, source_target_pairs={{0,12},{1,13},{2,14},{3,15},{4,8},{5,9},{6,10},{7,11},{8,4},{9,5},... | collective-permute-start | bytes 73736 | tf_op jit(solution)/shard_map/ppermute | solution.py:98
  21.3 0.0 collective-permute-done.7.refs_8_
  21.3 1.3 %collective-permute-start.12 = (bf16[3,32,128]{2,1,0:T(8,128)(2,1)S(1)}, bf16[3,32,128]{2,1,0:T(8,128)(2,1)S(1)}, u32[]{:S(2)}, u32[]{:S(2)}) collective-permute-start(bf16[3,32,128]{2,1,0:T(8,128)(2,1)S(1)} %get-tuple-element.50), channel_id=1, source_target_pairs={{0,13},{1,12},{2,15},{3,14},{4,9},{5,8},{6,11},{7,10},{8,5},{9,4},... | collective-permute-start | bytes 73736 | tf_op jit(solution)/shard_map/ppermute | solution.py:98
  22.6 0.0 collective-permute-done.8.refs_9_
  22.6 3.6 %collective-permute-start.13 = (bf16[3,32,128]{2,1,0:T(8,128)(2,1)S(1)}, bf16[3,32,128]{2,1,0:T(8,128)(2,1)S(1)}, u32[]{:S(2)}, u32[]{:S(2)}) collective-permute-start(bf16[3,32,128]{2,1,0:T(8,128)(2,1)S(1)} %get-tuple-element.51), channel_id=1, source_target_pairs={{0,14},{1,15},{2,12},{3,13},{4,10},{5,11},{6,8},{7,9},{8,6},{9,7},... | collective-permute-start | bytes 73736 | tf_op jit(solution)/shard_map/ppermute | solution.py:98
  26.3 0.0 collective-permute-done.9.refs_10_
  26.3 0.1 collective-permute-start.14
  26.4 0.0 collective-permute-done.10.refs_11_
  26.4 0.0 collective-permute-done.11.refs_12_
  26.4 0.0 collective-permute-done.12.refs_13_
  26.4 1.7 %collective-permute-done.13.refs_14_ = bf16[3,32,128]{2,1,0:T(8,128)(2,1)S(1)} collective-permute-done((bf16[3,32,128]{2,1,0:T(8,128)(2,1)S(1)}, bf16[3,32,128]{2,1,0:T(8,128)(2,1)S(1)}, u32[]{:S(2)}, u32[]{:S(2)}) %collective-permute-start.13) | collective-permute-done | bytes 24608 | tf_op jit(solution)/shard_map/ppermute | solution.py:98
  28.1 4.2 %collective-permute-done.14.refs_15_ = bf16[3,32,128]{2,1,0:T(8,128)(2,1)S(1)} collective-permute-done((bf16[3,32,128]{2,1,0:T(8,128)(2,1)S(1)}, bf16[3,32,128]{2,1,0:T(8,128)(2,1)S(1)}, u32[]{:S(2)}, u32[]{:S(2)}) %collective-permute-start.14) | collective-permute-done | bytes 24608 | tf_op jit(solution)/shard_map/ppermute | solution.py:98
  32.3 1.8 %shard_map.65 = (bf16[32,128]{1,0:T(8,128)(2,1)S(1)}, bf16[32,128]{1,0:T(8,128)(2,1)S(1)}, bf16[32,128]{1,0:T(8,128)(2,1)S(1)}, bf16[32,128]{1,0:T(8,128)(2,1)S(...) custom-call(s32[1]{0:T(128)} %bitcast.index_ref, ...), custom_call_target="tpu_custom_call" | custom-call | tf_op jit(solution)/shard_map/pallas_call | solution.py:124
  34.1 0.3 collective-permute-start.15
  34.4 0.0 collective-permute-start.16
  34.4 2.4 %collective-permute-start.17 = (bf16[32,128]{1,0:T(8,128)(2,1)S(1)}, bf16[32,128]{1,0:T(8,128)(2,1)S(1)}, u32[]{:S(2)}, u32[]{:S(2)}) collective-permute-start(bf16[32,128]{1,0:T(8,128)(2,1)S(1)} %get-tuple-element.56), channel_id=1, source_target_pairs={{0,3},{1,2},{2,1},{3,0},{4,7},{5,6},{6,5},{7,4},{8,11},{9,10},{10,... | collective-permute-start | bytes 24584 | tf_op jit(solution)/shard_map/ppermute | solution.py:98
  36.8 1.0 %collective-permute-start.18 = (bf16[32,128]{1,0:T(8,128)(2,1)S(1)}, bf16[32,128]{1,0:T(8,128)(2,1)S(1)}, u32[]{:S(2)}, u32[]{:S(2)}) collective-permute-start(bf16[32,128]{1,0:T(8,128)(2,1)S(1)} %get-tuple-element.57), channel_id=1, source_target_pairs={{0,4},{1,5},{2,6},{3,7},{4,0},{5,1},{6,2},{7,3},{8,12},{9,13},{10,... | collective-permute-start | bytes 24584 | tf_op jit(solution)/shard_map/ppermute | solution.py:98
  37.8 1.3 %collective-permute-start.19 = (bf16[32,128]{1,0:T(8,128)(2,1)S(1)}, bf16[32,128]{1,0:T(8,128)(2,1)S(1)}, u32[]{:S(2)}, u32[]{:S(2)}) collective-permute-start(bf16[32,128]{1,0:T(8,128)(2,1)S(1)} %get-tuple-element.58), channel_id=1, source_target_pairs={{0,5},{1,4},{2,7},{3,6},{4,1},{5,0},{6,3},{7,2},{8,13},{9,12},{10,... | collective-permute-start | bytes 24584 | tf_op jit(solution)/shard_map/ppermute | solution.py:98
  39.1 0.0 collective-permute-done.15.refs_1_
  39.1 3.1 %collective-permute-start.20 = (bf16[32,128]{1,0:T(8,128)(2,1)S(1)}, bf16[32,128]{1,0:T(8,128)(2,1)S(1)}, u32[]{:S(2)}, u32[]{:S(2)}) collective-permute-start(bf16[32,128]{1,0:T(8,128)(2,1)S(1)} %get-tuple-element.59), channel_id=1, source_target_pairs={{0,6},{1,7},{2,4},{3,5},{4,2},{5,3},{6,0},{7,1},{8,14},{9,15},{10,... | collective-permute-start | bytes 24584 | tf_op jit(solution)/shard_map/ppermute | solution.py:98
  42.3 0.0 collective-permute-done.16.refs_2_
  42.3 1.0 %collective-permute-start.21 = (bf16[32,128]{1,0:T(8,128)(2,1)S(1)}, bf16[32,128]{1,0:T(8,128)(2,1)S(1)}, u32[]{:S(2)}, u32[]{:S(2)}) collective-permute-start(bf16[32,128]{1,0:T(8,128)(2,1)S(1)} %get-tuple-element.60), channel_id=1, source_target_pairs={{0,7},{1,6},{2,5},{3,4},{4,3},{5,2},{6,1},{7,0},{8,15},{9,14},{10,... | collective-permute-start | bytes 24584 | tf_op jit(solution)/shard_map/ppermute | solution.py:98
  43.3 0.0 collective-permute-done.17.refs_3_
  43.3 2.0 %collective-permute-start.22 = (bf16[32,128]{1,0:T(8,128)(2,1)S(1)}, bf16[32,128]{1,0:T(8,128)(2,1)S(1)}, u32[]{:S(2)}, u32[]{:S(2)}) collective-permute-start(bf16[32,128]{1,0:T(8,128)(2,1)S(1)} %get-tuple-element.61), channel_id=1, source_target_pairs={{0,8},{1,9},{2,10},{3,11},{4,12},{5,13},{6,14},{7,15},{8,0},{9,1},... | collective-permute-start | bytes 24584 | tf_op jit(solution)/shard_map/ppermute | solution.py:98
  45.4 0.0 collective-permute-done.18.refs_4_
  45.4 0.3 collective-permute-start.23
  45.7 0.0 collective-permute-done.19.refs_5_
  45.7 0.0 collective-permute-start.24
  45.7 0.0 collective-permute-done.20.refs_6_
  45.7 2.6 %collective-permute-start.25 = (bf16[32,128]{1,0:T(8,128)(2,1)S(1)}, bf16[32,128]{1,0:T(8,128)(2,1)S(1)}, u32[]{:S(2)}, u32[]{:S(2)}) collective-permute-start(bf16[32,128]{1,0:T(8,128)(2,1)S(1)} %get-tuple-element.64), channel_id=1, source_target_pairs={{0,11},{1,10},{2,9},{3,8},{4,15},{5,14},{6,13},{7,12},{8,3},{9,2},... | collective-permute-start | bytes 24584 | tf_op jit(solution)/shard_map/ppermute | solution.py:98
  48.3 0.0 collective-permute-done.21.refs_7_
  48.3 0.0 collective-permute-start.26
  48.3 0.0 collective-permute-done.22.refs_8_
  48.3 2.7 %collective-permute-start.27 = (bf16[32,128]{1,0:T(8,128)(2,1)S(1)}, bf16[32,128]{1,0:T(8,128)(2,1)S(1)}, u32[]{:S(2)}, u32[]{:S(2)}) collective-permute-start(bf16[32,128]{1,0:T(8,128)(2,1)S(1)} %get-tuple-element.66), channel_id=1, source_target_pairs={{0,13},{1,12},{2,15},{3,14},{4,9},{5,8},{6,11},{7,10},{8,5},{9,4},... | collective-permute-start | bytes 24584 | tf_op jit(solution)/shard_map/ppermute | solution.py:98
  51.0 0.0 collective-permute-done.23.refs_9_
  51.0 3.0 %collective-permute-start.28 = (bf16[32,128]{1,0:T(8,128)(2,1)S(1)}, bf16[32,128]{1,0:T(8,128)(2,1)S(1)}, u32[]{:S(2)}, u32[]{:S(2)}) collective-permute-start(bf16[32,128]{1,0:T(8,128)(2,1)S(1)} %get-tuple-element.67), channel_id=1, source_target_pairs={{0,14},{1,15},{2,12},{3,13},{4,10},{5,11},{6,8},{7,9},{8,6},{9,7},... | collective-permute-start | bytes 24584 | tf_op jit(solution)/shard_map/ppermute | solution.py:98
  54.0 0.0 collective-permute-done.24.refs_10_
  54.0 1.4 %collective-permute-start.29 = (bf16[32,128]{1,0:T(8,128)(2,1)S(1)}, bf16[32,128]{1,0:T(8,128)(2,1)S(1)}, u32[]{:S(2)}, u32[]{:S(2)}) collective-permute-start(bf16[32,128]{1,0:T(8,128)(2,1)S(1)} %get-tuple-element.68), channel_id=1, source_target_pairs={{0,15},{1,14},{2,13},{3,12},{4,11},{5,10},{6,9},{7,8},{8,7},{9,6},... | collective-permute-start | bytes 24584 | tf_op jit(solution)/shard_map/ppermute | solution.py:98
  55.4 0.0 collective-permute-done.27.refs_13_
  55.4 0.5 collective-permute-done.28.refs_14_
  55.9 3.8 %collective-permute-done.29.refs_15_ = bf16[32,128]{1,0:T(8,128)(2,1)S(1)} collective-permute-done((bf16[32,128]{1,0:T(8,128)(2,1)S(1)}, bf16[32,128]{1,0:T(8,128)(2,1)S(1)}, u32[]{:S(2)}, u32[]{:S(2)}) %collective-permute-start.29) | collective-permute-done | bytes 8224 | tf_op jit(solution)/shard_map/ppermute | solution.py:98
  59.7 0.7 %shard_map.66 = bf16[32,2048]{1,0:T(8,128)(2,1)} custom-call(s32[1]{0:T(128)} %bitcast.index_ref, bf16[32,128]{1,0:T(8,128)(2,1)S(1)} %get-tuple-element.53.refs_0_, bf16[32,128]{1,0:T(8,128)(2,1)S(1)} %collective-permute-done.15.refs_1_, bf16[32,128]{1,0:T(8,128)(2,1)S(1)} %collective-permute-done.16.refs_2_, ...), custom_call_target="tpu_custom_call" | custom-call | tf_op jit(solution)/shard_map/pallas_call | solution.py:132
  (11 shorter events, 0.0 us)
Async XLA Ops:
  0.0 0.9 %copy-start = (bf16[1,4,8,2048]{3,2,1,0:T(8,128)(2,1)S(1)}, bf16[1,4,8,2048]{3,2,1,0:T(8,128)(2,1)}, u32[]{:S(2)}) copy-start(bf16[1,4,8,2048]{3,2,1,0:T(8,128)(2,1)} %param.6) | copy-start | bytes 393220
  0.9 0.9 %copy-start.1 = (bf16[1,4,8,2048]{3,2,1,0:T(8,128)(2,1)S(1)}, bf16[1,4,8,2048]{3,2,1,0:T(8,128)(2,1)}, u32[]{:S(2)}) copy-start(bf16[1,4,8,2048]{3,2,1,0:T(8,128)(2,1)} %param.7) | copy-start | bytes 393220
  1.8 0.9 %copy-start.2 = (bf16[1,4,8,2048]{3,2,1,0:T(8,128)(2,1)S(1)}, bf16[1,4,8,2048]{3,2,1,0:T(8,128)(2,1)}, u32[]{:S(2)}) copy-start(bf16[1,4,8,2048]{3,2,1,0:T(8,128)(2,1)} %param.8) | copy-start | bytes 393220
  2.7 29.5 %copy-start.3 = (f32[8,2048]{1,0:T(8,128)S(1)}, f32[8,2048]{1,0:T(8,128)}, u32[]{:S(2)}) copy-start(f32[8,2048]{1,0:T(8,128)} %gate_ref.1) | copy-start | bytes 196612
  3.4 6.8 %collective-permute-start = (bf16[3,32,128]{2,1,0:T(8,128)(2,1)S(1)}, bf16[3,32,128]{2,1,0:T(8,128)(2,1)S(1)}, u32[]{:S(2)}, u32[]{:S(2)}) collective-permute-start(bf16[3,32,128]{2,1,0:T(8,128)(2,1)S(1)} %get-tuple-element.38), channel_id=1, source_target_pairs={{0,1},{1,0},{2,3},{3,2},{4,5},{5,4},{6,7},{7,6},{8,9},{9,8},{10,11... | collective-permute-start | bytes 73736 | tf_op jit(solution)/shard_map/ppermute | solution.py:98
  5.6 8.1 %collective-permute-start.1 = (bf16[3,32,128]{2,1,0:T(8,128)(2,1)S(1)}, bf16[3,32,128]{2,1,0:T(8,128)(2,1)S(1)}, u32[]{:S(2)}, u32[]{:S(2)}) collective-permute-start(bf16[3,32,128]{2,1,0:T(8,128)(2,1)S(1)} %get-tuple-element.39), channel_id=1, source_target_pairs={{0,2},{1,3},{2,0},{3,1},{4,6},{5,7},{6,4},{7,5},{8,10},{9,11},{10,... | collective-permute-start | bytes 73736 | tf_op jit(solution)/shard_map/ppermute | solution.py:98
  6.9 6.8 %collective-permute-start.2 = (bf16[3,32,128]{2,1,0:T(8,128)(2,1)S(1)}, bf16[3,32,128]{2,1,0:T(8,128)(2,1)S(1)}, u32[]{:S(2)}, u32[]{:S(2)}) collective-permute-start(bf16[3,32,128]{2,1,0:T(8,128)(2,1)S(1)} %get-tuple-element.40), channel_id=1, source_target_pairs={{0,3},{1,2},{2,1},{3,0},{4,7},{5,6},{6,5},{7,4},{8,11},{9,10},{10,... | collective-permute-start | bytes 73736 | tf_op jit(solution)/shard_map/ppermute | solution.py:98
  6.9 9.2 %collective-permute-start.3 = (bf16[3,32,128]{2,1,0:T(8,128)(2,1)S(1)}, bf16[3,32,128]{2,1,0:T(8,128)(2,1)S(1)}, u32[]{:S(2)}, u32[]{:S(2)}) collective-permute-start(bf16[3,32,128]{2,1,0:T(8,128)(2,1)S(1)} %get-tuple-element.41), channel_id=1, source_target_pairs={{0,4},{1,5},{2,6},{3,7},{4,0},{5,1},{6,2},{7,3},{8,12},{9,13},{10,... | collective-permute-start | bytes 73736 | tf_op jit(solution)/shard_map/ppermute | solution.py:98
  9.3 8.0 %collective-permute-start.4 = (bf16[3,32,128]{2,1,0:T(8,128)(2,1)S(1)}, bf16[3,32,128]{2,1,0:T(8,128)(2,1)S(1)}, u32[]{:S(2)}, u32[]{:S(2)}) collective-permute-start(bf16[3,32,128]{2,1,0:T(8,128)(2,1)S(1)} %get-tuple-element.42), channel_id=1, source_target_pairs={{0,5},{1,4},{2,7},{3,6},{4,1},{5,0},{6,3},{7,2},{8,13},{9,12},{10,... | collective-permute-start | bytes 73736 | tf_op jit(solution)/shard_map/ppermute | solution.py:98
  10.3 7.6 %collective-permute-start.5 = (bf16[3,32,128]{2,1,0:T(8,128)(2,1)S(1)}, bf16[3,32,128]{2,1,0:T(8,128)(2,1)S(1)}, u32[]{:S(2)}, u32[]{:S(2)}) collective-permute-start(bf16[3,32,128]{2,1,0:T(8,128)(2,1)S(1)} %get-tuple-element.43), channel_id=1, source_target_pairs={{0,6},{1,7},{2,4},{3,5},{4,2},{5,3},{6,0},{7,1},{8,14},{9,15},{10,... | collective-permute-start | bytes 73736 | tf_op jit(solution)/shard_map/ppermute | solution.py:98
  13.6 5.4 %collective-permute-start.6 = (bf16[3,32,128]{2,1,0:T(8,128)(2,1)S(1)}, bf16[3,32,128]{2,1,0:T(8,128)(2,1)S(1)}, u32[]{:S(2)}, u32[]{:S(2)}) collective-permute-start(bf16[3,32,128]{2,1,0:T(8,128)(2,1)S(1)} %get-tuple-element.44), channel_id=1, source_target_pairs={{0,7},{1,6},{2,5},{3,4},{4,3},{5,2},{6,1},{7,0},{8,15},{9,14},{10,... | collective-permute-start | bytes 73736 | tf_op jit(solution)/shard_map/ppermute | solution.py:98
  13.7 7.6 %collective-permute-start.7 = (bf16[3,32,128]{2,1,0:T(8,128)(2,1)S(1)}, bf16[3,32,128]{2,1,0:T(8,128)(2,1)S(1)}, u32[]{:S(2)}, u32[]{:S(2)}) collective-permute-start(bf16[3,32,128]{2,1,0:T(8,128)(2,1)S(1)} %get-tuple-element.45), channel_id=1, source_target_pairs={{0,8},{1,9},{2,10},{3,11},{4,12},{5,13},{6,14},{7,15},{8,0},{9,1},... | collective-permute-start | bytes 73736 | tf_op jit(solution)/shard_map/ppermute | solution.py:98
  16.0 6.6 %collective-permute-start.8 = (bf16[3,32,128]{2,1,0:T(8,128)(2,1)S(1)}, bf16[3,32,128]{2,1,0:T(8,128)(2,1)S(1)}, u32[]{:S(2)}, u32[]{:S(2)}) collective-permute-start(bf16[3,32,128]{2,1,0:T(8,128)(2,1)S(1)} %get-tuple-element.46), channel_id=1, source_target_pairs={{0,9},{1,8},{2,11},{3,10},{4,13},{5,12},{6,15},{7,14},{8,1},{9,0},... | collective-permute-start | bytes 73736 | tf_op jit(solution)/shard_map/ppermute | solution.py:98
  17.3 9.0 %collective-permute-start.9 = (bf16[3,32,128]{2,1,0:T(8,128)(2,1)S(1)}, bf16[3,32,128]{2,1,0:T(8,128)(2,1)S(1)}, u32[]{:S(2)}, u32[]{:S(2)}) collective-permute-start(bf16[3,32,128]{2,1,0:T(8,128)(2,1)S(1)} %get-tuple-element.47), channel_id=1, source_target_pairs={{0,10},{1,11},{2,8},{3,9},{4,14},{5,15},{6,12},{7,13},{8,2},{9,3},... | collective-permute-start | bytes 73736 | tf_op jit(solution)/shard_map/ppermute | solution.py:98
  17.9 8.5 %collective-permute-start.10 = (bf16[3,32,128]{2,1,0:T(8,128)(2,1)S(1)}, bf16[3,32,128]{2,1,0:T(8,128)(2,1)S(1)}, u32[]{:S(2)}, u32[]{:S(2)}) collective-permute-start(bf16[3,32,128]{2,1,0:T(8,128)(2,1)S(1)} %get-tuple-element.48), channel_id=1, source_target_pairs={{0,11},{1,10},{2,9},{3,8},{4,15},{5,14},{6,13},{7,12},{8,3},{9,2},... | collective-permute-start | bytes 73736 | tf_op jit(solution)/shard_map/ppermute | solution.py:98
  19.0 7.4 %collective-permute-start.11 = (bf16[3,32,128]{2,1,0:T(8,128)(2,1)S(1)}, bf16[3,32,128]{2,1,0:T(8,128)(2,1)S(1)}, u32[]{:S(2)}, u32[]{:S(2)}) collective-permute-start(bf16[3,32,128]{2,1,0:T(8,128)(2,1)S(1)} %get-tuple-element.49), channel_id=1, source_target_pairs={{0,12},{1,13},{2,14},{3,15},{4,8},{5,9},{6,10},{7,11},{8,4},{9,5},... | collective-permute-start | bytes 73736 | tf_op jit(solution)/shard_map/ppermute | solution.py:98
  21.3 5.1 %collective-permute-start.12 = (bf16[3,32,128]{2,1,0:T(8,128)(2,1)S(1)}, bf16[3,32,128]{2,1,0:T(8,128)(2,1)S(1)}, u32[]{:S(2)}, u32[]{:S(2)}) collective-permute-start(bf16[3,32,128]{2,1,0:T(8,128)(2,1)S(1)} %get-tuple-element.50), channel_id=1, source_target_pairs={{0,13},{1,12},{2,15},{3,14},{4,9},{5,8},{6,11},{7,10},{8,5},{9,4},... | collective-permute-start | bytes 73736 | tf_op jit(solution)/shard_map/ppermute | solution.py:98
  22.6 5.4 %collective-permute-start.13 = (bf16[3,32,128]{2,1,0:T(8,128)(2,1)S(1)}, bf16[3,32,128]{2,1,0:T(8,128)(2,1)S(1)}, u32[]{:S(2)}, u32[]{:S(2)}) collective-permute-start(bf16[3,32,128]{2,1,0:T(8,128)(2,1)S(1)} %get-tuple-element.51), channel_id=1, source_target_pairs={{0,14},{1,15},{2,12},{3,13},{4,10},{5,11},{6,8},{7,9},{8,6},{9,7},... | collective-permute-start | bytes 73736 | tf_op jit(solution)/shard_map/ppermute | solution.py:98
  26.3 6.0 %copy-start.5 = (s32[2,4]{1,0:T(2,128)S(1)}, s32[2,4]{1,0:T(2,128)}, u32[]{:S(2)}) copy-start(s32[2,4]{1,0:T(2,128)} %level_ref.1) | copy-start | bytes 100
  26.3 6.0 %copy-start.4 = (s32[2,4]{1,0:T(2,128)S(1)}, s32[2,4]{1,0:T(2,128)}, u32[]{:S(2)}) copy-start(s32[2,4]{1,0:T(2,128)} %slot_ref.1) | copy-start | bytes 100
  26.3 5.9 %collective-permute-start.14 = (bf16[3,32,128]{2,1,0:T(8,128)(2,1)S(1)}, bf16[3,32,128]{2,1,0:T(8,128)(2,1)S(1)}, u32[]{:S(2)}, u32[]{:S(2)}) collective-permute-start(bf16[3,32,128]{2,1,0:T(8,128)(2,1)S(1)} %get-tuple-element.52), channel_id=1, source_target_pairs={{0,15},{1,14},{2,13},{3,12},{4,11},{5,10},{6,9},{7,8},{8,7},{9,6},... | collective-permute-start | bytes 73736 | tf_op jit(solution)/shard_map/ppermute | solution.py:98
  34.1 5.1 %collective-permute-start.15 = (bf16[32,128]{1,0:T(8,128)(2,1)S(1)}, bf16[32,128]{1,0:T(8,128)(2,1)S(1)}, u32[]{:S(2)}, u32[]{:S(2)}) collective-permute-start(bf16[32,128]{1,0:T(8,128)(2,1)S(1)} %get-tuple-element.54), channel_id=1, source_target_pairs={{0,1},{1,0},{2,3},{3,2},{4,5},{5,4},{6,7},{7,6},{8,9},{9,8},{10,11... | collective-permute-start | bytes 24584 | tf_op jit(solution)/shard_map/ppermute | solution.py:98
  34.4 7.9 %collective-permute-start.16 = (bf16[32,128]{1,0:T(8,128)(2,1)S(1)}, bf16[32,128]{1,0:T(8,128)(2,1)S(1)}, u32[]{:S(2)}, u32[]{:S(2)}) collective-permute-start(bf16[32,128]{1,0:T(8,128)(2,1)S(1)} %get-tuple-element.55), channel_id=1, source_target_pairs={{0,2},{1,3},{2,0},{3,1},{4,6},{5,7},{6,4},{7,5},{8,10},{9,11},{10,... | collective-permute-start | bytes 24584 | tf_op jit(solution)/shard_map/ppermute | solution.py:98
  34.4 8.9 %collective-permute-start.17 = (bf16[32,128]{1,0:T(8,128)(2,1)S(1)}, bf16[32,128]{1,0:T(8,128)(2,1)S(1)}, u32[]{:S(2)}, u32[]{:S(2)}) collective-permute-start(bf16[32,128]{1,0:T(8,128)(2,1)S(1)} %get-tuple-element.56), channel_id=1, source_target_pairs={{0,3},{1,2},{2,1},{3,0},{4,7},{5,6},{6,5},{7,4},{8,11},{9,10},{10,... | collective-permute-start | bytes 24584 | tf_op jit(solution)/shard_map/ppermute | solution.py:98
  36.8 8.6 %collective-permute-start.18 = (bf16[32,128]{1,0:T(8,128)(2,1)S(1)}, bf16[32,128]{1,0:T(8,128)(2,1)S(1)}, u32[]{:S(2)}, u32[]{:S(2)}) collective-permute-start(bf16[32,128]{1,0:T(8,128)(2,1)S(1)} %get-tuple-element.57), channel_id=1, source_target_pairs={{0,4},{1,5},{2,6},{3,7},{4,0},{5,1},{6,2},{7,3},{8,12},{9,13},{10,... | collective-permute-start | bytes 24584 | tf_op jit(solution)/shard_map/ppermute | solution.py:98
  37.8 7.8 %collective-permute-start.19 = (bf16[32,128]{1,0:T(8,128)(2,1)S(1)}, bf16[32,128]{1,0:T(8,128)(2,1)S(1)}, u32[]{:S(2)}, u32[]{:S(2)}) collective-permute-start(bf16[32,128]{1,0:T(8,128)(2,1)S(1)} %get-tuple-element.58), channel_id=1, source_target_pairs={{0,5},{1,4},{2,7},{3,6},{4,1},{5,0},{6,3},{7,2},{8,13},{9,12},{10,... | collective-permute-start | bytes 24584 | tf_op jit(solution)/shard_map/ppermute | solution.py:98
  39.1 6.5 %collective-permute-start.20 = (bf16[32,128]{1,0:T(8,128)(2,1)S(1)}, bf16[32,128]{1,0:T(8,128)(2,1)S(1)}, u32[]{:S(2)}, u32[]{:S(2)}) collective-permute-start(bf16[32,128]{1,0:T(8,128)(2,1)S(1)} %get-tuple-element.59), channel_id=1, source_target_pairs={{0,6},{1,7},{2,4},{3,5},{4,2},{5,3},{6,0},{7,1},{8,14},{9,15},{10,... | collective-permute-start | bytes 24584 | tf_op jit(solution)/shard_map/ppermute | solution.py:98
  42.3 6.0 %collective-permute-start.21 = (bf16[32,128]{1,0:T(8,128)(2,1)S(1)}, bf16[32,128]{1,0:T(8,128)(2,1)S(1)}, u32[]{:S(2)}, u32[]{:S(2)}) collective-permute-start(bf16[32,128]{1,0:T(8,128)(2,1)S(1)} %get-tuple-element.60), channel_id=1, source_target_pairs={{0,7},{1,6},{2,5},{3,4},{4,3},{5,2},{6,1},{7,0},{8,15},{9,14},{10,... | collective-permute-start | bytes 24584 | tf_op jit(solution)/shard_map/ppermute | solution.py:98
  43.3 4.9 %collective-permute-start.22 = (bf16[32,128]{1,0:T(8,128)(2,1)S(1)}, bf16[32,128]{1,0:T(8,128)(2,1)S(1)}, u32[]{:S(2)}, u32[]{:S(2)}) collective-permute-start(bf16[32,128]{1,0:T(8,128)(2,1)S(1)} %get-tuple-element.61), channel_id=1, source_target_pairs={{0,8},{1,9},{2,10},{3,11},{4,12},{5,13},{6,14},{7,15},{8,0},{9,1},... | collective-permute-start | bytes 24584 | tf_op jit(solution)/shard_map/ppermute | solution.py:98
  45.4 5.6 %collective-permute-start.23 = (bf16[32,128]{1,0:T(8,128)(2,1)S(1)}, bf16[32,128]{1,0:T(8,128)(2,1)S(1)}, u32[]{:S(2)}, u32[]{:S(2)}) collective-permute-start(bf16[32,128]{1,0:T(8,128)(2,1)S(1)} %get-tuple-element.62), channel_id=1, source_target_pairs={{0,9},{1,8},{2,11},{3,10},{4,13},{5,12},{6,15},{7,14},{8,1},{9,0},... | collective-permute-start | bytes 24584 | tf_op jit(solution)/shard_map/ppermute | solution.py:98
  45.7 8.3 %collective-permute-start.24 = (bf16[32,128]{1,0:T(8,128)(2,1)S(1)}, bf16[32,128]{1,0:T(8,128)(2,1)S(1)}, u32[]{:S(2)}, u32[]{:S(2)}) collective-permute-start(bf16[32,128]{1,0:T(8,128)(2,1)S(1)} %get-tuple-element.63), channel_id=1, source_target_pairs={{0,10},{1,11},{2,8},{3,9},{4,14},{5,15},{6,12},{7,13},{8,2},{9,3},... | collective-permute-start | bytes 24584 | tf_op jit(solution)/shard_map/ppermute | solution.py:98
  45.7 9.7 %collective-permute-start.25 = (bf16[32,128]{1,0:T(8,128)(2,1)S(1)}, bf16[32,128]{1,0:T(8,128)(2,1)S(1)}, u32[]{:S(2)}, u32[]{:S(2)}) collective-permute-start(bf16[32,128]{1,0:T(8,128)(2,1)S(1)} %get-tuple-element.64), channel_id=1, source_target_pairs={{0,11},{1,10},{2,9},{3,8},{4,15},{5,14},{6,13},{7,12},{8,3},{9,2},... | collective-permute-start | bytes 24584 | tf_op jit(solution)/shard_map/ppermute | solution.py:98
  48.3 7.1 %collective-permute-start.26 = (bf16[32,128]{1,0:T(8,128)(2,1)S(1)}, bf16[32,128]{1,0:T(8,128)(2,1)S(1)}, u32[]{:S(2)}, u32[]{:S(2)}) collective-permute-start(bf16[32,128]{1,0:T(8,128)(2,1)S(1)} %get-tuple-element.65), channel_id=1, source_target_pairs={{0,12},{1,13},{2,14},{3,15},{4,8},{5,9},{6,10},{7,11},{8,4},{9,5},... | collective-permute-start | bytes 24584 | tf_op jit(solution)/shard_map/ppermute | solution.py:98
  48.3 7.1 %collective-permute-start.27 = (bf16[32,128]{1,0:T(8,128)(2,1)S(1)}, bf16[32,128]{1,0:T(8,128)(2,1)S(1)}, u32[]{:S(2)}, u32[]{:S(2)}) collective-permute-start(bf16[32,128]{1,0:T(8,128)(2,1)S(1)} %get-tuple-element.66), channel_id=1, source_target_pairs={{0,13},{1,12},{2,15},{3,14},{4,9},{5,8},{6,11},{7,10},{8,5},{9,4},... | collective-permute-start | bytes 24584 | tf_op jit(solution)/shard_map/ppermute | solution.py:98
  51.0 4.9 %collective-permute-start.28 = (bf16[32,128]{1,0:T(8,128)(2,1)S(1)}, bf16[32,128]{1,0:T(8,128)(2,1)S(1)}, u32[]{:S(2)}, u32[]{:S(2)}) collective-permute-start(bf16[32,128]{1,0:T(8,128)(2,1)S(1)} %get-tuple-element.67), channel_id=1, source_target_pairs={{0,14},{1,15},{2,12},{3,13},{4,10},{5,11},{6,8},{7,9},{8,6},{9,7},... | collective-permute-start | bytes 24584 | tf_op jit(solution)/shard_map/ppermute | solution.py:98
  54.0 5.8 %collective-permute-start.29 = (bf16[32,128]{1,0:T(8,128)(2,1)S(1)}, bf16[32,128]{1,0:T(8,128)(2,1)S(1)}, u32[]{:S(2)}, u32[]{:S(2)}) collective-permute-start(bf16[32,128]{1,0:T(8,128)(2,1)S(1)} %get-tuple-element.68), channel_id=1, source_target_pairs={{0,15},{1,14},{2,13},{3,12},{4,11},{5,10},{6,9},{7,8},{8,7},{9,6},... | collective-permute-start | bytes 24584 | tf_op jit(solution)/shard_map/ppermute | solution.py:98

commit v2 on v0

v2 whole, which is shorter than its diff:
```python
import functools
import math

import jax
import jax.numpy as jnp
from jax import lax
from jax.experimental import pallas as pl
from jax.experimental.pallas import tpu as pltpu
from jax.sharding import PartitionSpec as P

H = 16
HEAD = 128
AXES = ("frame", "seq")
SMEM = pl.BlockSpec(memory_space=pltpu.SMEM)
VMEM = pl.BlockSpec(memory_space=pltpu.VMEM)
PARAMS = pltpu.CompilerParams(vmem_limit_bytes=32 * 1024 * 1024)


def pack(query_ref, key_ref, value_ref, pair_ref, own_ref, held_ref, sems):
    copies = [
        pltpu.make_async_copy(ref, held_ref.at[place], sems.at[place])
        for place, ref in enumerate((key_ref, value_ref, query_ref))
    ]
    for copy in copies:
        copy.start()
    width = own_ref.shape[-1]
    for place, copy in enumerate(copies):
        copy.wait()
        for device in range(own_ref.shape[0]):
            taken = held_ref[place, :, device * width : (device + 1) * width]
            if place < 2:
                pair_ref[device, place] = taken
            else:
                own_ref[device] = taken


def unpack(held_ref, out_ref):
    width = held_ref.shape[-1]
    for device in range(held_ref.shape[0]):
        out_ref[:, device * width : (device + 1) * width] = held_ref[device]


def attend(index_ref, slot_ref, level_ref, gate_ref, query_ref, *refs, tokens):
    pair_refs, out_ref = refs[:-1], refs[-1]
    group_count = len(pair_refs)
    devices, _, rows, width = pair_refs[0].shape
    local_frames = rows // tokens
    key_count = group_count * devices * rows
    group = index_ref[0]
    index = lax.broadcasted_iota(jnp.int32, (1, key_count), 1)
    frame = (index // (devices * rows) + group) % group_count * local_frames
    frame = frame + index // tokens % local_frames
    key_slots = jnp.zeros((1, key_count), jnp.int32)
    for one in range(group_count * local_frames):
        slot = slot_ref[one // local_frames, one % local_frames]
        key_slots = jnp.where(frame == one, slot, key_slots)
    shown = []
    for local in range(local_frames):
        visible = key_slots <= slot_ref[group, local]
        shown.append(jnp.where(visible, 0.0, -jnp.inf).reshape(1, 1, 1, key_count))
    shown = jnp.concatenate(shown, axis=1)
    scale = math.log2(math.e) / math.sqrt(HEAD)
    step = max(1, min(devices, 128 // rows))
    for column in range(0, width, HEAD):
        part = pl.ds(column, HEAD)
        gate_column = pl.ds(pl.multiple_of(index_ref[1] * width + column, HEAD), HEAD)
        gate_block = gate_ref[:, gate_column]
        level_rows = lax.broadcasted_iota(jnp.int32, gate_block.shape, 0)
        gates = []
        for local in range(local_frames):
            gate = jnp.where(level_rows == level_ref[group, local], gate_block, 0.0)
            gates.append(jnp.sum(gate, axis=0).reshape(1, 1, 1, HEAD))
        gates = jnp.concatenate(gates, axis=1)
        keys, values = (
            jnp.concatenate(
                [ref[:, place, :, part].reshape(devices * rows, HEAD) for ref in pair_refs]
            )
            for place in range(2)
        )
        for start in range(0, devices, step):
            queries = query_ref[start : start + step, :, part].reshape(step * rows, HEAD)
            scores = lax.dot_general(
                queries, keys, (((1,), (1,)), ((), ())), preferred_element_type=jnp.float32
            )
            scores = scores.reshape(step, local_frames, tokens, key_count) * scale + shown
            scores = scores.reshape(step * rows, key_count)
            weights = jnp.exp2(scores - jnp.max(scores, axis=1, keepdims=True))
            weights = weights.astype(jnp.bfloat16)
            total = jnp.sum(weights.astype(jnp.float32), axis=1, keepdims=True)
            mixed = jnp.dot(weights, values, preferred_element_type=jnp.float32) / total
            mixed = mixed.reshape(step, local_frames, tokens, HEAD) * gates
            out_ref[start : start + step, :, part] = mixed.reshape(step, rows, HEAD).astype(
                out_ref.dtype
            )


def whole_heads(queries, keys, values, slot_of, level_of, gate_table):
    devices = lax.axis_size("seq")
    _, local_frames, tokens, all_width = queries.shape
    rows, width = local_frames * tokens, all_width // devices
    exchange = functools.partial(
        lax.all_to_all, axis_name="seq", split_axis=0, concat_axis=0, tiled=True
    )
    index = jnp.stack([lax.axis_index("frame"), lax.axis_index("seq")])
    pair, own = pl.pallas_call(
        pack,
        out_shape=[
            jax.ShapeDtypeStruct((devices, 2, rows, width), queries.dtype),
            jax.ShapeDtypeStruct((devices, rows, width), queries.dtype),
        ],
        in_specs=[pl.BlockSpec(memory_space=pltpu.HBM)] * 3,
        out_specs=[VMEM] * 2,
        scratch_shapes=[
            pltpu.VMEM((3, rows, all_width), queries.dtype),
            pltpu.SemaphoreType.DMA((3,)),
        ],
        compiler_params=PARAMS,
    )(
        *(
            pltpu.with_memory_space_constraint(taken.reshape(rows, all_width), pltpu.HBM)
            for taken in (queries, keys, values)
        )
    )
    pair = exchange(pair)
    own = exchange(own)
    groups = lax.axis_size("frame")
    pairs = [pair] + [
        lax.ppermute(pair, "frame", [(one, (one - away) % groups) for one in range(groups)])
        for away in range(1, groups)
    ]
    answer = pl.pallas_call(
        functools.partial(attend, tokens=tokens),
        out_shape=jax.ShapeDtypeStruct((devices, rows, width), queries.dtype),
        in_specs=[SMEM] * 3 + [VMEM] * (2 + groups),
        out_specs=VMEM,
        compiler_params=PARAMS,
    )(index, slot_of, level_of, gate_table, own, *pairs)
    answer = exchange(answer)
    answer = pl.pallas_call(
        unpack,
        out_shape=jax.ShapeDtypeStruct((rows, all_width), queries.dtype),
        in_specs=[VMEM],
        out_specs=VMEM,
        compiler_params=PARAMS,
    )(answer)
    return answer.reshape(queries.shape)


def shared_heads(queries, keys, values, slot_of, level_of, gate_table):
    devices = lax.axis_size("frame") * lax.axis_size("seq")
    _, local_frames, tokens, _ = queries.shape
    rows, blocks = local_frames * tokens, devices // H
    block_rows = rows // blocks
    exchange = functools.partial(
        lax.all_to_all, axis_name=AXES, split_axis=0, concat_axis=0, tiled=True
    )

    def by_head(taken):
        return taken.reshape(rows, H, HEAD).transpose(1, 0, 2)

    def key_pieces(taken):
        pieces = jnp.broadcast_to(by_head(taken)[:, None], (H, blocks, rows, HEAD))
        return exchange(pieces.reshape(devices, rows, HEAD)).reshape(devices * rows, HEAD)

    key_rows, value_rows = key_pieces(keys), key_pieces(values)
    query_rows = exchange(by_head(queries).reshape(devices, block_rows, HEAD))
    query_rows = query_rows.reshape(devices * block_rows, HEAD)
    device_index = lax.axis_index("frame") * lax.axis_size("seq") + lax.axis_index("seq")
    head, block = device_index // blocks, device_index % blocks

    def per_row(table):
        table = jnp.repeat(table, tokens, axis=1)[:, None]
        return jnp.broadcast_to(table, (table.shape[0], lax.axis_size("seq"), rows))

    row_slots, row_levels = per_row(slot_of), per_row(level_of)
    query_slots = lax.dynamic_slice_in_dim(row_slots, block * block_rows, block_rows, 2)
    levels = lax.dynamic_slice_in_dim(row_levels, block * block_rows, block_rows, 2).reshape(-1)
    scores = lax.dot_general(
        query_rows, key_rows, (((1,), (1,)), ((), ())), preferred_element_type=jnp.float32
    )
    visible = row_slots.reshape(1, -1) <= query_slots.reshape(-1, 1)
    scores = jnp.where(visible, scores * (1.0 / math.sqrt(HEAD)), -jnp.inf)
    weights = jnp.exp(scores - jnp.max(scores, axis=1, keepdims=True)).astype(jnp.bfloat16)
    total = jnp.sum(weights.astype(jnp.float32), axis=1, keepdims=True)
    mixed = jnp.dot(weights, value_rows, preferred_element_type=jnp.float32) / total
    gates = lax.dynamic_slice_in_dim(gate_table, head * HEAD, HEAD, 1)[levels]
    answer = exchange((mixed * gates).astype(queries.dtype).reshape(devices, block_rows, HEAD))
    return answer.reshape(H, rows, HEAD).transpose(1, 0, 2).reshape(queries.shape)


def body(queries, *others):
    if lax.axis_size("seq") > H:
        return shared_heads(queries, *others)
    return whole_heads(queries, *others)


def solution(mesh):
    return jax.shard_map(
        body,
        mesh=mesh,
        in_specs=(
            P(("rollout", "frame"), None, "seq", None),
            P(("rollout", "frame"), None, "seq", None),
            P(("rollout", "frame"), None, "seq", None),
            P("rollout", None),
            P("rollout", None),
            P(),
        ),
        out_specs=P(("rollout", "frame"), None, "seq", None),
        check_vma=False,
    )
```

time: 37 us -> 41.7 us (1.13)
  blocking collectives: 10.2 us -> 25.8 us
  waiting for transfers between devices: 13 us -> 7.57 us
  starting transfers between devices: 7.36 us -> 3.72 us
  local copies, waits for them, and re-layouts: 2.77 us -> 0.01 us
  Pallas kernels: 3.23 us -> 4.14 us
    all_to_all x1 -> x2, blocking collectives: 10.2 us -> 25.8 us  [the longest x1 16 us: whole_heads(): pair = exchange(pair)]
    all_to_all x1, waiting for transfers between devices: 13 us -> 7.57 us  [whole_heads(): own = exchange(own)]
    all_to_all x1, starting transfers between devices: 7.36 us -> 3.72 us  [whole_heads(): own = exchange(own)]
    unnamed x12 -> x6, local copies, waits for them, and re-layouts: 2.76 us -> 0.01 us
    pallas_call x3, Pallas kernels: 3.23 us -> 4.14 us  [the longest x1 1.76 us: whole_heads(): pl.pallas_call(functools.partial(attend, tokens=tokens), out_shape=jax.Sh...]
  transfers between devices with their start and end apart: 1 -> 2, of which waited for: 1 -> 1; matrix products, arithmetic and copies ran while one was open for 0% -> 0% of each run, Pallas kernels for 0% -> 0%
where the time goes in v2:
time: 41.7 us; the launch traced here: 41.4 us
  blocking collectives  25.8 us (62%)
  waiting for transfers between devices  7.57 us (18%)
  Pallas kernels  4.14 us (10%)
  starting transfers between devices  3.72 us (9%)
    all_to_all x1, blocking collectives, whole_heads(): pair = exchange(pair)  16 us
    all_to_all x1, blocking collectives, whole_heads(): answer = exchange(answer)  9.85 us
    all_to_all x1, waiting for transfers between devices, whole_heads(): own = exchange(own)  7.57 us
    all_to_all x1, starting transfers between devices, whole_heads(): own = exchange(own)  3.72 us
    pallas_call x1, Pallas kernels, whole_heads(): pl.pallas_call(functools.partial(attend, tokens=tokens), out_shape=jax.Sh...  1.76 us
    pallas_call x1, Pallas kernels, whole_heads(): pl.pallas_call(pack, out_shape=[jax.ShapeDtypeStruct((devices, 2, rows, w...  1.72 us
  transfers between devices with their start and end apart: 2, of which 1 were waited for; matrix products, arithmetic and copies ran while one was open for 0% of the time, Pallas kernels for 0%

profile of v2, /device:TPU:0, one launch (start us, length us, event | category | flops | bytes accessed | tf_op | source)
XLA Modules:
  0.0 41.4 jit_solution(14210813960635669911)
XLA Ops:
  0.0 1.7 %shard_map.64 = (bf16[8,2,32,256]{3,2,1,0:T(8,128)(2,1)S(1)}, bf16[8,32,256]{2,1,0:T(8,128)(2,1)}) custom-call(bf16[32,2048]{1,0:T(8,128)(2,1)} %bitcast.6, bf16[32,2048]{1,0:T(8,128)(2,1)} %bitcast.7, bf16[32,2048]{1,0:T(8,128)(2,1)} %bitcast.8), custom_call_target="tpu_custom_call" | custom-call | tf_op jit(solution)/shard_map/pallas_call | solution.py:105
  1.7 16.0 %all_to_all.15.refs_0_ = bf16[8,2,32,256]{3,2,1,0:T(8,128)(2,1)S(1)} all-to-all(bf16[8,2,32,256]{3,2,1,0:T(8,128)(2,1)S(1)} %get-tuple-element.8), channel_id=1, replica_groups=mesh['rollout'=2,'frame'=2,'seq'=8] {'seq'}, dimensions={0} | all-to-all | bytes 524288 | tf_op jit(solution)/shard_map/all_to_all | solution.py:124
  17.7 0.0 collective-permute-start
  17.7 0.0 copy-start
  17.7 3.7 %all-to-all-start = ((bf16[8,32,256]{2,1,0:T(8,128)(2,1)}), bf16[8,32,256]{2,1,0:T(8,128)(2,1)S(1)}, u32[]{:S(2)}, u32[]{:S(2)}) async-start(bf16[8,32,256]{2,1,0:T(8,128)(2,1)} %get-tuple-element.7), calls=%async_computation | async-start | bytes 262144 | tf_op jit(solution)/shard_map/all_to_all | solution.py:125
  21.4 0.0 copy-start.2
  21.4 0.0 copy-start.1
  21.4 0.1 pad_add_fusion.index_ref
  21.5 7.6 %all-to-all-done.query_ref = bf16[8,32,256]{2,1,0:T(8,128)(2,1)S(1)} async-done(((bf16[8,32,256]{2,1,0:T(8,128)(2,1)}), bf16[8,32,256]{2,1,0:T(8,128)(2,1)S(1)}, u32[]{:S(2)}, u32[]{:S(2)}) %all-to-all-start) | async-done | bytes 131104 | tf_op jit(solution)/shard_map/all_to_all | solution.py:125
  29.1 0.0 collective-permute-done.refs_1_
  29.1 0.0 copy-done
  29.1 0.0 copy-done.2
  29.1 0.0 copy-done.1
  29.1 1.8 %shard_map.65 = bf16[8,32,256]{2,1,0:T(8,128)(2,1)S(1)} custom-call(s32[2]{0:T(128)S(1)} %pad_add_fusion.index_ref, s32[2,4]{1,0:T(2,128)S(1)} %copy-done.1, s32[2,4]{1,0:T(2,128)S(1)} %copy-done.2, f32[8,2048]{1,0:T(8,128)S(1)} %copy-done, bf16[8,32,256]{2,1,0:T(8,128)(2,1)S(1)} %all-to-all-done.query_ref, bf16[8,2,32,256]{3,2,1,0:T(8,128)(2,1)S(1)} %all_to_all.15.refs_0_, ...), custom_call_target="tpu_custom_call" | custom-call | tf_op jit(solution)/shard_map/pallas_call | solution.py:131
  30.9 9.8 %all_to_all.16.held_ref = bf16[8,32,256]{2,1,0:T(8,128)(2,1)S(1)} all-to-all(bf16[8,32,256]{2,1,0:T(8,128)(2,1)S(1)} %shard_map.65), channel_id=1, replica_groups=mesh['rollout'=2,'frame'=2,'seq'=8] {'seq'}, dimensions={0} | all-to-all | bytes 262144 | tf_op jit(solution)/shard_map/all_to_all | solution.py:138
  40.7 0.7 %shard_map.66 = bf16[32,2048]{1,0:T(8,128)(2,1)} custom-call(bf16[8,32,256]{2,1,0:T(8,128)(2,1)S(1)} %all_to_all.16.held_ref), custom_call_target="tpu_custom_call" | custom-call | tf_op jit(solution)/shard_map/pallas_call | solution.py:139
Async XLA Ops:
  17.7 11.4 %collective-permute-start = (bf16[8,2,32,256]{3,2,1,0:T(8,128)(2,1)S(1)}, bf16[8,2,32,256]{3,2,1,0:T(8,128)(2,1)S(1)}, u32[]{:S(2)}, u32[]{:S(2)}) collective-permute-start(bf16[8,2,32,256]{3,2,1,0:T(8,128)(2,1)S(1)} %all_to_all.15.refs_0_), channel_id=1, source_target_pairs={{0,8},{8,0},{1,9},{9,1},{2,10},{10,2},{3,11},{11,3},{4,12},{12,4},... | collective-permute-start | bytes 786440 | tf_op jit(solution)/shard_map/ppermute | solution.py:128
  17.7 11.4 %copy-start = (f32[8,2048]{1,0:T(8,128)S(1)}, f32[8,2048]{1,0:T(8,128)}, u32[]{:S(2)}) copy-start(f32[8,2048]{1,0:T(8,128)} %gate_ref.1) | copy-start | bytes 196612
  17.7 11.4 %all-to-all-start = ((bf16[8,32,256]{2,1,0:T(8,128)(2,1)}), bf16[8,32,256]{2,1,0:T(8,128)(2,1)S(1)}, u32[]{:S(2)}, u32[]{:S(2)}) async-start(bf16[8,32,256]{2,1,0:T(8,128)(2,1)} %get-tuple-element.7), calls=%async_computation | async-start | bytes 262144 | tf_op jit(solution)/shard_map/all_to_all | solution.py:125
  21.4 7.7 %copy-start.2 = (s32[2,4]{1,0:T(2,128)S(1)}, s32[2,4]{1,0:T(2,128)}, u32[]{:S(2)}) copy-start(s32[2,4]{1,0:T(2,128)} %level_ref.1) | copy-start | bytes 100
  21.4 7.7 %copy-start.1 = (s32[2,4]{1,0:T(2,128)S(1)}, s32[2,4]{1,0:T(2,128)}, u32[]{:S(2)}) copy-start(s32[2,4]{1,0:T(2,128)} %slot_ref.1) | copy-start | bytes 100

commit v3 on v2

--- a/solution.py
+++ b/solution.py
@@ -12,38 +12,47 @@
 HEAD = 128
 AXES = ("frame", "seq")
 SMEM = pl.BlockSpec(memory_space=pltpu.SMEM)
+HBM = pl.BlockSpec(memory_space=pltpu.HBM)
 VMEM = pl.BlockSpec(memory_space=pltpu.VMEM)
 PARAMS = pltpu.CompilerParams(vmem_limit_bytes=32 * 1024 * 1024)
 
 
-def pack(query_ref, key_ref, value_ref, pair_ref, own_ref, held_ref, sems):
+def pack(*refs):
+    out_ref, sems = refs[-2:]
+    width = out_ref.shape[-1]
     copies = [
-        pltpu.make_async_copy(ref, held_ref.at[place], sems.at[place])
-        for place, ref in enumerate((key_ref, value_ref, query_ref))
+        pltpu.make_async_copy(
+            ref.at[:, pl.ds(device * width, width)],
+            out_ref.at[device, place],
+            sems.at[device, place],
+        )
+        for place, ref in enumerate(refs[:-2])
+        for device in range(out_ref.shape[0])
     ]
     for copy in copies:
         copy.start()
-    width = own_ref.shape[-1]
-    for place, copy in enumerate(copies):
+    for copy in copies:
         copy.wait()
-        for device in range(own_ref.shape[0]):
-            taken = held_ref[place, :, device * width : (device + 1) * width]
-            if place < 2:
-                pair_ref[device, place] = taken
-            else:
-                own_ref[device] = taken
-
-
-def unpack(held_ref, out_ref):
+
+
+def unpack(held_ref, out_ref, sems):
     width = held_ref.shape[-1]
-    for device in range(held_ref.shape[0]):
-        out_ref[:, device * width : (device + 1) * width] = held_ref[device]
-
-
-def attend(index_ref, slot_ref, level_ref, gate_ref, query_ref, *refs, tokens):
-    pair_refs, out_ref = refs[:-1], refs[-1]
-    group_count = len(pair_refs)
-    devices, _, rows, width = pair_refs[0].shape
+    copies = [
+        pltpu.make_async_copy(
+            held_ref.at[device], out_ref.at[:, pl.ds(device * width, width)], sems.at[device]
+        )
+        for device in range(held_ref.shape[0])
+    ]
+    for copy in copies:
+        copy.start()
+    for copy in copies:
+        copy.wait()
+
+
+def attend(index_ref, slot_ref, level_ref, gate_ref, *refs, tokens):
+    packed_refs, out_ref = refs[:-1], refs[-1]
+    group_count = len(packed_refs)
+    devices, _, rows, width = packed_refs[0].shape
     local_frames = rows // tokens
     key_count = group_count * devices * rows
     group = index_ref[0]
@@ -59,6 +68,7 @@
         visible = key_slots <= slot_ref[group, local]
         shown.append(jnp.where(visible, 0.0, -jnp.inf).reshape(1, 1, 1, key_count))
     shown = jnp.concatenate(shown, axis=1)
+    ones = jnp.ones((key_count, HEAD), jnp.bfloat16)
     scale = math.log2(math.e) / math.sqrt(HEAD)
     step = max(1, min(devices, 128 // rows))
     for column in range(0, width, HEAD):
@@ -73,21 +83,23 @@
         gates = jnp.concatenate(gates, axis=1)
         keys, values = (
             jnp.concatenate(
-                [ref[:, place, :, part].reshape(devices * rows, HEAD) for ref in pair_refs]
-            )
-            for place in range(2)
-        )
+                [ref[:, place, :, part].reshape(devices * rows, HEAD) for ref in packed_refs]
+            )
+            for place in (1, 2)
+        )
+        values = jnp.concatenate([values, ones], axis=1)
         for start in range(0, devices, step):
-            queries = query_ref[start : start + step, :, part].reshape(step * rows, HEAD)
+            queries = packed_refs[0][start : start + step, 0, :, part].reshape(step * rows, HEAD)
             scores = lax.dot_general(
                 queries, keys, (((1,), (1,)), ((), ())), preferred_element_type=jnp.float32
             )
             scores = scores.reshape(step, local_frames, tokens, key_count) * scale + shown
             scores = scores.reshape(step * rows, key_count)
             weights = jnp.exp2(scores - jnp.max(scores, axis=1, keepdims=True))
-            weights = weights.astype(jnp.bfloat16)
-            total = jnp.sum(weights.astype(jnp.float32), axis=1, keepdims=True)
-            mixed = jnp.dot(weights, values, preferred_element_type=jnp.float32) / total
+            mixed = jnp.dot(
+                weights.astype(jnp.bfloat16), values, preferred_element_type=jnp.float32
+            )
+            mixed = mixed[:, :HEAD] / mixed[:, HEAD:]
             mixed = mixed.reshape(step, local_frames, tokens, HEAD) * gates
             out_ref[start : start + step, :, part] = mixed.reshape(step, rows, HEAD).astype(
                 out_ref.dtype
@@ -95,25 +107,19 @@
 
 
 def whole_heads(queries, keys, values, slot_of, level_of, gate_table):
-    devices = lax.axis_size("seq")
+    devices, groups = lax.axis_size("seq"), lax.axis_size("frame")
     _, local_frames, tokens, all_width = queries.shape
     rows, width = local_frames * tokens, all_width // devices
     exchange = functools.partial(
         lax.all_to_all, axis_name="seq", split_axis=0, concat_axis=0, tiled=True
     )
     index = jnp.stack([lax.axis_index("frame"), lax.axis_index("seq")])
-    pair, own = pl.pallas_call(
+    packed = pl.pallas_call(
         pack,
-        out_shape=[
-            jax.ShapeDtypeStruct((devices, 2, rows, width), queries.dtype),
-            jax.ShapeDtypeStruct((devices, rows, width), queries.dtype),
-        ],
-        in_specs=[pl.BlockSpec(memory_space=pltpu.HBM)] * 3,
-        out_specs=[VMEM] * 2,
-        scratch_shapes=[
-            pltpu.VMEM((3, rows, all_width), queries.dtype),
-            pltpu.SemaphoreType.DMA((3,)),
-        ],
+        out_shape=jax.ShapeDtypeStruct((devices, 3, rows, width), queries.dtype),
+        in_specs=[HBM] * 3,
+        out_specs=VMEM,
+        scratch_shapes=[pltpu.SemaphoreType.DMA((devices, 3))],
         compiler_params=PARAMS,
     )(
         *(
@@ -121,26 +127,25 @@
             for taken in (queries, keys, values)
         )
     )
-    pair = exchange(pair)
-    own = exchange(own)
-    groups = lax.axis_size("frame")
-    pairs = [pair] + [
-        lax.ppermute(pair, "frame", [(one, (one - away) % groups) for one in range(groups)])
+    packed = exchange(packed)
+    packs = [packed] + [
+        lax.ppermute(packed, "frame", [(one, (one - away) % groups) for one in range(groups)])
         for away in range(1, groups)
     ]
     answer = pl.pallas_call(
         functools.partial(attend, tokens=tokens),
         out_shape=jax.ShapeDtypeStruct((devices, rows, width), queries.dtype),
-        in_specs=[SMEM] * 3 + [VMEM] * (2 + groups),
+        in_specs=[SMEM] * 3 + [VMEM] * (1 + groups),
         out_specs=VMEM,
         compiler_params=PARAMS,
-    )(index, slot_of, level_of, gate_table, own, *pairs)
+    )(index, slot_of, level_of, gate_table, *packs)
     answer = exchange(answer)
     answer = pl.pallas_call(
         unpack,
         out_shape=jax.ShapeDtypeStruct((rows, all_width), queries.dtype),
         in_specs=[VMEM],
-        out_specs=VMEM,
+        out_specs=HBM,
+        scratch_shapes=[pltpu.SemaphoreType.DMA((devices,))],
         compiler_params=PARAMS,
     )(answer)
     return answer.reshape(queries.shape)

time: 41.7 us -> 34.8 us (0.83)
  waiting for transfers between devices: 7.57 us -> 1.64 us
  blocking collectives: 25.8 us -> 29.6 us
  starting transfers between devices: 3.72 us -> 0.01 us
  Pallas kernels: 4.14 us -> 3.11 us
    all_to_all x1 -> x0, waiting for transfers between devices: 7.57 us -> none  [whole_heads(): own = exchange(own)]
    all_to_all x1 -> x0, starting transfers between devices: 3.72 us -> none  [whole_heads(): own = exchange(own)]
    all_to_all x1, blocking collectives: 16 us -> 19.3 us  [whole_heads(): packed = exchange(packed)]
    ppermute x1, waiting for transfers between devices: 0.01 us -> 1.64 us  [whole_heads(): lax.ppermute(packed, 'frame', [(one, (one - away) % groups) for one in ra...]
    pallas_call x1, Pallas kernels: 1.72 us -> 1.16 us  [whole_heads(): pl.pallas_call(pack, out_shape=jax.ShapeDtypeStruct((devices, 3, rows, wi...]
    all_to_all x1, blocking collectives: 9.85 us -> 10.4 us  [whole_heads(): answer = exchange(answer)]
    pallas_call x1, Pallas kernels: 1.76 us -> 1.24 us  [whole_heads(): pl.pallas_call(functools.partial(attend, tokens=tokens), out_shape=jax.Sh...]
  transfers between devices with their start and end apart: 2 -> 1, of which waited for: 1 -> 1; matrix products, arithmetic and copies ran while one was open for 0% -> 0% of each run, Pallas kernels for 0% -> 0%
where the time goes in v3:
time: 34.8 us; the launch traced here: 34.5 us
  blocking collectives  29.6 us (85%)
  Pallas kernels  3.11 us (9%)
  waiting for transfers between devices  1.64 us (5%)
    all_to_all x1, blocking collectives, whole_heads(): packed = exchange(packed)  19.3 us
    all_to_all x1, blocking collectives, whole_heads(): answer = exchange(answer)  10.4 us
    ppermute x1, waiting for transfers between devices, whole_heads(): lax.ppermute(packed, 'frame', [(one, (one - away) % groups) for one in ra...  1.64 us
    pallas_call x1, Pallas kernels, whole_heads(): pl.pallas_call(functools.partial(attend, tokens=tokens), out_shape=jax.Sh...  1.24 us
    pallas_call x1, Pallas kernels, whole_heads(): pl.pallas_call(pack, out_shape=jax.ShapeDtypeStruct((devices, 3, rows, wi...  1.16 us
    pallas_call x1, Pallas kernels, whole_heads(): pl.pallas_call(unpack, out_shape=jax.ShapeDtypeStruct((rows, all_width),...  0.71 us
  transfers between devices with their start and end apart: 1, of which 1 were waited for; matrix products, arithmetic and copies ran while one was open for 0% of the time, Pallas kernels for 0%

profile of v3, /device:TPU:0, one launch (start us, length us, event | category | flops | bytes accessed | tf_op | source)
XLA Modules:
  0.0 34.5 jit_solution(6465627677309216636)
XLA Ops:
  0.0 1.2 %shard_map.64 = bf16[8,3,32,256]{3,2,1,0:T(8,128)(2,1)S(1)} custom-call(bf16[32,2048]{1,0:T(8,128)(2,1)} %bitcast.6, bf16[32,2048]{1,0:T(8,128)(2,1)} %bitcast.7, bf16[32,2048]{1,0:T(8,128)(2,1)} %bitcast.8), custom_call_target="tpu_custom_call" | custom-call | tf_op jit(solution)/shard_map/pallas_call | solution.py:117
  1.2 0.0 copy-start
  1.2 0.0 copy-start.2
  1.2 19.3 %all_to_all.10.refs_0_ = bf16[8,3,32,256]{3,2,1,0:T(8,128)(2,1)S(1)} all-to-all(bf16[8,3,32,256]{3,2,1,0:T(8,128)(2,1)S(1)} %shard_map.64), channel_id=1, replica_groups=mesh['rollout'=2,'frame'=2,'seq'=8] {'seq'}, dimensions={0} | all-to-all | bytes 786432 | tf_op jit(solution)/shard_map/all_to_all | solution.py:130
  20.5 0.0 collective-permute-start
  20.5 0.0 copy-start.1
  20.5 0.1 pad_add_fusion.index_ref
  20.5 1.6 %collective-permute-done.refs_1_ = bf16[8,3,32,256]{3,2,1,0:T(8,128)(2,1)S(1)} collective-permute-done((bf16[8,3,32,256]{3,2,1,0:T(8,128)(2,1)S(1)}, bf16[8,3,32,256]{3,2,1,0:T(8,128)(2,1)S(1)}, u32[]{:S(2)}, u32[]{:S(2)}) %collective-permute-start) | collective-permute-done | bytes 393248 | tf_op jit(solution)/shard_map/ppermute | solution.py:132
  22.2 0.0 copy-done
  22.2 0.0 copy-done.2
  22.2 0.0 copy-done.1
  22.2 1.2 %shard_map.65 = bf16[8,32,256]{2,1,0:T(8,128)(2,1)S(1)} custom-call(s32[2]{0:T(128)S(1)} %pad_add_fusion.index_ref, s32[2,4]{1,0:T(2,128)S(1)} %copy-done.1, s32[2,4]{1,0:T(2,128)S(1)} %copy-done.2, f32[8,2048]{1,0:T(8,128)S(1)} %copy-done, bf16[8,3,32,256]{3,2,1,0:T(8,128)(2,1)S(1)} %all_to_all.10.refs_0_, ...), custom_call_target="tpu_custom_call" | custom-call | tf_op jit(solution)/shard_map/pallas_call | solution.py:135
  23.4 10.4 %all_to_all.11.held_ref = bf16[8,32,256]{2,1,0:T(8,128)(2,1)S(1)} all-to-all(bf16[8,32,256]{2,1,0:T(8,128)(2,1)S(1)} %shard_map.65), channel_id=1, replica_groups=mesh['rollout'=2,'frame'=2,'seq'=8] {'seq'}, dimensions={0} | all-to-all | bytes 262144 | tf_op jit(solution)/shard_map/all_to_all | solution.py:142
  33.8 0.7 %shard_map.66 = bf16[32,2048]{1,0:T(8,128)(2,1)} custom-call(bf16[8,32,256]{2,1,0:T(8,128)(2,1)S(1)} %all_to_all.11.held_ref), custom_call_target="tpu_custom_call" | custom-call | tf_op jit(solution)/shard_map/pallas_call | solution.py:143
Async XLA Ops:
  1.2 21.0 %copy-start = (f32[8,2048]{1,0:T(8,128)S(1)}, f32[8,2048]{1,0:T(8,128)}, u32[]{:S(2)}) copy-start(f32[8,2048]{1,0:T(8,128)} %gate_ref.1) | copy-start | bytes 196612
  1.2 21.0 %copy-start.2 = (s32[2,4]{1,0:T(2,128)S(1)}, s32[2,4]{1,0:T(2,128)}, u32[]{:S(2)}) copy-start(s32[2,4]{1,0:T(2,128)} %level_ref.1) | copy-start | bytes 100
  20.5 1.7 %collective-permute-start = (bf16[8,3,32,256]{3,2,1,0:T(8,128)(2,1)S(1)}, bf16[8,3,32,256]{3,2,1,0:T(8,128)(2,1)S(1)}, u32[]{:S(2)}, u32[]{:S(2)}) collective-permute-start(bf16[8,3,32,256]{3,2,1,0:T(8,128)(2,1)S(1)} %all_to_all.10.refs_0_), channel_id=1, source_target_pairs={{0,8},{8,0},{1,9},{9,1},{2,10},{10,2},{3,11},{11,3},{4,12},{12,4},... | collective-permute-start | bytes 1179656 | tf_op jit(solution)/shard_map/ppermute | solution.py:132
  20.5 1.7 %copy-start.1 = (s32[2,4]{1,0:T(2,128)S(1)}, s32[2,4]{1,0:T(2,128)}, u32[]{:S(2)}) copy-start(s32[2,4]{1,0:T(2,128)} %slot_ref.1) | copy-start | bytes 100

commit v4 on v3

--- a/solution.py
+++ b/solution.py
@@ -17,17 +17,31 @@
 PARAMS = pltpu.CompilerParams(vmem_limit_bytes=32 * 1024 * 1024)
 
 
-def pack(*refs):
-    out_ref, sems = refs[-2:]
-    width = out_ref.shape[-1]
+def far_first(devices):
+    return sorted(range(devices), key=lambda away: (away > 0, -(2 * away // devices), away % 2, -away))
+
+
+def pack(index_ref, *refs):
+    operands, outs, sems = refs[:3], refs[3:-1], refs[-1]
+    width = outs[0].shape[-1]
+    copies = []
+    for away, out_ref in zip(far_first(len(outs)), outs):
+        column = pl.ds(pl.multiple_of((index_ref[1] ^ away) * width, width), width)
+        copies += [
+            pltpu.make_async_copy(ref.at[:, column], out_ref.at[place], sems.at[away, place])
+            for place, ref in enumerate(operands)
+        ]
+    for copy in copies:
+        copy.start()
+    for copy in copies:
+        copy.wait()
+
+
+def stack(*refs):
+    pieces, out_ref, sems = refs[:-2], refs[-2], refs[-1]
     copies = [
-        pltpu.make_async_copy(
-            ref.at[:, pl.ds(device * width, width)],
-            out_ref.at[device, place],
-            sems.at[device, place],
-        )
-        for place, ref in enumerate(refs[:-2])
-        for device in range(out_ref.shape[0])
+        pltpu.make_async_copy(ref.at[pl.ds(1, 2)], out_ref.at[away], sems.at[away])
+        for away, ref in enumerate(pieces)
     ]
     for copy in copies:
         copy.start()
@@ -50,9 +64,10 @@
 
 
 def attend(index_ref, slot_ref, level_ref, gate_ref, *refs, tokens):
-    packed_refs, out_ref = refs[:-1], refs[-1]
-    group_count = len(packed_refs)
-    devices, _, rows, width = packed_refs[0].shape
+    out_ref = refs[-1]
+    devices, rows, width = out_ref.shape
+    own_refs, pair_refs = refs[:devices], refs[devices:-1]
+    group_count = 1 + len(pair_refs)
     local_frames = rows // tokens
     key_count = group_count * devices * rows
     group = index_ref[0]
@@ -83,13 +98,14 @@
         gates = jnp.concatenate(gates, axis=1)
         keys, values = (
             jnp.concatenate(
-                [ref[:, place, :, part].reshape(devices * rows, HEAD) for ref in packed_refs]
+                [ref[1 + place, :, part] for ref in own_refs]
+                + [ref[:, place, :, part].reshape(devices * rows, HEAD) for ref in pair_refs]
             )
-            for place in (1, 2)
+            for place in range(2)
         )
         values = jnp.concatenate([values, ones], axis=1)
         for start in range(0, devices, step):
-            queries = packed_refs[0][start : start + step, 0, :, part].reshape(step * rows, HEAD)
+            queries = jnp.concatenate([ref[0, :, part] for ref in own_refs[start : start + step]])
             scores = lax.dot_general(
                 queries, keys, (((1,), (1,)), ((), ())), preferred_element_type=jnp.float32
             )
@@ -101,45 +117,56 @@
             )
             mixed = mixed[:, :HEAD] / mixed[:, HEAD:]
             mixed = mixed.reshape(step, local_frames, tokens, HEAD) * gates
-            out_ref[start : start + step, :, part] = mixed.reshape(step, rows, HEAD).astype(
-                out_ref.dtype
-            )
+            mixed = mixed.reshape(step, rows, HEAD).astype(out_ref.dtype)
+            for place, away in enumerate(far_first(devices)[start : start + step]):
+                out_ref[index_ref[1] ^ away, :, part] = mixed[place]
 
 
 def whole_heads(queries, keys, values, slot_of, level_of, gate_table):
     devices, groups = lax.axis_size("seq"), lax.axis_size("frame")
     _, local_frames, tokens, all_width = queries.shape
     rows, width = local_frames * tokens, all_width // devices
-    exchange = functools.partial(
-        lax.all_to_all, axis_name="seq", split_axis=0, concat_axis=0, tiled=True
-    )
     index = jnp.stack([lax.axis_index("frame"), lax.axis_index("seq")])
-    packed = pl.pallas_call(
+    pieces = pl.pallas_call(
         pack,
-        out_shape=jax.ShapeDtypeStruct((devices, 3, rows, width), queries.dtype),
-        in_specs=[HBM] * 3,
-        out_specs=VMEM,
+        out_shape=[jax.ShapeDtypeStruct((3, rows, width), queries.dtype)] * devices,
+        in_specs=[SMEM] + [HBM] * 3,
+        out_specs=[VMEM] * devices,
         scratch_shapes=[pltpu.SemaphoreType.DMA((devices, 3))],
         compiler_params=PARAMS,
     )(
+        index,
         *(
             pltpu.with_memory_space_constraint(taken.reshape(rows, all_width), pltpu.HBM)
             for taken in (queries, keys, values)
-        )
-    )
-    packed = exchange(packed)
-    packs = [packed] + [
-        lax.ppermute(packed, "frame", [(one, (one - away) % groups) for one in range(groups)])
+        ),
+    )
+    pieces = [
+        lax.ppermute(piece, "seq", [(one, one ^ away) for one in range(devices)])
+        if away
+        else piece
+        for away, piece in zip(far_first(devices), pieces)
+    ]
+    pair = pl.pallas_call(
+        stack,
+        out_shape=jax.ShapeDtypeStruct((devices, 2, rows, width), queries.dtype),
+        in_specs=[VMEM] * devices,
+        out_specs=VMEM,
+        scratch_shapes=[pltpu.SemaphoreType.DMA((devices,))],
+        compiler_params=PARAMS,
+    )(*pieces)
+    pairs = [
+        lax.ppermute(pair, "frame", [(one, (one - away) % groups) for one in range(groups)])
         for away in range(1, groups)
     ]
     answer = pl.pallas_call(
         functools.partial(attend, tokens=tokens),
         out_shape=jax.ShapeDtypeStruct((devices, rows, width), queries.dtype),
-        in_specs=[SMEM] * 3 + [VMEM] * (1 + groups),
+        in_specs=[SMEM] * 3 + [VMEM] * (devices + groups),
         out_specs=VMEM,
         compiler_params=PARAMS,
-    )(index, slot_of, level_of, gate_table, *packs)
-    answer = exchange(answer)
+    )(index, slot_of, level_of, gate_table, *pieces, *pairs)
+    answer = lax.all_to_all(answer, "seq", split_axis=0, concat_axis=0, tiled=True)
     answer = pl.pallas_call(
         unpack,
         out_shape=jax.ShapeDtypeStruct((rows, all_width), queries.dtype),
@@ -194,7 +221,8 @@
 
 
 def body(queries, *others):
-    if lax.axis_size("seq") > H:
+    devices = lax.axis_size("seq")
+    if devices > H or devices & (devices - 1):
         return shared_heads(queries, *others)
     return whole_heads(queries, *others)
 

time: 34.8 us -> 34.3 us (0.986)
  blocking collectives: 29.6 us -> 12.4 us
  starting transfers between devices: 0.01 us -> 12.9 us
  waiting for transfers between devices: 1.64 us -> 4.6 us
  Pallas kernels: 3.11 us -> 4.08 us
    all_to_all x2 -> x1, blocking collectives: 29.6 us -> 12.4 us  [whole_heads(): lax.all_to_all(answer, 'seq', split_axis=0, concat_axis=0, tiled=True)]
    ppermute x1 -> x8, starting transfers between devices: 0.01 us -> 12.9 us  [the longest x7 12.8 us: whole_heads(): lax.ppermute(piece, 'seq', [(one, one ^ away) for one in range(devices)])]
    ppermute x1 -> x8, waiting for transfers between devices: 1.64 us -> 4.6 us  [the longest x7 3.08 us: whole_heads(): lax.ppermute(piece, 'seq', [(one, one ^ away) for one in range(devices)])]
    pallas_call x1 -> x2, Pallas kernels: 1.16 us -> 2.12 us  [the longest x1 1.7 us: whole_heads(): pl.pallas_call(pack, out_shape=[jax.ShapeDtypeStruct((3, rows, width), qu...]
  transfers between devices with their start and end apart: 1 -> 8, of which waited for: 1 -> 4; matrix products, arithmetic and copies ran while one was open for 0% -> 0% of each run, Pallas kernels for 0% -> 0%
where the time goes in v4:
time: 34.3 us; the launch traced here: 34.1 us
  starting transfers between devices  12.9 us (38%)
  blocking collectives  12.4 us (36%)
  waiting for transfers between devices  4.6 us (13%)
  Pallas kernels  4.08 us (12%)
    ppermute x7, starting transfers between devices, whole_heads(): lax.ppermute(piece, 'seq', [(one, one ^ away) for one in range(devices)])  12.8 us
    all_to_all x1, blocking collectives, whole_heads(): lax.all_to_all(answer, 'seq', split_axis=0, concat_axis=0, tiled=True)  12.4 us
    ppermute x7, waiting for transfers between devices, whole_heads(): lax.ppermute(piece, 'seq', [(one, one ^ away) for one in range(devices)])  3.08 us
    pallas_call x1, Pallas kernels, whole_heads(): pl.pallas_call(pack, out_shape=[jax.ShapeDtypeStruct((3, rows, width), qu...  1.7 us
    ppermute x1, waiting for transfers between devices, whole_heads(): lax.ppermute(pair, 'frame', [(one, (one - away) % groups) for one in rang...  1.52 us
    pallas_call x1, Pallas kernels, whole_heads(): pl.pallas_call(functools.partial(attend, tokens=tokens), out_shape=jax.Sh...  1.25 us
    pallas_call x1, Pallas kernels, whole_heads(): pl.pallas_call(unpack, out_shape=jax.ShapeDtypeStruct((rows, all_width),...  0.71 us
  transfers between devices with their start and end apart: 8, of which 4 were waited for; matrix products, arithmetic and copies ran while one was open for 0% of the time, Pallas kernels for 0%

profile of v4, /device:TPU:0, one launch (start us, length us, event | category | flops | bytes accessed | tf_op | source)
XLA Modules:
  0.0 34.1 jit_solution(16330278759171400887)
XLA Ops:
  0.0 0.1 pad_add_fusion.index_ref
  0.1 1.7 %shard_map.64 = (bf16[3,32,256]{2,1,0:T(8,128)(2,1)S(1)}, bf16[3,32,256]{2,1,0:T(8,128)(2,1)S(1)}, bf16[3,32,256]{2,1,0:T(8,128)(2,1)S(1)}, bf16[3,32,256]{2,1,0...) custom-call(s32[2]{0:T(128)S(1)} %pad_add_fusion.index_ref, ...), custom_call_target="tpu_custom_call" | custom-call | tf_op jit(solution)/shard_map/pallas_call | solution.py:130
  1.8 5.1 %collective-permute-start = (bf16[3,32,256]{2,1,0:T(8,128)(2,1)S(1)}, bf16[3,32,256]{2,1,0:T(8,128)(2,1)S(1)}, u32[]{:S(2)}, u32[]{:S(2)}) collective-permute-start(bf16[3,32,256]{2,1,0:T(8,128)(2,1)S(1)} %get-tuple-element.14), channel_id=1, source_target_pairs={{0,6},{1,7},{2,4},{3,5},{4,2},{5,3},{6,0},{7,1},{8,14},{9,15},{10,... | collective-permute-start | bytes 147464 | tf_op jit(solution)/shard_map/ppermute | solution.py:145
  6.9 0.0 collective-permute-start.1
  6.9 2.8 %collective-permute-start.2 = (bf16[3,32,256]{2,1,0:T(8,128)(2,1)S(1)}, bf16[3,32,256]{2,1,0:T(8,128)(2,1)S(1)}, u32[]{:S(2)}, u32[]{:S(2)}) collective-permute-start(bf16[3,32,256]{2,1,0:T(8,128)(2,1)S(1)} %get-tuple-element.16), channel_id=1, source_target_pairs={{0,7},{1,6},{2,5},{3,4},{4,3},{5,2},{6,1},{7,0},{8,15},{9,14},{10,... | collective-permute-start | bytes 147464 | tf_op jit(solution)/shard_map/ppermute | solution.py:145
  9.7 1.0 %collective-permute-start.3 = (bf16[3,32,256]{2,1,0:T(8,128)(2,1)S(1)}, bf16[3,32,256]{2,1,0:T(8,128)(2,1)S(1)}, u32[]{:S(2)}, u32[]{:S(2)}) collective-permute-start(bf16[3,32,256]{2,1,0:T(8,128)(2,1)S(1)} %get-tuple-element.17), channel_id=1, source_target_pairs={{0,5},{1,4},{2,7},{3,6},{4,1},{5,0},{6,3},{7,2},{8,13},{9,12},{10,... | collective-permute-start | bytes 147464 | tf_op jit(solution)/shard_map/ppermute | solution.py:145
  10.8 1.4 %collective-permute-start.4 = (bf16[3,32,256]{2,1,0:T(8,128)(2,1)S(1)}, bf16[3,32,256]{2,1,0:T(8,128)(2,1)S(1)}, u32[]{:S(2)}, u32[]{:S(2)}) collective-permute-start(bf16[3,32,256]{2,1,0:T(8,128)(2,1)S(1)} %get-tuple-element.18), channel_id=1, source_target_pairs={{0,2},{1,3},{2,0},{3,1},{4,6},{5,7},{6,4},{7,5},{8,10},{9,11},{10,... | collective-permute-start | bytes 147464 | tf_op jit(solution)/shard_map/ppermute | solution.py:145
  12.2 0.0 collective-permute-done.refs_1_
  12.2 0.9 %collective-permute-start.5 = (bf16[3,32,256]{2,1,0:T(8,128)(2,1)S(1)}, bf16[3,32,256]{2,1,0:T(8,128)(2,1)S(1)}, u32[]{:S(2)}, u32[]{:S(2)}) collective-permute-start(bf16[3,32,256]{2,1,0:T(8,128)(2,1)S(1)} %get-tuple-element.19), channel_id=1, source_target_pairs={{0,3},{1,2},{2,1},{3,0},{4,7},{5,6},{6,5},{7,4},{8,11},{9,10},{10,... | collective-permute-start | bytes 147464 | tf_op jit(solution)/shard_map/ppermute | solution.py:145
  13.1 0.0 collective-permute-done.1.refs_2_
  13.1 1.5 %collective-permute-start.6 = (bf16[3,32,256]{2,1,0:T(8,128)(2,1)S(1)}, bf16[3,32,256]{2,1,0:T(8,128)(2,1)S(1)}, u32[]{:S(2)}, u32[]{:S(2)}) collective-permute-start(bf16[3,32,256]{2,1,0:T(8,128)(2,1)S(1)} %get-tuple-element.20), channel_id=1, source_target_pairs={{0,1},{1,0},{2,3},{3,2},{4,5},{5,4},{6,7},{7,6},{8,9},{9,8},{10,11... | collective-permute-start | bytes 147464 | tf_op jit(solution)/shard_map/ppermute | solution.py:145
  14.6 0.0 collective-permute-done.2.refs_3_
  14.6 1.7 %collective-permute-done.3.refs_4_ = bf16[3,32,256]{2,1,0:T(8,128)(2,1)S(1)} collective-permute-done((bf16[3,32,256]{2,1,0:T(8,128)(2,1)S(1)}, bf16[3,32,256]{2,1,0:T(8,128)(2,1)S(1)}, u32[]{:S(2)}, u32[]{:S(2)}) %collective-permute-start.3) | collective-permute-done | bytes 49184 | tf_op jit(solution)/shard_map/ppermute | solution.py:145
  16.3 0.0 collective-permute-done.4.refs_5_
  16.3 0.9 %collective-permute-done.5.refs_6_ = bf16[3,32,256]{2,1,0:T(8,128)(2,1)S(1)} collective-permute-done((bf16[3,32,256]{2,1,0:T(8,128)(2,1)S(1)}, bf16[3,32,256]{2,1,0:T(8,128)(2,1)S(1)}, u32[]{:S(2)}, u32[]{:S(2)}) %collective-permute-start.5) | collective-permute-done | bytes 49184 | tf_op jit(solution)/shard_map/ppermute | solution.py:145
  17.2 0.5 %collective-permute-done.6.refs_7_ = bf16[3,32,256]{2,1,0:T(8,128)(2,1)S(1)} collective-permute-done((bf16[3,32,256]{2,1,0:T(8,128)(2,1)S(1)}, bf16[3,32,256]{2,1,0:T(8,128)(2,1)S(1)}, u32[]{:S(2)}, u32[]{:S(2)}) %collective-permute-start.6) | collective-permute-done | bytes 49184 | tf_op jit(solution)/shard_map/ppermute | solution.py:145
  17.7 0.0 copy-start
  17.7 0.0 copy-start.1
  17.7 0.0 copy-start.2
  17.7 0.4 %shard_map.65 = bf16[8,2,32,256]{3,2,1,0:T(8,128)(2,1)S(1)} custom-call(bf16[3,32,256]{2,1,0:T(8,128)(2,1)S(1)} %get-tuple-element.13.refs_0_, bf16[3,32,256]{2,1,0:T(8,128)(2,1)S(1)} %collective-permute-done.refs_1_, bf16[3,32,256]{2,1,0:T(8,128)(2,1)S(1)} %collective-permute-done.1.refs_2_, bf16[3,32,256]{2,1,0:T(8,128)(2,1)S(1)} %collective-permute-done.2.refs_3_, ...), custom_call_target="tpu_custom_call" | custom-call | tf_op jit(solution)/shard_map/pallas_call | solution.py:150
  18.1 0.1 collective-permute-start.7
  18.2 1.5 %collective-permute-done.7.refs_8_ = bf16[8,2,32,256]{3,2,1,0:T(8,128)(2,1)S(1)} collective-permute-done((bf16[8,2,32,256]{3,2,1,0:T(8,128)(2,1)S(1)}, bf16[8,2,32,256]{3,2,1,0:T(8,128)(2,1)S(1)}, u32[]{:S(2)}, u32[]{:S(2)}) %collective-permute-start.7) | collective-permute-done | bytes 262176 | tf_op jit(solution)/shard_map/ppermute | solution.py:159
  19.7 0.0 copy-done
  19.8 0.0 copy-done.1
  19.8 0.0 copy-done.2
  19.8 1.2 %shard_map.66 = bf16[8,32,256]{2,1,0:T(8,128)(2,1)S(1)} custom-call(s32[2]{0:T(128)S(1)} %pad_add_fusion.index_ref, s32[2,4]{1,0:T(2,128)S(1)} %copy-done.1, s32[2,4]{1,0:T(2,128)S(1)} %copy-done.2, f32[8,2048]{1,0:T(8,128)S(1)} %copy-done, bf16[3,32,256]{2,1,0:T(8,128)(2,1)S(1)} %get-tuple-element.13.refs_0_, ...), custom_call_target="tpu_custom_call" | custom-call | tf_op jit(solution)/shard_map/pallas_call | solution.py:162
  21.0 12.4 %all_to_all.5.held_ref = bf16[8,32,256]{2,1,0:T(8,128)(2,1)S(1)} all-to-all(bf16[8,32,256]{2,1,0:T(8,128)(2,1)S(1)} %shard_map.66), channel_id=1, replica_groups=mesh['rollout'=2,'frame'=2,'seq'=8] {'seq'}, dimensions={0} | all-to-all | bytes 262144 | tf_op jit(solution)/shard_map/all_to_all | solution.py:169
  33.4 0.7 %shard_map.67 = bf16[32,2048]{1,0:T(8,128)(2,1)} custom-call(bf16[8,32,256]{2,1,0:T(8,128)(2,1)S(1)} %all_to_all.5.held_ref), custom_call_target="tpu_custom_call" | custom-call | tf_op jit(solution)/shard_map/pallas_call | solution.py:170
Async XLA Ops:
  1.8 10.4 %collective-permute-start = (bf16[3,32,256]{2,1,0:T(8,128)(2,1)S(1)}, bf16[3,32,256]{2,1,0:T(8,128)(2,1)S(1)}, u32[]{:S(2)}, u32[]{:S(2)}) collective-permute-start(bf16[3,32,256]{2,1,0:T(8,128)(2,1)S(1)} %get-tuple-element.14), channel_id=1, source_target_pairs={{0,6},{1,7},{2,4},{3,5},{4,2},{5,3},{6,0},{7,1},{8,14},{9,15},{10,... | collective-permute-start | bytes 147464 | tf_op jit(solution)/shard_map/ppermute | solution.py:145
  6.9 6.2 %collective-permute-start.1 = (bf16[3,32,256]{2,1,0:T(8,128)(2,1)S(1)}, bf16[3,32,256]{2,1,0:T(8,128)(2,1)S(1)}, u32[]{:S(2)}, u32[]{:S(2)}) collective-permute-start(bf16[3,32,256]{2,1,0:T(8,128)(2,1)S(1)} %get-tuple-element.15), channel_id=1, source_target_pairs={{0,4},{1,5},{2,6},{3,7},{4,0},{5,1},{6,2},{7,3},{8,12},{9,13},{10,... | collective-permute-start | bytes 147464 | tf_op jit(solution)/shard_map/ppermute | solution.py:145
  6.9 7.7 %collective-permute-start.2 = (bf16[3,32,256]{2,1,0:T(8,128)(2,1)S(1)}, bf16[3,32,256]{2,1,0:T(8,128)(2,1)S(1)}, u32[]{:S(2)}, u32[]{:S(2)}) collective-permute-start(bf16[3,32,256]{2,1,0:T(8,128)(2,1)S(1)} %get-tuple-element.16), channel_id=1, source_target_pairs={{0,7},{1,6},{2,5},{3,4},{4,3},{5,2},{6,1},{7,0},{8,15},{9,14},{10,... | collective-permute-start | bytes 147464 | tf_op jit(solution)/shard_map/ppermute | solution.py:145
  9.7 6.6 %collective-permute-start.3 = (bf16[3,32,256]{2,1,0:T(8,128)(2,1)S(1)}, bf16[3,32,256]{2,1,0:T(8,128)(2,1)S(1)}, u32[]{:S(2)}, u32[]{:S(2)}) collective-permute-start(bf16[3,32,256]{2,1,0:T(8,128)(2,1)S(1)} %get-tuple-element.17), channel_id=1, source_target_pairs={{0,5},{1,4},{2,7},{3,6},{4,1},{5,0},{6,3},{7,2},{8,13},{9,12},{10,... | collective-permute-start | bytes 147464 | tf_op jit(solution)/shard_map/ppermute | solution.py:145
  10.8 5.5 %collective-permute-start.4 = (bf16[3,32,256]{2,1,0:T(8,128)(2,1)S(1)}, bf16[3,32,256]{2,1,0:T(8,128)(2,1)S(1)}, u32[]{:S(2)}, u32[]{:S(2)}) collective-permute-start(bf16[3,32,256]{2,1,0:T(8,128)(2,1)S(1)} %get-tuple-element.18), channel_id=1, source_target_pairs={{0,2},{1,3},{2,0},{3,1},{4,6},{5,7},{6,4},{7,5},{8,10},{9,11},{10,... | collective-permute-start | bytes 147464 | tf_op jit(solution)/shard_map/ppermute | solution.py:145
  12.2 5.0 %collective-permute-start.5 = (bf16[3,32,256]{2,1,0:T(8,128)(2,1)S(1)}, bf16[3,32,256]{2,1,0:T(8,128)(2,1)S(1)}, u32[]{:S(2)}, u32[]{:S(2)}) collective-permute-start(bf16[3,32,256]{2,1,0:T(8,128)(2,1)S(1)} %get-tuple-element.19), channel_id=1, source_target_pairs={{0,3},{1,2},{2,1},{3,0},{4,7},{5,6},{6,5},{7,4},{8,11},{9,10},{10,... | collective-permute-start | bytes 147464 | tf_op jit(solution)/shard_map/ppermute | solution.py:145
  13.1 4.6 %collective-permute-start.6 = (bf16[3,32,256]{2,1,0:T(8,128)(2,1)S(1)}, bf16[3,32,256]{2,1,0:T(8,128)(2,1)S(1)}, u32[]{:S(2)}, u32[]{:S(2)}) collective-permute-start(bf16[3,32,256]{2,1,0:T(8,128)(2,1)S(1)} %get-tuple-element.20), channel_id=1, source_target_pairs={{0,1},{1,0},{2,3},{3,2},{4,5},{5,4},{6,7},{7,6},{8,9},{9,8},{10,11... | collective-permute-start | bytes 147464 | tf_op jit(solution)/shard_map/ppermute | solution.py:145
  17.7 2.0 %copy-start = (f32[8,2048]{1,0:T(8,128)S(1)}, f32[8,2048]{1,0:T(8,128)}, u32[]{:S(2)}) copy-start(f32[8,2048]{1,0:T(8,128)} %gate_ref.1) | copy-start | bytes 196612
  17.7 2.0 %copy-start.1 = (s32[2,4]{1,0:T(2,128)S(1)}, s32[2,4]{1,0:T(2,128)}, u32[]{:S(2)}) copy-start(s32[2,4]{1,0:T(2,128)} %slot_ref.1) | copy-start | bytes 100
  17.7 2.0 %copy-start.2 = (s32[2,4]{1,0:T(2,128)S(1)}, s32[2,4]{1,0:T(2,128)}, u32[]{:S(2)}) copy-start(s32[2,4]{1,0:T(2,128)} %level_ref.1) | copy-start | bytes 100
  18.1 1.6 %collective-permute-start.7 = (bf16[8,2,32,256]{3,2,1,0:T(8,128)(2,1)S(1)}, bf16[8,2,32,256]{3,2,1,0:T(8,128)(2,1)S(1)}, u32[]{:S(2)}, u32[]{:S(2)}) collective-permute-start(bf16[8,2,32,256]{3,2,1,0:T(8,128)(2,1)S(1)} %shard_map.65), channel_id=1, source_target_pairs={{0,8},{8,0},{1,9},{9,1},{2,10},{10,2},{3,11},{11,3},{4,12},{12,4},... | collective-permute-start | bytes 786440 | tf_op jit(solution)/shard_map/ppermute | solution.py:159

commit v5 on v4

v5 whole, which is shorter than its diff:
```python
import functools
import math

import jax
import jax.numpy as jnp
from jax import lax
from jax.experimental import pallas as pl
from jax.experimental.pallas import tpu as pltpu
from jax.sharding import PartitionSpec as P

H = 16
HEAD = 128
AXES = ("frame", "seq")
SMEM = pl.BlockSpec(memory_space=pltpu.SMEM)
HBM = pl.BlockSpec(memory_space=pltpu.HBM)
VMEM = pl.BlockSpec(memory_space=pltpu.VMEM)
PARAMS = pltpu.CompilerParams(vmem_limit_bytes=32 * 1024 * 1024)


def far_first(count):
    return sorted(range(count), key=lambda away: (away > 0, -(2 * away // count), away % 2, -away))


def columns_of(place, width):
    return pl.ds(pl.multiple_of(place * width, width), width)


def run(copies):
    for copy in copies:
        copy.start()
    for copy in copies:
        copy.wait()


def pack(*refs, near):
    operands, outs, sems = refs[:3], refs[3:-1], refs[-1]
    place = lax.axis_index("seq") // near
    copies = []
    for number, (away, out_ref) in enumerate(zip(far_first(len(outs)), outs)):
        columns = columns_of(place ^ away, out_ref.shape[-1])
        copies += [
            pltpu.make_async_copy(ref.at[:, columns], out_ref.at[kind], sems.at[number, kind])
            for kind, ref in enumerate(operands)
        ]
    run(copies)


def stack(*refs):
    pieces, out_ref, sems = refs[:-2], refs[-2], refs[-1]
    run(
        [
            pltpu.make_async_copy(ref.at[pl.ds(1, 2)], out_ref.at[number], sems.at[number])
            for number, ref in enumerate(pieces)
        ]
    )


def unpack(*refs, near):
    answers, out_ref, sems = refs[:-2], refs[-2], refs[-1]
    place = lax.axis_index("seq") // near
    run(
        [
            pltpu.make_async_copy(
                ref, out_ref.at[:, columns_of(place ^ away, ref.shape[-1])], sems.at[number]
            )
            for number, (away, ref) in enumerate(zip(far_first(len(answers)), answers))
        ]
    )


def attend(slot_ref, level_ref, gate_ref, *refs, pieces, near, tokens):
    held_refs, pair_refs, outs = refs[: near * pieces], refs[near * pieces : -pieces], refs[-pieces:]
    rows, width = outs[0].shape
    group_count = 1 + len(pair_refs)
    local_frames = rows // tokens
    group_keys = near * pieces * rows
    key_count = group_count * group_keys
    group = lax.axis_index("frame")
    index = lax.broadcasted_iota(jnp.int32, (1, key_count), 1)
    frame = (index // group_keys + group) % group_count * local_frames
    frame = frame + index // tokens % local_frames
    key_slots = jnp.zeros((1, key_count), jnp.int32)
    for one in range(group_count * local_frames):
        slot = slot_ref[one // local_frames, one % local_frames]
        key_slots = jnp.where(frame == one, slot, key_slots)
    shown = []
    for local in range(local_frames):
        visible = key_slots <= slot_ref[group, local]
        shown.append(jnp.where(visible, 0.0, -jnp.inf).reshape(1, 1, 1, key_count))
    shown = jnp.concatenate(shown, axis=1)
    ones = jnp.ones((key_count, HEAD), jnp.bfloat16)
    scale = math.log2(math.e) / math.sqrt(HEAD)
    gate_blocks = gate_ref[:, columns_of(lax.axis_index("seq") // near, width)]
    level_rows = lax.broadcasted_iota(jnp.int32, gate_blocks.shape, 0)
    gate_rows = [
        jnp.sum(
            jnp.where(level_rows == level_ref[group, local], gate_blocks, 0.0),
            axis=0,
            keepdims=True,
        )
        for local in range(local_frames)
    ]
    step = max(1, min(pieces, 128 // rows))
    for column in range(0, width, HEAD):
        part = slice(column, column + HEAD)
        gates = jnp.concatenate([row[:, part].reshape(1, 1, 1, HEAD) for row in gate_rows], axis=1)
        keys, values = (
            jnp.concatenate(
                [ref[1 + kind, :, part] for ref in held_refs]
                + [ref[:, kind, :, part].reshape(group_keys, HEAD) for ref in pair_refs]
            )
            for kind in range(2)
        )
        values = jnp.concatenate([values, ones], axis=1)
        for start in range(0, pieces, step):
            queries = jnp.concatenate([ref[0, :, part] for ref in held_refs[start : start + step]])
            scores = lax.dot_general(
                queries, keys, (((1,), (1,)), ((), ())), preferred_element_type=jnp.float32
            )
            scores = scores.reshape(step, local_frames, tokens, key_count) * scale + shown
            scores = scores.reshape(step * rows, key_count)
            weights = jnp.exp2(scores - jnp.max(scores, axis=1, keepdims=True))
            mixed = jnp.dot(
                weights.astype(jnp.bfloat16), values, preferred_element_type=jnp.float32
            )
            mixed = mixed[:, :HEAD] / mixed[:, HEAD:]
            mixed = mixed.reshape(step, local_frames, tokens, HEAD) * gates
            mixed = mixed.reshape(step, rows, HEAD).astype(jnp.bfloat16)
            for number in range(step):
                outs[start + number][:, part] = mixed[number]


def whole_heads(queries, keys, values, slot_of, level_of, gate_table):
    devices, groups = lax.axis_size("seq"), lax.axis_size("frame")
    near = min(2, devices)
    count = devices // near
    _, local_frames, tokens, all_width = queries.shape
    rows, width = local_frames * tokens, all_width // count

    def swap(taken, away):
        return lax.ppermute(taken, "seq", [(one, one ^ away) for one in range(devices)])

    def swap_far(taken):
        return [
            swap(one, away * near) if away else one for away, one in zip(far_first(count), taken)
        ]

    pieces = pl.pallas_call(
        functools.partial(pack, near=near),
        out_shape=[jax.ShapeDtypeStruct((3, rows, width), queries.dtype)] * count,
        in_specs=[HBM] * 3,
        out_specs=[VMEM] * count,
        scratch_shapes=[pltpu.SemaphoreType.DMA((count, 3))],
        compiler_params=PARAMS,
    )(
        *(
            pltpu.with_memory_space_constraint(taken.reshape(rows, all_width), pltpu.HBM)
            for taken in (queries, keys, values)
        ),
    )
    pieces = swap_far(pieces)
    held = pieces + [swap(piece, away) for away in range(1, near) for piece in pieces]
    pair = pl.pallas_call(
        stack,
        out_shape=jax.ShapeDtypeStruct((len(held), 2, rows, width), queries.dtype),
        in_specs=[VMEM] * len(held),
        out_specs=VMEM,
        scratch_shapes=[pltpu.SemaphoreType.DMA((len(held),))],
        compiler_params=PARAMS,
    )(*held)
    pairs = [
        lax.ppermute(pair, "frame", [(one, (one - away) % groups) for one in range(groups)])
        for away in range(1, groups)
    ]
    answers = pl.pallas_call(
        functools.partial(attend, pieces=count, near=near, tokens=tokens),
        out_shape=[jax.ShapeDtypeStruct((rows, width), queries.dtype)] * count,
        in_specs=[SMEM] * 2 + [VMEM] * (len(held) + groups),
        out_specs=[VMEM] * count,
        compiler_params=PARAMS,
    )(slot_of, level_of, gate_table, *held, *pairs)
    answers = swap_far(answers)
    answer = pl.pallas_call(
        functools.partial(unpack, near=near),
        out_shape=jax.ShapeDtypeStruct((rows, all_width), queries.dtype),
        in_specs=[VMEM] * count,
        out_specs=HBM,
        scratch_shapes=[pltpu.SemaphoreType.DMA((count,))],
        compiler_params=PARAMS,
    )(*answers)
    return answer.reshape(queries.shape)


def shared_heads(queries, keys, values, slot_of, level_of, gate_table):
    devices = lax.axis_size("frame") * lax.axis_size("seq")
    _, local_frames, tokens, _ = queries.shape
    rows, blocks = local_frames * tokens, devices // H
    block_rows = rows // blocks
    exchange = functools.partial(
        lax.all_to_all, axis_name=AXES, split_axis=0, concat_axis=0, tiled=True
    )

    def by_head(taken):
        return taken.reshape(rows, H, HEAD).transpose(1, 0, 2)

    def key_pieces(taken):
        pieces = jnp.broadcast_to(by_head(taken)[:, None], (H, blocks, rows, HEAD))
        return exchange(pieces.reshape(devices, rows, HEAD)).reshape(devices * rows, HEAD)

    key_rows, value_rows = key_pieces(keys), key_pieces(values)
    query_rows = exchange(by_head(queries).reshape(devices, block_rows, HEAD))
    query_rows = query_rows.reshape(devices * block_rows, HEAD)
    device_index = lax.axis_index("frame") * lax.axis_size("seq") + lax.axis_index("seq")
    head, block = device_index // blocks, device_index % blocks

    def per_row(table):
        table = jnp.repeat(table, tokens, axis=1)[:, None]
        return jnp.broadcast_to(table, (table.shape[0], lax.axis_size("seq"), rows))

    row_slots, row_levels = per_row(slot_of), per_row(level_of)
    query_slots = lax.dynamic_slice_in_dim(row_slots, block * block_rows, block_rows, 2)
    levels = lax.dynamic_slice_in_dim(row_levels, block * block_rows, block_rows, 2).reshape(-1)
    scores = lax.dot_general(
        query_rows, key_rows, (((1,), (1,)), ((), ())), preferred_element_type=jnp.float32
    )
    visible = row_slots.reshape(1, -1) <= query_slots.reshape(-1, 1)
    scores = jnp.where(visible, scores * (1.0 / math.sqrt(HEAD)), -jnp.inf)
    weights = jnp.exp(scores - jnp.max(scores, axis=1, keepdims=True)).astype(jnp.bfloat16)
    total = jnp.sum(weights.astype(jnp.float32), axis=1, keepdims=True)
    mixed = jnp.dot(weights, value_rows, preferred_element_type=jnp.float32) / total
    gates = lax.dynamic_slice_in_dim(gate_table, head * HEAD, HEAD, 1)[levels]
    answer = exchange((mixed * gates).astype(queries.dtype).reshape(devices, block_rows, HEAD))
    return answer.reshape(H, rows, HEAD).transpose(1, 0, 2).reshape(queries.shape)


def body(queries, *others):
    devices = lax.axis_size("seq")
    if devices > H or devices & (devices - 1):
        return shared_heads(queries, *others)
    return whole_heads(queries, *others)


def solution(mesh):
    return jax.shard_map(
        body,
        mesh=mesh,
        in_specs=(
            P(("rollout", "frame"), None, "seq", None),
            P(("rollout", "frame"), None, "seq", None),
            P(("rollout", "frame"), None, "seq", None),
            P("rollout", None),
            P("rollout", None),
            P(),
        ),
        out_specs=P(("rollout", "frame"), None, "seq", None),
        check_vma=False,
    )
```

time: 34.3 us -> 34.4 us (level)
  blocking collectives: 12.4 us -> 0 us
  waiting for transfers between devices: 4.6 us -> 14.6 us
  starting transfers between devices: 12.9 us -> 15.9 us
  Pallas kernels: 4.08 us -> 3.69 us
    all_to_all x1 -> x0, blocking collectives: 12.4 us -> none  [whole_heads(): lax.all_to_all(answer, 'seq', split_axis=0, concat_axis=0, tiled=True)]
    ppermute x7 -> x10, waiting for transfers between devices: 3.08 us -> 12.7 us  [swap(): lax.ppermute(taken, 'seq', [(one, one ^ away) for one in range(devices)])]
    ppermute x7 -> x10, starting transfers between devices: 12.8 us -> 15.8 us  [swap(): lax.ppermute(taken, 'seq', [(one, one ^ away) for one in range(devices)])]
    pallas_call x4, Pallas kernels: 4.08 us -> 3.69 us  [the longest x1 1.23 us: whole_heads(): pl.pallas_call(functools.partial(attend, pieces=count, near=near, tokens=...]
    ppermute x1, waiting for transfers between devices: 1.52 us -> 1.9 us  [whole_heads(): lax.ppermute(pair, 'frame', [(one, (one - away) % groups) for one in rang...]
  transfers between devices with their start and end apart: 8 -> 11, of which waited for: 4 -> 7; matrix products, arithmetic and copies ran while one was open for 0% -> 0% of each run, Pallas kernels for 0% -> 0%
where the time goes in v5:
time: 34.4 us; the launch traced here: 34.2 us
  starting transfers between devices  15.9 us (46%)
  waiting for transfers between devices  14.6 us (42%)
  Pallas kernels  3.69 us (11%)
    ppermute x10, starting transfers between devices, swap(): lax.ppermute(taken, 'seq', [(one, one ^ away) for one in range(devices)])  15.8 us
    ppermute x10, waiting for transfers between devices, swap(): lax.ppermute(taken, 'seq', [(one, one ^ away) for one in range(devices)])  12.7 us
    ppermute x1, waiting for transfers between devices, whole_heads(): lax.ppermute(pair, 'frame', [(one, (one - away) % groups) for one in rang...  1.9 us
    pallas_call x1, Pallas kernels, whole_heads(): pl.pallas_call(functools.partial(attend, pieces=count, near=near, tokens=...  1.23 us
    pallas_call x1, Pallas kernels, whole_heads(): pl.pallas_call(functools.partial(pack, near=near), out_shape=[jax.ShapeDt...  1.04 us
    pallas_call x1, Pallas kernels, whole_heads(): pl.pallas_call(stack, out_shape=jax.ShapeDtypeStruct((len(held), 2, rows,...  0.73 us
  transfers between devices with their start and end apart: 11, of which 7 were waited for; matrix products, arithmetic and copies ran while one was open for 0% of the time, Pallas kernels for 0%

profile of v5, /device:TPU:0, one launch (start us, length us, event | category | flops | bytes accessed | tf_op | source)
XLA Modules:
  0.0 34.2 jit_solution(5627820504259187235)
XLA Ops:
  0.0 1.0 %shard_map.64 = (bf16[3,32,512]{2,1,0:T(8,128)(2,1)S(1)}, bf16[3,32,512]{2,1,0:T(8,128)(2,1)S(1)}, bf16[3,32,512]{2,1,0:T(8,128)(2,1)S(1)}, bf16[3,32,512]{2,1,0:T(8,128)(2,1)S(1)}) custom-call(bf16[32,2048]{1,0:T(8,128)(2,1)} %bitcast.4, bf16[32,2048]{1,0:T(8,128)(2,1)} %bitcast.5, bf16[32,2048]{1,0:T(8,128)(2,1)} %bitcast.6), custom_call_target="tpu_custom_call" | custom-call | tf_op jit(solution)/shard_map/pallas_call | solution.py:148
  1.0 4.1 %collective-permute-start = (bf16[3,32,512]{2,1,0:T(8,128)(2,1)S(1)}, bf16[3,32,512]{2,1,0:T(8,128)(2,1)S(1)}, u32[]{:S(2)}, u32[]{:S(2)}) collective-permute-start(bf16[3,32,512]{2,1,0:T(8,128)(2,1)S(1)} %get-tuple-element.14), channel_id=1, source_target_pairs={{0,4},{1,5},{2,6},{3,7},{4,0},{5,1},{6,2},{7,3},{8,12},{9,13},{10,... | collective-permute-start | bytes 294920 | tf_op jit(solution)/shard_map/ppermute | solution.py:141
  5.1 1.3 %collective-permute-start.1 = (bf16[3,32,512]{2,1,0:T(8,128)(2,1)S(1)}, bf16[3,32,512]{2,1,0:T(8,128)(2,1)S(1)}, u32[]{:S(2)}, u32[]{:S(2)}) collective-permute-start(bf16[3,32,512]{2,1,0:T(8,128)(2,1)S(1)} %get-tuple-element.15), channel_id=1, source_target_pairs={{0,6},{1,7},{2,4},{3,5},{4,2},{5,3},{6,0},{7,1},{8,14},{9,15},{10,... | collective-permute-start | bytes 294920 | tf_op jit(solution)/shard_map/ppermute | solution.py:141
  6.5 0.2 collective-permute-start.2
  6.7 0.0 copy-start
  6.7 0.0 copy-start.1
  6.7 0.0 copy-start.2
  6.7 1.5 %collective-permute-start.3 = (bf16[3,32,512]{2,1,0:T(8,128)(2,1)S(1)}, bf16[3,32,512]{2,1,0:T(8,128)(2,1)S(1)}, u32[]{:S(2)}, u32[]{:S(2)}) collective-permute-start(bf16[3,32,512]{2,1,0:T(8,128)(2,1)S(1)} %get-tuple-element.13.refs_0_), channel_id=1, source_target_pairs={{0,1},{1,0},{2,3},{3,2},{4,5},{5,4},{6,7},{7,6},{8,9},{9,8},{10,11... | collective-permute-start | bytes 294920 | tf_op jit(solution)/shard_map/ppermute | solution.py:141
  8.2 4.8 %collective-permute-done.refs_1_ = bf16[3,32,512]{2,1,0:T(8,128)(2,1)S(1)} collective-permute-done((bf16[3,32,512]{2,1,0:T(8,128)(2,1)S(1)}, bf16[3,32,512]{2,1,0:T(8,128)(2,1)S(1)}, u32[]{:S(2)}, u32[]{:S(2)}) %collective-permute-start) | collective-permute-done | bytes 98336 | tf_op jit(solution)/shard_map/ppermute | solution.py:141
  13.0 1.7 %collective-permute-start.4 = (bf16[3,32,512]{2,1,0:T(8,128)(2,1)S(1)}, bf16[3,32,512]{2,1,0:T(8,128)(2,1)S(1)}, u32[]{:S(2)}, u32[]{:S(2)}) collective-permute-start(bf16[3,32,512]{2,1,0:T(8,128)(2,1)S(1)} %collective-permute-done.refs_1_), channel_id=1, source_target_pairs={{0,1},{1,0},{2,3},{3,2},{4,5},{5,4},{6,7},{7,6},{8,9},{9,8},{10,11... | collective-permute-start | bytes 294920 | tf_op jit(solution)/shard_map/ppermute | solution.py:141
  14.7 0.0 collective-permute-done.1.refs_2_
  14.7 0.3 collective-permute-start.5
  15.1 0.0 collective-permute-done.2.refs_3_
  15.1 1.7 %collective-permute-start.6 = (bf16[3,32,512]{2,1,0:T(8,128)(2,1)S(1)}, bf16[3,32,512]{2,1,0:T(8,128)(2,1)S(1)}, u32[]{:S(2)}, u32[]{:S(2)}) collective-permute-start(bf16[3,32,512]{2,1,0:T(8,128)(2,1)S(1)} %collective-permute-done.2.refs_3_), channel_id=1, source_target_pairs={{0,1},{1,0},{2,3},{3,2},{4,5},{5,4},{6,7},{7,6},{8,9},{9,8},{10,11... | collective-permute-start | bytes 294920 | tf_op jit(solution)/shard_map/ppermute | solution.py:141
  16.8 0.0 collective-permute-done.3.refs_4_
  16.8 0.9 %collective-permute-done.4.refs_5_ = bf16[3,32,512]{2,1,0:T(8,128)(2,1)S(1)} collective-permute-done((bf16[3,32,512]{2,1,0:T(8,128)(2,1)S(1)}, bf16[3,32,512]{2,1,0:T(8,128)(2,1)S(1)}, u32[]{:S(2)}, u32[]{:S(2)}) %collective-permute-start.4) | collective-permute-done | bytes 98336 | tf_op jit(solution)/shard_map/ppermute | solution.py:141
  17.6 1.7 %collective-permute-done.5.refs_6_ = bf16[3,32,512]{2,1,0:T(8,128)(2,1)S(1)} collective-permute-done((bf16[3,32,512]{2,1,0:T(8,128)(2,1)S(1)}, bf16[3,32,512]{2,1,0:T(8,128)(2,1)S(1)}, u32[]{:S(2)}, u32[]{:S(2)}) %collective-permute-start.5) | collective-permute-done | bytes 98336 | tf_op jit(solution)/shard_map/ppermute | solution.py:141
  19.4 1.1 %collective-permute-done.6.refs_7_ = bf16[3,32,512]{2,1,0:T(8,128)(2,1)S(1)} collective-permute-done((bf16[3,32,512]{2,1,0:T(8,128)(2,1)S(1)}, bf16[3,32,512]{2,1,0:T(8,128)(2,1)S(1)}, u32[]{:S(2)}, u32[]{:S(2)}) %collective-permute-start.6) | collective-permute-done | bytes 98336 | tf_op jit(solution)/shard_map/ppermute | solution.py:141
  20.4 0.7 %shard_map.65 = bf16[8,2,32,512]{3,2,1,0:T(8,128)(2,1)S(1)} custom-call(bf16[3,32,512]{2,1,0:T(8,128)(2,1)S(1)} %get-tuple-element.13.refs_0_, bf16[3,32,512]{2,1,0:T(8,128)(2,1)S(1)} %collective-permute-done.refs_1_, bf16[3,32,512]{2,1,0:T(8,128)(2,1)S(1)} %collective-permute-done.1.refs_2_, bf16[3,32,512]{2,1,0:T(8,128)(2,1)S(1)} %collective-permute-done.2.refs_3_, ...), custom_call_target="tpu_custom_call" | custom-call | tf_op jit(solution)/shard_map/pallas_call | solution.py:163
  21.1 0.1 collective-permute-start.7
  21.2 1.9 %collective-permute-done.7.refs_8_ = bf16[8,2,32,512]{3,2,1,0:T(8,128)(2,1)S(1)} collective-permute-done((bf16[8,2,32,512]{3,2,1,0:T(8,128)(2,1)S(1)}, bf16[8,2,32,512]{3,2,1,0:T(8,128)(2,1)S(1)}, u32[]{:S(2)}, u32[]{:S(2)}) %collective-permute-start.7) | collective-permute-done | bytes 524320 | tf_op jit(solution)/shard_map/ppermute | solution.py:172
  23.1 0.0 copy-done
  23.1 0.0 copy-done.1
  23.1 0.0 copy-done.2
  23.1 1.2 %shard_map.66 = (bf16[32,512]{1,0:T(8,128)(2,1)S(1)}, bf16[32,512]{1,0:T(8,128)(2,1)S(1)}, bf16[32,512]{1,0:T(8,128)(2,1)S(1)}, bf16[32,512]{1,0:T(8,128)(2,1)S(1)}) custom-call(s32[2,4]{1,0:T(2,128)S(1)} %copy-done.1, s32[2,4]{1,0:T(2,128)S(1)} %copy-done.2, f32[8,2048]{1,0:T(8,128)S(1)} %copy-done, bf16[3,32,512]{2,1,0:T(8,128)(2,1)S(1)} %get-tuple-element.13.refs_0_, ...), custom_call_target="tpu_custom_call" | custom-call | tf_op jit(solution)/shard_map/pallas_call | solution.py:175
  24.4 3.4 %collective-permute-start.8 = (bf16[32,512]{1,0:T(8,128)(2,1)S(1)}, bf16[32,512]{1,0:T(8,128)(2,1)S(1)}, u32[]{:S(2)}, u32[]{:S(2)}) collective-permute-start(bf16[32,512]{1,0:T(8,128)(2,1)S(1)} %get-tuple-element.18), channel_id=1, source_target_pairs={{0,4},{1,5},{2,6},{3,7},{4,0},{5,1},{6,2},{7,3},{8,12},{9,13},{10,... | collective-permute-start | bytes 98312 | tf_op jit(solution)/shard_map/ppermute | solution.py:141
  27.8 1.0 %collective-permute-start.9 = (bf16[32,512]{1,0:T(8,128)(2,1)S(1)}, bf16[32,512]{1,0:T(8,128)(2,1)S(1)}, u32[]{:S(2)}, u32[]{:S(2)}) collective-permute-start(bf16[32,512]{1,0:T(8,128)(2,1)S(1)} %get-tuple-element.19), channel_id=1, source_target_pairs={{0,6},{1,7},{2,4},{3,5},{4,2},{5,3},{6,0},{7,1},{8,14},{9,15},{10,... | collective-permute-start | bytes 98312 | tf_op jit(solution)/shard_map/ppermute | solution.py:141
  28.8 0.5 %collective-permute-start.10 = (bf16[32,512]{1,0:T(8,128)(2,1)S(1)}, bf16[32,512]{1,0:T(8,128)(2,1)S(1)}, u32[]{:S(2)}, u32[]{:S(2)}) collective-permute-start(bf16[32,512]{1,0:T(8,128)(2,1)S(1)} %get-tuple-element.20), channel_id=1, source_target_pairs={{0,2},{1,3},{2,0},{3,1},{4,6},{5,7},{6,4},{7,5},{8,10},{9,11},{10,... | collective-permute-start | bytes 98312 | tf_op jit(solution)/shard_map/ppermute | solution.py:141
  29.3 0.4 %collective-permute-done.8.refs_1_ = bf16[32,512]{1,0:T(8,128)(2,1)S(1)} collective-permute-done((bf16[32,512]{1,0:T(8,128)(2,1)S(1)}, bf16[32,512]{1,0:T(8,128)(2,1)S(1)}, u32[]{:S(2)}, u32[]{:S(2)}) %collective-permute-start.8) | collective-permute-done | bytes 32800 | tf_op jit(solution)/shard_map/ppermute | solution.py:141
  29.7 3.8 %collective-permute-done.9.refs_2_ = bf16[32,512]{1,0:T(8,128)(2,1)S(1)} collective-permute-done((bf16[32,512]{1,0:T(8,128)(2,1)S(1)}, bf16[32,512]{1,0:T(8,128)(2,1)S(1)}, u32[]{:S(2)}, u32[]{:S(2)}) %collective-permute-start.9) | collective-permute-done | bytes 32800 | tf_op jit(solution)/shard_map/ppermute | solution.py:141
  33.5 0.0 collective-permute-done.10.refs_3_
  33.5 0.7 %shard_map.67 = bf16[32,2048]{1,0:T(8,128)(2,1)} custom-call(bf16[32,512]{1,0:T(8,128)(2,1)S(1)} %get-tuple-element.17.refs_0_, bf16[32,512]{1,0:T(8,128)(2,1)S(1)} %collective-permute-done.8.refs_1_, bf16[32,512]{1,0:T(8,128)(2,1)S(1)} %collective-permute-done.9.refs_2_, bf16[32,512]{1,0:T(8,128)(2,1)S(1)} %collective-permute-done.10.refs_3_), custom_call_target="tpu_custom_call" | custom-call | tf_op jit(solution)/shard_map/pallas_call | solution.py:183
Async XLA Ops:
  1.0 12.0 %collective-permute-start = (bf16[3,32,512]{2,1,0:T(8,128)(2,1)S(1)}, bf16[3,32,512]{2,1,0:T(8,128)(2,1)S(1)}, u32[]{:S(2)}, u32[]{:S(2)}) collective-permute-start(bf16[3,32,512]{2,1,0:T(8,128)(2,1)S(1)} %get-tuple-element.14), channel_id=1, source_target_pairs={{0,4},{1,5},{2,6},{3,7},{4,0},{5,1},{6,2},{7,3},{8,12},{9,13},{10,... | collective-permute-start | bytes 294920 | tf_op jit(solution)/shard_map/ppermute | solution.py:141
  5.1 9.6 %collective-permute-start.1 = (bf16[3,32,512]{2,1,0:T(8,128)(2,1)S(1)}, bf16[3,32,512]{2,1,0:T(8,128)(2,1)S(1)}, u32[]{:S(2)}, u32[]{:S(2)}) collective-permute-start(bf16[3,32,512]{2,1,0:T(8,128)(2,1)S(1)} %get-tuple-element.15), channel_id=1, source_target_pairs={{0,6},{1,7},{2,4},{3,5},{4,2},{5,3},{6,0},{7,1},{8,14},{9,15},{10,... | collective-permute-start | bytes 294920 | tf_op jit(solution)/shard_map/ppermute | solution.py:141
  6.5 8.6 %collective-permute-start.2 = (bf16[3,32,512]{2,1,0:T(8,128)(2,1)S(1)}, bf16[3,32,512]{2,1,0:T(8,128)(2,1)S(1)}, u32[]{:S(2)}, u32[]{:S(2)}) collective-permute-start(bf16[3,32,512]{2,1,0:T(8,128)(2,1)S(1)} %get-tuple-element.16), channel_id=1, source_target_pairs={{0,2},{1,3},{2,0},{3,1},{4,6},{5,7},{6,4},{7,5},{8,10},{9,11},{10,... | collective-permute-start | bytes 294920 | tf_op jit(solution)/shard_map/ppermute | solution.py:141
  6.7 16.4 %copy-start = (f32[8,2048]{1,0:T(8,128)S(1)}, f32[8,2048]{1,0:T(8,128)}, u32[]{:S(2)}) copy-start(f32[8,2048]{1,0:T(8,128)} %gate_ref.1) | copy-start | bytes 196612
  6.7 16.4 %copy-start.1 = (s32[2,4]{1,0:T(2,128)S(1)}, s32[2,4]{1,0:T(2,128)}, u32[]{:S(2)}) copy-start(s32[2,4]{1,0:T(2,128)} %slot_ref.1) | copy-start | bytes 100
  6.7 16.4 %copy-start.2 = (s32[2,4]{1,0:T(2,128)S(1)}, s32[2,4]{1,0:T(2,128)}, u32[]{:S(2)}) copy-start(s32[2,4]{1,0:T(2,128)} %level_ref.1) | copy-start | bytes 100
  6.7 10.0 %collective-permute-start.3 = (bf16[3,32,512]{2,1,0:T(8,128)(2,1)S(1)}, bf16[3,32,512]{2,1,0:T(8,128)(2,1)S(1)}, u32[]{:S(2)}, u32[]{:S(2)}) collective-permute-start(bf16[3,32,512]{2,1,0:T(8,128)(2,1)S(1)} %get-tuple-element.13.refs_0_), channel_id=1, source_target_pairs={{0,1},{1,0},{2,3},{3,2},{4,5},{5,4},{6,7},{7,6},{8,9},{9,8},{10,11... | collective-permute-start | bytes 294920 | tf_op jit(solution)/shard_map/ppermute | solution.py:141
  13.0 4.6 %collective-permute-start.4 = (bf16[3,32,512]{2,1,0:T(8,128)(2,1)S(1)}, bf16[3,32,512]{2,1,0:T(8,128)(2,1)S(1)}, u32[]{:S(2)}, u32[]{:S(2)}) collective-permute-start(bf16[3,32,512]{2,1,0:T(8,128)(2,1)S(1)} %collective-permute-done.refs_1_), channel_id=1, source_target_pairs={{0,1},{1,0},{2,3},{3,2},{4,5},{5,4},{6,7},{7,6},{8,9},{9,8},{10,11... | collective-permute-start | bytes 294920 | tf_op jit(solution)/shard_map/ppermute | solution.py:141
  14.7 4.6 %collective-permute-start.5 = (bf16[3,32,512]{2,1,0:T(8,128)(2,1)S(1)}, bf16[3,32,512]{2,1,0:T(8,128)(2,1)S(1)}, u32[]{:S(2)}, u32[]{:S(2)}) collective-permute-start(bf16[3,32,512]{2,1,0:T(8,128)(2,1)S(1)} %collective-permute-done.1.refs_2_), channel_id=1, source_target_pairs={{0,1},{1,0},{2,3},{3,2},{4,5},{5,4},{6,7},{7,6},{8,9},{9,8},{10,11... | collective-permute-start | bytes 294920 | tf_op jit(solution)/shard_map/ppermute | solution.py:141
  15.1 5.3 %collective-permute-start.6 = (bf16[3,32,512]{2,1,0:T(8,128)(2,1)S(1)}, bf16[3,32,512]{2,1,0:T(8,128)(2,1)S(1)}, u32[]{:S(2)}, u32[]{:S(2)}) collective-permute-start(bf16[3,32,512]{2,1,0:T(8,128)(2,1)S(1)} %collective-permute-done.2.refs_3_), channel_id=1, source_target_pairs={{0,1},{1,0},{2,3},{3,2},{4,5},{5,4},{6,7},{7,6},{8,9},{9,8},{10,11... | collective-permute-start | bytes 294920 | tf_op jit(solution)/shard_map/ppermute | solution.py:141
  21.1 2.0 %collective-permute-start.7 = (bf16[8,2,32,512]{3,2,1,0:T(8,128)(2,1)S(1)}, bf16[8,2,32,512]{3,2,1,0:T(8,128)(2,1)S(1)}, u32[]{:S(2)}, u32[]{:S(2)}) collective-permute-start(bf16[8,2,32,512]{3,2,1,0:T(8,128)(2,1)S(1)} %shard_map.65), channel_id=1, source_target_pairs={{0,8},{8,0},{1,9},{9,1},{2,10},{10,2},{3,11},{11,3},{4,12},{12,4},... | collective-permute-start | bytes 1572872 | tf_op jit(solution)/shard_map/ppermute | solution.py:172
  24.4 5.3 %collective-permute-start.8 = (bf16[32,512]{1,0:T(8,128)(2,1)S(1)}, bf16[32,512]{1,0:T(8,128)(2,1)S(1)}, u32[]{:S(2)}, u32[]{:S(2)}) collective-permute-start(bf16[32,512]{1,0:T(8,128)(2,1)S(1)} %get-tuple-element.18), channel_id=1, source_target_pairs={{0,4},{1,5},{2,6},{3,7},{4,0},{5,1},{6,2},{7,3},{8,12},{9,13},{10,... | collective-permute-start | bytes 98312 | tf_op jit(solution)/shard_map/ppermute | solution.py:141
  27.8 5.7 %collective-permute-start.9 = (bf16[32,512]{1,0:T(8,128)(2,1)S(1)}, bf16[32,512]{1,0:T(8,128)(2,1)S(1)}, u32[]{:S(2)}, u32[]{:S(2)}) collective-permute-start(bf16[32,512]{1,0:T(8,128)(2,1)S(1)} %get-tuple-element.19), channel_id=1, source_target_pairs={{0,6},{1,7},{2,4},{3,5},{4,2},{5,3},{6,0},{7,1},{8,14},{9,15},{10,... | collective-permute-start | bytes 98312 | tf_op jit(solution)/shard_map/ppermute | solution.py:141
  28.8 4.7 %collective-permute-start.10 = (bf16[32,512]{1,0:T(8,128)(2,1)S(1)}, bf16[32,512]{1,0:T(8,128)(2,1)S(1)}, u32[]{:S(2)}, u32[]{:S(2)}) collective-permute-start(bf16[32,512]{1,0:T(8,128)(2,1)S(1)} %get-tuple-element.20), channel_id=1, source_target_pairs={{0,2},{1,3},{2,0},{3,1},{4,6},{5,7},{6,4},{7,5},{8,10},{9,11},{10,... | collective-permute-start | bytes 98312 | tf_op jit(solution)/shard_map/ppermute | solution.py:141

commit v6 on v5

--- a/solution.py
+++ b/solution.py
@@ -33,23 +33,25 @@
 
 
 def pack(*refs, near):
-    operands, outs, sems = refs[:3], refs[3:-1], refs[-1]
+    query_ref, key_ref, value_ref, *outs, sems = refs
     place = lax.axis_index("seq") // near
+    count = len(outs) // 2
     copies = []
-    for number, (away, out_ref) in enumerate(zip(far_first(len(outs)), outs)):
-        columns = columns_of(place ^ away, out_ref.shape[-1])
-        copies += [
-            pltpu.make_async_copy(ref.at[:, columns], out_ref.at[kind], sems.at[number, kind])
-            for kind, ref in enumerate(operands)
-        ]
+    for number, away in enumerate(far_first(count)):
+        pair_ref, own_ref = outs[number], outs[count + number]
+        columns = columns_of(place ^ away, own_ref.shape[-1])
+        for kind, (ref, out_ref) in enumerate(
+            ((key_ref, pair_ref.at[0]), (value_ref, pair_ref.at[1]), (query_ref, own_ref))
+        ):
+            copies.append(pltpu.make_async_copy(ref.at[:, columns], out_ref, sems.at[number, kind]))
     run(copies)
 
 
 def stack(*refs):
-    pieces, out_ref, sems = refs[:-2], refs[-2], refs[-1]
+    *pieces, out_ref, sems = refs
     run(
         [
-            pltpu.make_async_copy(ref.at[pl.ds(1, 2)], out_ref.at[number], sems.at[number])
+            pltpu.make_async_copy(ref, out_ref.at[number], sems.at[number])
             for number, ref in enumerate(pieces)
         ]
     )
@@ -69,9 +71,10 @@
 
 
 def attend(slot_ref, level_ref, gate_ref, *refs, pieces, near, tokens):
-    held_refs, pair_refs, outs = refs[: near * pieces], refs[near * pieces : -pieces], refs[-pieces:]
+    query_refs, refs, outs = refs[:pieces], refs[pieces:-pieces], refs[-pieces:]
+    held_refs, stack_refs = refs[: near * pieces], refs[near * pieces :]
     rows, width = outs[0].shape
-    group_count = 1 + len(pair_refs)
+    group_count = 1 + len(stack_refs) // near
     local_frames = rows // tokens
     group_keys = near * pieces * rows
     key_count = group_count * group_keys
@@ -106,14 +109,14 @@
         gates = jnp.concatenate([row[:, part].reshape(1, 1, 1, HEAD) for row in gate_rows], axis=1)
         keys, values = (
             jnp.concatenate(
-                [ref[1 + kind, :, part] for ref in held_refs]
-                + [ref[:, kind, :, part].reshape(group_keys, HEAD) for ref in pair_refs]
+                [ref[kind, :, part] for ref in held_refs]
+                + [ref[:, kind, :, part].reshape(pieces * rows, HEAD) for ref in stack_refs]
             )
             for kind in range(2)
         )
         values = jnp.concatenate([values, ones], axis=1)
         for start in range(0, pieces, step):
-            queries = jnp.concatenate([ref[0, :, part] for ref in held_refs[start : start + step]])
+            queries = jnp.concatenate([ref[:, part] for ref in query_refs[start : start + step]])
             scores = lax.dot_general(
                 queries, keys, (((1,), (1,)), ((), ())), preferred_element_type=jnp.float32
             )
@@ -145,11 +148,12 @@
             swap(one, away * near) if away else one for away, one in zip(far_first(count), taken)
         ]
 
-    pieces = pl.pallas_call(
+    sent = pl.pallas_call(
         functools.partial(pack, near=near),
-        out_shape=[jax.ShapeDtypeStruct((3, rows, width), queries.dtype)] * count,
+        out_shape=[jax.ShapeDtypeStruct((2, rows, width), queries.dtype)] * count
+        + [jax.ShapeDtypeStruct((rows, width), queries.dtype)] * count,
         in_specs=[HBM] * 3,
-        out_specs=[VMEM] * count,
+        out_specs=[VMEM] * (2 * count),
         scratch_shapes=[pltpu.SemaphoreType.DMA((count, 3))],
         compiler_params=PARAMS,
     )(
@@ -158,27 +162,33 @@
             for taken in (queries, keys, values)
         ),
     )
-    pieces = swap_far(pieces)
-    held = pieces + [swap(piece, away) for away in range(1, near) for piece in pieces]
-    pair = pl.pallas_call(
-        stack,
-        out_shape=jax.ShapeDtypeStruct((len(held), 2, rows, width), queries.dtype),
-        in_specs=[VMEM] * len(held),
-        out_specs=VMEM,
-        scratch_shapes=[pltpu.SemaphoreType.DMA((len(held),))],
-        compiler_params=PARAMS,
-    )(*held)
-    pairs = [
-        lax.ppermute(pair, "frame", [(one, (one - away) % groups) for one in range(groups)])
+    pairs = swap_far(sent[:count])
+    own = swap_far(sent[count:])
+    held = [pairs] + [[swap(piece, away) for piece in pairs] for away in range(1, near)]
+    stacks = [
+        pl.pallas_call(
+            stack,
+            out_shape=jax.ShapeDtypeStruct((count, 2, rows, width), queries.dtype),
+            in_specs=[VMEM] * count,
+            out_specs=VMEM,
+            scratch_shapes=[pltpu.SemaphoreType.DMA((count,))],
+            compiler_params=PARAMS,
+        )(*taken)
+        for taken in held
+    ]
+    stacks = [
+        lax.ppermute(taken, "frame", [(one, (one - away) % groups) for one in range(groups)])
         for away in range(1, groups)
+        for taken in stacks
     ]
+    held = sum(held, [])
     answers = pl.pallas_call(
         functools.partial(attend, pieces=count, near=near, tokens=tokens),
         out_shape=[jax.ShapeDtypeStruct((rows, width), queries.dtype)] * count,
-        in_specs=[SMEM] * 2 + [VMEM] * (len(held) + groups),
+        in_specs=[SMEM] * 2 + [VMEM] * (1 + count + len(held) + len(stacks)),
         out_specs=[VMEM] * count,
         compiler_params=PARAMS,
-    )(slot_of, level_of, gate_table, *held, *pairs)
+    )(slot_of, level_of, gate_table, *own, *held, *stacks)
     answers = swap_far(answers)
     answer = pl.pallas_call(
         functools.partial(unpack, near=near),

time: 34.4 us -> 35 us (1.017)
  starting transfers between devices: 15.9 us -> 19.5 us
  waiting for transfers between devices: 14.6 us -> 11.5 us
    ppermute x10 -> x13, starting transfers between devices: 15.8 us -> 19.4 us  [swap(): lax.ppermute(taken, 'seq', [(one, one ^ away) for one in range(devices)])]
    ppermute x1 -> x2, waiting for transfers between devices: 1.9 us -> 0.01 us  [whole_heads(): lax.ppermute(taken, 'frame', [(one, (one - away) % groups) for one in ran...]
    ppermute x10 -> x13, waiting for transfers between devices: 12.7 us -> 11.5 us  [swap(): lax.ppermute(taken, 'seq', [(one, one ^ away) for one in range(devices)])]
    pallas_call x1 -> x2, Pallas kernels: 0.73 us -> 0.7 us  [whole_heads(): pl.pallas_call(stack, out_shape=jax.ShapeDtypeStruct((count, 2, rows, wid...]
  transfers between devices with their start and end apart: 11 -> 15, of which waited for: 7 -> 7; matrix products, arithmetic and copies ran while one was open for 0% -> 0% of each run, Pallas kernels for 0% -> 2%
where the time goes in v6:
time: 35 us; the launch traced here: 34.8 us
  starting transfers between devices  19.5 us (56%)
  waiting for transfers between devices  11.5 us (33%)
  Pallas kernels  3.66 us (10%)
    ppermute x13, starting transfers between devices, swap(): lax.ppermute(taken, 'seq', [(one, one ^ away) for one in range(devices)])  19.4 us
    ppermute x13, waiting for transfers between devices, swap(): lax.ppermute(taken, 'seq', [(one, one ^ away) for one in range(devices)])  11.5 us
    pallas_call x1, Pallas kernels, whole_heads(): pl.pallas_call(functools.partial(attend, pieces=count, near=near, tokens=...  1.24 us
    pallas_call x1, Pallas kernels, whole_heads(): pl.pallas_call(functools.partial(pack, near=near), out_shape=[jax.ShapeDt...  1.04 us
  transfers between devices with their start and end apart: 15, of which 7 were waited for; matrix products, arithmetic and copies ran while one was open for 0% of the time, Pallas kernels for 2%

profile of v6, /device:TPU:0, one launch (start us, length us, event | category | flops | bytes accessed | tf_op | source)
XLA Modules:
  0.0 34.8 jit_solution(9470261859166654054)
XLA Ops:
  0.0 1.0 %shard_map.64 = (bf16[2,32,512]{2,1,0:T(8,128)(2,1)S(1)}, bf16[2,32,512]{2,1,0:T(8,128)(2,1)S(1)}, bf16[2,32,512]{2,1,0:T(8,128)(2,1)S(1)}, bf16[2,32,512]{2,1,0...) custom-call(bf16[32,2048]{1,0:T(8,128)(2,1)} %bitcast.4, ...), custom_call_target="tpu_custom_call" | custom-call | tf_op jit(solution)/shard_map/pallas_call | solution.py:151
  1.0 4.1 %collective-permute-start.3 = (bf16[2,32,512]{2,1,0:T(8,128)(2,1)S(1)}, bf16[2,32,512]{2,1,0:T(8,128)(2,1)S(1)}, u32[]{:S(2)}, u32[]{:S(2)}) collective-permute-start(bf16[2,32,512]{2,1,0:T(8,128)(2,1)S(1)} %get-tuple-element.22), channel_id=1, source_target_pairs={{0,4},{1,5},{2,6},{3,7},{4,0},{5,1},{6,2},{7,3},{8,12},{9,13},{10,... | collective-permute-start | bytes 196616 | tf_op jit(solution)/shard_map/ppermute | solution.py:144
  5.1 1.3 %collective-permute-start.4 = (bf16[2,32,512]{2,1,0:T(8,128)(2,1)S(1)}, bf16[2,32,512]{2,1,0:T(8,128)(2,1)S(1)}, u32[]{:S(2)}, u32[]{:S(2)}) collective-permute-start(bf16[2,32,512]{2,1,0:T(8,128)(2,1)S(1)} %get-tuple-element.23), channel_id=1, source_target_pairs={{0,6},{1,7},{2,4},{3,5},{4,2},{5,3},{6,0},{7,1},{8,14},{9,15},{10,... | collective-permute-start | bytes 196616 | tf_op jit(solution)/shard_map/ppermute | solution.py:144
  6.5 0.2 collective-permute-start.5
  6.7 1.5 %collective-permute-start.6 = (bf16[2,32,512]{2,1,0:T(8,128)(2,1)S(1)}, bf16[2,32,512]{2,1,0:T(8,128)(2,1)S(1)}, u32[]{:S(2)}, u32[]{:S(2)}) collective-permute-start(bf16[2,32,512]{2,1,0:T(8,128)(2,1)S(1)} %get-tuple-element.21.refs_0_.refs_4_), channel_id=1, source_target_pairs={{0,1},{1,0},{2,3},{3,2},{4,5},{5,4},{6,7},{7,6},{8,9},{9,8},{10,11... | collective-permute-start | bytes 196616 | tf_op jit(solution)/shard_map/ppermute | solution.py:144
  8.2 0.7 %collective-permute-done.3.refs_1_.refs_5_ = bf16[2,32,512]{2,1,0:T(8,128)(2,1)S(1)} collective-permute-done((bf16[2,32,512]{2,1,0:T(8,128)(2,1)S(1)}, bf16[2,32,512]{2,1,0:T(8,128)(2,1)S(1)}, u32[]{:S(2)}, u32[]{:S(2)}) %collective-permute-start.3) | collective-permute-done | bytes 65568 | tf_op jit(solution)/shard_map/ppermute | solution.py:144
  8.9 2.5 %collective-permute-start.7 = (bf16[2,32,512]{2,1,0:T(8,128)(2,1)S(1)}, bf16[2,32,512]{2,1,0:T(8,128)(2,1)S(1)}, u32[]{:S(2)}, u32[]{:S(2)}) collective-permute-start(bf16[2,32,512]{2,1,0:T(8,128)(2,1)S(1)} %collective-permute-done.3.refs_1_.refs_5_), channel_id=1, source_target_pairs={{0,1},{1,0},{2,3},{3,2},{4,5},{5,4},{6,7},{7,6},{8,9},{9,8},{10,11... | collective-permute-start | bytes 196616 | tf_op jit(solution)/shard_map/ppermute | solution.py:144
  11.4 0.0 collective-permute-done.4.refs_2_.refs_6_
  11.4 1.4 %collective-permute-start.8 = (bf16[2,32,512]{2,1,0:T(8,128)(2,1)S(1)}, bf16[2,32,512]{2,1,0:T(8,128)(2,1)S(1)}, u32[]{:S(2)}, u32[]{:S(2)}) collective-permute-start(bf16[2,32,512]{2,1,0:T(8,128)(2,1)S(1)} %collective-permute-done.4.refs_2_.refs_6_), channel_id=1, source_target_pairs={{0,1},{1,0},{2,3},{3,2},{4,5},{5,4},{6,7},{7,6},{8,9},{9,8},{10,11... | collective-permute-start | bytes 196616 | tf_op jit(solution)/shard_map/ppermute | solution.py:144
  12.9 0.0 collective-permute-done.5.refs_3_.refs_7_
  12.9 0.6 %collective-permute-start.9 = (bf16[2,32,512]{2,1,0:T(8,128)(2,1)S(1)}, bf16[2,32,512]{2,1,0:T(8,128)(2,1)S(1)}, u32[]{:S(2)}, u32[]{:S(2)}) collective-permute-start(bf16[2,32,512]{2,1,0:T(8,128)(2,1)S(1)} %collective-permute-done.5.refs_3_.refs_7_), channel_id=1, source_target_pairs={{0,1},{1,0},{2,3},{3,2},{4,5},{5,4},{6,7},{7,6},{8,9},{9,8},{10,11... | collective-permute-start | bytes 196616 | tf_op jit(solution)/shard_map/ppermute | solution.py:144
  13.5 0.3 shard_map.65
  13.8 0.0 copy-start
  13.8 0.1 collective-permute-start.10
  13.9 0.0 collective-permute-done.6.refs_0_.refs_8_
  13.9 0.0 collective-permute-done.7.refs_1_.refs_9_
  13.9 1.8 %collective-permute-done.8.refs_2_.refs_10_ = bf16[2,32,512]{2,1,0:T(8,128)(2,1)S(1)} collective-permute-done((bf16[2,32,512]{2,1,0:T(8,128)(2,1)S(1)}, bf16[2,32,512]{2,1,0:T(8,128)(2,1)S(1)}, u32[]{:S(2)}, u32[]{:S(2)}) %collective-permute-start.8) | collective-permute-done | bytes 65568 | tf_op jit(solution)/shard_map/ppermute | solution.py:144
  15.7 1.4 %collective-permute-done.9.refs_3_.refs_11_ = bf16[2,32,512]{2,1,0:T(8,128)(2,1)S(1)} collective-permute-done((bf16[2,32,512]{2,1,0:T(8,128)(2,1)S(1)}, bf16[2,32,512]{2,1,0:T(8,128)(2,1)S(1)}, u32[]{:S(2)}, u32[]{:S(2)}) %collective-permute-start.9) | collective-permute-done | bytes 65568 | tf_op jit(solution)/shard_map/ppermute | solution.py:144
  17.1 0.3 %shard_map.66 = bf16[4,2,32,512]{3,2,1,0:T(8,128)(2,1)S(1)} custom-call(bf16[2,32,512]{2,1,0:T(8,128)(2,1)S(1)} %collective-permute-done.6.refs_0_.refs_8_, bf16[2,32,512]{2,1,0:T(8,128)(2,1)S(1)} %collective-permute-done.7.refs_1_.refs_9_, bf16[2,32,512]{2,1,0:T(8,128)(2,1)S(1)} %collective-permute-done.8.refs_2_.refs_10_, ...), custom_call_target="tpu_custom_call" | custom-call | tf_op jit(solution)/shard_map/pallas_call | solution.py:169
  17.5 0.1 collective-permute-start.11
  17.6 2.8 %collective-permute-start = (bf16[32,512]{1,0:T(8,128)(2,1)S(1)}, bf16[32,512]{1,0:T(8,128)(2,1)S(1)}, u32[]{:S(2)}, u32[]{:S(2)}) collective-permute-start(bf16[32,512]{1,0:T(8,128)(2,1)S(1)} %get-tuple-element.18), channel_id=1, source_target_pairs={{0,4},{1,5},{2,6},{3,7},{4,0},{5,1},{6,2},{7,3},{8,12},{9,13},{10,... | collective-permute-start | bytes 98312 | tf_op jit(solution)/shard_map/ppermute | solution.py:144
  20.4 0.8 %collective-permute-start.1 = (bf16[32,512]{1,0:T(8,128)(2,1)S(1)}, bf16[32,512]{1,0:T(8,128)(2,1)S(1)}, u32[]{:S(2)}, u32[]{:S(2)}) collective-permute-start(bf16[32,512]{1,0:T(8,128)(2,1)S(1)} %get-tuple-element.19), channel_id=1, source_target_pairs={{0,6},{1,7},{2,4},{3,5},{4,2},{5,3},{6,0},{7,1},{8,14},{9,15},{10,... | collective-permute-start | bytes 98312 | tf_op jit(solution)/shard_map/ppermute | solution.py:144
  21.2 0.0 copy-start.2
  21.2 0.0 copy-start.1
  21.2 0.5 %collective-permute-start.2 = (bf16[32,512]{1,0:T(8,128)(2,1)S(1)}, bf16[32,512]{1,0:T(8,128)(2,1)S(1)}, u32[]{:S(2)}, u32[]{:S(2)}) collective-permute-start(bf16[32,512]{1,0:T(8,128)(2,1)S(1)} %get-tuple-element.20), channel_id=1, source_target_pairs={{0,2},{1,3},{2,0},{3,1},{4,6},{5,7},{6,4},{7,5},{8,10},{9,11},{10,... | collective-permute-start | bytes 98312 | tf_op jit(solution)/shard_map/ppermute | solution.py:144
  21.7 0.8 %collective-permute-done.refs_1_ = bf16[32,512]{1,0:T(8,128)(2,1)S(1)} collective-permute-done((bf16[32,512]{1,0:T(8,128)(2,1)S(1)}, bf16[32,512]{1,0:T(8,128)(2,1)S(1)}, u32[]{:S(2)}, u32[]{:S(2)}) %collective-permute-start) | collective-permute-done | bytes 32800 | tf_op jit(solution)/shard_map/ppermute | solution.py:144
  22.5 3.7 %collective-permute-done.1.refs_2_ = bf16[32,512]{1,0:T(8,128)(2,1)S(1)} collective-permute-done((bf16[32,512]{1,0:T(8,128)(2,1)S(1)}, bf16[32,512]{1,0:T(8,128)(2,1)S(1)}, u32[]{:S(2)}, u32[]{:S(2)}) %collective-permute-start.1) | collective-permute-done | bytes 32800 | tf_op jit(solution)/shard_map/ppermute | solution.py:144
  26.1 0.0 collective-permute-done.2.refs_3_
  26.1 0.0 collective-permute-done.10.refs_12_
  26.1 0.0 collective-permute-done.11.refs_13_
  26.1 0.0 copy-done
  26.1 0.0 copy-done.2
  26.1 0.0 copy-done.1
  26.2 1.2 %shard_map.67 = (bf16[32,512]{1,0:T(8,128)(2,1)S(1)}, bf16[32,512]{1,0:T(8,128)(2,1)S(1)}, bf16[32,512]{1,0:T(8,128)(2,1)S(1)}, bf16[32,512]{1,0:T(8,128)(2,1)S(1)}) custom-call(s32[2,4]{1,0:T(2,128)S(1)} %copy-done.1, s32[2,4]{1,0:T(2,128)S(1)} %copy-done.2, f32[8,2048]{1,0:T(8,128)S(1)} %copy-done, bf16[32,512]{1,0:T(8,128)(2,1)S(1)} %get-tuple-element.17.refs_0_, ...), custom_call_target="tpu_custom_call" | custom-call | tf_op jit(solution)/shard_map/pallas_call | solution.py:185
  27.4 1.0 %collective-permute-start.12 = (bf16[32,512]{1,0:T(8,128)(2,1)S(1)}, bf16[32,512]{1,0:T(8,128)(2,1)S(1)}, u32[]{:S(2)}, u32[]{:S(2)}) collective-permute-start(bf16[32,512]{1,0:T(8,128)(2,1)S(1)} %get-tuple-element.26), channel_id=1, source_target_pairs={{0,4},{1,5},{2,6},{3,7},{4,0},{5,1},{6,2},{7,3},{8,12},{9,13},{10,... | collective-permute-start | bytes 98312 | tf_op jit(solution)/shard_map/ppermute | solution.py:144
  28.4 1.2 %collective-permute-start.13 = (bf16[32,512]{1,0:T(8,128)(2,1)S(1)}, bf16[32,512]{1,0:T(8,128)(2,1)S(1)}, u32[]{:S(2)}, u32[]{:S(2)}) collective-permute-start(bf16[32,512]{1,0:T(8,128)(2,1)S(1)} %get-tuple-element.27), channel_id=1, source_target_pairs={{0,6},{1,7},{2,4},{3,5},{4,2},{5,3},{6,0},{7,1},{8,14},{9,15},{10,... | collective-permute-start | bytes 98312 | tf_op jit(solution)/shard_map/ppermute | solution.py:144
  29.6 1.4 %collective-permute-start.14 = (bf16[32,512]{1,0:T(8,128)(2,1)S(1)}, bf16[32,512]{1,0:T(8,128)(2,1)S(1)}, u32[]{:S(2)}, u32[]{:S(2)}) collective-permute-start(bf16[32,512]{1,0:T(8,128)(2,1)S(1)} %get-tuple-element.28), channel_id=1, source_target_pairs={{0,2},{1,3},{2,0},{3,1},{4,6},{5,7},{6,4},{7,5},{8,10},{9,11},{10,... | collective-permute-start | bytes 98312 | tf_op jit(solution)/shard_map/ppermute | solution.py:144
  31.0 1.3 %collective-permute-done.12.refs_1_ = bf16[32,512]{1,0:T(8,128)(2,1)S(1)} collective-permute-done((bf16[32,512]{1,0:T(8,128)(2,1)S(1)}, bf16[32,512]{1,0:T(8,128)(2,1)S(1)}, u32[]{:S(2)}, u32[]{:S(2)}) %collective-permute-start.12) | collective-permute-done | bytes 32800 | tf_op jit(solution)/shard_map/ppermute | solution.py:144
  32.3 1.8 %collective-permute-done.13.refs_2_ = bf16[32,512]{1,0:T(8,128)(2,1)S(1)} collective-permute-done((bf16[32,512]{1,0:T(8,128)(2,1)S(1)}, bf16[32,512]{1,0:T(8,128)(2,1)S(1)}, u32[]{:S(2)}, u32[]{:S(2)}) %collective-permute-start.13) | collective-permute-done | bytes 32800 | tf_op jit(solution)/shard_map/ppermute | solution.py:144
  34.1 0.0 collective-permute-done.14.refs_3_
  34.1 0.7 %shard_map.68 = bf16[32,2048]{1,0:T(8,128)(2,1)} custom-call(bf16[32,512]{1,0:T(8,128)(2,1)S(1)} %get-tuple-element.25.refs_0_, bf16[32,512]{1,0:T(8,128)(2,1)S(1)} %collective-permute-done.12.refs_1_, bf16[32,512]{1,0:T(8,128)(2,1)S(1)} %collective-permute-done.13.refs_2_, bf16[32,512]{1,0:T(8,128)(2,1)S(1)} %collective-permute-done.14.refs_3_), custom_call_target="tpu_custom_call" | custom-call | tf_op jit(solution)/shard_map/pallas_call | solution.py:193
Async XLA Ops:
  1.0 7.9 %collective-permute-start.3 = (bf16[2,32,512]{2,1,0:T(8,128)(2,1)S(1)}, bf16[2,32,512]{2,1,0:T(8,128)(2,1)S(1)}, u32[]{:S(2)}, u32[]{:S(2)}) collective-permute-start(bf16[2,32,512]{2,1,0:T(8,128)(2,1)S(1)} %get-tuple-element.22), channel_id=1, source_target_pairs={{0,4},{1,5},{2,6},{3,7},{4,0},{5,1},{6,2},{7,3},{8,12},{9,13},{10,... | collective-permute-start | bytes 196616 | tf_op jit(solution)/shard_map/ppermute | solution.py:144
  5.1 6.3 %collective-permute-start.4 = (bf16[2,32,512]{2,1,0:T(8,128)(2,1)S(1)}, bf16[2,32,512]{2,1,0:T(8,128)(2,1)S(1)}, u32[]{:S(2)}, u32[]{:S(2)}) collective-permute-start(bf16[2,32,512]{2,1,0:T(8,128)(2,1)S(1)} %get-tuple-element.23), channel_id=1, source_target_pairs={{0,6},{1,7},{2,4},{3,5},{4,2},{5,3},{6,0},{7,1},{8,14},{9,15},{10,... | collective-permute-start | bytes 196616 | tf_op jit(solution)/shard_map/ppermute | solution.py:144
  6.5 6.4 %collective-permute-start.5 = (bf16[2,32,512]{2,1,0:T(8,128)(2,1)S(1)}, bf16[2,32,512]{2,1,0:T(8,128)(2,1)S(1)}, u32[]{:S(2)}, u32[]{:S(2)}) collective-permute-start(bf16[2,32,512]{2,1,0:T(8,128)(2,1)S(1)} %get-tuple-element.24), channel_id=1, source_target_pairs={{0,2},{1,3},{2,0},{3,1},{4,6},{5,7},{6,4},{7,5},{8,10},{9,11},{10,... | collective-permute-start | bytes 196616 | tf_op jit(solution)/shard_map/ppermute | solution.py:144
  6.7 7.2 %collective-permute-start.6 = (bf16[2,32,512]{2,1,0:T(8,128)(2,1)S(1)}, bf16[2,32,512]{2,1,0:T(8,128)(2,1)S(1)}, u32[]{:S(2)}, u32[]{:S(2)}) collective-permute-start(bf16[2,32,512]{2,1,0:T(8,128)(2,1)S(1)} %get-tuple-element.21.refs_0_.refs_4_), channel_id=1, source_target_pairs={{0,1},{1,0},{2,3},{3,2},{4,5},{5,4},{6,7},{7,6},{8,9},{9,8},{10,11... | collective-permute-start | bytes 196616 | tf_op jit(solution)/shard_map/ppermute | solution.py:144
  8.9 5.0 %collective-permute-start.7 = (bf16[2,32,512]{2,1,0:T(8,128)(2,1)S(1)}, bf16[2,32,512]{2,1,0:T(8,128)(2,1)S(1)}, u32[]{:S(2)}, u32[]{:S(2)}) collective-permute-start(bf16[2,32,512]{2,1,0:T(8,128)(2,1)S(1)} %collective-permute-done.3.refs_1_.refs_5_), channel_id=1, source_target_pairs={{0,1},{1,0},{2,3},{3,2},{4,5},{5,4},{6,7},{7,6},{8,9},{9,8},{10,11... | collective-permute-start | bytes 196616 | tf_op jit(solution)/shard_map/ppermute | solution.py:144
  11.4 4.3 %collective-permute-start.8 = (bf16[2,32,512]{2,1,0:T(8,128)(2,1)S(1)}, bf16[2,32,512]{2,1,0:T(8,128)(2,1)S(1)}, u32[]{:S(2)}, u32[]{:S(2)}) collective-permute-start(bf16[2,32,512]{2,1,0:T(8,128)(2,1)S(1)} %collective-permute-done.4.refs_2_.refs_6_), channel_id=1, source_target_pairs={{0,1},{1,0},{2,3},{3,2},{4,5},{5,4},{6,7},{7,6},{8,9},{9,8},{10,11... | collective-permute-start | bytes 196616 | tf_op jit(solution)/shard_map/ppermute | solution.py:144
  12.9 4.3 %collective-permute-start.9 = (bf16[2,32,512]{2,1,0:T(8,128)(2,1)S(1)}, bf16[2,32,512]{2,1,0:T(8,128)(2,1)S(1)}, u32[]{:S(2)}, u32[]{:S(2)}) collective-permute-start(bf16[2,32,512]{2,1,0:T(8,128)(2,1)S(1)} %collective-permute-done.5.refs_3_.refs_7_), channel_id=1, source_target_pairs={{0,1},{1,0},{2,3},{3,2},{4,5},{5,4},{6,7},{7,6},{8,9},{9,8},{10,11... | collective-permute-start | bytes 196616 | tf_op jit(solution)/shard_map/ppermute | solution.py:144
  13.8 12.3 %copy-start = (f32[8,2048]{1,0:T(8,128)S(1)}, f32[8,2048]{1,0:T(8,128)}, u32[]{:S(2)}) copy-start(f32[8,2048]{1,0:T(8,128)} %gate_ref.1) | copy-start | bytes 196612
  13.8 12.3 %collective-permute-start.10 = (bf16[4,2,32,512]{3,2,1,0:T(8,128)(2,1)S(1)}, bf16[4,2,32,512]{3,2,1,0:T(8,128)(2,1)S(1)}, u32[]{:S(2)}, u32[]{:S(2)}) collective-permute-start(bf16[4,2,32,512]{3,2,1,0:T(8,128)(2,1)S(1)} %shard_map.65), channel_id=1, source_target_pairs={{0,8},{8,0},{1,9},{9,1},{2,10},{10,2},{3,11},{11,3},{4,12},{12,4},... | collective-permute-start | bytes 786440 | tf_op jit(solution)/shard_map/ppermute | solution.py:180
  17.5 8.6 %collective-permute-start.11 = (bf16[4,2,32,512]{3,2,1,0:T(8,128)(2,1)S(1)}, bf16[4,2,32,512]{3,2,1,0:T(8,128)(2,1)S(1)}, u32[]{:S(2)}, u32[]{:S(2)}) collective-permute-start(bf16[4,2,32,512]{3,2,1,0:T(8,128)(2,1)S(1)} %shard_map.66), channel_id=1, source_target_pairs={{0,8},{8,0},{1,9},{9,1},{2,10},{10,2},{3,11},{11,3},{4,12},{12,4},... | collective-permute-start | bytes 786440 | tf_op jit(solution)/shard_map/ppermute | solution.py:180
  17.6 4.9 %collective-permute-start = (bf16[32,512]{1,0:T(8,128)(2,1)S(1)}, bf16[32,512]{1,0:T(8,128)(2,1)S(1)}, u32[]{:S(2)}, u32[]{:S(2)}) collective-permute-start(bf16[32,512]{1,0:T(8,128)(2,1)S(1)} %get-tuple-element.18), channel_id=1, source_target_pairs={{0,4},{1,5},{2,6},{3,7},{4,0},{5,1},{6,2},{7,3},{8,12},{9,13},{10,... | collective-permute-start | bytes 98312 | tf_op jit(solution)/shard_map/ppermute | solution.py:144
  20.4 5.7 %collective-permute-start.1 = (bf16[32,512]{1,0:T(8,128)(2,1)S(1)}, bf16[32,512]{1,0:T(8,128)(2,1)S(1)}, u32[]{:S(2)}, u32[]{:S(2)}) collective-permute-start(bf16[32,512]{1,0:T(8,128)(2,1)S(1)} %get-tuple-element.19), channel_id=1, source_target_pairs={{0,6},{1,7},{2,4},{3,5},{4,2},{5,3},{6,0},{7,1},{8,14},{9,15},{10,... | collective-permute-start | bytes 98312 | tf_op jit(solution)/shard_map/ppermute | solution.py:144
  21.2 5.0 %copy-start.2 = (s32[2,4]{1,0:T(2,128)S(1)}, s32[2,4]{1,0:T(2,128)}, u32[]{:S(2)}) copy-start(s32[2,4]{1,0:T(2,128)} %level_ref.1) | copy-start | bytes 100
  21.2 5.0 %copy-start.1 = (s32[2,4]{1,0:T(2,128)S(1)}, s32[2,4]{1,0:T(2,128)}, u32[]{:S(2)}) copy-start(s32[2,4]{1,0:T(2,128)} %slot_ref.1) | copy-start | bytes 100
  21.2 4.9 %collective-permute-start.2 = (bf16[32,512]{1,0:T(8,128)(2,1)S(1)}, bf16[32,512]{1,0:T(8,128)(2,1)S(1)}, u32[]{:S(2)}, u32[]{:S(2)}) collective-permute-start(bf16[32,512]{1,0:T(8,128)(2,1)S(1)} %get-tuple-element.20), channel_id=1, source_target_pairs={{0,2},{1,3},{2,0},{3,1},{4,6},{5,7},{6,4},{7,5},{8,10},{9,11},{10,... | collective-permute-start | bytes 98312 | tf_op jit(solution)/shard_map/ppermute | solution.py:144
  27.4 4.9 %collective-permute-start.12 = (bf16[32,512]{1,0:T(8,128)(2,1)S(1)}, bf16[32,512]{1,0:T(8,128)(2,1)S(1)}, u32[]{:S(2)}, u32[]{:S(2)}) collective-permute-start(bf16[32,512]{1,0:T(8,128)(2,1)S(1)} %get-tuple-element.26), channel_id=1, source_target_pairs={{0,4},{1,5},{2,6},{3,7},{4,0},{5,1},{6,2},{7,3},{8,12},{9,13},{10,... | collective-permute-start | bytes 98312 | tf_op jit(solution)/shard_map/ppermute | solution.py:144
  28.4 5.7 %collective-permute-start.13 = (bf16[32,512]{1,0:T(8,128)(2,1)S(1)}, bf16[32,512]{1,0:T(8,128)(2,1)S(1)}, u32[]{:S(2)}, u32[]{:S(2)}) collective-permute-start(bf16[32,512]{1,0:T(8,128)(2,1)S(1)} %get-tuple-element.27), channel_id=1, source_target_pairs={{0,6},{1,7},{2,4},{3,5},{4,2},{5,3},{6,0},{7,1},{8,14},{9,15},{10,... | collective-permute-start | bytes 98312 | tf_op jit(solution)/shard_map/ppermute | solution.py:144
  29.6 4.5 %collective-permute-start.14 = (bf16[32,512]{1,0:T(8,128)(2,1)S(1)}, bf16[32,512]{1,0:T(8,128)(2,1)S(1)}, u32[]{:S(2)}, u32[]{:S(2)}) collective-permute-start(bf16[32,512]{1,0:T(8,128)(2,1)S(1)} %get-tuple-element.28), channel_id=1, source_target_pairs={{0,2},{1,3},{2,0},{3,1},{4,6},{5,7},{6,4},{7,5},{8,10},{9,11},{10,... | collective-permute-start | bytes 98312 | tf_op jit(solution)/shard_map/ppermute | solution.py:144

commit v7 on v6

--- a/solution.py
+++ b/solution.py
@@ -17,10 +17,6 @@
 PARAMS = pltpu.CompilerParams(vmem_limit_bytes=32 * 1024 * 1024)
 
 
-def far_first(count):
-    return sorted(range(count), key=lambda away: (away > 0, -(2 * away // count), away % 2, -away))
-
-
 def columns_of(place, width):
     return pl.ds(pl.multiple_of(place * width, width), width)
 
@@ -37,41 +33,43 @@
     place = lax.axis_index("seq") // near
     count = len(outs) // 2
     copies = []
-    for number, away in enumerate(far_first(count)):
-        pair_ref, own_ref = outs[number], outs[count + number]
+    for away in range(count):
+        pair_ref, own_ref = outs[away], outs[count + away]
         columns = columns_of(place ^ away, own_ref.shape[-1])
         for kind, (ref, out_ref) in enumerate(
             ((key_ref, pair_ref.at[0]), (value_ref, pair_ref.at[1]), (query_ref, own_ref))
         ):
-            copies.append(pltpu.make_async_copy(ref.at[:, columns], out_ref, sems.at[number, kind]))
+            copies.append(pltpu.make_async_copy(ref.at[:, columns], out_ref, sems.at[away, kind]))
     run(copies)
 
 
-def stack(*refs):
-    *pieces, out_ref, sems = refs
+def stack(*refs, count):
+    *refs, sems = refs
+    outs = refs[-(len(refs) // (count + 1)) :]
     run(
         [
-            pltpu.make_async_copy(ref, out_ref.at[number], sems.at[number])
-            for number, ref in enumerate(pieces)
+            pltpu.make_async_copy(ref, outs[number // count].at[number % count], sems.at[number])
+            for number, ref in enumerate(refs[: -len(outs)])
         ]
     )
 
 
 def unpack(*refs, near):
-    answers, out_ref, sems = refs[:-2], refs[-2], refs[-1]
+    *answers, out_ref, sems = refs
     place = lax.axis_index("seq") // near
     run(
         [
             pltpu.make_async_copy(
-                ref, out_ref.at[:, columns_of(place ^ away, ref.shape[-1])], sems.at[number]
-            )
-            for number, (away, ref) in enumerate(zip(far_first(len(answers)), answers))
+                ref, out_ref.at[:, columns_of(place ^ away, ref.shape[-1])], sems.at[away]
+            )
+            for away, ref in enumerate(answers)
         ]
     )
 
 
-def attend(slot_ref, level_ref, gate_ref, *refs, pieces, near, tokens):
-    query_refs, refs, outs = refs[:pieces], refs[pieces:-pieces], refs[-pieces:]
+def attend(slot_ref, level_ref, gate_ref, query_ref, *refs, near, tokens):
+    pieces = query_ref.shape[0]
+    refs, outs = refs[:-pieces], refs[-pieces:]
     held_refs, stack_refs = refs[: near * pieces], refs[near * pieces :]
     rows, width = outs[0].shape
     group_count = 1 + len(stack_refs) // near
@@ -116,7 +114,7 @@
         )
         values = jnp.concatenate([values, ones], axis=1)
         for start in range(0, pieces, step):
-            queries = jnp.concatenate([ref[:, part] for ref in query_refs[start : start + step]])
+            queries = query_ref[start : start + step, :, part].reshape(step * rows, HEAD)
             scores = lax.dot_general(
                 queries, keys, (((1,), (1,)), ((), ())), preferred_element_type=jnp.float32
             )
@@ -144,9 +142,7 @@
         return lax.ppermute(taken, "seq", [(one, one ^ away) for one in range(devices)])
 
     def swap_far(taken):
-        return [
-            swap(one, away * near) if away else one for away, one in zip(far_first(count), taken)
-        ]
+        return [swap(one, away * near) if away else one for away, one in enumerate(taken)]
 
     sent = pl.pallas_call(
         functools.partial(pack, near=near),
@@ -165,17 +161,22 @@
     pairs = swap_far(sent[:count])
     own = swap_far(sent[count:])
     held = [pairs] + [[swap(piece, away) for piece in pairs] for away in range(1, near)]
-    stacks = [
-        pl.pallas_call(
-            stack,
-            out_shape=jax.ShapeDtypeStruct((count, 2, rows, width), queries.dtype),
-            in_specs=[VMEM] * count,
-            out_specs=VMEM,
-            scratch_shapes=[pltpu.SemaphoreType.DMA((count,))],
+
+    def stacked(*kinds):
+        return pl.pallas_call(
+            functools.partial(stack, count=count),
+            out_shape=[
+                jax.ShapeDtypeStruct((count,) + taken[0].shape, queries.dtype) for taken in kinds
+            ],
+            in_specs=[VMEM] * (len(kinds) * count),
+            out_specs=[VMEM] * len(kinds),
+            scratch_shapes=[pltpu.SemaphoreType.DMA((len(kinds) * count,))],
             compiler_params=PARAMS,
-        )(*taken)
-        for taken in held
-    ]
+        )(*sum(kinds, []))
+
+    stacks = [stacked(taken)[0] for taken in held[:-1]]
+    last, own = stacked(held[-1], own)
+    stacks.append(last)
     stacks = [
         lax.ppermute(taken, "frame", [(one, (one - away) % groups) for one in range(groups)])
         for away in range(1, groups)
@@ -183,12 +184,12 @@
     ]
     held = sum(held, [])
     answers = pl.pallas_call(
-        functools.partial(attend, pieces=count, near=near, tokens=tokens),
+        functools.partial(attend, near=near, tokens=tokens),
         out_shape=[jax.ShapeDtypeStruct((rows, width), queries.dtype)] * count,
-        in_specs=[SMEM] * 2 + [VMEM] * (1 + count + len(held) + len(stacks)),
+        in_specs=[SMEM] * 2 + [VMEM] * (2 + len(held) + len(stacks)),
         out_specs=[VMEM] * count,
         compiler_params=PARAMS,
-    )(slot_of, level_of, gate_table, *own, *held, *stacks)
+    )(slot_of, level_of, gate_table, own, *held, *stacks)
     answers = swap_far(answers)
     answer = pl.pallas_call(
         functools.partial(unpack, near=near),

time: 35 us -> 35.2 us (level)
  starting transfers between devices: 19.5 us -> 22.1 us
  waiting for transfers between devices: 11.5 us -> 8.96 us
    ppermute x13, waiting for transfers between devices: 11.5 us -> 7.8 us  [swap(): lax.ppermute(taken, 'seq', [(one, one ^ away) for one in range(devices)])]
    ppermute x13, starting transfers between devices: 19.4 us -> 21.5 us  [swap(): lax.ppermute(taken, 'seq', [(one, one ^ away) for one in range(devices)])]
    ppermute x2, waiting for transfers between devices: 0.01 us -> 1.16 us  [whole_heads(): lax.ppermute(taken, 'frame', [(one, (one - away) % groups) for one in ran...]
    ppermute x2, starting transfers between devices: 0.14 us -> 0.57 us  [whole_heads(): lax.ppermute(taken, 'frame', [(one, (one - away) % groups) for one in ran...]
  transfers between devices with their start and end apart: 15 -> 15, of which waited for: 7 -> 6; matrix products, arithmetic and copies ran while one was open for 0% -> 0% of each run, Pallas kernels for 2% -> 3%
where the time goes in v7:
time: 35.2 us; the launch traced here: 35.1 us
  starting transfers between devices  22.1 us (63%)
  waiting for transfers between devices  8.96 us (25%)
  Pallas kernels  3.89 us (11%)
    ppermute x13, starting transfers between devices, swap(): lax.ppermute(taken, 'seq', [(one, one ^ away) for one in range(devices)])  21.5 us
    ppermute x13, waiting for transfers between devices, swap(): lax.ppermute(taken, 'seq', [(one, one ^ away) for one in range(devices)])  7.8 us
    pallas_call x1, Pallas kernels, whole_heads(): pl.pallas_call(functools.partial(attend, near=near, tokens=tokens), out_s...  1.23 us
    ppermute x2, waiting for transfers between devices, whole_heads(): lax.ppermute(taken, 'frame', [(one, (one - away) % groups) for one in ran...  1.16 us
    pallas_call x1, Pallas kernels, whole_heads(): pl.pallas_call(functools.partial(pack, near=near), out_shape=[jax.ShapeDt...  1.04 us
    pallas_call x2, Pallas kernels, stacked(): pl.pallas_call(functools.partial(stack, count=count), out_shape=[jax.Shap...  0.94 us
  transfers between devices with their start and end apart: 15, of which 6 were waited for; matrix products, arithmetic and copies ran while one was open for 0% of the time, Pallas kernels for 3%

profile of v7, /device:TPU:0, one launch (start us, length us, event | category | flops | bytes accessed | tf_op | source)
XLA Modules:
  0.0 35.1 jit_solution(272549210598093159)
XLA Ops:
  0.0 1.0 %shard_map.64 = (bf16[2,32,512]{2,1,0:T(8,128)(2,1)S(1)}, bf16[2,32,512]{2,1,0:T(8,128)(2,1)S(1)}, bf16[2,32,512]{2,1,0:T(8,128)(2,1)S(1)}, bf16[2,32,512]{2,1,0...) custom-call(bf16[32,2048]{1,0:T(8,128)(2,1)} %bitcast.4, ...), custom_call_target="tpu_custom_call" | custom-call | tf_op jit(solution)/shard_map/pallas_call | solution.py:147
  1.0 3.1 %collective-permute-start.1 = (bf16[2,32,512]{2,1,0:T(8,128)(2,1)S(1)}, bf16[2,32,512]{2,1,0:T(8,128)(2,1)S(1)}, u32[]{:S(2)}, u32[]{:S(2)}) collective-permute-start(bf16[2,32,512]{2,1,0:T(8,128)(2,1)S(1)} %get-tuple-element.20), channel_id=1, source_target_pairs={{0,2},{1,3},{2,0},{3,1},{4,6},{5,7},{6,4},{7,5},{8,10},{9,11},{10,... | collective-permute-start | bytes 196616 | tf_op jit(solution)/shard_map/ppermute | solution.py:142
  4.1 2.6 %collective-permute-start.3 = (bf16[2,32,512]{2,1,0:T(8,128)(2,1)S(1)}, bf16[2,32,512]{2,1,0:T(8,128)(2,1)S(1)}, u32[]{:S(2)}, u32[]{:S(2)}) collective-permute-start(bf16[2,32,512]{2,1,0:T(8,128)(2,1)S(1)} %get-tuple-element.21), channel_id=1, source_target_pairs={{0,4},{1,5},{2,6},{3,7},{4,0},{5,1},{6,2},{7,3},{8,12},{9,13},{10,... | collective-permute-start | bytes 196616 | tf_op jit(solution)/shard_map/ppermute | solution.py:142
  6.7 0.0 collective-permute-start.5
  6.7 0.9 %collective-permute-start.7 = (bf16[32,512]{1,0:T(8,128)(2,1)S(1)}, bf16[32,512]{1,0:T(8,128)(2,1)S(1)}, u32[]{:S(2)}, u32[]{:S(2)}) collective-permute-start(bf16[32,512]{1,0:T(8,128)(2,1)S(1)} %get-tuple-element.24), channel_id=1, source_target_pairs={{0,2},{1,3},{2,0},{3,1},{4,6},{5,7},{6,4},{7,5},{8,10},{9,11},{10,... | collective-permute-start | bytes 98312 | tf_op jit(solution)/shard_map/ppermute | solution.py:142
  7.6 3.5 %collective-permute-start.8 = (bf16[32,512]{1,0:T(8,128)(2,1)S(1)}, bf16[32,512]{1,0:T(8,128)(2,1)S(1)}, u32[]{:S(2)}, u32[]{:S(2)}) collective-permute-start(bf16[32,512]{1,0:T(8,128)(2,1)S(1)} %get-tuple-element.25), channel_id=1, source_target_pairs={{0,4},{1,5},{2,6},{3,7},{4,0},{5,1},{6,2},{7,3},{8,12},{9,13},{10,... | collective-permute-start | bytes 98312 | tf_op jit(solution)/shard_map/ppermute | solution.py:142
  11.1 0.5 %collective-permute-done.7.refs_5_ = bf16[32,512]{1,0:T(8,128)(2,1)S(1)} collective-permute-done((bf16[32,512]{1,0:T(8,128)(2,1)S(1)}, bf16[32,512]{1,0:T(8,128)(2,1)S(1)}, u32[]{:S(2)}, u32[]{:S(2)}) %collective-permute-start.7) | collective-permute-done | bytes 32800 | tf_op jit(solution)/shard_map/ppermute | solution.py:142
  11.6 1.6 %collective-permute-start = (bf16[2,32,512]{2,1,0:T(8,128)(2,1)S(1)}, bf16[2,32,512]{2,1,0:T(8,128)(2,1)S(1)}, u32[]{:S(2)}, u32[]{:S(2)}) collective-permute-start(bf16[2,32,512]{2,1,0:T(8,128)(2,1)S(1)} %get-tuple-element.19.refs_0_), channel_id=1, source_target_pairs={{0,1},{1,0},{2,3},{3,2},{4,5},{5,4},{6,7},{7,6},{8,9},{9,8},{10,11... | collective-permute-start | bytes 196616 | tf_op jit(solution)/shard_map/ppermute | solution.py:142
  13.2 0.0 collective-permute-done.1.refs_1_
  13.2 0.4 %collective-permute-start.2 = (bf16[2,32,512]{2,1,0:T(8,128)(2,1)S(1)}, bf16[2,32,512]{2,1,0:T(8,128)(2,1)S(1)}, u32[]{:S(2)}, u32[]{:S(2)}) collective-permute-start(bf16[2,32,512]{2,1,0:T(8,128)(2,1)S(1)} %collective-permute-done.1.refs_1_), channel_id=1, source_target_pairs={{0,1},{1,0},{2,3},{3,2},{4,5},{5,4},{6,7},{7,6},{8,9},{9,8},{10,11... | collective-permute-start | bytes 196616 | tf_op jit(solution)/shard_map/ppermute | solution.py:142
  13.7 0.0 collective-permute-done.3.refs_2_
  13.7 1.6 %collective-permute-start.4 = (bf16[2,32,512]{2,1,0:T(8,128)(2,1)S(1)}, bf16[2,32,512]{2,1,0:T(8,128)(2,1)S(1)}, u32[]{:S(2)}, u32[]{:S(2)}) collective-permute-start(bf16[2,32,512]{2,1,0:T(8,128)(2,1)S(1)} %collective-permute-done.3.refs_2_), channel_id=1, source_target_pairs={{0,1},{1,0},{2,3},{3,2},{4,5},{5,4},{6,7},{7,6},{8,9},{9,8},{10,11... | collective-permute-start | bytes 196616 | tf_op jit(solution)/shard_map/ppermute | solution.py:142
  15.3 0.0 collective-permute-done.5.refs_3_
  15.3 0.4 %collective-permute-start.6 = (bf16[2,32,512]{2,1,0:T(8,128)(2,1)S(1)}, bf16[2,32,512]{2,1,0:T(8,128)(2,1)S(1)}, u32[]{:S(2)}, u32[]{:S(2)}) collective-permute-start(bf16[2,32,512]{2,1,0:T(8,128)(2,1)S(1)} %collective-permute-done.5.refs_3_), channel_id=1, source_target_pairs={{0,1},{1,0},{2,3},{3,2},{4,5},{5,4},{6,7},{7,6},{8,9},{9,8},{10,11... | collective-permute-start | bytes 196616 | tf_op jit(solution)/shard_map/ppermute | solution.py:142
  15.7 0.0 collective-permute-done.8.refs_6_
  15.7 2.9 %collective-permute-start.9 = (bf16[32,512]{1,0:T(8,128)(2,1)S(1)}, bf16[32,512]{1,0:T(8,128)(2,1)S(1)}, u32[]{:S(2)}, u32[]{:S(2)}) collective-permute-start(bf16[32,512]{1,0:T(8,128)(2,1)S(1)} %get-tuple-element.26), channel_id=1, source_target_pairs={{0,6},{1,7},{2,4},{3,5},{4,2},{5,3},{6,0},{7,1},{8,14},{9,15},{10,... | collective-permute-start | bytes 98312 | tf_op jit(solution)/shard_map/ppermute | solution.py:142
  18.6 0.3 shard_map.66
  19.0 2.4 %collective-permute-done.9.refs_7_ = bf16[32,512]{1,0:T(8,128)(2,1)S(1)} collective-permute-done((bf16[32,512]{1,0:T(8,128)(2,1)S(1)}, bf16[32,512]{1,0:T(8,128)(2,1)S(1)}, u32[]{:S(2)}, u32[]{:S(2)}) %collective-permute-start.9) | collective-permute-done | bytes 32800 | tf_op jit(solution)/shard_map/ppermute | solution.py:142
  21.4 0.0 collective-permute-start.10
  21.4 0.0 collective-permute-done.refs_0_.refs_4_
  21.4 0.0 collective-permute-done.2.refs_1_.refs_5_
  21.4 0.0 collective-permute-done.4.refs_2_.refs_6_
  21.5 0.0 collective-permute-done.6.refs_3_.refs_7_
  21.5 0.0 copy-start
  21.5 0.6 %shard_map.65 = (bf16[4,2,32,512]{3,2,1,0:T(8,128)(2,1)S(1)}, bf16[4,32,512]{2,1,0:T(8,128)(2,1)S(1)}) custom-call(bf16[2,32,512]{2,1,0:T(8,128)(2,1)S(1)} %collective-permute-done.refs_0_.refs_4_, bf16[2,32,512]{2,1,0:T(8,128)(2,1)S(1)} %collective-permute-done.2.refs_1_.refs_5_, bf16[2,32,512]{2,1,0:T(8,128)(2,1)S(1)} %collective-permute-done.4.refs_2_.refs_6_, ...), custom_call_target="tpu_custom_call" | custom-call | tf_op jit(solution)/shard_map/pallas_call | solution.py:166
  22.1 0.0 copy-start.2
  22.1 0.0 copy-start.1
  22.1 0.6 %collective-permute-start.11 = (bf16[4,2,32,512]{3,2,1,0:T(8,128)(2,1)S(1)}, bf16[4,2,32,512]{3,2,1,0:T(8,128)(2,1)S(1)}, u32[]{:S(2)}, u32[]{:S(2)}) collective-permute-start(bf16[4,2,32,512]{3,2,1,0:T(8,128)(2,1)S(1)} %get-tuple-element.28), channel_id=1, source_target_pairs={{0,8},{8,0},{1,9},{9,1},{2,10},{10,2},{3,11},{11,3},{4,12},{12,4},... | collective-permute-start | bytes 786440 | tf_op jit(solution)/shard_map/ppermute | solution.py:181
  22.7 0.3 collective-permute-done.10.refs_8_
  23.0 0.9 %collective-permute-done.11.refs_9_ = bf16[4,2,32,512]{3,2,1,0:T(8,128)(2,1)S(1)} collective-permute-done((bf16[4,2,32,512]{3,2,1,0:T(8,128)(2,1)S(1)}, bf16[4,2,32,512]{3,2,1,0:T(8,128)(2,1)S(1)}, u32[]{:S(2)}, u32[]{:S(2)}) %collective-permute-start.11) | collective-permute-done | bytes 262176 | tf_op jit(solution)/shard_map/ppermute | solution.py:181
  23.8 0.0 copy-done
  23.8 0.0 copy-done.2
  23.8 0.0 copy-done.1
  23.8 1.2 %shard_map.67 = (bf16[32,512]{1,0:T(8,128)(2,1)S(1)}, bf16[32,512]{1,0:T(8,128)(2,1)S(1)}, bf16[32,512]{1,0:T(8,128)(2,1)S(1)}, bf16[32,512]{1,0:T(8,128)(2,1)S(1)}) custom-call(s32[2,4]{1,0:T(2,128)S(1)} %copy-done.1, s32[2,4]{1,0:T(2,128)S(1)} %copy-done.2, f32[8,2048]{1,0:T(8,128)S(1)} %copy-done, bf16[4,32,512]{2,1,0:T(8,128)(2,1)S(1)} %get-tuple-element.27.query_ref, ...), custom_call_target="tpu_custom_call" | custom-call | tf_op jit(solution)/shard_map/pallas_call | solution.py:186
  25.1 0.1 collective-permute-start.12
  25.2 3.5 %collective-permute-start.13 = (bf16[32,512]{1,0:T(8,128)(2,1)S(1)}, bf16[32,512]{1,0:T(8,128)(2,1)S(1)}, u32[]{:S(2)}, u32[]{:S(2)}) collective-permute-start(bf16[32,512]{1,0:T(8,128)(2,1)S(1)} %get-tuple-element.31), channel_id=1, source_target_pairs={{0,4},{1,5},{2,6},{3,7},{4,0},{5,1},{6,2},{7,3},{8,12},{9,13},{10,... | collective-permute-start | bytes 98312 | tf_op jit(solution)/shard_map/ppermute | solution.py:142
  28.7 0.9 %collective-permute-start.14 = (bf16[32,512]{1,0:T(8,128)(2,1)S(1)}, bf16[32,512]{1,0:T(8,128)(2,1)S(1)}, u32[]{:S(2)}, u32[]{:S(2)}) collective-permute-start(bf16[32,512]{1,0:T(8,128)(2,1)S(1)} %get-tuple-element.32), channel_id=1, source_target_pairs={{0,6},{1,7},{2,4},{3,5},{4,2},{5,3},{6,0},{7,1},{8,14},{9,15},{10,... | collective-permute-start | bytes 98312 | tf_op jit(solution)/shard_map/ppermute | solution.py:142
  29.6 0.0 collective-permute-done.12.refs_1_
  29.6 1.4 %collective-permute-done.13.refs_2_ = bf16[32,512]{1,0:T(8,128)(2,1)S(1)} collective-permute-done((bf16[32,512]{1,0:T(8,128)(2,1)S(1)}, bf16[32,512]{1,0:T(8,128)(2,1)S(1)}, u32[]{:S(2)}, u32[]{:S(2)}) %collective-permute-start.13) | collective-permute-done | bytes 32800 | tf_op jit(solution)/shard_map/ppermute | solution.py:142
  31.0 3.4 %collective-permute-done.14.refs_3_ = bf16[32,512]{1,0:T(8,128)(2,1)S(1)} collective-permute-done((bf16[32,512]{1,0:T(8,128)(2,1)S(1)}, bf16[32,512]{1,0:T(8,128)(2,1)S(1)}, u32[]{:S(2)}, u32[]{:S(2)}) %collective-permute-start.14) | collective-permute-done | bytes 32800 | tf_op jit(solution)/shard_map/ppermute | solution.py:142
  34.4 0.7 %shard_map.68 = bf16[32,2048]{1,0:T(8,128)(2,1)} custom-call(bf16[32,512]{1,0:T(8,128)(2,1)S(1)} %get-tuple-element.29.refs_0_, bf16[32,512]{1,0:T(8,128)(2,1)S(1)} %collective-permute-done.12.refs_1_, bf16[32,512]{1,0:T(8,128)(2,1)S(1)} %collective-permute-done.13.refs_2_, bf16[32,512]{1,0:T(8,128)(2,1)S(1)} %collective-permute-done.14.refs_3_), custom_call_target="tpu_custom_call" | custom-call | tf_op jit(solution)/shard_map/pallas_call | solution.py:194
Async XLA Ops:
  1.0 12.2 %collective-permute-start.1 = (bf16[2,32,512]{2,1,0:T(8,128)(2,1)S(1)}, bf16[2,32,512]{2,1,0:T(8,128)(2,1)S(1)}, u32[]{:S(2)}, u32[]{:S(2)}) collective-permute-start(bf16[2,32,512]{2,1,0:T(8,128)(2,1)S(1)} %get-tuple-element.20), channel_id=1, source_target_pairs={{0,2},{1,3},{2,0},{3,1},{4,6},{5,7},{6,4},{7,5},{8,10},{9,11},{10,... | collective-permute-start | bytes 196616 | tf_op jit(solution)/shard_map/ppermute | solution.py:142
  4.1 9.5 %collective-permute-start.3 = (bf16[2,32,512]{2,1,0:T(8,128)(2,1)S(1)}, bf16[2,32,512]{2,1,0:T(8,128)(2,1)S(1)}, u32[]{:S(2)}, u32[]{:S(2)}) collective-permute-start(bf16[2,32,512]{2,1,0:T(8,128)(2,1)S(1)} %get-tuple-element.21), channel_id=1, source_target_pairs={{0,4},{1,5},{2,6},{3,7},{4,0},{5,1},{6,2},{7,3},{8,12},{9,13},{10,... | collective-permute-start | bytes 196616 | tf_op jit(solution)/shard_map/ppermute | solution.py:142
  6.7 8.6 %collective-permute-start.5 = (bf16[2,32,512]{2,1,0:T(8,128)(2,1)S(1)}, bf16[2,32,512]{2,1,0:T(8,128)(2,1)S(1)}, u32[]{:S(2)}, u32[]{:S(2)}) collective-permute-start(bf16[2,32,512]{2,1,0:T(8,128)(2,1)S(1)} %get-tuple-element.22), channel_id=1, source_target_pairs={{0,6},{1,7},{2,4},{3,5},{4,2},{5,3},{6,0},{7,1},{8,14},{9,15},{10,... | collective-permute-start | bytes 196616 | tf_op jit(solution)/shard_map/ppermute | solution.py:142
  6.7 4.9 %collective-permute-start.7 = (bf16[32,512]{1,0:T(8,128)(2,1)S(1)}, bf16[32,512]{1,0:T(8,128)(2,1)S(1)}, u32[]{:S(2)}, u32[]{:S(2)}) collective-permute-start(bf16[32,512]{1,0:T(8,128)(2,1)S(1)} %get-tuple-element.24), channel_id=1, source_target_pairs={{0,2},{1,3},{2,0},{3,1},{4,6},{5,7},{6,4},{7,5},{8,10},{9,11},{10,... | collective-permute-start | bytes 98312 | tf_op jit(solution)/shard_map/ppermute | solution.py:142
  7.6 8.1 %collective-permute-start.8 = (bf16[32,512]{1,0:T(8,128)(2,1)S(1)}, bf16[32,512]{1,0:T(8,128)(2,1)S(1)}, u32[]{:S(2)}, u32[]{:S(2)}) collective-permute-start(bf16[32,512]{1,0:T(8,128)(2,1)S(1)} %get-tuple-element.25), channel_id=1, source_target_pairs={{0,4},{1,5},{2,6},{3,7},{4,0},{5,1},{6,2},{7,3},{8,12},{9,13},{10,... | collective-permute-start | bytes 98312 | tf_op jit(solution)/shard_map/ppermute | solution.py:142
  11.6 9.8 %collective-permute-start = (bf16[2,32,512]{2,1,0:T(8,128)(2,1)S(1)}, bf16[2,32,512]{2,1,0:T(8,128)(2,1)S(1)}, u32[]{:S(2)}, u32[]{:S(2)}) collective-permute-start(bf16[2,32,512]{2,1,0:T(8,128)(2,1)S(1)} %get-tuple-element.19.refs_0_), channel_id=1, source_target_pairs={{0,1},{1,0},{2,3},{3,2},{4,5},{5,4},{6,7},{7,6},{8,9},{9,8},{10,11... | collective-permute-start | bytes 196616 | tf_op jit(solution)/shard_map/ppermute | solution.py:142
  13.2 8.2 %collective-permute-start.2 = (bf16[2,32,512]{2,1,0:T(8,128)(2,1)S(1)}, bf16[2,32,512]{2,1,0:T(8,128)(2,1)S(1)}, u32[]{:S(2)}, u32[]{:S(2)}) collective-permute-start(bf16[2,32,512]{2,1,0:T(8,128)(2,1)S(1)} %collective-permute-done.1.refs_1_), channel_id=1, source_target_pairs={{0,1},{1,0},{2,3},{3,2},{4,5},{5,4},{6,7},{7,6},{8,9},{9,8},{10,11... | collective-permute-start | bytes 196616 | tf_op jit(solution)/shard_map/ppermute | solution.py:142
  13.7 7.8 %collective-permute-start.4 = (bf16[2,32,512]{2,1,0:T(8,128)(2,1)S(1)}, bf16[2,32,512]{2,1,0:T(8,128)(2,1)S(1)}, u32[]{:S(2)}, u32[]{:S(2)}) collective-permute-start(bf16[2,32,512]{2,1,0:T(8,128)(2,1)S(1)} %collective-permute-done.3.refs_2_), channel_id=1, source_target_pairs={{0,1},{1,0},{2,3},{3,2},{4,5},{5,4},{6,7},{7,6},{8,9},{9,8},{10,11... | collective-permute-start | bytes 196616 | tf_op jit(solution)/shard_map/ppermute | solution.py:142
  15.3 6.2 %collective-permute-start.6 = (bf16[2,32,512]{2,1,0:T(8,128)(2,1)S(1)}, bf16[2,32,512]{2,1,0:T(8,128)(2,1)S(1)}, u32[]{:S(2)}, u32[]{:S(2)}) collective-permute-start(bf16[2,32,512]{2,1,0:T(8,128)(2,1)S(1)} %collective-permute-done.5.refs_3_), channel_id=1, source_target_pairs={{0,1},{1,0},{2,3},{3,2},{4,5},{5,4},{6,7},{7,6},{8,9},{9,8},{10,11... | collective-permute-start | bytes 196616 | tf_op jit(solution)/shard_map/ppermute | solution.py:142
  15.7 5.7 %collective-permute-start.9 = (bf16[32,512]{1,0:T(8,128)(2,1)S(1)}, bf16[32,512]{1,0:T(8,128)(2,1)S(1)}, u32[]{:S(2)}, u32[]{:S(2)}) collective-permute-start(bf16[32,512]{1,0:T(8,128)(2,1)S(1)} %get-tuple-element.26), channel_id=1, source_target_pairs={{0,6},{1,7},{2,4},{3,5},{4,2},{5,3},{6,0},{7,1},{8,14},{9,15},{10,... | collective-permute-start | bytes 98312 | tf_op jit(solution)/shard_map/ppermute | solution.py:142
  21.4 1.5 %collective-permute-start.10 = (bf16[4,2,32,512]{3,2,1,0:T(8,128)(2,1)S(1)}, bf16[4,2,32,512]{3,2,1,0:T(8,128)(2,1)S(1)}, u32[]{:S(2)}, u32[]{:S(2)}) collective-permute-start(bf16[4,2,32,512]{3,2,1,0:T(8,128)(2,1)S(1)} %shard_map.66), channel_id=1, source_target_pairs={{0,8},{8,0},{1,9},{9,1},{2,10},{10,2},{3,11},{11,3},{4,12},{12,4},... | collective-permute-start | bytes 786440 | tf_op jit(solution)/shard_map/ppermute | solution.py:181
  21.5 2.4 %copy-start = (f32[8,2048]{1,0:T(8,128)S(1)}, f32[8,2048]{1,0:T(8,128)}, u32[]{:S(2)}) copy-start(f32[8,2048]{1,0:T(8,128)} %gate_ref.1) | copy-start | bytes 196612
  22.1 1.8 %copy-start.2 = (s32[2,4]{1,0:T(2,128)S(1)}, s32[2,4]{1,0:T(2,128)}, u32[]{:S(2)}) copy-start(s32[2,4]{1,0:T(2,128)} %level_ref.1) | copy-start | bytes 100
  22.1 1.7 %copy-start.1 = (s32[2,4]{1,0:T(2,128)S(1)}, s32[2,4]{1,0:T(2,128)}, u32[]{:S(2)}) copy-start(s32[2,4]{1,0:T(2,128)} %slot_ref.1) | copy-start | bytes 100
  22.1 1.7 %collective-permute-start.11 = (bf16[4,2,32,512]{3,2,1,0:T(8,128)(2,1)S(1)}, bf16[4,2,32,512]{3,2,1,0:T(8,128)(2,1)S(1)}, u32[]{:S(2)}, u32[]{:S(2)}) collective-permute-start(bf16[4,2,32,512]{3,2,1,0:T(8,128)(2,1)S(1)} %get-tuple-element.28), channel_id=1, source_target_pairs={{0,8},{8,0},{1,9},{9,1},{2,10},{10,2},{3,11},{11,3},{4,12},{12,4},... | collective-permute-start | bytes 786440 | tf_op jit(solution)/shard_map/ppermute | solution.py:181
  25.1 4.5 %collective-permute-start.12 = (bf16[32,512]{1,0:T(8,128)(2,1)S(1)}, bf16[32,512]{1,0:T(8,128)(2,1)S(1)}, u32[]{:S(2)}, u32[]{:S(2)}) collective-permute-start(bf16[32,512]{1,0:T(8,128)(2,1)S(1)} %get-tuple-element.30), channel_id=1, source_target_pairs={{0,2},{1,3},{2,0},{3,1},{4,6},{5,7},{6,4},{7,5},{8,10},{9,11},{10,... | collective-permute-start | bytes 98312 | tf_op jit(solution)/shard_map/ppermute | solution.py:142
  25.2 5.8 %collective-permute-start.13 = (bf16[32,512]{1,0:T(8,128)(2,1)S(1)}, bf16[32,512]{1,0:T(8,128)(2,1)S(1)}, u32[]{:S(2)}, u32[]{:S(2)}) collective-permute-start(bf16[32,512]{1,0:T(8,128)(2,1)S(1)} %get-tuple-element.31), channel_id=1, source_target_pairs={{0,4},{1,5},{2,6},{3,7},{4,0},{5,1},{6,2},{7,3},{8,12},{9,13},{10,... | collective-permute-start | bytes 98312 | tf_op jit(solution)/shard_map/ppermute | solution.py:142
  28.7 5.7 %collective-permute-start.14 = (bf16[32,512]{1,0:T(8,128)(2,1)S(1)}, bf16[32,512]{1,0:T(8,128)(2,1)S(1)}, u32[]{:S(2)}, u32[]{:S(2)}) collective-permute-start(bf16[32,512]{1,0:T(8,128)(2,1)S(1)} %get-tuple-element.32), channel_id=1, source_target_pairs={{0,6},{1,7},{2,4},{3,5},{4,2},{5,3},{6,0},{7,1},{8,14},{9,15},{10,... | collective-permute-start | bytes 98312 | tf_op jit(solution)/shard_map/ppermute | solution.py:142

commit v8 on v0

v8 whole, which is shorter than its diff:
```python
import functools
import math

import jax
import jax.numpy as jnp
from jax import lax
from jax.experimental import pallas as pl
from jax.experimental.pallas import tpu as pltpu
from jax.sharding import PartitionSpec as P

H = 16
HEAD = 128
AXES = ("frame", "seq")
SMEM = pl.BlockSpec(memory_space=pltpu.SMEM)
HBM = pl.BlockSpec(memory_space=pltpu.HBM)
VMEM = pl.BlockSpec(memory_space=pltpu.VMEM)
PARAMS = pltpu.CompilerParams(vmem_limit_bytes=32 * 1024 * 1024)


def attend(slot_ref, level_ref, gate_ref, query_ref, key_ref, value_ref, out_ref, *, tokens):
    rows, width = query_ref.shape
    groups, local_frames = slot_ref.shape
    group = lax.axis_index("frame")
    key_count = key_ref.shape[0]
    index = lax.broadcasted_iota(jnp.int32, (1, key_count), 1)
    frame = index // (key_count // groups) * local_frames + index // tokens % local_frames
    key_slots = jnp.zeros((1, key_count), jnp.int32)
    for one in range(groups * local_frames):
        slot = slot_ref[one // local_frames, one % local_frames]
        key_slots = jnp.where(frame == one, slot, key_slots)
    shown = []
    for local in range(local_frames):
        visible = key_slots <= slot_ref[group, local]
        shown.append(jnp.where(visible, 0.0, -jnp.inf).reshape(1, 1, key_count))
    shown = jnp.concatenate(shown, axis=0)
    gate_blocks = gate_ref[...]
    level_rows = lax.broadcasted_iota(jnp.int32, gate_blocks.shape, 0)
    gate_rows = [
        jnp.sum(
            jnp.where(level_rows == level_ref[group, local], gate_blocks, 0.0),
            axis=0,
            keepdims=True,
        )
        for local in range(local_frames)
    ]
    ones = jnp.ones((key_count, HEAD), jnp.bfloat16)
    scale = math.log2(math.e) / math.sqrt(HEAD)
    for column in range(0, width, HEAD):
        part = slice(column, column + HEAD)
        gates = jnp.concatenate([row[:, part].reshape(1, 1, HEAD) for row in gate_rows], axis=0)
        scores = lax.dot_general(
            query_ref[:, part],
            key_ref[:, part],
            (((1,), (1,)), ((), ())),
            preferred_element_type=jnp.float32,
        )
        scores = scores.reshape(local_frames, tokens, key_count) * scale + shown
        scores = scores.reshape(rows, key_count)
        weights = jnp.exp2(scores - jnp.max(scores, axis=1, keepdims=True))
        values = jnp.concatenate([value_ref[:, part], ones], axis=1)
        mixed = jnp.dot(weights.astype(jnp.bfloat16), values, preferred_element_type=jnp.float32)
        mixed = (mixed[:, :HEAD] / mixed[:, HEAD:]).reshape(local_frames, tokens, HEAD) * gates
        out_ref[:, part] = mixed.reshape(rows, HEAD).astype(out_ref.dtype)


def whole_heads(queries, keys, values, slot_of, level_of, gate_table):
    _, local_frames, tokens, width = queries.shape
    rows = local_frames * tokens
    keys, values = (
        lax.all_gather(taken.reshape(rows, width), AXES, axis=0, tiled=True)
        for taken in (keys, values)
    )
    answer = pl.pallas_call(
        functools.partial(attend, tokens=tokens),
        out_shape=jax.ShapeDtypeStruct((rows, width), queries.dtype),
        in_specs=[SMEM] * 2 + [VMEM] * 4,
        out_specs=VMEM,
        compiler_params=PARAMS,
    )(slot_of, level_of, gate_table, queries.reshape(rows, width), keys, values)
    return answer.reshape(queries.shape)


def shared_heads(queries, keys, values, slot_of, level_of, gate_table):
    devices = lax.axis_size("frame") * lax.axis_size("seq")
    _, local_frames, tokens, _ = queries.shape
    rows, blocks = local_frames * tokens, devices // H
    block_rows = rows // blocks
    exchange = functools.partial(
        lax.all_to_all, axis_name=AXES, split_axis=0, concat_axis=0, tiled=True
    )

    def by_head(taken):
        return taken.reshape(rows, H, HEAD).transpose(1, 0, 2)

    def key_pieces(taken):
        pieces = jnp.broadcast_to(by_head(taken)[:, None], (H, blocks, rows, HEAD))
        return exchange(pieces.reshape(devices, rows, HEAD)).reshape(devices * rows, HEAD)

    key_rows, value_rows = key_pieces(keys), key_pieces(values)
    query_rows = exchange(by_head(queries).reshape(devices, block_rows, HEAD))
    query_rows = query_rows.reshape(devices * block_rows, HEAD)
    device_index = lax.axis_index("frame") * lax.axis_size("seq") + lax.axis_index("seq")
    head, block = device_index // blocks, device_index % blocks

    def per_row(table):
        table = jnp.repeat(table, tokens, axis=1)[:, None]
        return jnp.broadcast_to(table, (table.shape[0], lax.axis_size("seq"), rows))

    row_slots, row_levels = per_row(slot_of), per_row(level_of)
    query_slots = lax.dynamic_slice_in_dim(row_slots, block * block_rows, block_rows, 2)
    levels = lax.dynamic_slice_in_dim(row_levels, block * block_rows, block_rows, 2).reshape(-1)
    scores = lax.dot_general(
        query_rows, key_rows, (((1,), (1,)), ((), ())), preferred_element_type=jnp.float32
    )
    visible = row_slots.reshape(1, -1) <= query_slots.reshape(-1, 1)
    scores = jnp.where(visible, scores * (1.0 / math.sqrt(HEAD)), -jnp.inf)
    weights = jnp.exp(scores - jnp.max(scores, axis=1, keepdims=True)).astype(jnp.bfloat16)
    total = jnp.sum(weights.astype(jnp.float32), axis=1, keepdims=True)
    mixed = jnp.dot(weights, value_rows, preferred_element_type=jnp.float32) / total
    gates = lax.dynamic_slice_in_dim(gate_table, head * HEAD, HEAD, 1)[levels]
    answer = exchange((mixed * gates).astype(queries.dtype).reshape(devices, block_rows, HEAD))
    return answer.reshape(H, rows, HEAD).transpose(1, 0, 2).reshape(queries.shape)


def body(queries, *others):
    if lax.axis_size("seq") > H:
        return shared_heads(queries, *others)
    return whole_heads(queries, *others)


def solution(mesh):
    return jax.shard_map(
        body,
        mesh=mesh,
        in_specs=(
            P(("rollout", "frame"), None, "seq", None),
            P(("rollout", "frame"), None, "seq", None),
            P(("rollout", "frame"), None, "seq", None),
            P("rollout", None),
            P("rollout", None),
            P(),
        ),
        out_specs=P(("rollout", "frame"), None, "seq", None),
        check_vma=False,
    )
```

time: 37 us -> 112 us (3.03)
  waiting for transfers between devices: 13 us -> 89.5 us
  between operations: 0.06 us -> 13.4 us
  blocking collectives: 10.2 us -> 0 us
  starting transfers between devices: 7.36 us -> 0.04 us
  local copies, waits for them, and re-layouts: 2.77 us -> 6.28 us
    all_gather x0 -> x2, waiting for transfers between devices: none -> 88.1 us  [whole_heads(): lax.all_gather(taken.reshape(rows, width), AXES, axis=0, tiled=True)]
    all_to_all x1 -> x0, waiting for transfers between devices: 13 us -> none  [one_head_each(): packed = exchange(packed)]
    all_to_all x1 -> x0, blocking collectives: 10.2 us -> none  [one_head_each(): answer = exchange(answer)]
    all_to_all x1 -> x0, starting transfers between devices: 7.36 us -> none  [one_head_each(): packed = exchange(packed)]
    unnamed x12, local copies, waits for them, and re-layouts: 2.76 us -> 6.28 us
    unnamed x0 -> x2, waiting for transfers between devices: none -> 1.41 us
    pallas_call x3 -> x1, Pallas kernels: 3.23 us -> 2.95 us  [whole_heads(): pl.pallas_call(functools.partial(attend, tokens=tokens), out_shape=jax.Sh...]
  transfers between devices with their start and end apart: 1 -> 2, of which waited for: 1 -> 2; matrix products, arithmetic and copies ran while one was open for 0% -> 0% of each run, Pallas kernels for 0% -> 0%
where the time goes in v8:
time: 112 us
  waiting for transfers between devices  89.5 us (80%)
  between operations  13.4 us (12%)
  local copies, waits for them, and re-layouts  6.28 us (6%)
  Pallas kernels  2.95 us (3%)
    all_gather x2, waiting for transfers between devices, whole_heads(): lax.all_gather(taken.reshape(rows, width), AXES, axis=0, tiled=True)  88.1 us
    unnamed x12, local copies, waits for them, and re-layouts  6.28 us
    pallas_call x1, Pallas kernels, whole_heads(): pl.pallas_call(functools.partial(attend, tokens=tokens), out_shape=jax.Sh...  2.95 us
  transfers between devices with their start and end apart: 2, of which 2 were waited for; matrix products, arithmetic and copies ran while one was open for 0% of the time, Pallas kernels for 0%

profile of v8, /device:TPU:0, one launch (start us, length us, event | category | flops | bytes accessed | tf_op | source)
XLA Modules:
  0.0 112.2 jit_solution(12806624917188538081)
XLA Ops:
  6.5 0.0 all-gather.3.cloned.1.call-start
  6.5 0.7 all-gather.3.cloned.1.call-update
  7.3 0.0 all-gather.5.cloned.1.call-start
  7.3 0.7 all-gather.5.cloned.1.call-update
  8.0 45.7 %all-gather.3.cloned.1.call-done.key_ref = bf16[512,2048]{1,0:T(8,128)(2,1)} async-done(((bf16[32,2048]{1,0:T(8,128)(2,1)}), bf16[512,2048]{1,0:T(8,128)(2,1)}) %all-gather.3.cloned.1.call-update) | async-done | bytes 2097168 | tf_op jit(solution)/shard_map/all_gather | solution.py:70
  53.7 42.4 %all-gather.5.cloned.1.call-done.value_ref = bf16[512,2048]{1,0:T(8,128)(2,1)} async-done(((bf16[32,2048]{1,0:T(8,128)(2,1)}), bf16[512,2048]{1,0:T(8,128)(2,1)}) %all-gather.5.cloned.1.call-update) | async-done | bytes 2097168 | tf_op jit(solution)/shard_map/all_gather | solution.py:70
  96.1 0.0 copy-start
  96.1 1.6 %copy-done = bf16[512,2048]{1,0:T(8,128)(2,1)S(1)} copy-done((bf16[512,2048]{1,0:T(8,128)(2,1)S(1)}, bf16[512,2048]{1,0:T(8,128)(2,1)}, u32[]{:S(2)}) %copy-start) | copy-done | bytes 2097176
  97.7 0.0 copy-start.1
  97.7 1.6 %copy-done.1 = bf16[512,2048]{1,0:T(8,128)(2,1)S(1)} copy-done((bf16[512,2048]{1,0:T(8,128)(2,1)S(1)}, bf16[512,2048]{1,0:T(8,128)(2,1)}, u32[]{:S(2)}) %copy-start.1) | copy-done | bytes 2097176
  99.3 0.0 copy-start.2
  99.3 0.9 copy-done.2
  100.2 0.0 copy-start.3
  100.2 0.8 copy-done.3
  101.0 0.0 copy-start.4
  101.0 0.7 copy-done.4
  101.7 0.0 copy-start.5
  101.7 0.7 copy-done.5
  102.4 3.0 %shard_map.64 = bf16[32,2048]{1,0:T(8,128)(2,1)} custom-call(s32[2,4]{1,0:T(2,128)S(1)} %copy-done.4, s32[2,4]{1,0:T(2,128)S(1)} %copy-done.5, f32[8,2048]{1,0:T(8,128)S(1)} %copy-done.3, bf16[32,2048]{1,0:T(8,128)(2,1)S(1)} %bitcast.4, bf16[512,2048]{1,0:T(8,128)(2,1)S(1)} %copy-done, bf16[512,2048]{1,0:T(8,128)(2,1)S(1)} %copy-done.1), custom_call_target="tpu_custom_call" | custom-call | tf_op jit(solution)/shard_map/pallas_call | solution.py:73
Async XLA Ops:
  6.5 47.2 %all-gather.3.cloned.1.call-start = ((), (), s32[]{:S(2)}) async-start(), calls=%async_computation | async-start | bytes 2228224 | tf_op jit(solution)/shard_map/all_gather | solution.py:70
  7.3 88.8 %all-gather.5.cloned.1.call-start = ((), (), s32[]{:S(2)}) async-start(), calls=%async_computation.1 | async-start | bytes 2228224 | tf_op jit(solution)/shard_map/all_gather | solution.py:70
  96.1 1.6 %copy-start = (bf16[512,2048]{1,0:T(8,128)(2,1)S(1)}, bf16[512,2048]{1,0:T(8,128)(2,1)}, u32[]{:S(2)}) copy-start(bf16[512,2048]{1,0:T(8,128)(2,1)} %all-gather.3.cloned.1.call-done.key_ref) | copy-start | bytes 6291460
  97.7 1.6 %copy-start.1 = (bf16[512,2048]{1,0:T(8,128)(2,1)S(1)}, bf16[512,2048]{1,0:T(8,128)(2,1)}, u32[]{:S(2)}) copy-start(bf16[512,2048]{1,0:T(8,128)(2,1)} %all-gather.5.cloned.1.call-done.value_ref) | copy-start | bytes 6291460
  99.3 0.9 copy-start.2
  100.2 0.8 copy-start.3
  101.0 0.7 copy-start.4
  101.7 0.7 copy-start.5
Sparse Core Ops, SparseCore 0:
  9.6 44.0 all-gather.2
  55.9 40.1 all-gather.4

commit v9 on v0

--- a/solution.py
+++ b/solution.py
@@ -12,51 +12,83 @@
 HEAD = 128
 AXES = ("frame", "seq")
 SMEM = pl.BlockSpec(memory_space=pltpu.SMEM)
+HBM = pl.BlockSpec(memory_space=pltpu.HBM)
 VMEM = pl.BlockSpec(memory_space=pltpu.VMEM)
 PARAMS = pltpu.CompilerParams(vmem_limit_bytes=32 * 1024 * 1024)
 
 
+def columns_of(place, width):
+    return pl.ds(pl.multiple_of(place * width, width), width)
+
+
+def run(copies):
+    for copy in copies:
+        copy.start()
+    for copy in copies:
+        copy.wait()
+
+
 def pack(*refs):
-    out_ref = refs[-1]
-    width = out_ref.shape[-1]
-    for place, ref in enumerate(refs[:-1]):
-        for device in range(out_ref.shape[0]):
-            out_ref[device, place] = ref[:, device * width : (device + 1) * width]
-
-
-def unpack(held_ref, out_ref):
-    width = held_ref.shape[-1]
-    for device in range(held_ref.shape[0]):
-        out_ref[:, device * width : (device + 1) * width] = held_ref[device]
-
-
-def attend(slot_ref, level_ref, packed_ref, gate_ref, out_ref, *, group_devices, tokens):
-    devices, _, rows, width = packed_ref.shape
-    local_frames = rows // tokens
-    group_count = devices // group_devices
+    *operands, out_ref, sems = refs
+    run(
+        [
+            pltpu.make_async_copy(
+                ref.at[:, columns_of(device, out_ref.shape[-1])],
+                out_ref.at[device, kind],
+                sems.at[device, kind],
+            )
+            for device in range(out_ref.shape[0])
+            for kind, ref in enumerate(operands)
+        ]
+    )
+
+
+def unpack(held_ref, out_ref, sems):
+    devices, _, width = held_ref.shape
+    run(
+        [
+            pltpu.make_async_copy(
+                held_ref.at[device], out_ref.at[:, columns_of(device, width)], sems.at[device]
+            )
+            for device in range(devices)
+        ]
+    )
+
+
+def attend(slot_ref, level_ref, gate_ref, packed_ref, out_ref, *, tokens):
+    groups, local_frames = slot_ref.shape
+    devices, rows, width = out_ref.shape
+    group_devices = devices // groups
+    group_rows = group_devices * rows
     key_count = devices * rows
     index = lax.broadcasted_iota(jnp.int32, (1, key_count), 1)
-    frame = index // (group_devices * rows) * local_frames + index // tokens % local_frames
+    frame = index // group_rows * local_frames + index // tokens % local_frames
     key_slots = jnp.zeros((1, key_count), jnp.int32)
-    for one in range(group_count * local_frames):
+    for one in range(groups * local_frames):
         slot = slot_ref[one // local_frames, one % local_frames]
         key_slots = jnp.where(frame == one, slot, key_slots)
+    gate_blocks = gate_ref[
+        :, columns_of(lax.axis_index("frame") * lax.axis_size("seq") + lax.axis_index("seq"), width)
+    ]
+    level_rows = lax.broadcasted_iota(jnp.int32, gate_blocks.shape, 0)
+    ones = jnp.ones((key_count, HEAD), jnp.bfloat16)
     scale = math.log2(math.e) / math.sqrt(HEAD)
     step = max(1, min(group_devices, 128 // rows))
-    for column in range(0, width, HEAD):
-        part = pl.ds(column, HEAD)
-        keys = packed_ref[:, 1, :, part].reshape(key_count, HEAD)
-        values = packed_ref[:, 2, :, part].reshape(key_count, HEAD)
-        for group in range(group_count):
-            shown = []
-            gates = []
-            for local in range(local_frames):
-                visible = key_slots <= slot_ref[group, local]
-                shown.append(jnp.where(visible, 0.0, -jnp.inf).reshape(1, 1, 1, key_count))
-                level = level_ref[group, local]
-                gates.append(gate_ref[pl.ds(level, 1), part].reshape(1, 1, 1, HEAD))
-            shown = jnp.concatenate(shown, axis=1)
+    for group in range(groups):
+        shown, gate_rows = [], []
+        for local in range(local_frames):
+            visible = key_slots <= slot_ref[group, local]
+            shown.append(jnp.where(visible, 0.0, -jnp.inf).reshape(1, 1, 1, key_count))
+            gate = jnp.where(level_rows == level_ref[group, local], gate_blocks, 0.0)
+            gate_rows.append(jnp.sum(gate, axis=0, keepdims=True))
+        shown = jnp.concatenate(shown, axis=1)
+        for column in range(0, width, HEAD):
+            part = slice(column, column + HEAD)
+            gates = [row[:, part].reshape(1, 1, 1, HEAD) for row in gate_rows]
             gates = jnp.concatenate(gates, axis=1)
+            keys = packed_ref[:, 1, :, part].reshape(key_count, HEAD)
+            values = packed_ref[:, 2, :, part].reshape(key_count, HEAD)
+            values = jnp.concatenate([values, ones], axis=1)
             for start in range(group * group_devices, (group + 1) * group_devices, step):
                 queries = packed_ref[start : start + step, 0, :, part].reshape(step * rows, HEAD)
                 scores = lax.dot_general(
@@ -65,18 +97,18 @@
                 scores = scores.reshape(step, local_frames, tokens, key_count) * scale + shown
                 scores = scores.reshape(step * rows, key_count)
                 weights = jnp.exp2(scores - jnp.max(scores, axis=1, keepdims=True))
-                weights = weights.astype(jnp.bfloat16)
-                total = jnp.sum(weights.astype(jnp.float32), axis=1, keepdims=True)
-                mixed = jnp.dot(weights, values, preferred_element_type=jnp.float32) / total
+                mixed = jnp.dot(
+                    weights.astype(jnp.bfloat16), values, preferred_element_type=jnp.float32
+                )
+                mixed = mixed[:, :HEAD] / mixed[:, HEAD:]
                 mixed = mixed.reshape(step, local_frames, tokens, HEAD) * gates
                 out_ref[start : start + step, :, part] = mixed.reshape(step, rows, HEAD).astype(
                     out_ref.dtype
                 )
 
 
-def one_head_each(queries, keys, values, slot_of, level_of, gate_table):
-    seq_count = lax.axis_size("seq")
-    devices = lax.axis_size("frame") * seq_count
+def whole_heads(queries, keys, values, slot_of, level_of, gate_table):
+    devices = lax.axis_size("frame") * lax.axis_size("seq")
     _, local_frames, tokens, all_width = queries.shape
     rows, width = local_frames * tokens, all_width // devices
     exchange = functools.partial(
@@ -85,28 +117,31 @@
     packed = pl.pallas_call(
         pack,
         out_shape=jax.ShapeDtypeStruct((devices, 3, rows, width), queries.dtype),
-        in_specs=[VMEM] * 3,
+        in_specs=[HBM] * 3,
+        out_specs=VMEM,
+        scratch_shapes=[pltpu.SemaphoreType.DMA((devices, 3))],
+        compiler_params=PARAMS,
+    )(
+        *(
+            pltpu.with_memory_space_constraint(taken.reshape(rows, all_width), pltpu.HBM)
+            for taken in (queries, keys, values)
+        )
+    )
+    answer = pl.pallas_call(
+        functools.partial(attend, tokens=tokens),
+        out_shape=jax.ShapeDtypeStruct((devices, rows, width), queries.dtype),
+        in_specs=[SMEM] * 2 + [VMEM] * 2,
         out_specs=VMEM,
         compiler_params=PARAMS,
-    )(*(taken.reshape(rows, all_width) for taken in (queries, keys, values)))
-    packed = exchange(packed)
-    device_index = lax.axis_index("frame") * seq_count + lax.axis_index("seq")
-    gates = lax.dynamic_slice_in_dim(gate_table, device_index * width, width, 1)
-    answer = pl.pallas_call(
-        functools.partial(attend, group_devices=seq_count, tokens=tokens),
-        out_shape=jax.ShapeDtypeStruct((devices, rows, width), queries.dtype),
-        in_specs=[SMEM, SMEM, VMEM, VMEM],
-        out_specs=VMEM,
-        compiler_params=PARAMS,
-    )(slot_of, level_of, packed, gates)
-    answer = exchange(answer)
+    )(slot_of, level_of, gate_table, exchange(packed))
     answer = pl.pallas_call(
         unpack,
         out_shape=jax.ShapeDtypeStruct((rows, all_width), queries.dtype),
         in_specs=[VMEM],
-        out_specs=VMEM,
+        out_specs=HBM,
+        scratch_shapes=[pltpu.SemaphoreType.DMA((devices,))],
         compiler_params=PARAMS,
-    )(answer)
+    )(exchange(answer))
     return answer.reshape(queries.shape)
 
 
@@ -153,10 +188,9 @@
 
 
 def body(queries, *others):
-    devices = lax.axis_size("frame") * lax.axis_size("seq")
-    if devices > H:
+    if lax.axis_size("frame") * lax.axis_size("seq") > H:
         return shared_heads(queries, *others)
-    return one_head_each(queries, *others)
+    return whole_heads(queries, *others)
 
 
 def solution(mesh):

time: 37 us -> 34.4 us (0.930)
  blocking collectives: 10.2 us -> 30.6 us
  waiting for transfers between devices: 13 us -> 0 us
  starting transfers between devices: 7.36 us -> 0 us
  local copies, waits for them, and re-layouts: 2.77 us -> 0.02 us
    all_to_all x1 -> x2, blocking collectives: 10.2 us -> 30.6 us  [the longest x1 20.4 us: whole_heads(): exchange(packed)]
    all_to_all x1 -> x0, waiting for transfers between devices: 13 us -> none  [one_head_each(): packed = exchange(packed)]
    all_to_all x1 -> x0, starting transfers between devices: 7.36 us -> none  [one_head_each(): packed = exchange(packed)]
    unnamed x12 -> x6, local copies, waits for them, and re-layouts: 2.76 us -> 0.02 us
  transfers between devices with their start and end apart: 1 -> 0, of which waited for: 1 -> 0; matrix products, arithmetic and copies ran while one was open for 0% -> 0% of each run, Pallas kernels for 0% -> 0%
where the time goes in v9:
time: 34.4 us; the launch traced here: 34.1 us
  blocking collectives  30.6 us (89%)
  Pallas kernels  3.46 us (10%)
    all_to_all x1, blocking collectives, whole_heads(): exchange(packed)  20.4 us
    all_to_all x1, blocking collectives, whole_heads(): exchange(answer)  10.2 us
    pallas_call x1, Pallas kernels, whole_heads(): pl.pallas_call(pack, out_shape=jax.ShapeDtypeStruct((devices, 3, rows, wi...  1.43 us
    pallas_call x1, Pallas kernels, whole_heads(): pl.pallas_call(functools.partial(attend, tokens=tokens), out_shape=jax.Sh...  1.23 us
    pallas_call x1, Pallas kernels, whole_heads(): pl.pallas_call(unpack, out_shape=jax.ShapeDtypeStruct((rows, all_width),...  0.8 us

profile of v9, /device:TPU:0, one launch (start us, length us, event | category | flops | bytes accessed | tf_op | source)
XLA Modules:
  0.0 34.1 jit_solution(6998528137473458496)
XLA Ops:
  0.0 1.4 %shard_map.64 = bf16[16,3,32,128]{3,2,1,0:T(8,128)(2,1)S(1)} custom-call(bf16[32,2048]{1,0:T(8,128)(2,1)} %bitcast.4, bf16[32,2048]{1,0:T(8,128)(2,1)} %bitcast.5, bf16[32,2048]{1,0:T(8,128)(2,1)} %bitcast.6), custom_call_target="tpu_custom_call" | custom-call | tf_op jit(solution)/shard_map/pallas_call | solution.py:117
  1.4 0.0 copy-start
  1.4 0.0 copy-start.1
  1.5 0.0 copy-start.2
  1.5 20.4 %all_to_all.10.packed_ref = bf16[16,3,32,128]{3,2,1,0:T(8,128)(2,1)S(1)} all-to-all(bf16[16,3,32,128]{3,2,1,0:T(8,128)(2,1)S(1)} %shard_map.64), channel_id=1, replica_groups=mesh['rollout'=2,'frame'=2,'seq'=8] {'frame','seq'}, dimensions={0} | all-to-all | bytes 786432 | tf_op jit(solution)/shard_map/all_to_all | solution.py:136
  21.9 0.0 copy-done
  21.9 0.0 copy-done.1
  21.9 0.0 copy-done.2
  21.9 1.2 %shard_map.65 = bf16[16,32,128]{2,1,0:T(8,128)(2,1)S(1)} custom-call(s32[2,4]{1,0:T(2,128)S(1)} %copy-done.1, s32[2,4]{1,0:T(2,128)S(1)} %copy-done.2, f32[8,2048]{1,0:T(8,128)S(1)} %copy-done, bf16[16,3,32,128]{3,2,1,0:T(8,128)(2,1)S(1)} %all_to_all.10.packed_ref), custom_call_target="tpu_custom_call" | custom-call | tf_op jit(solution)/shard_map/pallas_call | solution.py:130
  23.1 10.2 %all_to_all.11.held_ref = bf16[16,32,128]{2,1,0:T(8,128)(2,1)S(1)} all-to-all(bf16[16,32,128]{2,1,0:T(8,128)(2,1)S(1)} %shard_map.65), channel_id=1, replica_groups=mesh['rollout'=2,'frame'=2,'seq'=8] {'frame','seq'}, dimensions={0} | all-to-all | bytes 262144 | tf_op jit(solution)/shard_map/all_to_all | solution.py:144
  33.3 0.8 %shard_map.66 = bf16[32,2048]{1,0:T(8,128)(2,1)} custom-call(bf16[16,32,128]{2,1,0:T(8,128)(2,1)S(1)} %all_to_all.11.held_ref), custom_call_target="tpu_custom_call" | custom-call | tf_op jit(solution)/shard_map/pallas_call | solution.py:137
Async XLA Ops:
  1.4 20.4 %copy-start = (f32[8,2048]{1,0:T(8,128)S(1)}, f32[8,2048]{1,0:T(8,128)}, u32[]{:S(2)}) copy-start(f32[8,2048]{1,0:T(8,128)} %gate_ref.1) | copy-start | bytes 196612
  1.4 20.4 %copy-start.1 = (s32[2,4]{1,0:T(2,128)S(1)}, s32[2,4]{1,0:T(2,128)}, u32[]{:S(2)}) copy-start(s32[2,4]{1,0:T(2,128)} %slot_ref.1) | copy-start | bytes 100
  1.5 20.4 %copy-start.2 = (s32[2,4]{1,0:T(2,128)S(1)}, s32[2,4]{1,0:T(2,128)}, u32[]{:S(2)}) copy-start(s32[2,4]{1,0:T(2,128)} %level_ref.1) | copy-start | bytes 100

commit v10 on v7

--- a/solution.py
+++ b/solution.py
@@ -43,13 +43,15 @@
     run(copies)
 
 
-def stack(*refs, count):
+def move(*refs, plan):
     *refs, sems = refs
-    outs = refs[-(len(refs) // (count + 1)) :]
+    outs = refs[len(plan) :]
     run(
         [
-            pltpu.make_async_copy(ref, outs[number // count].at[number % count], sems.at[number])
-            for number, ref in enumerate(refs[: -len(outs)])
+            pltpu.make_async_copy(
+                ref, outs[number] if at is None else outs[number].at[at], sems.at[one]
+            )
+            for one, (ref, (number, at)) in enumerate(zip(refs, plan))
         ]
     )
 
@@ -72,7 +74,7 @@
     refs, outs = refs[:-pieces], refs[-pieces:]
     held_refs, stack_refs = refs[: near * pieces], refs[near * pieces :]
     rows, width = outs[0].shape
-    group_count = 1 + len(stack_refs) // near
+    group_count = slot_ref.shape[0]
     local_frames = rows // tokens
     group_keys = near * pieces * rows
     key_count = group_count * group_keys
@@ -108,7 +110,7 @@
         keys, values = (
             jnp.concatenate(
                 [ref[kind, :, part] for ref in held_refs]
-                + [ref[:, kind, :, part].reshape(pieces * rows, HEAD) for ref in stack_refs]
+                + [ref[:, kind, :, part].reshape(ref.shape[0] * rows, HEAD) for ref in stack_refs]
             )
             for kind in range(2)
         )
@@ -158,25 +160,33 @@
             for taken in (queries, keys, values)
         ),
     )
+    def moved(taken, plan, shapes):
+        return pl.pallas_call(
+            functools.partial(move, plan=plan),
+            out_shape=[jax.ShapeDtypeStruct(shape, queries.dtype) for shape in shapes],
+            in_specs=[VMEM] * len(taken),
+            out_specs=[VMEM] * len(shapes),
+            scratch_shapes=[pltpu.SemaphoreType.DMA((len(taken),))],
+            compiler_params=PARAMS,
+        )(*taken)
+
+    pair_shape, own_shape = (2, rows, width), (rows, width)
     pairs = swap_far(sent[:count])
-    own = swap_far(sent[count:])
-    held = [pairs] + [[swap(piece, away) for piece in pairs] for away in range(1, near)]
-
-    def stacked(*kinds):
-        return pl.pallas_call(
-            functools.partial(stack, count=count),
-            out_shape=[
-                jax.ShapeDtypeStruct((count,) + taken[0].shape, queries.dtype) for taken in kinds
-            ],
-            in_specs=[VMEM] * (len(kinds) * count),
-            out_specs=[VMEM] * len(kinds),
-            scratch_shapes=[pltpu.SemaphoreType.DMA((len(kinds) * count,))],
-            compiler_params=PARAMS,
-        )(*sum(kinds, []))
-
-    stacks = [stacked(taken)[0] for taken in held[:-1]]
-    last, own = stacked(held[-1], own)
-    stacks.append(last)
+    held = [[piece] + [swap(piece, away) for away in range(1, near)] for piece in pairs]
+    half = max(1, count // 2)
+    early, late = sum(held[:half], []), sum(held[half:], [])
+    first, *own = moved(
+        [*early, *sent[count:]],
+        [(0, at) for at in range(len(early))] + [(1 + at, None) for at in range(count)],
+        [(len(early), *pair_shape)] + [own_shape] * count,
+    )
+    second, own = moved(
+        [*late, *swap_far(own)],
+        [(0, at) for at in range(len(late))] + [(1, at) for at in range(count)],
+        [(len(late), *pair_shape), (count, *own_shape)],
+    )
+    stacks = [first, second]
+    held = [early, late]
     stacks = [
         lax.ppermute(taken, "frame", [(one, (one - away) % groups) for one in range(groups)])
         for away in range(1, groups)

time: 35.2 us -> 35.7 us (1.014)
  waiting for transfers between devices: 8.96 us -> 11.7 us
  starting transfers between devices: 22.1 us -> 19.6 us
    ppermute x13, waiting for transfers between devices: 7.8 us -> 10.2 us  [swap(): lax.ppermute(taken, 'seq', [(one, one ^ away) for one in range(devices)])]
    ppermute x13, starting transfers between devices: 21.5 us -> 19.5 us  [swap(): lax.ppermute(taken, 'seq', [(one, one ^ away) for one in range(devices)])]
    ppermute x2, starting transfers between devices: 0.57 us -> 0.07 us  [whole_heads(): lax.ppermute(taken, 'frame', [(one, (one - away) % groups) for one in ran...]
where the time goes in v10:
time: 35.7 us; the launch traced here: 35.5 us
  starting transfers between devices  19.6 us (55%)
  waiting for transfers between devices  11.7 us (33%)
  Pallas kernels  4.11 us (12%)
    ppermute x13, starting transfers between devices, swap(): lax.ppermute(taken, 'seq', [(one, one ^ away) for one in range(devices)])  19.5 us
    ppermute x13, waiting for transfers between devices, swap(): lax.ppermute(taken, 'seq', [(one, one ^ away) for one in range(devices)])  10.2 us
    ppermute x2, waiting for transfers between devices, whole_heads(): lax.ppermute(taken, 'frame', [(one, (one - away) % groups) for one in ran...  1.51 us
    pallas_call x1, Pallas kernels, whole_heads(): pl.pallas_call(functools.partial(attend, near=near, tokens=tokens), out_s...  1.24 us
    pallas_call x2, Pallas kernels, moved(): pl.pallas_call(functools.partial(move, plan=plan), out_shape=[jax.ShapeDt...  1.15 us
    pallas_call x1, Pallas kernels, whole_heads(): pl.pallas_call(functools.partial(pack, near=near), out_shape=[jax.ShapeDt...  1.04 us
  transfers between devices with their start and end apart: 15, of which 6 were waited for; matrix products, arithmetic and copies ran while one was open for 0% of the time, Pallas kernels for 3%

profile of v10, /device:TPU:0, one launch (start us, length us, event | category | flops | bytes accessed | tf_op | source)
XLA Modules:
  0.0 35.5 jit_solution(14383205878567185853)
XLA Ops:
  0.0 1.0 %shard_map.64 = (bf16[2,32,512]{2,1,0:T(8,128)(2,1)S(1)}, bf16[2,32,512]{2,1,0:T(8,128)(2,1)S(1)}, bf16[2,32,512]{2,1,0:T(8,128)(2,1)S(1)}, bf16[2,32,512]{2,1,0...) custom-call(bf16[32,2048]{1,0:T(8,128)(2,1)} %bitcast.4, ...), custom_call_target="tpu_custom_call" | custom-call | tf_op jit(solution)/shard_map/pallas_call | solution.py:149
  1.0 3.1 %collective-permute-start.5 = (bf16[2,32,512]{2,1,0:T(8,128)(2,1)S(1)}, bf16[2,32,512]{2,1,0:T(8,128)(2,1)S(1)}, u32[]{:S(2)}, u32[]{:S(2)}) collective-permute-start(bf16[2,32,512]{2,1,0:T(8,128)(2,1)S(1)} %get-tuple-element.27), channel_id=1, source_target_pairs={{0,2},{1,3},{2,0},{3,1},{4,6},{5,7},{6,4},{7,5},{8,10},{9,11},{10,... | collective-permute-start | bytes 196616 | tf_op jit(solution)/shard_map/ppermute | solution.py:144
  4.1 2.6 %collective-permute-start = (bf16[2,32,512]{2,1,0:T(8,128)(2,1)S(1)}, bf16[2,32,512]{2,1,0:T(8,128)(2,1)S(1)}, u32[]{:S(2)}, u32[]{:S(2)}) collective-permute-start(bf16[2,32,512]{2,1,0:T(8,128)(2,1)S(1)} %get-tuple-element.24), channel_id=1, source_target_pairs={{0,4},{1,5},{2,6},{3,7},{4,0},{5,1},{6,2},{7,3},{8,12},{9,13},{10,... | collective-permute-start | bytes 196616 | tf_op jit(solution)/shard_map/ppermute | solution.py:144
  6.7 0.0 collective-permute-start.2
  6.7 1.7 %collective-permute-start.4 = (bf16[2,32,512]{2,1,0:T(8,128)(2,1)S(1)}, bf16[2,32,512]{2,1,0:T(8,128)(2,1)S(1)}, u32[]{:S(2)}, u32[]{:S(2)}) collective-permute-start(bf16[2,32,512]{2,1,0:T(8,128)(2,1)S(1)} %get-tuple-element.26.refs_0_), channel_id=1, source_target_pairs={{0,1},{1,0},{2,3},{3,2},{4,5},{5,4},{6,7},{7,6},{8,9},{9,8},{10,11... | collective-permute-start | bytes 196616 | tf_op jit(solution)/shard_map/ppermute | solution.py:144
  8.4 0.0 collective-permute-done.5.refs_2_
  8.4 0.3 collective-permute-start.6
  8.8 2.6 %collective-permute-done.refs_0_.refs_4_ = bf16[2,32,512]{2,1,0:T(8,128)(2,1)S(1)} collective-permute-done((bf16[2,32,512]{2,1,0:T(8,128)(2,1)S(1)}, bf16[2,32,512]{2,1,0:T(8,128)(2,1)S(1)}, u32[]{:S(2)}, u32[]{:S(2)}) %collective-permute-start) | collective-permute-done | bytes 65568 | tf_op jit(solution)/shard_map/ppermute | solution.py:144
  11.4 1.5 %collective-permute-start.1 = (bf16[2,32,512]{2,1,0:T(8,128)(2,1)S(1)}, bf16[2,32,512]{2,1,0:T(8,128)(2,1)S(1)}, u32[]{:S(2)}, u32[]{:S(2)}) collective-permute-start(bf16[2,32,512]{2,1,0:T(8,128)(2,1)S(1)} %collective-permute-done.refs_0_.refs_4_), channel_id=1, source_target_pairs={{0,1},{1,0},{2,3},{3,2},{4,5},{5,4},{6,7},{7,6},{8,9},{9,8},{10,11... | collective-permute-start | bytes 196616 | tf_op jit(solution)/shard_map/ppermute | solution.py:144
  12.9 0.0 collective-permute-done.2.refs_2_.refs_6_
  12.9 1.4 %collective-permute-start.3 = (bf16[2,32,512]{2,1,0:T(8,128)(2,1)S(1)}, bf16[2,32,512]{2,1,0:T(8,128)(2,1)S(1)}, u32[]{:S(2)}, u32[]{:S(2)}) collective-permute-start(bf16[2,32,512]{2,1,0:T(8,128)(2,1)S(1)} %collective-permute-done.2.refs_2_.refs_6_), channel_id=1, source_target_pairs={{0,1},{1,0},{2,3},{3,2},{4,5},{5,4},{6,7},{7,6},{8,9},{9,8},{10,11... | collective-permute-start | bytes 196616 | tf_op jit(solution)/shard_map/ppermute | solution.py:144
  14.3 0.0 collective-permute-done.4.refs_1_
  14.3 0.0 collective-permute-done.6.refs_3_
  14.3 0.6 %shard_map.65 = (bf16[4,2,32,512]{3,2,1,0:T(8,128)(2,1)S(1)}, bf16[32,512]{1,0:T(8,128)(2,1)S(1)}, bf16[32,512]{1,0:T(8,128)(2,1)S(1)}, bf16[32,512]{1,0:T(8,128)(2,1)S(1)}, bf16[32,512]{1,0:T(8,128)(2,1)S(1)}) custom-call(bf16[2,32,512]{2,1,0:T(8,128)(2,1)S(1)} %get-tuple-element.26.refs_0_, bf16[2,32,512]{2,1,0:T(8,128)(2,1)S(1)} %collective-permute-done.4.refs_1_, ...), custom_call_target="tpu_custom_call" | custom-call | tf_op jit(solution)/shard_map/pallas_call | solution.py:164
  14.9 0.1 collective-permute-start.7
  15.0 3.1 %collective-permute-start.8 = (bf16[32,512]{1,0:T(8,128)(2,1)S(1)}, bf16[32,512]{1,0:T(8,128)(2,1)S(1)}, u32[]{:S(2)}, u32[]{:S(2)}) collective-permute-start(bf16[32,512]{1,0:T(8,128)(2,1)S(1)} %get-tuple-element.34), channel_id=1, source_target_pairs={{0,4},{1,5},{2,6},{3,7},{4,0},{5,1},{6,2},{7,3},{8,12},{9,13},{10,... | collective-permute-start | bytes 98312 | tf_op jit(solution)/shard_map/ppermute | solution.py:144
  18.1 1.3 %collective-permute-start.9 = (bf16[32,512]{1,0:T(8,128)(2,1)S(1)}, bf16[32,512]{1,0:T(8,128)(2,1)S(1)}, u32[]{:S(2)}, u32[]{:S(2)}) collective-permute-start(bf16[32,512]{1,0:T(8,128)(2,1)S(1)} %get-tuple-element.35), channel_id=1, source_target_pairs={{0,6},{1,7},{2,4},{3,5},{4,2},{5,3},{6,0},{7,1},{8,14},{9,15},{10,... | collective-permute-start | bytes 98312 | tf_op jit(solution)/shard_map/ppermute | solution.py:144
  19.3 0.0 collective-permute-done.1.refs_1_.refs_5_
  19.3 0.0 collective-permute-start.10
  19.3 0.0 collective-permute-done.3.refs_3_.refs_7_
  19.4 0.0 collective-permute-done.7.refs_5_
  19.4 0.6 %collective-permute-done.8.refs_6_ = bf16[32,512]{1,0:T(8,128)(2,1)S(1)} collective-permute-done((bf16[32,512]{1,0:T(8,128)(2,1)S(1)}, bf16[32,512]{1,0:T(8,128)(2,1)S(1)}, u32[]{:S(2)}, u32[]{:S(2)}) %collective-permute-start.8) | collective-permute-done | bytes 32800 | tf_op jit(solution)/shard_map/ppermute | solution.py:144
  20.0 3.8 %collective-permute-done.9.refs_7_ = bf16[32,512]{1,0:T(8,128)(2,1)S(1)} collective-permute-done((bf16[32,512]{1,0:T(8,128)(2,1)S(1)}, bf16[32,512]{1,0:T(8,128)(2,1)S(1)}, u32[]{:S(2)}, u32[]{:S(2)}) %collective-permute-start.9) | collective-permute-done | bytes 32800 | tf_op jit(solution)/shard_map/ppermute | solution.py:144
  23.8 0.0 copy-start
  23.8 0.6 %shard_map.66 = (bf16[4,2,32,512]{3,2,1,0:T(8,128)(2,1)S(1)}, bf16[4,32,512]{2,1,0:T(8,128)(2,1)S(1)}) custom-call(bf16[2,32,512]{2,1,0:T(8,128)(2,1)S(1)} %collective-permute-done.refs_0_.refs_4_, bf16[2,32,512]{2,1,0:T(8,128)(2,1)S(1)} %collective-permute-done.1.refs_1_.refs_5_, bf16[2,32,512]{2,1,0:T(8,128)(2,1)S(1)} %collective-permute-done.2.refs_2_.refs_6_, ...), custom_call_target="tpu_custom_call" | custom-call | tf_op jit(solution)/shard_map/pallas_call | solution.py:164
  24.4 0.0 copy-start.2
  24.4 0.0 copy-start.1
  24.4 0.1 collective-permute-start.11
  24.5 0.0 collective-permute-done.10.refs_8_
  24.5 1.5 %collective-permute-done.11.refs_9_ = bf16[4,2,32,512]{3,2,1,0:T(8,128)(2,1)S(1)} collective-permute-done((bf16[4,2,32,512]{3,2,1,0:T(8,128)(2,1)S(1)}, bf16[4,2,32,512]{3,2,1,0:T(8,128)(2,1)S(1)}, u32[]{:S(2)}, u32[]{:S(2)}) %collective-permute-start.11) | collective-permute-done | bytes 262176 | tf_op jit(solution)/shard_map/ppermute | solution.py:191
  26.0 0.0 copy-done
  26.0 0.0 copy-done.2
  26.0 0.0 copy-done.1
  26.0 1.2 %shard_map.67 = (bf16[32,512]{1,0:T(8,128)(2,1)S(1)}, bf16[32,512]{1,0:T(8,128)(2,1)S(1)}, bf16[32,512]{1,0:T(8,128)(2,1)S(1)}, bf16[32,512]{1,0:T(8,128)(2,1)S(1)}) custom-call(s32[2,4]{1,0:T(2,128)S(1)} %copy-done.1, s32[2,4]{1,0:T(2,128)S(1)} %copy-done.2, f32[8,2048]{1,0:T(8,128)S(1)} %copy-done, bf16[4,32,512]{2,1,0:T(8,128)(2,1)S(1)} %get-tuple-element.36.query_ref, ...), custom_call_target="tpu_custom_call" | custom-call | tf_op jit(solution)/shard_map/pallas_call | solution.py:196
  27.2 0.1 collective-permute-start.12
  27.3 1.8 %collective-permute-start.13 = (bf16[32,512]{1,0:T(8,128)(2,1)S(1)}, bf16[32,512]{1,0:T(8,128)(2,1)S(1)}, u32[]{:S(2)}, u32[]{:S(2)}) collective-permute-start(bf16[32,512]{1,0:T(8,128)(2,1)S(1)} %get-tuple-element.41), channel_id=1, source_target_pairs={{0,4},{1,5},{2,6},{3,7},{4,0},{5,1},{6,2},{7,3},{8,12},{9,13},{10,... | collective-permute-start | bytes 98312 | tf_op jit(solution)/shard_map/ppermute | solution.py:144
  29.1 2.5 %collective-permute-start.14 = (bf16[32,512]{1,0:T(8,128)(2,1)S(1)}, bf16[32,512]{1,0:T(8,128)(2,1)S(1)}, u32[]{:S(2)}, u32[]{:S(2)}) collective-permute-start(bf16[32,512]{1,0:T(8,128)(2,1)S(1)} %get-tuple-element.42), channel_id=1, source_target_pairs={{0,6},{1,7},{2,4},{3,5},{4,2},{5,3},{6,0},{7,1},{8,14},{9,15},{10,... | collective-permute-start | bytes 98312 | tf_op jit(solution)/shard_map/ppermute | solution.py:144
  31.7 0.0 collective-permute-done.12.refs_1_
  31.7 0.5 %collective-permute-done.13.refs_2_ = bf16[32,512]{1,0:T(8,128)(2,1)S(1)} collective-permute-done((bf16[32,512]{1,0:T(8,128)(2,1)S(1)}, bf16[32,512]{1,0:T(8,128)(2,1)S(1)}, u32[]{:S(2)}, u32[]{:S(2)}) %collective-permute-start.13) | collective-permute-done | bytes 32800 | tf_op jit(solution)/shard_map/ppermute | solution.py:144
  32.2 2.7 %collective-permute-done.14.refs_3_ = bf16[32,512]{1,0:T(8,128)(2,1)S(1)} collective-permute-done((bf16[32,512]{1,0:T(8,128)(2,1)S(1)}, bf16[32,512]{1,0:T(8,128)(2,1)S(1)}, u32[]{:S(2)}, u32[]{:S(2)}) %collective-permute-start.14) | collective-permute-done | bytes 32800 | tf_op jit(solution)/shard_map/ppermute | solution.py:144
  34.9 0.7 %shard_map.68 = bf16[32,2048]{1,0:T(8,128)(2,1)} custom-call(bf16[32,512]{1,0:T(8,128)(2,1)S(1)} %get-tuple-element.39.refs_0_, bf16[32,512]{1,0:T(8,128)(2,1)S(1)} %collective-permute-done.12.refs_1_, bf16[32,512]{1,0:T(8,128)(2,1)S(1)} %collective-permute-done.13.refs_2_, bf16[32,512]{1,0:T(8,128)(2,1)S(1)} %collective-permute-done.14.refs_3_), custom_call_target="tpu_custom_call" | custom-call | tf_op jit(solution)/shard_map/pallas_call | solution.py:204
Async XLA Ops:
  1.0 7.4 %collective-permute-start.5 = (bf16[2,32,512]{2,1,0:T(8,128)(2,1)S(1)}, bf16[2,32,512]{2,1,0:T(8,128)(2,1)S(1)}, u32[]{:S(2)}, u32[]{:S(2)}) collective-permute-start(bf16[2,32,512]{2,1,0:T(8,128)(2,1)S(1)} %get-tuple-element.27), channel_id=1, source_target_pairs={{0,2},{1,3},{2,0},{3,1},{4,6},{5,7},{6,4},{7,5},{8,10},{9,11},{10,... | collective-permute-start | bytes 196616 | tf_op jit(solution)/shard_map/ppermute | solution.py:144
  4.1 7.3 %collective-permute-start = (bf16[2,32,512]{2,1,0:T(8,128)(2,1)S(1)}, bf16[2,32,512]{2,1,0:T(8,128)(2,1)S(1)}, u32[]{:S(2)}, u32[]{:S(2)}) collective-permute-start(bf16[2,32,512]{2,1,0:T(8,128)(2,1)S(1)} %get-tuple-element.24), channel_id=1, source_target_pairs={{0,4},{1,5},{2,6},{3,7},{4,0},{5,1},{6,2},{7,3},{8,12},{9,13},{10,... | collective-permute-start | bytes 196616 | tf_op jit(solution)/shard_map/ppermute | solution.py:144
  6.7 6.2 %collective-permute-start.2 = (bf16[2,32,512]{2,1,0:T(8,128)(2,1)S(1)}, bf16[2,32,512]{2,1,0:T(8,128)(2,1)S(1)}, u32[]{:S(2)}, u32[]{:S(2)}) collective-permute-start(bf16[2,32,512]{2,1,0:T(8,128)(2,1)S(1)} %get-tuple-element.25), channel_id=1, source_target_pairs={{0,6},{1,7},{2,4},{3,5},{4,2},{5,3},{6,0},{7,1},{8,14},{9,15},{10,... | collective-permute-start | bytes 196616 | tf_op jit(solution)/shard_map/ppermute | solution.py:144
  6.7 7.6 %collective-permute-start.4 = (bf16[2,32,512]{2,1,0:T(8,128)(2,1)S(1)}, bf16[2,32,512]{2,1,0:T(8,128)(2,1)S(1)}, u32[]{:S(2)}, u32[]{:S(2)}) collective-permute-start(bf16[2,32,512]{2,1,0:T(8,128)(2,1)S(1)} %get-tuple-element.26.refs_0_), channel_id=1, source_target_pairs={{0,1},{1,0},{2,3},{3,2},{4,5},{5,4},{6,7},{7,6},{8,9},{9,8},{10,11... | collective-permute-start | bytes 196616 | tf_op jit(solution)/shard_map/ppermute | solution.py:144
  8.4 5.9 %collective-permute-start.6 = (bf16[2,32,512]{2,1,0:T(8,128)(2,1)S(1)}, bf16[2,32,512]{2,1,0:T(8,128)(2,1)S(1)}, u32[]{:S(2)}, u32[]{:S(2)}) collective-permute-start(bf16[2,32,512]{2,1,0:T(8,128)(2,1)S(1)} %collective-permute-done.5.refs_2_), channel_id=1, source_target_pairs={{0,1},{1,0},{2,3},{3,2},{4,5},{5,4},{6,7},{7,6},{8,9},{9,8},{10,11... | collective-permute-start | bytes 196616 | tf_op jit(solution)/shard_map/ppermute | solution.py:144
  11.4 7.9 %collective-permute-start.1 = (bf16[2,32,512]{2,1,0:T(8,128)(2,1)S(1)}, bf16[2,32,512]{2,1,0:T(8,128)(2,1)S(1)}, u32[]{:S(2)}, u32[]{:S(2)}) collective-permute-start(bf16[2,32,512]{2,1,0:T(8,128)(2,1)S(1)} %collective-permute-done.refs_0_.refs_4_), channel_id=1, source_target_pairs={{0,1},{1,0},{2,3},{3,2},{4,5},{5,4},{6,7},{7,6},{8,9},{9,8},{10,11... | collective-permute-start | bytes 196616 | tf_op jit(solution)/shard_map/ppermute | solution.py:144
  12.9 6.5 %collective-permute-start.3 = (bf16[2,32,512]{2,1,0:T(8,128)(2,1)S(1)}, bf16[2,32,512]{2,1,0:T(8,128)(2,1)S(1)}, u32[]{:S(2)}, u32[]{:S(2)}) collective-permute-start(bf16[2,32,512]{2,1,0:T(8,128)(2,1)S(1)} %collective-permute-done.2.refs_2_.refs_6_), channel_id=1, source_target_pairs={{0,1},{1,0},{2,3},{3,2},{4,5},{5,4},{6,7},{7,6},{8,9},{9,8},{10,11... | collective-permute-start | bytes 196616 | tf_op jit(solution)/shard_map/ppermute | solution.py:144
  14.9 4.5 %collective-permute-start.7 = (bf16[32,512]{1,0:T(8,128)(2,1)S(1)}, bf16[32,512]{1,0:T(8,128)(2,1)S(1)}, u32[]{:S(2)}, u32[]{:S(2)}) collective-permute-start(bf16[32,512]{1,0:T(8,128)(2,1)S(1)} %get-tuple-element.33), channel_id=1, source_target_pairs={{0,2},{1,3},{2,0},{3,1},{4,6},{5,7},{6,4},{7,5},{8,10},{9,11},{10,... | collective-permute-start | bytes 98312 | tf_op jit(solution)/shard_map/ppermute | solution.py:144
  15.0 5.0 %collective-permute-start.8 = (bf16[32,512]{1,0:T(8,128)(2,1)S(1)}, bf16[32,512]{1,0:T(8,128)(2,1)S(1)}, u32[]{:S(2)}, u32[]{:S(2)}) collective-permute-start(bf16[32,512]{1,0:T(8,128)(2,1)S(1)} %get-tuple-element.34), channel_id=1, source_target_pairs={{0,4},{1,5},{2,6},{3,7},{4,0},{5,1},{6,2},{7,3},{8,12},{9,13},{10,... | collective-permute-start | bytes 98312 | tf_op jit(solution)/shard_map/ppermute | solution.py:144
  18.1 5.7 %collective-permute-start.9 = (bf16[32,512]{1,0:T(8,128)(2,1)S(1)}, bf16[32,512]{1,0:T(8,128)(2,1)S(1)}, u32[]{:S(2)}, u32[]{:S(2)}) collective-permute-start(bf16[32,512]{1,0:T(8,128)(2,1)S(1)} %get-tuple-element.35), channel_id=1, source_target_pairs={{0,6},{1,7},{2,4},{3,5},{4,2},{5,3},{6,0},{7,1},{8,14},{9,15},{10,... | collective-permute-start | bytes 98312 | tf_op jit(solution)/shard_map/ppermute | solution.py:144
  19.3 5.1 %collective-permute-start.10 = (bf16[4,2,32,512]{3,2,1,0:T(8,128)(2,1)S(1)}, bf16[4,2,32,512]{3,2,1,0:T(8,128)(2,1)S(1)}, u32[]{:S(2)}, u32[]{:S(2)}) collective-permute-start(bf16[4,2,32,512]{3,2,1,0:T(8,128)(2,1)S(1)} %get-tuple-element.37), channel_id=1, source_target_pairs={{0,8},{8,0},{1,9},{9,1},{2,10},{10,2},{3,11},{11,3},{4,12},{12,4},... | collective-permute-start | bytes 786440 | tf_op jit(solution)/shard_map/ppermute | solution.py:191
  23.8 2.2 %copy-start = (f32[8,2048]{1,0:T(8,128)S(1)}, f32[8,2048]{1,0:T(8,128)}, u32[]{:S(2)}) copy-start(f32[8,2048]{1,0:T(8,128)} %gate_ref.1) | copy-start | bytes 196612
  24.4 1.6 %copy-start.2 = (s32[2,4]{1,0:T(2,128)S(1)}, s32[2,4]{1,0:T(2,128)}, u32[]{:S(2)}) copy-start(s32[2,4]{1,0:T(2,128)} %level_ref.1) | copy-start | bytes 100
  24.4 1.6 %copy-start.1 = (s32[2,4]{1,0:T(2,128)S(1)}, s32[2,4]{1,0:T(2,128)}, u32[]{:S(2)}) copy-start(s32[2,4]{1,0:T(2,128)} %slot_ref.1) | copy-start | bytes 100
  24.4 1.6 %collective-permute-start.11 = (bf16[4,2,32,512]{3,2,1,0:T(8,128)(2,1)S(1)}, bf16[4,2,32,512]{3,2,1,0:T(8,128)(2,1)S(1)}, u32[]{:S(2)}, u32[]{:S(2)}) collective-permute-start(bf16[4,2,32,512]{3,2,1,0:T(8,128)(2,1)S(1)} %get-tuple-element.38), channel_id=1, source_target_pairs={{0,8},{8,0},{1,9},{9,1},{2,10},{10,2},{3,11},{11,3},{4,12},{12,4},... | collective-permute-start | bytes 786440 | tf_op jit(solution)/shard_map/ppermute | solution.py:191
  27.2 4.5 %collective-permute-start.12 = (bf16[32,512]{1,0:T(8,128)(2,1)S(1)}, bf16[32,512]{1,0:T(8,128)(2,1)S(1)}, u32[]{:S(2)}, u32[]{:S(2)}) collective-permute-start(bf16[32,512]{1,0:T(8,128)(2,1)S(1)} %get-tuple-element.40), channel_id=1, source_target_pairs={{0,2},{1,3},{2,0},{3,1},{4,6},{5,7},{6,4},{7,5},{8,10},{9,11},{10,... | collective-permute-start | bytes 98312 | tf_op jit(solution)/shard_map/ppermute | solution.py:144
  27.3 4.9 %collective-permute-start.13 = (bf16[32,512]{1,0:T(8,128)(2,1)S(1)}, bf16[32,512]{1,0:T(8,128)(2,1)S(1)}, u32[]{:S(2)}, u32[]{:S(2)}) collective-permute-start(bf16[32,512]{1,0:T(8,128)(2,1)S(1)} %get-tuple-element.41), channel_id=1, source_target_pairs={{0,4},{1,5},{2,6},{3,7},{4,0},{5,1},{6,2},{7,3},{8,12},{9,13},{10,... | collective-permute-start | bytes 98312 | tf_op jit(solution)/shard_map/ppermute | solution.py:144
  29.1 5.7 %collective-permute-start.14 = (bf16[32,512]{1,0:T(8,128)(2,1)S(1)}, bf16[32,512]{1,0:T(8,128)(2,1)S(1)}, u32[]{:S(2)}, u32[]{:S(2)}) collective-permute-start(bf16[32,512]{1,0:T(8,128)(2,1)S(1)} %get-tuple-element.42), channel_id=1, source_target_pairs={{0,6},{1,7},{2,4},{3,5},{4,2},{5,3},{6,0},{7,1},{8,14},{9,15},{10,... | collective-permute-start | bytes 98312 | tf_op jit(solution)/shard_map/ppermute | solution.py:144

commit v11 on v9

--- a/solution.py
+++ b/solution.py
@@ -11,14 +11,9 @@
 H = 16
 HEAD = 128
 AXES = ("frame", "seq")
-SMEM = pl.BlockSpec(memory_space=pltpu.SMEM)
 HBM = pl.BlockSpec(memory_space=pltpu.HBM)
 VMEM = pl.BlockSpec(memory_space=pltpu.VMEM)
 PARAMS = pltpu.CompilerParams(vmem_limit_bytes=32 * 1024 * 1024)
-
-
-def columns_of(place, width):
-    return pl.ds(pl.multiple_of(place * width, width), width)
 
 
 def run(copies):
@@ -32,27 +27,24 @@
     *operands, out_ref, sems = refs
     run(
         [
-            pltpu.make_async_copy(
-                ref.at[:, columns_of(device, out_ref.shape[-1])],
-                out_ref.at[device, kind],
-                sems.at[device, kind],
-            )
-            for device in range(out_ref.shape[0])
+            pltpu.make_async_copy(ref.at[frame], out_ref.at[:, kind, frame], sems.at[kind, frame])
             for kind, ref in enumerate(operands)
+            for frame in range(ref.shape[0])
         ]
     )
 
 
 def unpack(held_ref, out_ref, sems):
-    devices, _, width = held_ref.shape
     run(
         [
-            pltpu.make_async_copy(
-                held_ref.at[device], out_ref.at[:, columns_of(device, width)], sems.at[device]
-            )
-            for device in range(devices)
+            pltpu.make_async_copy(held_ref.at[:, frame], out_ref.at[frame], sems.at[frame])
+            for frame in range(out_ref.shape[0])
         ]
     )
+
+
+def entry(ref, row, column):
+    return ref[row : row + 1, column : column + 1]
 
 
 def attend(slot_ref, level_ref, gate_ref, packed_ref, out_ref, *, tokens):
@@ -65,11 +57,11 @@
     frame = index // group_rows * local_frames + index // tokens % local_frames
     key_slots = jnp.zeros((1, key_count), jnp.int32)
     for one in range(groups * local_frames):
-        slot = slot_ref[one // local_frames, one % local_frames]
-        key_slots = jnp.where(frame == one, slot, key_slots)
-    gate_blocks = gate_ref[
-        :, columns_of(lax.axis_index("frame") * lax.axis_size("seq") + lax.axis_index("seq"), width)
-    ]
+        key_slots = jnp.where(
+            frame == one, entry(slot_ref, one // local_frames, one % local_frames), key_slots
+        )
+    place = lax.axis_index("frame") * lax.axis_size("seq") + lax.axis_index("seq")
+    gate_blocks = gate_ref[:, pl.ds(pl.multiple_of(place * width, width), width)]
     level_rows = lax.broadcasted_iota(jnp.int32, gate_blocks.shape, 0)
     ones = jnp.ones((key_count, HEAD), jnp.bfloat16)
     scale = math.log2(math.e) / math.sqrt(HEAD)
@@ -77,9 +69,9 @@
     for group in range(groups):
         shown, gate_rows = [], []
         for local in range(local_frames):
-            visible = key_slots <= slot_ref[group, local]
+            visible = key_slots <= entry(slot_ref, group, local)
             shown.append(jnp.where(visible, 0.0, -jnp.inf).reshape(1, 1, 1, key_count))
-            gate = jnp.where(level_rows == level_ref[group, local], gate_blocks, 0.0)
+            gate = jnp.where(level_rows == entry(level_ref, group, local), gate_blocks, 0.0)
             gate_rows.append(jnp.sum(gate, axis=0, keepdims=True))
         shown = jnp.concatenate(shown, axis=1)
         for column in range(0, width, HEAD):
@@ -114,35 +106,40 @@
     exchange = functools.partial(
         lax.all_to_all, axis_name=AXES, split_axis=0, concat_axis=0, tiled=True
     )
+    def by_head(taken):
+        return taken.reshape(local_frames, tokens, devices, width).transpose(0, 2, 1, 3)
+
     packed = pl.pallas_call(
         pack,
-        out_shape=jax.ShapeDtypeStruct((devices, 3, rows, width), queries.dtype),
+        out_shape=jax.ShapeDtypeStruct((devices, 3, local_frames, tokens, width), queries.dtype),
         in_specs=[HBM] * 3,
         out_specs=VMEM,
-        scratch_shapes=[pltpu.SemaphoreType.DMA((devices, 3))],
+        scratch_shapes=[pltpu.SemaphoreType.DMA((3, local_frames))],
         compiler_params=PARAMS,
     )(
         *(
-            pltpu.with_memory_space_constraint(taken.reshape(rows, all_width), pltpu.HBM)
+            pltpu.with_memory_space_constraint(by_head(taken), pltpu.HBM)
             for taken in (queries, keys, values)
         )
     )
+    packed = exchange(packed)
     answer = pl.pallas_call(
         functools.partial(attend, tokens=tokens),
         out_shape=jax.ShapeDtypeStruct((devices, rows, width), queries.dtype),
-        in_specs=[SMEM] * 2 + [VMEM] * 2,
+        in_specs=[VMEM] * 4,
         out_specs=VMEM,
         compiler_params=PARAMS,
-    )(slot_of, level_of, gate_table, exchange(packed))
+    )(slot_of, level_of, gate_table, packed.reshape(devices, 3, rows, width))
+    answer = exchange(answer.reshape(devices, local_frames, tokens, width))
     answer = pl.pallas_call(
         unpack,
-        out_shape=jax.ShapeDtypeStruct((rows, all_width), queries.dtype),
+        out_shape=jax.ShapeDtypeStruct((local_frames, devices, tokens, width), queries.dtype),
         in_specs=[VMEM],
         out_specs=HBM,
-        scratch_shapes=[pltpu.SemaphoreType.DMA((devices,))],
+        scratch_shapes=[pltpu.SemaphoreType.DMA((local_frames,))],
         compiler_params=PARAMS,
-    )(exchange(answer))
-    return answer.reshape(queries.shape)
+    )(answer)
+    return answer.transpose(0, 2, 1, 3).reshape(queries.shape)
 
 
 def shared_heads(queries, keys, values, slot_of, level_of, gate_table):

time: 34.4 us -> 34.1 us (level)
  Pallas kernels: 3.46 us -> 2.47 us
  local copies, waits for them, and re-layouts: 0.02 us -> 0.69 us
    unnamed x6, local copies, waits for them, and re-layouts: 0.02 us -> 0.69 us
    pallas_call x2, Pallas kernels: 2.22 us -> 1.72 us  [the longest x1 1.04 us: whole_heads(): pl.pallas_call(pack, out_shape=jax.ShapeDtypeStruct((devices, 3, local_fr...]
    pallas_call x1, Pallas kernels: 1.23 us -> 0.75 us  [whole_heads(): pl.pallas_call(functools.partial(attend, tokens=tokens), out_shape=jax.Sh...]
where the time goes in v11:
time: 34.1 us; the launch traced here: 33.8 us
  blocking collectives  30.6 us (90%)
  Pallas kernels  2.47 us (7%)
  local copies, waits for them, and re-layouts  0.69 us (2%)
    all_to_all x1, blocking collectives, whole_heads(): packed = exchange(packed)  20.4 us
    all_to_all x1, blocking collectives, whole_heads(): answer = exchange(answer.reshape(devices, local_frames, tokens, width))  10.2 us
    pallas_call x1, Pallas kernels, whole_heads(): pl.pallas_call(pack, out_shape=jax.ShapeDtypeStruct((devices, 3, local_fr...  1.04 us
    pallas_call x1, Pallas kernels, whole_heads(): pl.pallas_call(functools.partial(attend, tokens=tokens), out_shape=jax.Sh...  0.75 us
    unnamed x6, local copies, waits for them, and re-layouts  0.69 us

profile of v11, /device:TPU:0, one launch (start us, length us, event | category | flops | bytes accessed | tf_op | source)
XLA Modules:
  0.0 33.8 jit_solution(10560006832361842603)
XLA Ops:
  0.0 1.0 %shard_map.64 = bf16[16,3,4,8,128]{4,3,2,1,0:T(8,128)(2,1)S(1)} custom-call(bf16[4,16,8,128]{3,2,1,0:T(8,128)(2,1)} %bitcast.16, bf16[4,16,8,128]{3,2,1,0:T(8,128)(2,1)} %bitcast.17, bf16[4,16,8,128]{3,2,1,0:T(8,128)(2,1)} %bitcast.18), custom_call_target="tpu_custom_call" | custom-call | tf_op jit(solution)/shard_map/pallas_call | solution.py:112
  1.0 0.0 copy-start
  1.1 0.0 copy-start.2
  1.1 20.4 %all_to_all.10 = bf16[16,3,4,8,128]{4,3,2,1,0:T(8,128)(2,1)S(1)} all-to-all(bf16[16,3,4,8,128]{4,3,2,1,0:T(8,128)(2,1)S(1)} %shard_map.64), channel_id=1, replica_groups=mesh['rollout'=2,'frame'=2,'seq'=8] {'frame','seq'}, dimensions={0} | all-to-all | bytes 786432 | tf_op jit(solution)/shard_map/all_to_all | solution.py:125
  21.4 0.0 copy-start.1
  21.4 0.0 copy-done
  21.5 0.0 copy-done.2
  21.5 0.7 %copy-done.1 = s32[2,4]{1,0:T(2,128)S(1)} copy-done((s32[2,4]{1,0:T(2,128)S(1)}, s32[2,4]{1,0:T(2,128)}, u32[]{:S(2)}) %copy-start.1) | copy-done | bytes 56
  22.1 0.8 %shard_map.65 = bf16[16,32,128]{2,1,0:T(8,128)(2,1)S(1)} custom-call(s32[2,4]{1,0:T(2,128)S(1)} %copy-done.1, s32[2,4]{1,0:T(2,128)S(1)} %copy-done.2, f32[8,2048]{1,0:T(8,128)S(1)} %copy-done, bf16[16,3,32,128]{3,2,1,0:T(8,128)(2,1)S(1)} %bitcast.14), custom_call_target="tpu_custom_call" | custom-call | tf_op jit(solution)/shard_map/pallas_call | solution.py:126
  22.9 10.2 %all_to_all.11.held_ref = bf16[16,4,8,128]{3,2,1,0:T(8,128)(2,1)S(1)} all-to-all(bf16[16,4,8,128]{3,2,1,0:T(8,128)(2,1)S(1)} %bitcast.15), channel_id=1, replica_groups=mesh['rollout'=2,'frame'=2,'seq'=8] {'frame','seq'}, dimensions={0} | all-to-all | bytes 262144 | tf_op jit(solution)/shard_map/all_to_all | solution.py:133
  33.1 0.7 %shard_map.66 = bf16[4,16,8,128]{3,2,1,0:T(8,128)(2,1)} custom-call(bf16[16,4,8,128]{3,2,1,0:T(8,128)(2,1)S(1)} %all_to_all.11.held_ref), custom_call_target="tpu_custom_call" | custom-call | tf_op jit(solution)/shard_map/pallas_call | solution.py:134
Async XLA Ops:
  1.0 20.4 %copy-start = (f32[8,2048]{1,0:T(8,128)S(1)}, f32[8,2048]{1,0:T(8,128)}, u32[]{:S(2)}) copy-start(f32[8,2048]{1,0:T(8,128)} %gate_ref.1) | copy-start | bytes 196612
  1.1 20.4 %copy-start.2 = (s32[2,4]{1,0:T(2,128)S(1)}, s32[2,4]{1,0:T(2,128)}, u32[]{:S(2)}) copy-start(s32[2,4]{1,0:T(2,128)} %level_ref.1) | copy-start | bytes 100
  21.4 0.7 %copy-start.1 = (s32[2,4]{1,0:T(2,128)S(1)}, s32[2,4]{1,0:T(2,128)}, u32[]{:S(2)}) copy-start(s32[2,4]{1,0:T(2,128)} %slot_ref.1) | copy-start | bytes 100

commit v12 on v11

--- a/solution.py
+++ b/solution.py
@@ -11,6 +11,7 @@
 H = 16
 HEAD = 128
 AXES = ("frame", "seq")
+SPLIT = ("frame", "far")
 HBM = pl.BlockSpec(memory_space=pltpu.HBM)
 VMEM = pl.BlockSpec(memory_space=pltpu.VMEM)
 PARAMS = pltpu.CompilerParams(vmem_limit_bytes=32 * 1024 * 1024)
@@ -24,14 +25,25 @@
 
 
 def pack(*refs):
-    *operands, out_ref, sems = refs
-    run(
-        [
-            pltpu.make_async_copy(ref.at[frame], out_ref.at[:, kind, frame], sems.at[kind, frame])
-            for kind, ref in enumerate(operands)
-            for frame in range(ref.shape[0])
-        ]
-    )
+    key_ref, value_ref, query_ref, slot_ref, level_ref, gate_ref = refs[:6]
+    pair_ref, own_ref, slot_out, level_out, gate_out, sems, table_sems = refs[6:]
+    width = gate_out.shape[-1]
+    place = lax.axis_index("frame") * lax.axis_size("far") + lax.axis_index("far")
+    columns = pl.ds(pl.multiple_of(place * width, width), width)
+    cut = [
+        pltpu.make_async_copy(ref.at[frame], out_ref.at[:, frame], sems.at[kind, frame])
+        for kind, (ref, out_ref) in enumerate(
+            ((key_ref, pair_ref.at[:, 0]), (value_ref, pair_ref.at[:, 1]), (query_ref, own_ref))
+        )
+        for frame in range(ref.shape[0])
+    ]
+    tables = [
+        pltpu.make_async_copy(ref, out_ref, table_sems.at[kind])
+        for kind, (ref, out_ref) in enumerate(
+            ((slot_ref, slot_out), (level_ref, level_out), (gate_ref.at[:, columns], gate_out))
+        )
+    ]
+    run(cut + tables)
 
 
 def unpack(held_ref, out_ref, sems):
@@ -47,24 +59,25 @@
     return ref[row : row + 1, column : column + 1]
 
 
-def attend(slot_ref, level_ref, gate_ref, packed_ref, out_ref, *, tokens):
+def attend(slot_ref, level_ref, gate_ref, query_ref, *refs, tokens):
+    *pair_refs, out_ref = refs
     groups, local_frames = slot_ref.shape
     devices, rows, width = out_ref.shape
-    group_devices = devices // groups
-    group_rows = group_devices * rows
-    key_count = devices * rows
+    group_rows = devices // groups * rows
+    pair_keys = devices * rows
+    key_count = len(pair_refs) * pair_keys
     index = lax.broadcasted_iota(jnp.int32, (1, key_count), 1)
-    frame = index // group_rows * local_frames + index // tokens % local_frames
+    frame = index % pair_keys // group_rows * local_frames + index // tokens % local_frames
     key_slots = jnp.zeros((1, key_count), jnp.int32)
     for one in range(groups * local_frames):
         key_slots = jnp.where(
             frame == one, entry(slot_ref, one // local_frames, one % local_frames), key_slots
         )
-    place = lax.axis_index("frame") * lax.axis_size("seq") + lax.axis_index("seq")
-    gate_blocks = gate_ref[:, pl.ds(pl.multiple_of(place * width, width), width)]
+    gate_blocks = gate_ref[...]
     level_rows = lax.broadcasted_iota(jnp.int32, gate_blocks.shape, 0)
     ones = jnp.ones((key_count, HEAD), jnp.bfloat16)
     scale = math.log2(math.e) / math.sqrt(HEAD)
+    group_devices = devices // groups
     step = max(1, min(group_devices, 128 // rows))
     for group in range(groups):
         shown, gate_rows = [], []
@@ -78,11 +91,13 @@
             part = slice(column, column + HEAD)
             gates = [row[:, part].reshape(1, 1, 1, HEAD) for row in gate_rows]
             gates = jnp.concatenate(gates, axis=1)
-            keys = packed_ref[:, 1, :, part].reshape(key_count, HEAD)
-            values = packed_ref[:, 2, :, part].reshape(key_count, HEAD)
+            keys, values = (
+                jnp.concatenate([ref[:, kind, :, part].reshape(pair_keys, HEAD) for ref in pair_refs])
+                for kind in range(2)
+            )
             values = jnp.concatenate([values, ones], axis=1)
             for start in range(group * group_devices, (group + 1) * group_devices, step):
-                queries = packed_ref[start : start + step, 0, :, part].reshape(step * rows, HEAD)
+                queries = query_ref[start : start + step, :, part].reshape(step * rows, HEAD)
                 scores = lax.dot_general(
                     queries, keys, (((1,), (1,)), ((), ())), preferred_element_type=jnp.float32
                 )
@@ -100,37 +115,51 @@
 
 
 def whole_heads(queries, keys, values, slot_of, level_of, gate_table):
-    devices = lax.axis_size("frame") * lax.axis_size("seq")
+    devices, near = lax.axis_size("frame") * lax.axis_size("far"), lax.axis_size("near")
     _, local_frames, tokens, all_width = queries.shape
     rows, width = local_frames * tokens, all_width // devices
     exchange = functools.partial(
-        lax.all_to_all, axis_name=AXES, split_axis=0, concat_axis=0, tiled=True
-    )
+        lax.all_to_all, axis_name=SPLIT, split_axis=0, concat_axis=0, tiled=True
+    )
+    piece = (local_frames, tokens, width)
+
+    def in_hbm(taken):
+        return pltpu.with_memory_space_constraint(taken, pltpu.HBM)
+
     def by_head(taken):
         return taken.reshape(local_frames, tokens, devices, width).transpose(0, 2, 1, 3)
 
-    packed = pl.pallas_call(
+    pair, own, slots, levels, gates = pl.pallas_call(
         pack,
-        out_shape=jax.ShapeDtypeStruct((devices, 3, local_frames, tokens, width), queries.dtype),
-        in_specs=[HBM] * 3,
-        out_specs=VMEM,
-        scratch_shapes=[pltpu.SemaphoreType.DMA((3, local_frames))],
+        out_shape=[
+            jax.ShapeDtypeStruct((devices, 2, *piece), queries.dtype),
+            jax.ShapeDtypeStruct((devices, *piece), queries.dtype),
+            jax.ShapeDtypeStruct(slot_of.shape, slot_of.dtype),
+            jax.ShapeDtypeStruct(level_of.shape, level_of.dtype),
+            jax.ShapeDtypeStruct((gate_table.shape[0], width), gate_table.dtype),
+        ],
+        in_specs=[HBM] * 6,
+        out_specs=[VMEM] * 5,
+        scratch_shapes=[pltpu.SemaphoreType.DMA((3, local_frames)), pltpu.SemaphoreType.DMA((3,))],
         compiler_params=PARAMS,
     )(
-        *(
-            pltpu.with_memory_space_constraint(by_head(taken), pltpu.HBM)
-            for taken in (queries, keys, values)
-        )
-    )
-    packed = exchange(packed)
+        *(in_hbm(by_head(taken)) for taken in (keys, values, queries)),
+        *(in_hbm(taken) for taken in (slot_of, level_of, gate_table)),
+    )
+    pair = exchange(pair).reshape(devices, 2, rows, width)
+    pairs = [pair] + [
+        lax.ppermute(pair, "near", [(one, (one - away) % near) for one in range(near)])
+        for away in range(1, near)
+    ]
+    own = exchange(own).reshape(devices, rows, width)
     answer = pl.pallas_call(
         functools.partial(attend, tokens=tokens),
         out_shape=jax.ShapeDtypeStruct((devices, rows, width), queries.dtype),
-        in_specs=[VMEM] * 4,
+        in_specs=[VMEM] * (4 + near),
         out_specs=VMEM,
         compiler_params=PARAMS,
-    )(slot_of, level_of, gate_table, packed.reshape(devices, 3, rows, width))
-    answer = exchange(answer.reshape(devices, local_frames, tokens, width))
+    )(slots, levels, gates, own, *pairs)
+    answer = exchange(answer.reshape(devices, *piece))
     answer = pl.pallas_call(
         unpack,
         out_shape=jax.ShapeDtypeStruct((local_frames, devices, tokens, width), queries.dtype),
@@ -184,24 +213,19 @@
     return answer.reshape(H, rows, HEAD).transpose(1, 0, 2).reshape(queries.shape)
 
 
-def body(queries, *others):
-    if lax.axis_size("frame") * lax.axis_size("seq") > H:
-        return shared_heads(queries, *others)
-    return whole_heads(queries, *others)
-
-
 def solution(mesh):
+    sizes = dict(mesh.shape)
+    body, seq = shared_heads, "seq"
+    if sizes["frame"] * sizes["seq"] <= H:
+        near = 2 - sizes["seq"] % 2
+        shape = (sizes["rollout"], sizes["frame"], sizes["seq"] // near, near)
+        mesh = jax.sharding.Mesh(mesh.devices.reshape(shape), ("rollout", "frame", "far", "near"))
+        body, seq = whole_heads, ("far", "near")
+    tokens = P(("rollout", "frame"), None, seq, None)
     return jax.shard_map(
         body,
         mesh=mesh,
-        in_specs=(
-            P(("rollout", "frame"), None, "seq", None),
-            P(("rollout", "frame"), None, "seq", None),
-            P(("rollout", "frame"), None, "seq", None),
-            P("rollout", None),
-            P("rollout", None),
-            P(),
-        ),
-        out_specs=P(("rollout", "frame"), None, "seq", None),
+        in_specs=(tokens, tokens, tokens, P("rollout", None), P("rollout", None), P()),
+        out_specs=tokens,
         check_vma=False,
     )

time: 34.1 us -> 38.5 us (1.13)
  blocking collectives: 30.6 us -> 34.2 us
  starting transfers between devices: 0 us -> 1.49 us
  local copies, waits for them, and re-layouts: 0.69 us -> 0 us
    all_to_all x2 -> x3, blocking collectives: 30.6 us -> 34.2 us  [the longest x1 15.5 us: whole_heads(): pair = exchange(pair).reshape(devices, 2, rows, width)]
    ppermute x0 -> x1, starting transfers between devices: none -> 1.49 us  [whole_heads(): lax.ppermute(pair, 'near', [(one, (one - away) % near) for one in range(n...]
    unnamed x6 -> x0, local copies, waits for them, and re-layouts: 0.69 us -> none
  transfers between devices with their start and end apart: 0 -> 1, of which waited for: 0 -> 0; matrix products, arithmetic and copies ran while one was open for 0% -> 0% of each run, Pallas kernels for 0% -> 0%
where the time goes in v12:
time: 38.5 us; the launch traced here: 38.2 us
  blocking collectives  34.2 us (89%)
  Pallas kernels  2.5 us (6%)
  starting transfers between devices  1.49 us (4%)
    all_to_all x1, blocking collectives, whole_heads(): pair = exchange(pair).reshape(devices, 2, rows, width)  15.5 us
    all_to_all x1, blocking collectives, whole_heads(): answer = exchange(answer.reshape(devices, *piece))  9.34 us
    all_to_all x1, blocking collectives, whole_heads(): own = exchange(own).reshape(devices, rows, width)  9.32 us
    ppermute x1, starting transfers between devices, whole_heads(): lax.ppermute(pair, 'near', [(one, (one - away) % near) for one in range(n...  1.49 us
    pallas_call x1, Pallas kernels, whole_heads(): pl.pallas_call(pack, out_shape=[jax.ShapeDtypeStruct((devices, 2, *piece)...  1.08 us
  transfers between devices with their start and end apart: 1, of which 0 were waited for; matrix products, arithmetic and copies ran while one was open for 0% of the time, Pallas kernels for 0%

profile of v12, /device:TPU:0, one launch (start us, length us, event | category | flops | bytes accessed | tf_op | source)
XLA Modules:
  0.0 38.2 jit_solution(7418865570115587405)
XLA Ops:
  0.0 1.1 %shard_map.64 = (bf16[8,2,4,8,256]{4,3,2,1,0:T(8,128)(2,1)S(1)}, bf16[8,4,8,256]{3,2,1,0:T(8,128)(2,1)S(1)}, s32[2,4]{1,0:T(2,128)S(1)}, s32[2,4]{1,0:T(2,128)S(1)}, f32[8,256]{1,0:T(8,128)S(1)}) custom-call(bf16[4,8,8,256]{3,2,1,0:T(8,128)(2,1)} %bitcast.19, bf16[4,8,8,256]{3,2,1,0:T(8,128)(2,1)} %bitcast.20, bf16[4,8,8,256]{3,2,1,0:T(8,128)(2,1)} %bitcast.21, ...), custom_call_target="tpu_custom_call" | custom-call | tf_op jit(solution)/shard_map/pallas_call | solution.py:132
  1.1 15.5 %all_to_all.15 = bf16[8,2,4,8,256]{4,3,2,1,0:T(8,128)(2,1)S(1)} all-to-all(bf16[8,2,4,8,256]{4,3,2,1,0:T(8,128)(2,1)S(1)} %get-tuple-element.14), channel_id=1, replica_groups=mesh['rollout'=2,'frame'=2,'far'=4,'near'=2] {'frame','far'}, dimensions={0} | all-to-all | bytes 524288 | tf_op jit(solution)/shard_map/all_to_all | solution.py:149
  16.6 1.5 %collective-permute-start = (bf16[8,2,32,256]{3,2,1,0:T(8,128)(2,1)S(1)}, bf16[8,2,32,256]{3,2,1,0:T(8,128)(2,1)S(1)}, u32[]{:S(2)}, u32[]{:S(2)}) collective-permute-start(bf16[8,2,32,256]{3,2,1,0:T(8,128)(2,1)S(1)} %bitcast.15), channel_id=1, source_target_pairs={{0,1},{1,0},{2,3},{3,2},{4,5},{5,4},{6,7},{7,6},{8,9},{9,8},{10,11... | collective-permute-start | bytes 786440 | tf_op jit(solution)/shard_map/ppermute | solution.py:151
  18.1 9.3 %all_to_all.16 = bf16[8,4,8,256]{3,2,1,0:T(8,128)(2,1)S(1)} all-to-all(bf16[8,4,8,256]{3,2,1,0:T(8,128)(2,1)S(1)} %get-tuple-element.13), channel_id=1, replica_groups=mesh['rollout'=2,'frame'=2,'far'=4,'near'=2] {'frame','far'}, dimensions={0} | all-to-all | bytes 262144 | tf_op jit(solution)/shard_map/all_to_all | solution.py:154
  27.4 0.0 collective-permute-done.refs_1_
  27.4 0.7 %shard_map.65 = bf16[8,32,256]{2,1,0:T(8,128)(2,1)S(1)} custom-call(s32[2,4]{1,0:T(2,128)S(1)} %get-tuple-element.10.slot_ref, s32[2,4]{1,0:T(2,128)S(1)} %get-tuple-element.11.level_ref, f32[8,256]{1,0:T(8,128)S(1)} %get-tuple-element.12.gate_ref, bf16[8,32,256]{2,1,0:T(8,128)(2,1)S(1)} %bitcast.17, bf16[8,2,32,256]{3,2,1,0:T(8,128)(2,1)S(1)} %bitcast.16, ...), custom_call_target="tpu_custom_call" | custom-call | tf_op jit(solution)/shard_map/pallas_call | solution.py:155
  28.2 9.3 %all_to_all.17.held_ref = bf16[8,4,8,256]{3,2,1,0:T(8,128)(2,1)S(1)} all-to-all(bf16[8,4,8,256]{3,2,1,0:T(8,128)(2,1)S(1)} %bitcast.18), channel_id=1, replica_groups=mesh['rollout'=2,'frame'=2,'far'=4,'near'=2] {'frame','far'}, dimensions={0} | all-to-all | bytes 262144 | tf_op jit(solution)/shard_map/all_to_all | solution.py:162
  37.5 0.7 %shard_map.66 = bf16[4,8,8,256]{3,2,1,0:T(8,128)(2,1)} custom-call(bf16[8,4,8,256]{3,2,1,0:T(8,128)(2,1)S(1)} %all_to_all.17.held_ref), custom_call_target="tpu_custom_call" | custom-call | tf_op jit(solution)/shard_map/pallas_call | solution.py:163
Async XLA Ops:
  16.6 10.8 %collective-permute-start = (bf16[8,2,32,256]{3,2,1,0:T(8,128)(2,1)S(1)}, bf16[8,2,32,256]{3,2,1,0:T(8,128)(2,1)S(1)}, u32[]{:S(2)}, u32[]{:S(2)}) collective-permute-start(bf16[8,2,32,256]{3,2,1,0:T(8,128)(2,1)S(1)} %bitcast.15), channel_id=1, source_target_pairs={{0,1},{1,0},{2,3},{3,2},{4,5},{5,4},{6,7},{7,6},{8,9},{9,8},{10,11... | collective-permute-start | bytes 786440 | tf_op jit(solution)/shard_map/ppermute | solution.py:151

commit v13 on v11

--- a/solution.py
+++ b/solution.py
@@ -24,12 +24,23 @@
 
 
 def pack(*refs):
-    *operands, out_ref, sems = refs
+    *operands, slot_ref, level_ref, gate_ref = refs[:6]
+    packed_ref, slot_out, level_out, gate_out, sems, table_sems = refs[6:]
+    width = gate_out.shape[-1]
+    place = lax.axis_index("frame") * lax.axis_size("seq") + lax.axis_index("seq")
+    columns = pl.ds(pl.multiple_of(place * width, width), width)
+    tables = ((slot_ref, slot_out), (level_ref, level_out), (gate_ref.at[:, columns], gate_out))
     run(
         [
-            pltpu.make_async_copy(ref.at[frame], out_ref.at[:, kind, frame], sems.at[kind, frame])
+            pltpu.make_async_copy(
+                ref.at[frame], packed_ref.at[:, kind, frame], sems.at[kind, frame]
+            )
             for kind, ref in enumerate(operands)
             for frame in range(ref.shape[0])
+        ]
+        + [
+            pltpu.make_async_copy(ref, out_ref, table_sems.at[kind])
+            for kind, (ref, out_ref) in enumerate(tables)
         ]
     )
 
@@ -60,8 +71,7 @@
         key_slots = jnp.where(
             frame == one, entry(slot_ref, one // local_frames, one % local_frames), key_slots
         )
-    place = lax.axis_index("frame") * lax.axis_size("seq") + lax.axis_index("seq")
-    gate_blocks = gate_ref[:, pl.ds(pl.multiple_of(place * width, width), width)]
+    gate_blocks = gate_ref[...]
     level_rows = lax.broadcasted_iota(jnp.int32, gate_blocks.shape, 0)
     ones = jnp.ones((key_count, HEAD), jnp.bfloat16)
     scale = math.log2(math.e) / math.sqrt(HEAD)
@@ -103,34 +113,42 @@
     devices = lax.axis_size("frame") * lax.axis_size("seq")
     _, local_frames, tokens, all_width = queries.shape
     rows, width = local_frames * tokens, all_width // devices
+    piece = (local_frames, tokens, width)
     exchange = functools.partial(
         lax.all_to_all, axis_name=AXES, split_axis=0, concat_axis=0, tiled=True
     )
+
+    def in_hbm(taken):
+        return pltpu.with_memory_space_constraint(taken, pltpu.HBM)
+
     def by_head(taken):
         return taken.reshape(local_frames, tokens, devices, width).transpose(0, 2, 1, 3)
 
-    packed = pl.pallas_call(
+    packed, slots, levels, gates = pl.pallas_call(
         pack,
-        out_shape=jax.ShapeDtypeStruct((devices, 3, local_frames, tokens, width), queries.dtype),
-        in_specs=[HBM] * 3,
-        out_specs=VMEM,
-        scratch_shapes=[pltpu.SemaphoreType.DMA((3, local_frames))],
+        out_shape=[
+            jax.ShapeDtypeStruct((devices, 3, *piece), queries.dtype),
+            jax.ShapeDtypeStruct(slot_of.shape, slot_of.dtype),
+            jax.ShapeDtypeStruct(level_of.shape, level_of.dtype),
+            jax.ShapeDtypeStruct((gate_table.shape[0], width), gate_table.dtype),
+        ],
+        in_specs=[HBM] * 6,
+        out_specs=[VMEM] * 4,
+        scratch_shapes=[pltpu.SemaphoreType.DMA((3, local_frames)), pltpu.SemaphoreType.DMA((3,))],
         compiler_params=PARAMS,
     )(
-        *(
-            pltpu.with_memory_space_constraint(by_head(taken), pltpu.HBM)
-            for taken in (queries, keys, values)
-        )
-    )
-    packed = exchange(packed)
+        *(in_hbm(by_head(taken)) for taken in (queries, keys, values)),
+        *(in_hbm(taken) for taken in (slot_of, level_of, gate_table)),
+    )
+    packed = exchange(packed).reshape(devices, 3, rows, width)
     answer = pl.pallas_call(
         functools.partial(attend, tokens=tokens),
         out_shape=jax.ShapeDtypeStruct((devices, rows, width), queries.dtype),
         in_specs=[VMEM] * 4,
         out_specs=VMEM,
         compiler_params=PARAMS,
-    )(slot_of, level_of, gate_table, packed.reshape(devices, 3, rows, width))
-    answer = exchange(answer.reshape(devices, local_frames, tokens, width))
+    )(slots, levels, gates, packed)
+    answer = exchange(answer.reshape(devices, *piece))
     answer = pl.pallas_call(
         unpack,
         out_shape=jax.ShapeDtypeStruct((local_frames, devices, tokens, width), queries.dtype),
@@ -184,24 +202,12 @@
     return answer.reshape(H, rows, HEAD).transpose(1, 0, 2).reshape(queries.shape)
 
 
-def body(queries, *others):
-    if lax.axis_size("frame") * lax.axis_size("seq") > H:
-        return shared_heads(queries, *others)
-    return whole_heads(queries, *others)
-
-
 def solution(mesh):
+    tokens = P(("rollout", "frame"), None, "seq", None)
     return jax.shard_map(
-        body,
+        whole_heads if mesh.shape["frame"] * mesh.shape["seq"] <= H else shared_heads,
         mesh=mesh,
-        in_specs=(
-            P(("rollout", "frame"), None, "seq", None),
-            P(("rollout", "frame"), None, "seq", None),
-            P(("rollout", "frame"), None, "seq", None),
-            P("rollout", None),
-            P("rollout", None),
-            P(),
-        ),
-        out_specs=P(("rollout", "frame"), None, "seq", None),
+        in_specs=(tokens, tokens, tokens, P("rollout", None), P("rollout", None), P()),
+        out_specs=tokens,
         check_vma=False,
     )

time: 34.1 us -> 33.3 us (0.977)
  local copies, waits for them, and re-layouts: 0.69 us -> 0 us
    unnamed x6 -> x0, local copies, waits for them, and re-layouts: 0.69 us -> none
where the time goes in v13:
time: 33.3 us; the launch traced here: 33 us
  blocking collectives  30.5 us (92%)
  Pallas kernels  2.51 us (8%)
    all_to_all x1, blocking collectives, whole_heads(): packed = exchange(packed).reshape(devices, 3, rows, width)  20.2 us
    all_to_all x1, blocking collectives, whole_heads(): answer = exchange(answer.reshape(devices, *piece))  10.2 us
    pallas_call x1, Pallas kernels, whole_heads(): pl.pallas_call(pack, out_shape=[jax.ShapeDtypeStruct((devices, 3, *piece)...  1.08 us
    pallas_call x1, Pallas kernels, whole_heads(): pl.pallas_call(functools.partial(attend, tokens=tokens), out_shape=jax.Sh...  0.75 us
    pallas_call x1, Pallas kernels, whole_heads(): pl.pallas_call(unpack, out_shape=jax.ShapeDtypeStruct((local_frames, devi...  0.68 us

profile of v13, /device:TPU:0, one launch (start us, length us, event | category | flops | bytes accessed | tf_op | source)
XLA Modules:
  0.0 33.0 jit_solution(10302832838307736757)
XLA Ops:
  0.0 1.1 %shard_map.64 = (bf16[16,3,4,8,128]{4,3,2,1,0:T(8,128)(2,1)S(1)}, s32[2,4]{1,0:T(2,128)S(1)}, s32[2,4]{1,0:T(2,128)S(1)}, f32[8,128]{1,0:T(8,128)S(1)}) custom-call(bf16[4,16,8,128]{3,2,1,0:T(8,128)(2,1)} %bitcast.16, bf16[4,16,8,128]{3,2,1,0:T(8,128)(2,1)} %bitcast.17, bf16[4,16,8,128]{3,2,1,0:T(8,128)(2,1)} %bitcast.18, s32[2,4]{1,0:T(2,128)} %refs_3_.1, ...), custom_call_target="tpu_custom_call" | custom-call | tf_op jit(solution)/shard_map/pallas_call | solution.py:127
  1.1 20.2 %all_to_all.10 = bf16[16,3,4,8,128]{4,3,2,1,0:T(8,128)(2,1)S(1)} all-to-all(bf16[16,3,4,8,128]{4,3,2,1,0:T(8,128)(2,1)S(1)} %get-tuple-element.12), channel_id=1, replica_groups=mesh['rollout'=2,'frame'=2,'seq'=8] {'frame','seq'}, dimensions={0} | all-to-all | bytes 786432 | tf_op jit(solution)/shard_map/all_to_all | solution.py:143
  21.3 0.7 %shard_map.65 = bf16[16,32,128]{2,1,0:T(8,128)(2,1)S(1)} custom-call(s32[2,4]{1,0:T(2,128)S(1)} %get-tuple-element.9.slot_ref, s32[2,4]{1,0:T(2,128)S(1)} %get-tuple-element.10.level_ref, f32[8,128]{1,0:T(8,128)S(1)} %get-tuple-element.11.gate_ref, bf16[16,3,32,128]{3,2,1,0:T(8,128)(2,1)S(1)} %bitcast.14), custom_call_target="tpu_custom_call" | custom-call | tf_op jit(solution)/shard_map/pallas_call | solution.py:144
  22.1 10.2 %all_to_all.11.held_ref = bf16[16,4,8,128]{3,2,1,0:T(8,128)(2,1)S(1)} all-to-all(bf16[16,4,8,128]{3,2,1,0:T(8,128)(2,1)S(1)} %bitcast.15), channel_id=1, replica_groups=mesh['rollout'=2,'frame'=2,'seq'=8] {'frame','seq'}, dimensions={0} | all-to-all | bytes 262144 | tf_op jit(solution)/shard_map/all_to_all | solution.py:151
  32.3 0.7 %shard_map.66 = bf16[4,16,8,128]{3,2,1,0:T(8,128)(2,1)} custom-call(bf16[16,4,8,128]{3,2,1,0:T(8,128)(2,1)S(1)} %all_to_all.11.held_ref), custom_call_target="tpu_custom_call" | custom-call | tf_op jit(solution)/shard_map/pallas_call | solution.py:152

commit v14 on v13

--- a/solution.py
+++ b/solution.py
@@ -10,7 +10,7 @@
 
 H = 16
 HEAD = 128
-AXES = ("frame", "seq")
+AXES = ("seq", "frame")
 HBM = pl.BlockSpec(memory_space=pltpu.HBM)
 VMEM = pl.BlockSpec(memory_space=pltpu.VMEM)
 PARAMS = pltpu.CompilerParams(vmem_limit_bytes=32 * 1024 * 1024)
@@ -27,7 +27,7 @@
     *operands, slot_ref, level_ref, gate_ref = refs[:6]
     packed_ref, slot_out, level_out, gate_out, sems, table_sems = refs[6:]
     width = gate_out.shape[-1]
-    place = lax.axis_index("frame") * lax.axis_size("seq") + lax.axis_index("seq")
+    place = lax.axis_index("seq") * lax.axis_size("frame") + lax.axis_index("frame")
     columns = pl.ds(pl.multiple_of(place * width, width), width)
     tables = ((slot_ref, slot_out), (level_ref, level_out), (gate_ref.at[:, columns], gate_out))
     run(
@@ -59,13 +59,11 @@
 
 
 def attend(slot_ref, level_ref, gate_ref, packed_ref, out_ref, *, tokens):
-    groups, local_frames = slot_ref.shape
-    devices, rows, width = out_ref.shape
-    group_devices = devices // groups
-    group_rows = group_devices * rows
-    key_count = devices * rows
+    local_frames = slot_ref.shape[1]
+    places, groups, rows, width = out_ref.shape
+    key_count = places * groups * rows
     index = lax.broadcasted_iota(jnp.int32, (1, key_count), 1)
-    frame = index // group_rows * local_frames + index // tokens % local_frames
+    frame = index // tokens % (groups * local_frames)
     key_slots = jnp.zeros((1, key_count), jnp.int32)
     for one in range(groups * local_frames):
         key_slots = jnp.where(
@@ -75,7 +73,7 @@
     level_rows = lax.broadcasted_iota(jnp.int32, gate_blocks.shape, 0)
     ones = jnp.ones((key_count, HEAD), jnp.bfloat16)
     scale = math.log2(math.e) / math.sqrt(HEAD)
-    step = max(1, min(group_devices, 128 // rows))
+    step = max(1, min(places, 128 // rows))
     for group in range(groups):
         shown, gate_rows = [], []
         for local in range(local_frames):
@@ -88,11 +86,12 @@
             part = slice(column, column + HEAD)
             gates = [row[:, part].reshape(1, 1, 1, HEAD) for row in gate_rows]
             gates = jnp.concatenate(gates, axis=1)
-            keys = packed_ref[:, 1, :, part].reshape(key_count, HEAD)
-            values = packed_ref[:, 2, :, part].reshape(key_count, HEAD)
+            keys = packed_ref[:, :, 1, :, part].reshape(key_count, HEAD)
+            values = packed_ref[:, :, 2, :, part].reshape(key_count, HEAD)
             values = jnp.concatenate([values, ones], axis=1)
-            for start in range(group * group_devices, (group + 1) * group_devices, step):
-                queries = packed_ref[start : start + step, 0, :, part].reshape(step * rows, HEAD)
+            for start in range(0, places, step):
+                queries = packed_ref[start : start + step, group, 0, :, part]
+                queries = queries.reshape(step * rows, HEAD)
                 scores = lax.dot_general(
                     queries, keys, (((1,), (1,)), ((), ())), preferred_element_type=jnp.float32
                 )
@@ -104,9 +103,9 @@
                 )
                 mixed = mixed[:, :HEAD] / mixed[:, HEAD:]
                 mixed = mixed.reshape(step, local_frames, tokens, HEAD) * gates
-                out_ref[start : start + step, :, part] = mixed.reshape(step, rows, HEAD).astype(
-                    out_ref.dtype
-                )
+                out_ref[start : start + step, group, :, part] = mixed.reshape(
+                    step, rows, HEAD
+                ).astype(out_ref.dtype)
 
 
 def whole_heads(queries, keys, values, slot_of, level_of, gate_table):
@@ -140,10 +139,11 @@
         *(in_hbm(by_head(taken)) for taken in (queries, keys, values)),
         *(in_hbm(taken) for taken in (slot_of, level_of, gate_table)),
     )
-    packed = exchange(packed).reshape(devices, 3, rows, width)
+    places = (lax.axis_size("seq"), lax.axis_size("frame"))
+    packed = exchange(packed).reshape(*places, 3, rows, width)
     answer = pl.pallas_call(
         functools.partial(attend, tokens=tokens),
-        out_shape=jax.ShapeDtypeStruct((devices, rows, width), queries.dtype),
+        out_shape=jax.ShapeDtypeStruct((*places, rows, width), queries.dtype),
         in_specs=[VMEM] * 4,
         out_specs=VMEM,
         compiler_params=PARAMS,

time: 33.3 us -> 33.4 us (level)
    all_to_all x1, blocking collectives: 10.2 us -> 11.3 us  [whole_heads(): answer = exchange(answer.reshape(devices, *piece))]
    all_to_all x1, blocking collectives: 20.2 us -> 19.4 us  [whole_heads(): packed = exchange(packed).reshape(*places, 3, rows, width)]
where the time goes in v14:
time: 33.4 us; the launch traced here: 33.1 us
  blocking collectives  30.6 us (92%)
  Pallas kernels  2.51 us (8%)
    all_to_all x1, blocking collectives, whole_heads(): packed = exchange(packed).reshape(*places, 3, rows, width)  19.4 us
    all_to_all x1, blocking collectives, whole_heads(): answer = exchange(answer.reshape(devices, *piece))  11.3 us
    pallas_call x1, Pallas kernels, whole_heads(): pl.pallas_call(pack, out_shape=[jax.ShapeDtypeStruct((devices, 3, *piece)...  1.08 us
    pallas_call x1, Pallas kernels, whole_heads(): pl.pallas_call(functools.partial(attend, tokens=tokens), out_shape=jax.Sh...  0.75 us
    pallas_call x1, Pallas kernels, whole_heads(): pl.pallas_call(unpack, out_shape=jax.ShapeDtypeStruct((local_frames, devi...  0.68 us

profile of v14, /device:TPU:0, one launch (start us, length us, event | category | flops | bytes accessed | tf_op | source)
XLA Modules:
  0.0 33.1 jit_solution(251816419680995255)
XLA Ops:
  0.0 1.1 %shard_map.64 = (bf16[16,3,4,8,128]{4,3,2,1,0:T(8,128)(2,1)S(1)}, s32[2,4]{1,0:T(2,128)S(1)}, s32[2,4]{1,0:T(2,128)S(1)}, f32[8,128]{1,0:T(8,128)S(1)}) custom-call(bf16[4,16,8,128]{3,2,1,0:T(8,128)(2,1)} %bitcast.16, bf16[4,16,8,128]{3,2,1,0:T(8,128)(2,1)} %bitcast.17, bf16[4,16,8,128]{3,2,1,0:T(8,128)(2,1)} %bitcast.18, s32[2,4]{1,0:T(2,128)} %refs_3_.1, ...), custom_call_target="tpu_custom_call" | custom-call | tf_op jit(solution)/shard_map/pallas_call | solution.py:126
  1.1 19.4 %all_to_all.10 = bf16[16,3,4,8,128]{4,3,2,1,0:T(8,128)(2,1)S(1)} all-to-all(bf16[16,3,4,8,128]{4,3,2,1,0:T(8,128)(2,1)S(1)} %get-tuple-element.12), channel_id=1, replica_groups=mesh['rollout'=2,'frame'=2,'seq'=8] {'seq','frame'}, dimensions={0} | all-to-all | bytes 786432 | tf_op jit(solution)/shard_map/all_to_all | solution.py:143
  20.4 0.8 %shard_map.65 = bf16[8,2,32,128]{3,2,1,0:T(8,128)(2,1)S(1)} custom-call(s32[2,4]{1,0:T(2,128)S(1)} %get-tuple-element.9.slot_ref, s32[2,4]{1,0:T(2,128)S(1)} %get-tuple-element.10.level_ref, f32[8,128]{1,0:T(8,128)S(1)} %get-tuple-element.11.gate_ref, bf16[8,2,3,32,128]{4,3,2,1,0:T(8,128)(2,1)S(1)} %bitcast.14), custom_call_target="tpu_custom_call" | custom-call | tf_op jit(solution)/shard_map/pallas_call | solution.py:144
  21.2 11.3 %all_to_all.11.held_ref = bf16[16,4,8,128]{3,2,1,0:T(8,128)(2,1)S(1)} all-to-all(bf16[16,4,8,128]{3,2,1,0:T(8,128)(2,1)S(1)} %bitcast.15), channel_id=1, replica_groups=mesh['rollout'=2,'frame'=2,'seq'=8] {'seq','frame'}, dimensions={0} | all-to-all | bytes 262144 | tf_op jit(solution)/shard_map/all_to_all | solution.py:151
  32.5 0.7 %shard_map.66 = bf16[4,16,8,128]{3,2,1,0:T(8,128)(2,1)} custom-call(bf16[16,4,8,128]{3,2,1,0:T(8,128)(2,1)S(1)} %all_to_all.11.held_ref), custom_call_target="tpu_custom_call" | custom-call | tf_op jit(solution)/shard_map/pallas_call | solution.py:152

commit v15 on v13

v15 whole, which is shorter than its diff:
```python
import functools
import math

import jax
import jax.numpy as jnp
from jax import lax
from jax.experimental import pallas as pl
from jax.experimental.pallas import tpu as pltpu
from jax.sharding import PartitionSpec as P

H = 16
HEAD = 128
AXES = ("frame", "seq")
HBM = pl.BlockSpec(memory_space=pltpu.HBM)
VMEM = pl.BlockSpec(memory_space=pltpu.VMEM)
PARAMS = pltpu.CompilerParams(vmem_limit_bytes=32 * 1024 * 1024)


def far_first(devices):
    return sorted(range(devices), key=lambda away: (-(2 * away // devices), away % 2, -away))


def run(copies):
    for copy in copies:
        copy.start()
    for copy in copies:
        copy.wait()


def pack(*refs):
    *operands, slot_ref, level_ref, gate_ref = refs[:6]
    *outs, slot_out, level_out, gate_out, sems, table_sems = refs[6:]
    width = gate_out.shape[-1]
    place = lax.axis_index("seq")

    def columns(place):
        return pl.ds(pl.multiple_of(place * width, width), width)

    tables = (
        (slot_ref, slot_out),
        (level_ref, level_out),
        (gate_ref.at[:, columns(place)], gate_out),
    )
    run(
        [
            pltpu.make_async_copy(
                ref.at[:, columns(place ^ away)], out_ref.at[kind], sems.at[away, kind]
            )
            for away, out_ref in zip(far_first(len(outs)), outs)
            for kind, ref in enumerate(operands)
        ]
        + [
            pltpu.make_async_copy(ref, out_ref, table_sems.at[kind])
            for kind, (ref, out_ref) in enumerate(tables)
        ]
    )


def stack(*refs):
    *pieces, out_ref, sems = refs
    run(
        [
            pltpu.make_async_copy(ref.at[pl.ds(1, 2)], out_ref.at[number], sems.at[number])
            for number, ref in enumerate(pieces)
        ]
    )


def unpack(held_ref, out_ref, sems):
    run(
        [
            pltpu.make_async_copy(held_ref.at[:, frame], out_ref.at[frame], sems.at[frame])
            for frame in range(out_ref.shape[0])
        ]
    )


def entry(ref, row, column):
    return ref[row : row + 1, column : column + 1]


def attend(slot_ref, level_ref, gate_ref, *refs, tokens):
    out_ref = refs[-1]
    devices, rows, width = out_ref.shape
    own_refs, pair_refs = refs[:devices], refs[devices:-1]
    groups, local_frames = slot_ref.shape
    group_keys = devices * rows
    key_count = groups * group_keys
    group = lax.axis_index("frame")
    index = lax.broadcasted_iota(jnp.int32, (1, key_count), 1)
    frame = (index // group_keys + group) % groups * local_frames + index // tokens % local_frames
    key_slots = jnp.zeros((1, key_count), jnp.int32)
    for one in range(groups * local_frames):
        key_slots = jnp.where(
            frame == one, entry(slot_ref, one // local_frames, one % local_frames), key_slots
        )
    gate_blocks = gate_ref[...]
    level_rows = lax.broadcasted_iota(jnp.int32, gate_blocks.shape, 0)
    shown, gate_rows = [], []
    for local in range(local_frames):
        slot, level = entry(slot_ref, 0, local), entry(level_ref, 0, local)
        for other in range(1, groups):
            slot = jnp.where(group == other, entry(slot_ref, other, local), slot)
            level = jnp.where(group == other, entry(level_ref, other, local), level)
        shown.append(jnp.where(key_slots <= slot, 0.0, -jnp.inf).reshape(1, 1, 1, key_count))
        gate = jnp.where(level_rows == level, gate_blocks, 0.0)
        gate_rows.append(jnp.sum(gate, axis=0, keepdims=True))
    shown = jnp.concatenate(shown, axis=1)
    ones = jnp.ones((key_count, HEAD), jnp.bfloat16)
    scale = math.log2(math.e) / math.sqrt(HEAD)
    step = max(1, min(devices, 128 // rows))
    for column in range(0, width, HEAD):
        part = slice(column, column + HEAD)
        gates = [row[:, part].reshape(1, 1, 1, HEAD) for row in gate_rows]
        gates = jnp.concatenate(gates, axis=1)
        keys, values = (
            jnp.concatenate(
                [ref[1 + kind, :, part] for ref in own_refs]
                + [ref[:, kind, :, part].reshape(ref.shape[0] * rows, HEAD) for ref in pair_refs]
            )
            for kind in range(2)
        )
        values = jnp.concatenate([values, ones], axis=1)
        for start in range(0, devices, step):
            queries = jnp.concatenate([ref[0, :, part] for ref in own_refs[start : start + step]])
            scores = lax.dot_general(
                queries, keys, (((1,), (1,)), ((), ())), preferred_element_type=jnp.float32
            )
            scores = scores.reshape(step, local_frames, tokens, key_count) * scale + shown
            scores = scores.reshape(step * rows, key_count)
            weights = jnp.exp2(scores - jnp.max(scores, axis=1, keepdims=True))
            mixed = jnp.dot(
                weights.astype(jnp.bfloat16), values, preferred_element_type=jnp.float32
            )
            mixed = mixed[:, :HEAD] / mixed[:, HEAD:]
            mixed = mixed.reshape(step, local_frames, tokens, HEAD) * gates
            mixed = mixed.reshape(step, rows, HEAD).astype(out_ref.dtype)
            for number, away in enumerate(far_first(devices)[start : start + step]):
                out_ref[lax.axis_index("seq") ^ away, :, part] = mixed[number]


def whole_heads(queries, keys, values, slot_of, level_of, gate_table):
    devices, groups = lax.axis_size("seq"), lax.axis_size("frame")
    _, local_frames, tokens, all_width = queries.shape
    rows, width = local_frames * tokens, all_width // devices
    half = max(1, devices // 2)

    def in_hbm(taken):
        return pltpu.with_memory_space_constraint(taken, pltpu.HBM)

    *pieces, slots, levels, gates = pl.pallas_call(
        pack,
        out_shape=[jax.ShapeDtypeStruct((3, rows, width), queries.dtype)] * devices
        + [
            jax.ShapeDtypeStruct(slot_of.shape, slot_of.dtype),
            jax.ShapeDtypeStruct(level_of.shape, level_of.dtype),
            jax.ShapeDtypeStruct((gate_table.shape[0], width), gate_table.dtype),
        ],
        in_specs=[HBM] * 6,
        out_specs=[VMEM] * (devices + 3),
        scratch_shapes=[pltpu.SemaphoreType.DMA((devices, 3)), pltpu.SemaphoreType.DMA((3,))],
        compiler_params=PARAMS,
    )(
        *(in_hbm(taken.reshape(rows, all_width)) for taken in (queries, keys, values)),
        *(in_hbm(taken) for taken in (slot_of, level_of, gate_table)),
    )
    pieces = [
        lax.ppermute(piece, "seq", [(one, one ^ away) for one in range(devices)])
        if away
        else piece
        for away, piece in zip(far_first(devices), pieces)
    ]

    def stacked(taken):
        return pl.pallas_call(
            stack,
            out_shape=jax.ShapeDtypeStruct((len(taken), 2, rows, width), queries.dtype),
            in_specs=[VMEM] * len(taken),
            out_specs=VMEM,
            scratch_shapes=[pltpu.SemaphoreType.DMA((len(taken),))],
            compiler_params=PARAMS,
        )(*taken)

    stacks = [stacked(taken) for taken in (pieces[half:], pieces[:half]) if taken]
    stacks = [
        lax.ppermute(taken, "frame", [(one, (one - away) % groups) for one in range(groups)])
        for away in range(1, groups)
        for taken in stacks
    ]
    answer = pl.pallas_call(
        functools.partial(attend, tokens=tokens),
        out_shape=jax.ShapeDtypeStruct((devices, rows, width), queries.dtype),
        in_specs=[VMEM] * (3 + devices + len(stacks)),
        out_specs=VMEM,
        compiler_params=PARAMS,
    )(slots, levels, gates, *pieces, *stacks)
    answer = answer.reshape(devices, local_frames, tokens, width)
    answer = lax.all_to_all(answer, "seq", split_axis=0, concat_axis=0, tiled=True)
    answer = pl.pallas_call(
        unpack,
        out_shape=jax.ShapeDtypeStruct((local_frames, devices, tokens, width), queries.dtype),
        in_specs=[VMEM],
        out_specs=HBM,
        scratch_shapes=[pltpu.SemaphoreType.DMA((local_frames,))],
        compiler_params=PARAMS,
    )(answer)
    return answer.transpose(0, 2, 1, 3).reshape(queries.shape)


def shared_heads(queries, keys, values, slot_of, level_of, gate_table):
    devices = lax.axis_size("frame") * lax.axis_size("seq")
    _, local_frames, tokens, _ = queries.shape
    rows, blocks = local_frames * tokens, devices // H
    block_rows = rows // blocks
    exchange = functools.partial(
        lax.all_to_all, axis_name=AXES, split_axis=0, concat_axis=0, tiled=True
    )

    def by_head(taken):
        return taken.reshape(rows, H, HEAD).transpose(1, 0, 2)

    def key_pieces(taken):
        pieces = jnp.broadcast_to(by_head(taken)[:, None], (H, blocks, rows, HEAD))
        return exchange(pieces.reshape(devices, rows, HEAD)).reshape(devices * rows, HEAD)

    key_rows, value_rows = key_pieces(keys), key_pieces(values)
    query_rows = exchange(by_head(queries).reshape(devices, block_rows, HEAD))
    query_rows = query_rows.reshape(devices * block_rows, HEAD)
    device_index = lax.axis_index("frame") * lax.axis_size("seq") + lax.axis_index("seq")
    head, block = device_index // blocks, device_index % blocks

    def per_row(table):
        table = jnp.repeat(table, tokens, axis=1)[:, None]
        return jnp.broadcast_to(table, (table.shape[0], lax.axis_size("seq"), rows))

    row_slots, row_levels = per_row(slot_of), per_row(level_of)
    query_slots = lax.dynamic_slice_in_dim(row_slots, block * block_rows, block_rows, 2)
    levels = lax.dynamic_slice_in_dim(row_levels, block * block_rows, block_rows, 2).reshape(-1)
    scores = lax.dot_general(
        query_rows, key_rows, (((1,), (1,)), ((), ())), preferred_element_type=jnp.float32
    )
    visible = row_slots.reshape(1, -1) <= query_slots.reshape(-1, 1)
    scores = jnp.where(visible, scores * (1.0 / math.sqrt(HEAD)), -jnp.inf)
    weights = jnp.exp(scores - jnp.max(scores, axis=1, keepdims=True)).astype(jnp.bfloat16)
    total = jnp.sum(weights.astype(jnp.float32), axis=1, keepdims=True)
    mixed = jnp.dot(weights, value_rows, preferred_element_type=jnp.float32) / total
    gates = lax.dynamic_slice_in_dim(gate_table, head * HEAD, HEAD, 1)[levels]
    answer = exchange((mixed * gates).astype(queries.dtype).reshape(devices, block_rows, HEAD))
    return answer.reshape(H, rows, HEAD).transpose(1, 0, 2).reshape(queries.shape)


def solution(mesh):
    seq = mesh.shape["seq"]
    tokens = P(("rollout", "frame"), None, "seq", None)
    return jax.shard_map(
        whole_heads if seq <= H and seq & (seq - 1) == 0 else shared_heads,
        mesh=mesh,
        in_specs=(tokens, tokens, tokens, P("rollout", None), P("rollout", None), P()),
        out_specs=tokens,
        check_vma=False,
    )
```

time: 33.3 us -> 32.7 us (0.982)
  blocking collectives: 30.5 us -> 12.4 us
  starting transfers between devices: 0 us -> 13 us
  waiting for transfers between devices: 0 us -> 4.13 us
  Pallas kernels: 2.51 us -> 2.93 us
    all_to_all x2 -> x1, blocking collectives: 30.5 us -> 12.4 us  [whole_heads(): lax.all_to_all(answer, 'seq', split_axis=0, concat_axis=0, tiled=True)]
    ppermute x0 -> x9, starting transfers between devices: none -> 13 us  [the longest x7 12.8 us: whole_heads(): lax.ppermute(piece, 'seq', [(one, one ^ away) for one in range(devices)])]
    ppermute x0 -> x9, waiting for transfers between devices: none -> 4.13 us  [the longest x7 2.81 us: whole_heads(): lax.ppermute(piece, 'seq', [(one, one ^ away) for one in range(devices)])]
    pallas_call x1 -> x3, Pallas kernels: 1.08 us -> 1.56 us  [the longest x1 1.2 us: whole_heads(): pl.pallas_call(pack, out_shape=[jax.ShapeDtypeStruct((3, rows, width), qu...]
  transfers between devices with their start and end apart: 0 -> 9, of which waited for: 0 -> 4; matrix products, arithmetic and copies ran while one was open for 0% -> 0% of each run, Pallas kernels for 0% -> 1%
where the time goes in v15:
time: 32.7 us; the launch traced here: 32.5 us
  starting transfers between devices  13 us (40%)
  blocking collectives  12.4 us (38%)
  waiting for transfers between devices  4.13 us (13%)
  Pallas kernels  2.93 us (9%)
    ppermute x7, starting transfers between devices, whole_heads(): lax.ppermute(piece, 'seq', [(one, one ^ away) for one in range(devices)])  12.8 us
    all_to_all x1, blocking collectives, whole_heads(): lax.all_to_all(answer, 'seq', split_axis=0, concat_axis=0, tiled=True)  12.4 us
    ppermute x7, waiting for transfers between devices, whole_heads(): lax.ppermute(piece, 'seq', [(one, one ^ away) for one in range(devices)])  2.81 us
    ppermute x2, waiting for transfers between devices, whole_heads(): lax.ppermute(taken, 'frame', [(one, (one - away) % groups) for one in ran...  1.33 us
    pallas_call x1, Pallas kernels, whole_heads(): pl.pallas_call(pack, out_shape=[jax.ShapeDtypeStruct((3, rows, width), qu...  1.2 us
    pallas_call x1, Pallas kernels, whole_heads(): pl.pallas_call(functools.partial(attend, tokens=tokens), out_shape=jax.Sh...  0.69 us
    pallas_call x1, Pallas kernels, whole_heads(): pl.pallas_call(unpack, out_shape=jax.ShapeDtypeStruct((local_frames, devi...  0.68 us
  transfers between devices with their start and end apart: 9, of which 4 were waited for; matrix products, arithmetic and copies ran while one was open for 0% of the time, Pallas kernels for 1%

profile of v15, /device:TPU:0, one launch (start us, length us, event | category | flops | bytes accessed | tf_op | source)
XLA Modules:
  0.0 32.5 jit_solution(10787726299929408893)
XLA Ops:
  0.0 1.2 %shard_map.64 = (bf16[3,32,256]{2,1,0:T(8,128)(2,1)S(1)}, bf16[3,32,256]{2,1,0:T(8,128)(2,1)S(1)}, bf16[3,32,256]{2,1,0:T(8,128)(2,1)S(1)}, bf16[3,32,256]{2,1,0...) custom-call(bf16[32,2048]{1,0:T(8,128)(2,1)} %bitcast.8, ...), custom_call_target="tpu_custom_call" | custom-call | tf_op jit(solution)/shard_map/pallas_call | solution.py:151
  1.2 5.1 %collective-permute-start = (bf16[3,32,256]{2,1,0:T(8,128)(2,1)S(1)}, bf16[3,32,256]{2,1,0:T(8,128)(2,1)S(1)}, u32[]{:S(2)}, u32[]{:S(2)}) collective-permute-start(bf16[3,32,256]{2,1,0:T(8,128)(2,1)S(1)} %get-tuple-element.19), channel_id=1, source_target_pairs={{0,6},{1,7},{2,4},{3,5},{4,2},{5,3},{6,0},{7,1},{8,14},{9,15},{10,... | collective-permute-start | bytes 147464 | tf_op jit(solution)/shard_map/ppermute | solution.py:168
  6.3 0.0 collective-permute-start.1
  6.3 2.8 %collective-permute-start.2 = (bf16[3,32,256]{2,1,0:T(8,128)(2,1)S(1)}, bf16[3,32,256]{2,1,0:T(8,128)(2,1)S(1)}, u32[]{:S(2)}, u32[]{:S(2)}) collective-permute-start(bf16[3,32,256]{2,1,0:T(8,128)(2,1)S(1)} %get-tuple-element.21), channel_id=1, source_target_pairs={{0,7},{1,6},{2,5},{3,4},{4,3},{5,2},{6,1},{7,0},{8,15},{9,14},{10,... | collective-permute-start | bytes 147464 | tf_op jit(solution)/shard_map/ppermute | solution.py:168
  9.2 1.0 %collective-permute-start.3 = (bf16[3,32,256]{2,1,0:T(8,128)(2,1)S(1)}, bf16[3,32,256]{2,1,0:T(8,128)(2,1)S(1)}, u32[]{:S(2)}, u32[]{:S(2)}) collective-permute-start(bf16[3,32,256]{2,1,0:T(8,128)(2,1)S(1)} %get-tuple-element.22), channel_id=1, source_target_pairs={{0,5},{1,4},{2,7},{3,6},{4,1},{5,0},{6,3},{7,2},{8,13},{9,12},{10,... | collective-permute-start | bytes 147464 | tf_op jit(solution)/shard_map/ppermute | solution.py:168
  10.2 1.4 %collective-permute-start.4 = (bf16[3,32,256]{2,1,0:T(8,128)(2,1)S(1)}, bf16[3,32,256]{2,1,0:T(8,128)(2,1)S(1)}, u32[]{:S(2)}, u32[]{:S(2)}) collective-permute-start(bf16[3,32,256]{2,1,0:T(8,128)(2,1)S(1)} %get-tuple-element.23), channel_id=1, source_target_pairs={{0,2},{1,3},{2,0},{3,1},{4,6},{5,7},{6,4},{7,5},{8,10},{9,11},{10,... | collective-permute-start | bytes 147464 | tf_op jit(solution)/shard_map/ppermute | solution.py:168
  11.6 0.0 collective-permute-done.refs_0_
  11.6 0.9 %collective-permute-start.5 = (bf16[3,32,256]{2,1,0:T(8,128)(2,1)S(1)}, bf16[3,32,256]{2,1,0:T(8,128)(2,1)S(1)}, u32[]{:S(2)}, u32[]{:S(2)}) collective-permute-start(bf16[3,32,256]{2,1,0:T(8,128)(2,1)S(1)} %get-tuple-element.25), channel_id=1, source_target_pairs={{0,3},{1,2},{2,1},{3,0},{4,7},{5,6},{6,5},{7,4},{8,11},{9,10},{10,... | collective-permute-start | bytes 147464 | tf_op jit(solution)/shard_map/ppermute | solution.py:168
  12.5 0.0 collective-permute-done.1.refs_1_
  12.5 1.5 %collective-permute-start.6 = (bf16[3,32,256]{2,1,0:T(8,128)(2,1)S(1)}, bf16[3,32,256]{2,1,0:T(8,128)(2,1)S(1)}, u32[]{:S(2)}, u32[]{:S(2)}) collective-permute-start(bf16[3,32,256]{2,1,0:T(8,128)(2,1)S(1)} %get-tuple-element.26), channel_id=1, source_target_pairs={{0,1},{1,0},{2,3},{3,2},{4,5},{5,4},{6,7},{7,6},{8,9},{9,8},{10,11... | collective-permute-start | bytes 147464 | tf_op jit(solution)/shard_map/ppermute | solution.py:168
  14.1 0.0 collective-permute-done.2.refs_2_
  14.1 1.7 %collective-permute-done.3.refs_3_ = bf16[3,32,256]{2,1,0:T(8,128)(2,1)S(1)} collective-permute-done((bf16[3,32,256]{2,1,0:T(8,128)(2,1)S(1)}, bf16[3,32,256]{2,1,0:T(8,128)(2,1)S(1)}, u32[]{:S(2)}, u32[]{:S(2)}) %collective-permute-start.3) | collective-permute-done | bytes 49184 | tf_op jit(solution)/shard_map/ppermute | solution.py:168
  15.7 0.2 shard_map.66
  15.9 0.1 collective-permute-start.8
  16.0 0.0 collective-permute-done.4.refs_0_.refs_4_
  16.0 0.7 %collective-permute-done.5.refs_2_.refs_6_ = bf16[3,32,256]{2,1,0:T(8,128)(2,1)S(1)} collective-permute-done((bf16[3,32,256]{2,1,0:T(8,128)(2,1)S(1)}, bf16[3,32,256]{2,1,0:T(8,128)(2,1)S(1)}, u32[]{:S(2)}, u32[]{:S(2)}) %collective-permute-start.5) | collective-permute-done | bytes 49184 | tf_op jit(solution)/shard_map/ppermute | solution.py:168
  16.7 0.5 %collective-permute-done.6.refs_3_.refs_7_ = bf16[3,32,256]{2,1,0:T(8,128)(2,1)S(1)} collective-permute-done((bf16[3,32,256]{2,1,0:T(8,128)(2,1)S(1)}, bf16[3,32,256]{2,1,0:T(8,128)(2,1)S(1)}, u32[]{:S(2)}, u32[]{:S(2)}) %collective-permute-start.6) | collective-permute-done | bytes 49184 | tf_op jit(solution)/shard_map/ppermute | solution.py:168
  17.1 0.2 shard_map.65
  17.3 0.1 collective-permute-start.7
  17.4 0.0 collective-permute-done.8.refs_9_
  17.4 1.3 %collective-permute-done.7.refs_8_ = bf16[4,2,32,256]{3,2,1,0:T(8,128)(2,1)S(1)} collective-permute-done((bf16[4,2,32,256]{3,2,1,0:T(8,128)(2,1)S(1)}, bf16[4,2,32,256]{3,2,1,0:T(8,128)(2,1)S(1)}, u32[]{:S(2)}, u32[]{:S(2)}) %collective-permute-start.7) | collective-permute-done | bytes 131104 | tf_op jit(solution)/shard_map/ppermute | solution.py:186
  18.7 0.7 %shard_map.67 = bf16[8,32,256]{2,1,0:T(8,128)(2,1)S(1)} custom-call(s32[2,4]{1,0:T(2,128)S(1)} %get-tuple-element.16.slot_ref, s32[2,4]{1,0:T(2,128)S(1)} %get-tuple-element.17.level_ref, f32[8,256]{1,0:T(8,128)S(1)} %get-tuple-element.18.gate_ref, bf16[3,32,256]{2,1,0:T(8,128)(2,1)S(1)} %collective-permute-done.refs_0_, ...), custom_call_target="tpu_custom_call" | custom-call | tf_op jit(solution)/shard_map/pallas_call | solution.py:190
  19.4 12.4 %all_to_all.5.held_ref = bf16[8,4,8,256]{3,2,1,0:T(8,128)(2,1)S(1)} all-to-all(bf16[8,4,8,256]{3,2,1,0:T(8,128)(2,1)S(1)} %bitcast.7), channel_id=1, replica_groups=mesh['rollout'=2,'frame'=2,'seq'=8] {'seq'}, dimensions={0} | all-to-all | bytes 262144 | tf_op jit(solution)/shard_map/all_to_all | solution.py:198
  31.8 0.7 %shard_map.68 = bf16[4,8,8,256]{3,2,1,0:T(8,128)(2,1)} custom-call(bf16[8,4,8,256]{3,2,1,0:T(8,128)(2,1)S(1)} %all_to_all.5.held_ref), custom_call_target="tpu_custom_call" | custom-call | tf_op jit(solution)/shard_map/pallas_call | solution.py:199
Async XLA Ops:
  1.2 10.4 %collective-permute-start = (bf16[3,32,256]{2,1,0:T(8,128)(2,1)S(1)}, bf16[3,32,256]{2,1,0:T(8,128)(2,1)S(1)}, u32[]{:S(2)}, u32[]{:S(2)}) collective-permute-start(bf16[3,32,256]{2,1,0:T(8,128)(2,1)S(1)} %get-tuple-element.19), channel_id=1, source_target_pairs={{0,6},{1,7},{2,4},{3,5},{4,2},{5,3},{6,0},{7,1},{8,14},{9,15},{10,... | collective-permute-start | bytes 147464 | tf_op jit(solution)/shard_map/ppermute | solution.py:168
  6.3 6.2 %collective-permute-start.1 = (bf16[3,32,256]{2,1,0:T(8,128)(2,1)S(1)}, bf16[3,32,256]{2,1,0:T(8,128)(2,1)S(1)}, u32[]{:S(2)}, u32[]{:S(2)}) collective-permute-start(bf16[3,32,256]{2,1,0:T(8,128)(2,1)S(1)} %get-tuple-element.20), channel_id=1, source_target_pairs={{0,4},{1,5},{2,6},{3,7},{4,0},{5,1},{6,2},{7,3},{8,12},{9,13},{10,... | collective-permute-start | bytes 147464 | tf_op jit(solution)/shard_map/ppermute | solution.py:168
  6.3 7.7 %collective-permute-start.2 = (bf16[3,32,256]{2,1,0:T(8,128)(2,1)S(1)}, bf16[3,32,256]{2,1,0:T(8,128)(2,1)S(1)}, u32[]{:S(2)}, u32[]{:S(2)}) collective-permute-start(bf16[3,32,256]{2,1,0:T(8,128)(2,1)S(1)} %get-tuple-element.21), channel_id=1, source_target_pairs={{0,7},{1,6},{2,5},{3,4},{4,3},{5,2},{6,1},{7,0},{8,15},{9,14},{10,... | collective-permute-start | bytes 147464 | tf_op jit(solution)/shard_map/ppermute | solution.py:168
  9.2 6.6 %collective-permute-start.3 = (bf16[3,32,256]{2,1,0:T(8,128)(2,1)S(1)}, bf16[3,32,256]{2,1,0:T(8,128)(2,1)S(1)}, u32[]{:S(2)}, u32[]{:S(2)}) collective-permute-start(bf16[3,32,256]{2,1,0:T(8,128)(2,1)S(1)} %get-tuple-element.22), channel_id=1, source_target_pairs={{0,5},{1,4},{2,7},{3,6},{4,1},{5,0},{6,3},{7,2},{8,13},{9,12},{10,... | collective-permute-start | bytes 147464 | tf_op jit(solution)/shard_map/ppermute | solution.py:168
  10.2 5.8 %collective-permute-start.4 = (bf16[3,32,256]{2,1,0:T(8,128)(2,1)S(1)}, bf16[3,32,256]{2,1,0:T(8,128)(2,1)S(1)}, u32[]{:S(2)}, u32[]{:S(2)}) collective-permute-start(bf16[3,32,256]{2,1,0:T(8,128)(2,1)S(1)} %get-tuple-element.23), channel_id=1, source_target_pairs={{0,2},{1,3},{2,0},{3,1},{4,6},{5,7},{6,4},{7,5},{8,10},{9,11},{10,... | collective-permute-start | bytes 147464 | tf_op jit(solution)/shard_map/ppermute | solution.py:168
  11.6 5.0 %collective-permute-start.5 = (bf16[3,32,256]{2,1,0:T(8,128)(2,1)S(1)}, bf16[3,32,256]{2,1,0:T(8,128)(2,1)S(1)}, u32[]{:S(2)}, u32[]{:S(2)}) collective-permute-start(bf16[3,32,256]{2,1,0:T(8,128)(2,1)S(1)} %get-tuple-element.25), channel_id=1, source_target_pairs={{0,3},{1,2},{2,1},{3,0},{4,7},{5,6},{6,5},{7,4},{8,11},{9,10},{10,... | collective-permute-start | bytes 147464 | tf_op jit(solution)/shard_map/ppermute | solution.py:168
  12.5 4.6 %collective-permute-start.6 = (bf16[3,32,256]{2,1,0:T(8,128)(2,1)S(1)}, bf16[3,32,256]{2,1,0:T(8,128)(2,1)S(1)}, u32[]{:S(2)}, u32[]{:S(2)}) collective-permute-start(bf16[3,32,256]{2,1,0:T(8,128)(2,1)S(1)} %get-tuple-element.26), channel_id=1, source_target_pairs={{0,1},{1,0},{2,3},{3,2},{4,5},{5,4},{6,7},{7,6},{8,9},{9,8},{10,11... | collective-permute-start | bytes 147464 | tf_op jit(solution)/shard_map/ppermute | solution.py:168
  15.9 1.5 %collective-permute-start.8 = (bf16[4,2,32,256]{3,2,1,0:T(8,128)(2,1)S(1)}, bf16[4,2,32,256]{3,2,1,0:T(8,128)(2,1)S(1)}, u32[]{:S(2)}, u32[]{:S(2)}) collective-permute-start(bf16[4,2,32,256]{3,2,1,0:T(8,128)(2,1)S(1)} %shard_map.66), channel_id=1, source_target_pairs={{0,8},{8,0},{1,9},{9,1},{2,10},{10,2},{3,11},{11,3},{4,12},{12,4},... | collective-permute-start | bytes 393224 | tf_op jit(solution)/shard_map/ppermute | solution.py:186
  17.3 1.4 %collective-permute-start.7 = (bf16[4,2,32,256]{3,2,1,0:T(8,128)(2,1)S(1)}, bf16[4,2,32,256]{3,2,1,0:T(8,128)(2,1)S(1)}, u32[]{:S(2)}, u32[]{:S(2)}) collective-permute-start(bf16[4,2,32,256]{3,2,1,0:T(8,128)(2,1)S(1)} %shard_map.65), channel_id=1, source_target_pairs={{0,8},{8,0},{1,9},{9,1},{2,10},{10,2},{3,11},{11,3},{4,12},{12,4},... | collective-permute-start | bytes 393224 | tf_op jit(solution)/shard_map/ppermute | solution.py:186

commit v16 on v15

--- a/solution.py
+++ b/solution.py
@@ -16,8 +16,9 @@
 PARAMS = pltpu.CompilerParams(vmem_limit_bytes=32 * 1024 * 1024)
 
 
-def far_first(devices):
-    return sorted(range(devices), key=lambda away: (-(2 * away // devices), away % 2, -away))
+def send_order(devices):
+    own = sorted(range(0, devices, 2), reverse=True)
+    return own + sorted(range(1, devices, 2), key=lambda away: (2 * away // devices, -away))
 
 
 def run(copies):
@@ -46,7 +47,7 @@
             pltpu.make_async_copy(
                 ref.at[:, columns(place ^ away)], out_ref.at[kind], sems.at[away, kind]
             )
-            for away, out_ref in zip(far_first(len(outs)), outs)
+            for away, out_ref in zip(send_order(len(outs)), outs)
             for kind, ref in enumerate(operands)
         ]
         + [
@@ -135,7 +136,7 @@
             mixed = mixed[:, :HEAD] / mixed[:, HEAD:]
             mixed = mixed.reshape(step, local_frames, tokens, HEAD) * gates
             mixed = mixed.reshape(step, rows, HEAD).astype(out_ref.dtype)
-            for number, away in enumerate(far_first(devices)[start : start + step]):
+            for number, away in enumerate(send_order(devices)[start : start + step]):
                 out_ref[lax.axis_index("seq") ^ away, :, part] = mixed[number]
 
 
@@ -168,7 +169,7 @@
         lax.ppermute(piece, "seq", [(one, one ^ away) for one in range(devices)])
         if away
         else piece
-        for away, piece in zip(far_first(devices), pieces)
+        for away, piece in zip(send_order(devices), pieces)
     ]
 
     def stacked(taken):
@@ -181,7 +182,7 @@
             compiler_params=PARAMS,
         )(*taken)
 
-    stacks = [stacked(taken) for taken in (pieces[half:], pieces[:half]) if taken]
+    stacks = [stacked(taken) for taken in (pieces[:half], pieces[half:]) if taken]
     stacks = [
         lax.ppermute(taken, "frame", [(one, (one - away) % groups) for one in range(groups)])
         for away in range(1, groups)

time: 32.7 us -> 33.3 us (1.018)
  waiting for transfers between devices: 4.13 us -> 7.34 us
  blocking collectives: 12.4 us -> 9.97 us
    ppermute x7, waiting for transfers between devices: 2.81 us -> 6.01 us  [whole_heads(): lax.ppermute(piece, 'seq', [(one, one ^ away) for one in range(devices)])]
    all_to_all x1, blocking collectives: 12.4 us -> 9.97 us  [whole_heads(): lax.all_to_all(answer, 'seq', split_axis=0, concat_axis=0, tiled=True)]
  transfers between devices with their start and end apart: 9 -> 9, of which waited for: 4 -> 3; matrix products, arithmetic and copies ran while one was open for 0% -> 0% of each run, Pallas kernels for 1% -> 1%
where the time goes in v16:
time: 33.3 us; the launch traced here: 33 us
  starting transfers between devices  12.7 us (38%)
  blocking collectives  9.97 us (30%)
  waiting for transfers between devices  7.34 us (22%)
  Pallas kernels  2.93 us (9%)
    ppermute x7, starting transfers between devices, whole_heads(): lax.ppermute(piece, 'seq', [(one, one ^ away) for one in range(devices)])  12.6 us
    all_to_all x1, blocking collectives, whole_heads(): lax.all_to_all(answer, 'seq', split_axis=0, concat_axis=0, tiled=True)  9.97 us
    ppermute x7, waiting for transfers between devices, whole_heads(): lax.ppermute(piece, 'seq', [(one, one ^ away) for one in range(devices)])  6.01 us
    ppermute x2, waiting for transfers between devices, whole_heads(): lax.ppermute(taken, 'frame', [(one, (one - away) % groups) for one in ran...  1.33 us
    pallas_call x1, Pallas kernels, whole_heads(): pl.pallas_call(pack, out_shape=[jax.ShapeDtypeStruct((3, rows, width), qu...  1.2 us
    pallas_call x1, Pallas kernels, whole_heads(): pl.pallas_call(functools.partial(attend, tokens=tokens), out_shape=jax.Sh...  0.69 us
    pallas_call x1, Pallas kernels, whole_heads(): pl.pallas_call(unpack, out_shape=jax.ShapeDtypeStruct((local_frames, devi...  0.68 us
  transfers between devices with their start and end apart: 9, of which 3 were waited for; matrix products, arithmetic and copies ran while one was open for 0% of the time, Pallas kernels for 1%

profile of v16, /device:TPU:0, one launch (start us, length us, event | category | flops | bytes accessed | tf_op | source)
XLA Modules:
  0.0 33.0 jit_solution(3057963621601896562)
XLA Ops:
  0.0 1.2 %shard_map.64 = (bf16[3,32,256]{2,1,0:T(8,128)(2,1)S(1)}, bf16[3,32,256]{2,1,0:T(8,128)(2,1)S(1)}, bf16[3,32,256]{2,1,0:T(8,128)(2,1)S(1)}, bf16[3,32,256]{2,1,0...) custom-call(bf16[32,2048]{1,0:T(8,128)(2,1)} %bitcast.8, ...), custom_call_target="tpu_custom_call" | custom-call | tf_op jit(solution)/shard_map/pallas_call | solution.py:152
  1.2 5.1 %collective-permute-start = (bf16[3,32,256]{2,1,0:T(8,128)(2,1)S(1)}, bf16[3,32,256]{2,1,0:T(8,128)(2,1)S(1)}, u32[]{:S(2)}, u32[]{:S(2)}) collective-permute-start(bf16[3,32,256]{2,1,0:T(8,128)(2,1)S(1)} %get-tuple-element.19), channel_id=1, source_target_pairs={{0,6},{1,7},{2,4},{3,5},{4,2},{5,3},{6,0},{7,1},{8,14},{9,15},{10,... | collective-permute-start | bytes 147464 | tf_op jit(solution)/shard_map/ppermute | solution.py:169
  6.3 0.0 collective-permute-start.1
  6.3 0.6 %collective-permute-start.2 = (bf16[3,32,256]{2,1,0:T(8,128)(2,1)S(1)}, bf16[3,32,256]{2,1,0:T(8,128)(2,1)S(1)}, u32[]{:S(2)}, u32[]{:S(2)}) collective-permute-start(bf16[3,32,256]{2,1,0:T(8,128)(2,1)S(1)} %get-tuple-element.21), channel_id=1, source_target_pairs={{0,2},{1,3},{2,0},{3,1},{4,6},{5,7},{6,4},{7,5},{8,10},{9,11},{10,... | collective-permute-start | bytes 147464 | tf_op jit(solution)/shard_map/ppermute | solution.py:169
  7.0 2.3 %collective-permute-start.3 = (bf16[3,32,256]{2,1,0:T(8,128)(2,1)S(1)}, bf16[3,32,256]{2,1,0:T(8,128)(2,1)S(1)}, u32[]{:S(2)}, u32[]{:S(2)}) collective-permute-start(bf16[3,32,256]{2,1,0:T(8,128)(2,1)S(1)} %get-tuple-element.23), channel_id=1, source_target_pairs={{0,3},{1,2},{2,1},{3,0},{4,7},{5,6},{6,5},{7,4},{8,11},{9,10},{10,... | collective-permute-start | bytes 147464 | tf_op jit(solution)/shard_map/ppermute | solution.py:169
  9.3 0.5 %collective-permute-start.4 = (bf16[3,32,256]{2,1,0:T(8,128)(2,1)S(1)}, bf16[3,32,256]{2,1,0:T(8,128)(2,1)S(1)}, u32[]{:S(2)}, u32[]{:S(2)}) collective-permute-start(bf16[3,32,256]{2,1,0:T(8,128)(2,1)S(1)} %get-tuple-element.24), channel_id=1, source_target_pairs={{0,1},{1,0},{2,3},{3,2},{4,5},{5,4},{6,7},{7,6},{8,9},{9,8},{10,11... | collective-permute-start | bytes 147464 | tf_op jit(solution)/shard_map/ppermute | solution.py:169
  9.8 0.0 collective-permute-done.refs_0_
  9.8 3.9 %collective-permute-start.5 = (bf16[3,32,256]{2,1,0:T(8,128)(2,1)S(1)}, bf16[3,32,256]{2,1,0:T(8,128)(2,1)S(1)}, u32[]{:S(2)}, u32[]{:S(2)}) collective-permute-start(bf16[3,32,256]{2,1,0:T(8,128)(2,1)S(1)} %get-tuple-element.25), channel_id=1, source_target_pairs={{0,7},{1,6},{2,5},{3,4},{4,3},{5,2},{6,1},{7,0},{8,15},{9,14},{10,... | collective-permute-start | bytes 147464 | tf_op jit(solution)/shard_map/ppermute | solution.py:169
  13.7 0.0 collective-permute-done.1.refs_1_
  13.7 0.1 collective-permute-start.6
  13.8 0.0 collective-permute-done.2.refs_2_
  13.8 0.2 shard_map.65
  14.0 0.1 collective-permute-start.7
  14.1 0.0 collective-permute-done.3.refs_0_.refs_4_
  14.1 0.0 collective-permute-done.4.refs_1_.refs_5_
  14.1 3.0 %collective-permute-done.5.refs_2_.refs_6_ = bf16[3,32,256]{2,1,0:T(8,128)(2,1)S(1)} collective-permute-done((bf16[3,32,256]{2,1,0:T(8,128)(2,1)S(1)}, bf16[3,32,256]{2,1,0:T(8,128)(2,1)S(1)}, u32[]{:S(2)}, u32[]{:S(2)}) %collective-permute-start.5) | collective-permute-done | bytes 49184 | tf_op jit(solution)/shard_map/ppermute | solution.py:169
  17.1 3.0 %collective-permute-done.6.refs_3_.refs_7_ = bf16[3,32,256]{2,1,0:T(8,128)(2,1)S(1)} collective-permute-done((bf16[3,32,256]{2,1,0:T(8,128)(2,1)S(1)}, bf16[3,32,256]{2,1,0:T(8,128)(2,1)S(1)}, u32[]{:S(2)}, u32[]{:S(2)}) %collective-permute-start.6) | collective-permute-done | bytes 49184 | tf_op jit(solution)/shard_map/ppermute | solution.py:169
  20.1 0.2 shard_map.66
  20.3 0.1 collective-permute-start.8
  20.4 0.0 collective-permute-done.7.refs_8_
  20.4 1.3 %collective-permute-done.8.refs_9_ = bf16[4,2,32,256]{3,2,1,0:T(8,128)(2,1)S(1)} collective-permute-done((bf16[4,2,32,256]{3,2,1,0:T(8,128)(2,1)S(1)}, bf16[4,2,32,256]{3,2,1,0:T(8,128)(2,1)S(1)}, u32[]{:S(2)}, u32[]{:S(2)}) %collective-permute-start.8) | collective-permute-done | bytes 131104 | tf_op jit(solution)/shard_map/ppermute | solution.py:187
  21.7 0.7 %shard_map.67 = bf16[8,32,256]{2,1,0:T(8,128)(2,1)S(1)} custom-call(s32[2,4]{1,0:T(2,128)S(1)} %get-tuple-element.16.slot_ref, s32[2,4]{1,0:T(2,128)S(1)} %get-tuple-element.17.level_ref, f32[8,256]{1,0:T(8,128)S(1)} %get-tuple-element.18.gate_ref, bf16[3,32,256]{2,1,0:T(8,128)(2,1)S(1)} %collective-permute-done.refs_0_, ...), custom_call_target="tpu_custom_call" | custom-call | tf_op jit(solution)/shard_map/pallas_call | solution.py:191
  22.4 10.0 %all_to_all.5.held_ref = bf16[8,4,8,256]{3,2,1,0:T(8,128)(2,1)S(1)} all-to-all(bf16[8,4,8,256]{3,2,1,0:T(8,128)(2,1)S(1)} %bitcast.7), channel_id=1, replica_groups=mesh['rollout'=2,'frame'=2,'seq'=8] {'seq'}, dimensions={0} | all-to-all | bytes 262144 | tf_op jit(solution)/shard_map/all_to_all | solution.py:199
  32.3 0.7 %shard_map.68 = bf16[4,8,8,256]{3,2,1,0:T(8,128)(2,1)} custom-call(bf16[8,4,8,256]{3,2,1,0:T(8,128)(2,1)S(1)} %all_to_all.5.held_ref), custom_call_target="tpu_custom_call" | custom-call | tf_op jit(solution)/shard_map/pallas_call | solution.py:200
Async XLA Ops:
  1.2 8.6 %collective-permute-start = (bf16[3,32,256]{2,1,0:T(8,128)(2,1)S(1)}, bf16[3,32,256]{2,1,0:T(8,128)(2,1)S(1)}, u32[]{:S(2)}, u32[]{:S(2)}) collective-permute-start(bf16[3,32,256]{2,1,0:T(8,128)(2,1)S(1)} %get-tuple-element.19), channel_id=1, source_target_pairs={{0,6},{1,7},{2,4},{3,5},{4,2},{5,3},{6,0},{7,1},{8,14},{9,15},{10,... | collective-permute-start | bytes 147464 | tf_op jit(solution)/shard_map/ppermute | solution.py:169
  6.3 7.4 %collective-permute-start.1 = (bf16[3,32,256]{2,1,0:T(8,128)(2,1)S(1)}, bf16[3,32,256]{2,1,0:T(8,128)(2,1)S(1)}, u32[]{:S(2)}, u32[]{:S(2)}) collective-permute-start(bf16[3,32,256]{2,1,0:T(8,128)(2,1)S(1)} %get-tuple-element.20), channel_id=1, source_target_pairs={{0,4},{1,5},{2,6},{3,7},{4,0},{5,1},{6,2},{7,3},{8,12},{9,13},{10,... | collective-permute-start | bytes 147464 | tf_op jit(solution)/shard_map/ppermute | solution.py:169
  6.3 7.5 %collective-permute-start.2 = (bf16[3,32,256]{2,1,0:T(8,128)(2,1)S(1)}, bf16[3,32,256]{2,1,0:T(8,128)(2,1)S(1)}, u32[]{:S(2)}, u32[]{:S(2)}) collective-permute-start(bf16[3,32,256]{2,1,0:T(8,128)(2,1)S(1)} %get-tuple-element.21), channel_id=1, source_target_pairs={{0,2},{1,3},{2,0},{3,1},{4,6},{5,7},{6,4},{7,5},{8,10},{9,11},{10,... | collective-permute-start | bytes 147464 | tf_op jit(solution)/shard_map/ppermute | solution.py:169
  7.0 7.1 %collective-permute-start.3 = (bf16[3,32,256]{2,1,0:T(8,128)(2,1)S(1)}, bf16[3,32,256]{2,1,0:T(8,128)(2,1)S(1)}, u32[]{:S(2)}, u32[]{:S(2)}) collective-permute-start(bf16[3,32,256]{2,1,0:T(8,128)(2,1)S(1)} %get-tuple-element.23), channel_id=1, source_target_pairs={{0,3},{1,2},{2,1},{3,0},{4,7},{5,6},{6,5},{7,4},{8,11},{9,10},{10,... | collective-permute-start | bytes 147464 | tf_op jit(solution)/shard_map/ppermute | solution.py:169
  9.3 4.8 %collective-permute-start.4 = (bf16[3,32,256]{2,1,0:T(8,128)(2,1)S(1)}, bf16[3,32,256]{2,1,0:T(8,128)(2,1)S(1)}, u32[]{:S(2)}, u32[]{:S(2)}) collective-permute-start(bf16[3,32,256]{2,1,0:T(8,128)(2,1)S(1)} %get-tuple-element.24), channel_id=1, source_target_pairs={{0,1},{1,0},{2,3},{3,2},{4,5},{5,4},{6,7},{7,6},{8,9},{9,8},{10,11... | collective-permute-start | bytes 147464 | tf_op jit(solution)/shard_map/ppermute | solution.py:169
  9.8 7.3 %collective-permute-start.5 = (bf16[3,32,256]{2,1,0:T(8,128)(2,1)S(1)}, bf16[3,32,256]{2,1,0:T(8,128)(2,1)S(1)}, u32[]{:S(2)}, u32[]{:S(2)}) collective-permute-start(bf16[3,32,256]{2,1,0:T(8,128)(2,1)S(1)} %get-tuple-element.25), channel_id=1, source_target_pairs={{0,7},{1,6},{2,5},{3,4},{4,3},{5,2},{6,1},{7,0},{8,15},{9,14},{10,... | collective-permute-start | bytes 147464 | tf_op jit(solution)/shard_map/ppermute | solution.py:169
  13.7 6.4 %collective-permute-start.6 = (bf16[3,32,256]{2,1,0:T(8,128)(2,1)S(1)}, bf16[3,32,256]{2,1,0:T(8,128)(2,1)S(1)}, u32[]{:S(2)}, u32[]{:S(2)}) collective-permute-start(bf16[3,32,256]{2,1,0:T(8,128)(2,1)S(1)} %get-tuple-element.26), channel_id=1, source_target_pairs={{0,5},{1,4},{2,7},{3,6},{4,1},{5,0},{6,3},{7,2},{8,13},{9,12},{10,... | collective-permute-start | bytes 147464 | tf_op jit(solution)/shard_map/ppermute | solution.py:169
  14.0 6.4 %collective-permute-start.7 = (bf16[4,2,32,256]{3,2,1,0:T(8,128)(2,1)S(1)}, bf16[4,2,32,256]{3,2,1,0:T(8,128)(2,1)S(1)}, u32[]{:S(2)}, u32[]{:S(2)}) collective-permute-start(bf16[4,2,32,256]{3,2,1,0:T(8,128)(2,1)S(1)} %shard_map.65), channel_id=1, source_target_pairs={{0,8},{8,0},{1,9},{9,1},{2,10},{10,2},{3,11},{11,3},{4,12},{12,4},... | collective-permute-start | bytes 393224 | tf_op jit(solution)/shard_map/ppermute | solution.py:187
  20.3 1.4 %collective-permute-start.8 = (bf16[4,2,32,256]{3,2,1,0:T(8,128)(2,1)S(1)}, bf16[4,2,32,256]{3,2,1,0:T(8,128)(2,1)S(1)}, u32[]{:S(2)}, u32[]{:S(2)}) collective-permute-start(bf16[4,2,32,256]{3,2,1,0:T(8,128)(2,1)S(1)} %shard_map.66), channel_id=1, source_target_pairs={{0,8},{8,0},{1,9},{9,1},{2,10},{10,2},{3,11},{11,3},{4,12},{12,4},... | collective-permute-start | bytes 393224 | tf_op jit(solution)/shard_map/ppermute | solution.py:187

commit v17 on v16

--- a/solution.py
+++ b/solution.py
@@ -17,8 +17,10 @@
 
 
 def send_order(devices):
-    own = sorted(range(0, devices, 2), reverse=True)
-    return own + sorted(range(1, devices, 2), key=lambda away: (2 * away // devices, -away))
+    return sorted(
+        range(devices),
+        key=lambda away: (away != 2, -(2 * away // devices), away % 2, -away),
+    )
 
 
 def run(copies):
@@ -144,7 +146,6 @@
     devices, groups = lax.axis_size("seq"), lax.axis_size("frame")
     _, local_frames, tokens, all_width = queries.shape
     rows, width = local_frames * tokens, all_width // devices
-    half = max(1, devices // 2)
 
     def in_hbm(taken):
         return pltpu.with_memory_space_constraint(taken, pltpu.HBM)
@@ -172,21 +173,17 @@
         for away, piece in zip(send_order(devices), pieces)
     ]
 
-    def stacked(taken):
-        return pl.pallas_call(
-            stack,
-            out_shape=jax.ShapeDtypeStruct((len(taken), 2, rows, width), queries.dtype),
-            in_specs=[VMEM] * len(taken),
-            out_specs=VMEM,
-            scratch_shapes=[pltpu.SemaphoreType.DMA((len(taken),))],
-            compiler_params=PARAMS,
-        )(*taken)
-
-    stacks = [stacked(taken) for taken in (pieces[:half], pieces[half:]) if taken]
+    stacked = pl.pallas_call(
+        stack,
+        out_shape=jax.ShapeDtypeStruct((devices, 2, rows, width), queries.dtype),
+        in_specs=[VMEM] * devices,
+        out_specs=VMEM,
+        scratch_shapes=[pltpu.SemaphoreType.DMA((devices,))],
+        compiler_params=PARAMS,
+    )(*pieces)
     stacks = [
-        lax.ppermute(taken, "frame", [(one, (one - away) % groups) for one in range(groups)])
+        lax.ppermute(stacked, "frame", [(one, (one - away) % groups) for one in range(groups)])
         for away in range(1, groups)
-        for taken in stacks
     ]
     answer = pl.pallas_call(
         functools.partial(attend, tokens=tokens),

time: 33.3 us -> 32.5 us (0.976)
  waiting for transfers between devices: 7.34 us -> 5.72 us
  blocking collectives: 9.97 us -> 11.1 us
    ppermute x7, waiting for transfers between devices: 6.01 us -> 4.2 us  [whole_heads(): lax.ppermute(piece, 'seq', [(one, one ^ away) for one in range(devices)])]
    all_to_all x1, blocking collectives: 9.97 us -> 11.1 us  [whole_heads(): lax.all_to_all(answer, 'seq', split_axis=0, concat_axis=0, tiled=True)]
    ppermute x2 -> x1, waiting for transfers between devices: 1.33 us -> 1.52 us  [whole_heads(): lax.ppermute(stacked, 'frame', [(one, (one - away) % groups) for one in r...]
  transfers between devices with their start and end apart: 9 -> 8, of which waited for: 3 -> 4; matrix products, arithmetic and copies ran while one was open for 0% -> 0% of each run, Pallas kernels for 1% -> 0%
where the time goes in v17:
time: 32.5 us; the launch traced here: 32.3 us
  starting transfers between devices  12.5 us (38%)
  blocking collectives  11.1 us (34%)
  waiting for transfers between devices  5.72 us (18%)
  Pallas kernels  2.96 us (9%)
    ppermute x7, starting transfers between devices, whole_heads(): lax.ppermute(piece, 'seq', [(one, one ^ away) for one in range(devices)])  12.4 us
    all_to_all x1, blocking collectives, whole_heads(): lax.all_to_all(answer, 'seq', split_axis=0, concat_axis=0, tiled=True)  11.1 us
    ppermute x7, waiting for transfers between devices, whole_heads(): lax.ppermute(piece, 'seq', [(one, one ^ away) for one in range(devices)])  4.2 us
    ppermute x1, waiting for transfers between devices, whole_heads(): lax.ppermute(stacked, 'frame', [(one, (one - away) % groups) for one in r...  1.52 us
    pallas_call x1, Pallas kernels, whole_heads(): pl.pallas_call(pack, out_shape=[jax.ShapeDtypeStruct((3, rows, width), qu...  1.2 us
    pallas_call x1, Pallas kernels, whole_heads(): pl.pallas_call(functools.partial(attend, tokens=tokens), out_shape=jax.Sh...  0.69 us
    pallas_call x1, Pallas kernels, whole_heads(): pl.pallas_call(unpack, out_shape=jax.ShapeDtypeStruct((local_frames, devi...  0.68 us
  transfers between devices with their start and end apart: 8, of which 4 were waited for; matrix products, arithmetic and copies ran while one was open for 0% of the time, Pallas kernels for 0%

profile of v17, /device:TPU:0, one launch (start us, length us, event | category | flops | bytes accessed | tf_op | source)
XLA Modules:
  0.0 32.3 jit_solution(6621820612149682633)
XLA Ops:
  0.0 1.2 %shard_map.64 = (bf16[3,32,256]{2,1,0:T(8,128)(2,1)S(1)}, bf16[3,32,256]{2,1,0:T(8,128)(2,1)S(1)}, bf16[3,32,256]{2,1,0:T(8,128)(2,1)S(1)}, bf16[3,32,256]{2,1,0...) custom-call(bf16[32,2048]{1,0:T(8,128)(2,1)} %bitcast.8, ...), custom_call_target="tpu_custom_call" | custom-call | tf_op jit(solution)/shard_map/pallas_call | solution.py:153
  1.2 3.1 %collective-permute-start = (bf16[3,32,256]{2,1,0:T(8,128)(2,1)S(1)}, bf16[3,32,256]{2,1,0:T(8,128)(2,1)S(1)}, u32[]{:S(2)}, u32[]{:S(2)}) collective-permute-start(bf16[3,32,256]{2,1,0:T(8,128)(2,1)S(1)} %get-tuple-element.19), channel_id=1, source_target_pairs={{0,2},{1,3},{2,0},{3,1},{4,6},{5,7},{6,4},{7,5},{8,10},{9,11},{10,... | collective-permute-start | bytes 147464 | tf_op jit(solution)/shard_map/ppermute | solution.py:170
  4.3 2.5 %collective-permute-start.1 = (bf16[3,32,256]{2,1,0:T(8,128)(2,1)S(1)}, bf16[3,32,256]{2,1,0:T(8,128)(2,1)S(1)}, u32[]{:S(2)}, u32[]{:S(2)}) collective-permute-start(bf16[3,32,256]{2,1,0:T(8,128)(2,1)S(1)} %get-tuple-element.20), channel_id=1, source_target_pairs={{0,6},{1,7},{2,4},{3,5},{4,2},{5,3},{6,0},{7,1},{8,14},{9,15},{10,... | collective-permute-start | bytes 147464 | tf_op jit(solution)/shard_map/ppermute | solution.py:170
  6.8 0.1 collective-permute-start.2
  6.9 3.8 %collective-permute-start.3 = (bf16[3,32,256]{2,1,0:T(8,128)(2,1)S(1)}, bf16[3,32,256]{2,1,0:T(8,128)(2,1)S(1)}, u32[]{:S(2)}, u32[]{:S(2)}) collective-permute-start(bf16[3,32,256]{2,1,0:T(8,128)(2,1)S(1)} %get-tuple-element.22), channel_id=1, source_target_pairs={{0,7},{1,6},{2,5},{3,4},{4,3},{5,2},{6,1},{7,0},{8,15},{9,14},{10,... | collective-permute-start | bytes 147464 | tf_op jit(solution)/shard_map/ppermute | solution.py:170
  10.7 0.3 collective-permute-start.4
  11.0 0.0 collective-permute-done.refs_0_
  11.0 2.1 %collective-permute-start.5 = (bf16[3,32,256]{2,1,0:T(8,128)(2,1)S(1)}, bf16[3,32,256]{2,1,0:T(8,128)(2,1)S(1)}, u32[]{:S(2)}, u32[]{:S(2)}) collective-permute-start(bf16[3,32,256]{2,1,0:T(8,128)(2,1)S(1)} %get-tuple-element.25), channel_id=1, source_target_pairs={{0,3},{1,2},{2,1},{3,0},{4,7},{5,6},{6,5},{7,4},{8,11},{9,10},{10,... | collective-permute-start | bytes 147464 | tf_op jit(solution)/shard_map/ppermute | solution.py:170
  13.1 0.0 collective-permute-done.1.refs_1_
  13.1 0.5 %collective-permute-start.6 = (bf16[3,32,256]{2,1,0:T(8,128)(2,1)S(1)}, bf16[3,32,256]{2,1,0:T(8,128)(2,1)S(1)}, u32[]{:S(2)}, u32[]{:S(2)}) collective-permute-start(bf16[3,32,256]{2,1,0:T(8,128)(2,1)S(1)} %get-tuple-element.26), channel_id=1, source_target_pairs={{0,1},{1,0},{2,3},{3,2},{4,5},{5,4},{6,7},{7,6},{8,9},{9,8},{10,11... | collective-permute-start | bytes 147464 | tf_op jit(solution)/shard_map/ppermute | solution.py:170
  13.6 0.8 %collective-permute-done.2.refs_2_ = bf16[3,32,256]{2,1,0:T(8,128)(2,1)S(1)} collective-permute-done((bf16[3,32,256]{2,1,0:T(8,128)(2,1)S(1)}, bf16[3,32,256]{2,1,0:T(8,128)(2,1)S(1)}, u32[]{:S(2)}, u32[]{:S(2)}) %collective-permute-start.2) | collective-permute-done | bytes 49184 | tf_op jit(solution)/shard_map/ppermute | solution.py:170
  14.5 0.0 collective-permute-done.3.refs_3_
  14.5 2.9 %collective-permute-done.4.refs_4_ = bf16[3,32,256]{2,1,0:T(8,128)(2,1)S(1)} collective-permute-done((bf16[3,32,256]{2,1,0:T(8,128)(2,1)S(1)}, bf16[3,32,256]{2,1,0:T(8,128)(2,1)S(1)}, u32[]{:S(2)}, u32[]{:S(2)}) %collective-permute-start.4) | collective-permute-done | bytes 49184 | tf_op jit(solution)/shard_map/ppermute | solution.py:170
  17.4 0.0 collective-permute-done.5.refs_6_
  17.4 0.5 %collective-permute-done.6.refs_7_ = bf16[3,32,256]{2,1,0:T(8,128)(2,1)S(1)} collective-permute-done((bf16[3,32,256]{2,1,0:T(8,128)(2,1)S(1)}, bf16[3,32,256]{2,1,0:T(8,128)(2,1)S(1)}, u32[]{:S(2)}, u32[]{:S(2)}) %collective-permute-start.6) | collective-permute-done | bytes 49184 | tf_op jit(solution)/shard_map/ppermute | solution.py:170
  17.8 0.4 %shard_map.65 = bf16[8,2,32,256]{3,2,1,0:T(8,128)(2,1)S(1)} custom-call(bf16[3,32,256]{2,1,0:T(8,128)(2,1)S(1)} %collective-permute-done.refs_0_, bf16[3,32,256]{2,1,0:T(8,128)(2,1)S(1)} %collective-permute-done.1.refs_1_, bf16[3,32,256]{2,1,0:T(8,128)(2,1)S(1)} %collective-permute-done.2.refs_2_, bf16[3,32,256]{2,1,0:T(8,128)(2,1)S(1)} %collective-permute-done.3.refs_3_, ...), custom_call_target="tpu_custom_call" | custom-call | tf_op jit(solution)/shard_map/pallas_call | solution.py:176
  18.2 0.1 collective-permute-start.7
  18.3 1.5 %collective-permute-done.7.refs_8_ = bf16[8,2,32,256]{3,2,1,0:T(8,128)(2,1)S(1)} collective-permute-done((bf16[8,2,32,256]{3,2,1,0:T(8,128)(2,1)S(1)}, bf16[8,2,32,256]{3,2,1,0:T(8,128)(2,1)S(1)}, u32[]{:S(2)}, u32[]{:S(2)}) %collective-permute-start.7) | collective-permute-done | bytes 262176 | tf_op jit(solution)/shard_map/ppermute | solution.py:185
  19.8 0.7 %shard_map.66 = bf16[8,32,256]{2,1,0:T(8,128)(2,1)S(1)} custom-call(s32[2,4]{1,0:T(2,128)S(1)} %get-tuple-element.16.slot_ref, s32[2,4]{1,0:T(2,128)S(1)} %get-tuple-element.17.level_ref, f32[8,256]{1,0:T(8,128)S(1)} %get-tuple-element.18.gate_ref, bf16[3,32,256]{2,1,0:T(8,128)(2,1)S(1)} %collective-permute-done.refs_0_, ...), custom_call_target="tpu_custom_call" | custom-call | tf_op jit(solution)/shard_map/pallas_call | solution.py:188
  20.5 11.1 %all_to_all.5.held_ref = bf16[8,4,8,256]{3,2,1,0:T(8,128)(2,1)S(1)} all-to-all(bf16[8,4,8,256]{3,2,1,0:T(8,128)(2,1)S(1)} %bitcast.7), channel_id=1, replica_groups=mesh['rollout'=2,'frame'=2,'seq'=8] {'seq'}, dimensions={0} | all-to-all | bytes 262144 | tf_op jit(solution)/shard_map/all_to_all | solution.py:196
  31.6 0.7 %shard_map.67 = bf16[4,8,8,256]{3,2,1,0:T(8,128)(2,1)} custom-call(bf16[8,4,8,256]{3,2,1,0:T(8,128)(2,1)S(1)} %all_to_all.5.held_ref), custom_call_target="tpu_custom_call" | custom-call | tf_op jit(solution)/shard_map/pallas_call | solution.py:197
Async XLA Ops:
  1.2 9.8 %collective-permute-start = (bf16[3,32,256]{2,1,0:T(8,128)(2,1)S(1)}, bf16[3,32,256]{2,1,0:T(8,128)(2,1)S(1)}, u32[]{:S(2)}, u32[]{:S(2)}) collective-permute-start(bf16[3,32,256]{2,1,0:T(8,128)(2,1)S(1)} %get-tuple-element.19), channel_id=1, source_target_pairs={{0,2},{1,3},{2,0},{3,1},{4,6},{5,7},{6,4},{7,5},{8,10},{9,11},{10,... | collective-permute-start | bytes 147464 | tf_op jit(solution)/shard_map/ppermute | solution.py:170
  4.3 8.8 %collective-permute-start.1 = (bf16[3,32,256]{2,1,0:T(8,128)(2,1)S(1)}, bf16[3,32,256]{2,1,0:T(8,128)(2,1)S(1)}, u32[]{:S(2)}, u32[]{:S(2)}) collective-permute-start(bf16[3,32,256]{2,1,0:T(8,128)(2,1)S(1)} %get-tuple-element.20), channel_id=1, source_target_pairs={{0,6},{1,7},{2,4},{3,5},{4,2},{5,3},{6,0},{7,1},{8,14},{9,15},{10,... | collective-permute-start | bytes 147464 | tf_op jit(solution)/shard_map/ppermute | solution.py:170
  6.8 7.7 %collective-permute-start.2 = (bf16[3,32,256]{2,1,0:T(8,128)(2,1)S(1)}, bf16[3,32,256]{2,1,0:T(8,128)(2,1)S(1)}, u32[]{:S(2)}, u32[]{:S(2)}) collective-permute-start(bf16[3,32,256]{2,1,0:T(8,128)(2,1)S(1)} %get-tuple-element.21), channel_id=1, source_target_pairs={{0,4},{1,5},{2,6},{3,7},{4,0},{5,1},{6,2},{7,3},{8,12},{9,13},{10,... | collective-permute-start | bytes 147464 | tf_op jit(solution)/shard_map/ppermute | solution.py:170
  6.9 7.6 %collective-permute-start.3 = (bf16[3,32,256]{2,1,0:T(8,128)(2,1)S(1)}, bf16[3,32,256]{2,1,0:T(8,128)(2,1)S(1)}, u32[]{:S(2)}, u32[]{:S(2)}) collective-permute-start(bf16[3,32,256]{2,1,0:T(8,128)(2,1)S(1)} %get-tuple-element.22), channel_id=1, source_target_pairs={{0,7},{1,6},{2,5},{3,4},{4,3},{5,2},{6,1},{7,0},{8,15},{9,14},{10,... | collective-permute-start | bytes 147464 | tf_op jit(solution)/shard_map/ppermute | solution.py:170
  10.7 6.6 %collective-permute-start.4 = (bf16[3,32,256]{2,1,0:T(8,128)(2,1)S(1)}, bf16[3,32,256]{2,1,0:T(8,128)(2,1)S(1)}, u32[]{:S(2)}, u32[]{:S(2)}) collective-permute-start(bf16[3,32,256]{2,1,0:T(8,128)(2,1)S(1)} %get-tuple-element.23), channel_id=1, source_target_pairs={{0,5},{1,4},{2,7},{3,6},{4,1},{5,0},{6,3},{7,2},{8,13},{9,12},{10,... | collective-permute-start | bytes 147464 | tf_op jit(solution)/shard_map/ppermute | solution.py:170
  11.0 6.3 %collective-permute-start.5 = (bf16[3,32,256]{2,1,0:T(8,128)(2,1)S(1)}, bf16[3,32,256]{2,1,0:T(8,128)(2,1)S(1)}, u32[]{:S(2)}, u32[]{:S(2)}) collective-permute-start(bf16[3,32,256]{2,1,0:T(8,128)(2,1)S(1)} %get-tuple-element.25), channel_id=1, source_target_pairs={{0,3},{1,2},{2,1},{3,0},{4,7},{5,6},{6,5},{7,4},{8,11},{9,10},{10,... | collective-permute-start | bytes 147464 | tf_op jit(solution)/shard_map/ppermute | solution.py:170
  13.1 4.7 %collective-permute-start.6 = (bf16[3,32,256]{2,1,0:T(8,128)(2,1)S(1)}, bf16[3,32,256]{2,1,0:T(8,128)(2,1)S(1)}, u32[]{:S(2)}, u32[]{:S(2)}) collective-permute-start(bf16[3,32,256]{2,1,0:T(8,128)(2,1)S(1)} %get-tuple-element.26), channel_id=1, source_target_pairs={{0,1},{1,0},{2,3},{3,2},{4,5},{5,4},{6,7},{7,6},{8,9},{9,8},{10,11... | collective-permute-start | bytes 147464 | tf_op jit(solution)/shard_map/ppermute | solution.py:170
  18.2 1.6 %collective-permute-start.7 = (bf16[8,2,32,256]{3,2,1,0:T(8,128)(2,1)S(1)}, bf16[8,2,32,256]{3,2,1,0:T(8,128)(2,1)S(1)}, u32[]{:S(2)}, u32[]{:S(2)}) collective-permute-start(bf16[8,2,32,256]{3,2,1,0:T(8,128)(2,1)S(1)} %shard_map.65), channel_id=1, source_target_pairs={{0,8},{8,0},{1,9},{9,1},{2,10},{10,2},{3,11},{11,3},{4,12},{12,4},... | collective-permute-start | bytes 786440 | tf_op jit(solution)/shard_map/ppermute | solution.py:185

commit v18 on v17

--- a/solution.py
+++ b/solution.py
@@ -17,10 +17,12 @@
 
 
 def send_order(devices):
-    return sorted(
-        range(devices),
-        key=lambda away: (away != 2, -(2 * away // devices), away % 2, -away),
-    )
+    half = devices // 2
+    far = [*range(half + 1, devices), half][:half]
+    order = far[:1]
+    for pair in zip(far[1:], range(half - 1, 0, -1)):
+        order += pair
+    return order + [0]
 
 
 def run(copies):

time: 32.5 us -> 32.2 us (level)
  waiting for transfers between devices: 5.72 us -> 5.08 us
    ppermute x7, waiting for transfers between devices: 4.2 us -> 3.56 us  [whole_heads(): lax.ppermute(piece, 'seq', [(one, one ^ away) for one in range(devices)])]
  transfers between devices with their start and end apart: 8 -> 8, of which waited for: 4 -> 5; matrix products, arithmetic and copies ran while one was open for 0% -> 0% of each run, Pallas kernels for 0% -> 0%
where the time goes in v18:
time: 32.2 us; the launch traced here: 32 us
  starting transfers between devices  12.5 us (39%)
  blocking collectives  11.4 us (35%)
  waiting for transfers between devices  5.08 us (16%)
  Pallas kernels  2.96 us (9%)
    ppermute x7, starting transfers between devices, whole_heads(): lax.ppermute(piece, 'seq', [(one, one ^ away) for one in range(devices)])  12.4 us
    all_to_all x1, blocking collectives, whole_heads(): lax.all_to_all(answer, 'seq', split_axis=0, concat_axis=0, tiled=True)  11.4 us
    ppermute x7, waiting for transfers between devices, whole_heads(): lax.ppermute(piece, 'seq', [(one, one ^ away) for one in range(devices)])  3.56 us
    ppermute x1, waiting for transfers between devices, whole_heads(): lax.ppermute(stacked, 'frame', [(one, (one - away) % groups) for one in r...  1.52 us
    pallas_call x1, Pallas kernels, whole_heads(): pl.pallas_call(pack, out_shape=[jax.ShapeDtypeStruct((3, rows, width), qu...  1.2 us
    pallas_call x1, Pallas kernels, whole_heads(): pl.pallas_call(functools.partial(attend, tokens=tokens), out_shape=jax.Sh...  0.69 us
    pallas_call x1, Pallas kernels, whole_heads(): pl.pallas_call(unpack, out_shape=jax.ShapeDtypeStruct((local_frames, devi...  0.68 us
  transfers between devices with their start and end apart: 8, of which 5 were waited for; matrix products, arithmetic and copies ran while one was open for 0% of the time, Pallas kernels for 0%

profile of v18, /device:TPU:0, one launch (start us, length us, event | category | flops | bytes accessed | tf_op | source)
XLA Modules:
  0.0 32.0 jit_solution(17076063823790627149)
XLA Ops:
  0.0 1.2 %shard_map.64 = (bf16[3,32,256]{2,1,0:T(8,128)(2,1)S(1)}, bf16[3,32,256]{2,1,0:T(8,128)(2,1)S(1)}, bf16[3,32,256]{2,1,0:T(8,128)(2,1)S(1)}, bf16[3,32,256]{2,1,0...) custom-call(bf16[32,2048]{1,0:T(8,128)(2,1)} %bitcast.8, ...), custom_call_target="tpu_custom_call" | custom-call | tf_op jit(solution)/shard_map/pallas_call | solution.py:155
  1.2 5.0 %collective-permute-start = (bf16[3,32,256]{2,1,0:T(8,128)(2,1)S(1)}, bf16[3,32,256]{2,1,0:T(8,128)(2,1)S(1)}, u32[]{:S(2)}, u32[]{:S(2)}) collective-permute-start(bf16[3,32,256]{2,1,0:T(8,128)(2,1)S(1)} %get-tuple-element.19), channel_id=1, source_target_pairs={{0,5},{1,4},{2,7},{3,6},{4,1},{5,0},{6,3},{7,2},{8,13},{9,12},{10,... | collective-permute-start | bytes 147464 | tf_op jit(solution)/shard_map/ppermute | solution.py:172
  6.2 1.3 %collective-permute-start.1 = (bf16[3,32,256]{2,1,0:T(8,128)(2,1)S(1)}, bf16[3,32,256]{2,1,0:T(8,128)(2,1)S(1)}, u32[]{:S(2)}, u32[]{:S(2)}) collective-permute-start(bf16[3,32,256]{2,1,0:T(8,128)(2,1)S(1)} %get-tuple-element.20), channel_id=1, source_target_pairs={{0,6},{1,7},{2,4},{3,5},{4,2},{5,3},{6,0},{7,1},{8,14},{9,15},{10,... | collective-permute-start | bytes 147464 | tf_op jit(solution)/shard_map/ppermute | solution.py:172
  7.6 0.2 collective-permute-start.2
  7.8 3.8 %collective-permute-start.3 = (bf16[3,32,256]{2,1,0:T(8,128)(2,1)S(1)}, bf16[3,32,256]{2,1,0:T(8,128)(2,1)S(1)}, u32[]{:S(2)}, u32[]{:S(2)}) collective-permute-start(bf16[3,32,256]{2,1,0:T(8,128)(2,1)S(1)} %get-tuple-element.22), channel_id=1, source_target_pairs={{0,7},{1,6},{2,5},{3,4},{4,3},{5,2},{6,1},{7,0},{8,15},{9,14},{10,... | collective-permute-start | bytes 147464 | tf_op jit(solution)/shard_map/ppermute | solution.py:172
  11.6 0.5 %collective-permute-start.4 = (bf16[3,32,256]{2,1,0:T(8,128)(2,1)S(1)}, bf16[3,32,256]{2,1,0:T(8,128)(2,1)S(1)}, u32[]{:S(2)}, u32[]{:S(2)}) collective-permute-start(bf16[3,32,256]{2,1,0:T(8,128)(2,1)S(1)} %get-tuple-element.23), channel_id=1, source_target_pairs={{0,2},{1,3},{2,0},{3,1},{4,6},{5,7},{6,4},{7,5},{8,10},{9,11},{10,... | collective-permute-start | bytes 147464 | tf_op jit(solution)/shard_map/ppermute | solution.py:172
  12.1 0.0 collective-permute-done.refs_0_
  12.1 1.0 %collective-permute-start.5 = (bf16[3,32,256]{2,1,0:T(8,128)(2,1)S(1)}, bf16[3,32,256]{2,1,0:T(8,128)(2,1)S(1)}, u32[]{:S(2)}, u32[]{:S(2)}) collective-permute-start(bf16[3,32,256]{2,1,0:T(8,128)(2,1)S(1)} %get-tuple-element.24), channel_id=1, source_target_pairs={{0,4},{1,5},{2,6},{3,7},{4,0},{5,1},{6,2},{7,3},{8,12},{9,13},{10,... | collective-permute-start | bytes 147464 | tf_op jit(solution)/shard_map/ppermute | solution.py:172
  13.1 0.0 collective-permute-done.1.refs_1_
  13.1 0.5 %collective-permute-start.6 = (bf16[3,32,256]{2,1,0:T(8,128)(2,1)S(1)}, bf16[3,32,256]{2,1,0:T(8,128)(2,1)S(1)}, u32[]{:S(2)}, u32[]{:S(2)}) collective-permute-start(bf16[3,32,256]{2,1,0:T(8,128)(2,1)S(1)} %get-tuple-element.25), channel_id=1, source_target_pairs={{0,1},{1,0},{2,3},{3,2},{4,5},{5,4},{6,7},{7,6},{8,9},{9,8},{10,11... | collective-permute-start | bytes 147464 | tf_op jit(solution)/shard_map/ppermute | solution.py:172
  13.6 0.0 collective-permute-done.2.refs_2_
  13.7 1.2 %collective-permute-done.3.refs_3_ = bf16[3,32,256]{2,1,0:T(8,128)(2,1)S(1)} collective-permute-done((bf16[3,32,256]{2,1,0:T(8,128)(2,1)S(1)}, bf16[3,32,256]{2,1,0:T(8,128)(2,1)S(1)}, u32[]{:S(2)}, u32[]{:S(2)}) %collective-permute-start.3) | collective-permute-done | bytes 49184 | tf_op jit(solution)/shard_map/ppermute | solution.py:172
  14.8 0.9 %collective-permute-done.4.refs_4_ = bf16[3,32,256]{2,1,0:T(8,128)(2,1)S(1)} collective-permute-done((bf16[3,32,256]{2,1,0:T(8,128)(2,1)S(1)}, bf16[3,32,256]{2,1,0:T(8,128)(2,1)S(1)}, u32[]{:S(2)}, u32[]{:S(2)}) %collective-permute-start.4) | collective-permute-done | bytes 49184 | tf_op jit(solution)/shard_map/ppermute | solution.py:172
  15.7 1.4 %collective-permute-done.5.refs_5_ = bf16[3,32,256]{2,1,0:T(8,128)(2,1)S(1)} collective-permute-done((bf16[3,32,256]{2,1,0:T(8,128)(2,1)S(1)}, bf16[3,32,256]{2,1,0:T(8,128)(2,1)S(1)}, u32[]{:S(2)}, u32[]{:S(2)}) %collective-permute-start.5) | collective-permute-done | bytes 49184 | tf_op jit(solution)/shard_map/ppermute | solution.py:172
  17.1 0.1 collective-permute-done.6.refs_6_
  17.2 0.4 %shard_map.65 = bf16[8,2,32,256]{3,2,1,0:T(8,128)(2,1)S(1)} custom-call(bf16[3,32,256]{2,1,0:T(8,128)(2,1)S(1)} %collective-permute-done.refs_0_, bf16[3,32,256]{2,1,0:T(8,128)(2,1)S(1)} %collective-permute-done.1.refs_1_, bf16[3,32,256]{2,1,0:T(8,128)(2,1)S(1)} %collective-permute-done.2.refs_2_, bf16[3,32,256]{2,1,0:T(8,128)(2,1)S(1)} %collective-permute-done.3.refs_3_, ...), custom_call_target="tpu_custom_call" | custom-call | tf_op jit(solution)/shard_map/pallas_call | solution.py:178
  17.6 0.1 collective-permute-start.7
  17.7 1.5 %collective-permute-done.7.refs_8_ = bf16[8,2,32,256]{3,2,1,0:T(8,128)(2,1)S(1)} collective-permute-done((bf16[8,2,32,256]{3,2,1,0:T(8,128)(2,1)S(1)}, bf16[8,2,32,256]{3,2,1,0:T(8,128)(2,1)S(1)}, u32[]{:S(2)}, u32[]{:S(2)}) %collective-permute-start.7) | collective-permute-done | bytes 262176 | tf_op jit(solution)/shard_map/ppermute | solution.py:187
  19.2 0.7 %shard_map.66 = bf16[8,32,256]{2,1,0:T(8,128)(2,1)S(1)} custom-call(s32[2,4]{1,0:T(2,128)S(1)} %get-tuple-element.16.slot_ref, s32[2,4]{1,0:T(2,128)S(1)} %get-tuple-element.17.level_ref, f32[8,256]{1,0:T(8,128)S(1)} %get-tuple-element.18.gate_ref, bf16[3,32,256]{2,1,0:T(8,128)(2,1)S(1)} %collective-permute-done.refs_0_, ...), custom_call_target="tpu_custom_call" | custom-call | tf_op jit(solution)/shard_map/pallas_call | solution.py:190
  19.9 11.4 %all_to_all.5.held_ref = bf16[8,4,8,256]{3,2,1,0:T(8,128)(2,1)S(1)} all-to-all(bf16[8,4,8,256]{3,2,1,0:T(8,128)(2,1)S(1)} %bitcast.7), channel_id=1, replica_groups=mesh['rollout'=2,'frame'=2,'seq'=8] {'seq'}, dimensions={0} | all-to-all | bytes 262144 | tf_op jit(solution)/shard_map/all_to_all | solution.py:198
  31.3 0.7 %shard_map.67 = bf16[4,8,8,256]{3,2,1,0:T(8,128)(2,1)} custom-call(bf16[8,4,8,256]{3,2,1,0:T(8,128)(2,1)S(1)} %all_to_all.5.held_ref), custom_call_target="tpu_custom_call" | custom-call | tf_op jit(solution)/shard_map/pallas_call | solution.py:199
Async XLA Ops:
  1.2 10.9 %collective-permute-start = (bf16[3,32,256]{2,1,0:T(8,128)(2,1)S(1)}, bf16[3,32,256]{2,1,0:T(8,128)(2,1)S(1)}, u32[]{:S(2)}, u32[]{:S(2)}) collective-permute-start(bf16[3,32,256]{2,1,0:T(8,128)(2,1)S(1)} %get-tuple-element.19), channel_id=1, source_target_pairs={{0,5},{1,4},{2,7},{3,6},{4,1},{5,0},{6,3},{7,2},{8,13},{9,12},{10,... | collective-permute-start | bytes 147464 | tf_op jit(solution)/shard_map/ppermute | solution.py:172
  6.2 6.9 %collective-permute-start.1 = (bf16[3,32,256]{2,1,0:T(8,128)(2,1)S(1)}, bf16[3,32,256]{2,1,0:T(8,128)(2,1)S(1)}, u32[]{:S(2)}, u32[]{:S(2)}) collective-permute-start(bf16[3,32,256]{2,1,0:T(8,128)(2,1)S(1)} %get-tuple-element.20), channel_id=1, source_target_pairs={{0,6},{1,7},{2,4},{3,5},{4,2},{5,3},{6,0},{7,1},{8,14},{9,15},{10,... | collective-permute-start | bytes 147464 | tf_op jit(solution)/shard_map/ppermute | solution.py:172
  7.6 6.1 %collective-permute-start.2 = (bf16[3,32,256]{2,1,0:T(8,128)(2,1)S(1)}, bf16[3,32,256]{2,1,0:T(8,128)(2,1)S(1)}, u32[]{:S(2)}, u32[]{:S(2)}) collective-permute-start(bf16[3,32,256]{2,1,0:T(8,128)(2,1)S(1)} %get-tuple-element.21), channel_id=1, source_target_pairs={{0,3},{1,2},{2,1},{3,0},{4,7},{5,6},{6,5},{7,4},{8,11},{9,10},{10,... | collective-permute-start | bytes 147464 | tf_op jit(solution)/shard_map/ppermute | solution.py:172
  7.8 7.1 %collective-permute-start.3 = (bf16[3,32,256]{2,1,0:T(8,128)(2,1)S(1)}, bf16[3,32,256]{2,1,0:T(8,128)(2,1)S(1)}, u32[]{:S(2)}, u32[]{:S(2)}) collective-permute-start(bf16[3,32,256]{2,1,0:T(8,128)(2,1)S(1)} %get-tuple-element.22), channel_id=1, source_target_pairs={{0,7},{1,6},{2,5},{3,4},{4,3},{5,2},{6,1},{7,0},{8,15},{9,14},{10,... | collective-permute-start | bytes 147464 | tf_op jit(solution)/shard_map/ppermute | solution.py:172
  11.6 4.1 %collective-permute-start.4 = (bf16[3,32,256]{2,1,0:T(8,128)(2,1)S(1)}, bf16[3,32,256]{2,1,0:T(8,128)(2,1)S(1)}, u32[]{:S(2)}, u32[]{:S(2)}) collective-permute-start(bf16[3,32,256]{2,1,0:T(8,128)(2,1)S(1)} %get-tuple-element.23), channel_id=1, source_target_pairs={{0,2},{1,3},{2,0},{3,1},{4,6},{5,7},{6,4},{7,5},{8,10},{9,11},{10,... | collective-permute-start | bytes 147464 | tf_op jit(solution)/shard_map/ppermute | solution.py:172
  12.1 5.0 %collective-permute-start.5 = (bf16[3,32,256]{2,1,0:T(8,128)(2,1)S(1)}, bf16[3,32,256]{2,1,0:T(8,128)(2,1)S(1)}, u32[]{:S(2)}, u32[]{:S(2)}) collective-permute-start(bf16[3,32,256]{2,1,0:T(8,128)(2,1)S(1)} %get-tuple-element.24), channel_id=1, source_target_pairs={{0,4},{1,5},{2,6},{3,7},{4,0},{5,1},{6,2},{7,3},{8,12},{9,13},{10,... | collective-permute-start | bytes 147464 | tf_op jit(solution)/shard_map/ppermute | solution.py:172
  13.1 4.1 %collective-permute-start.6 = (bf16[3,32,256]{2,1,0:T(8,128)(2,1)S(1)}, bf16[3,32,256]{2,1,0:T(8,128)(2,1)S(1)}, u32[]{:S(2)}, u32[]{:S(2)}) collective-permute-start(bf16[3,32,256]{2,1,0:T(8,128)(2,1)S(1)} %get-tuple-element.25), channel_id=1, source_target_pairs={{0,1},{1,0},{2,3},{3,2},{4,5},{5,4},{6,7},{7,6},{8,9},{9,8},{10,11... | collective-permute-start | bytes 147464 | tf_op jit(solution)/shard_map/ppermute | solution.py:172
  17.6 1.6 %collective-permute-start.7 = (bf16[8,2,32,256]{3,2,1,0:T(8,128)(2,1)S(1)}, bf16[8,2,32,256]{3,2,1,0:T(8,128)(2,1)S(1)}, u32[]{:S(2)}, u32[]{:S(2)}) collective-permute-start(bf16[8,2,32,256]{3,2,1,0:T(8,128)(2,1)S(1)} %shard_map.65), channel_id=1, source_target_pairs={{0,8},{8,0},{1,9},{9,1},{2,10},{10,2},{3,11},{11,3},{4,12},{12,4},... | collective-permute-start | bytes 786440 | tf_op jit(solution)/shard_map/ppermute | solution.py:187

commit v19 on v18

--- a/solution.py
+++ b/solution.py
@@ -19,10 +19,8 @@
 def send_order(devices):
     half = devices // 2
     far = [*range(half + 1, devices), half][:half]
-    order = far[:1]
-    for pair in zip(far[1:], range(half - 1, 0, -1)):
-        order += pair
-    return order + [0]
+    far[:2] = far[1::-1]
+    return far + [*range(half - 1, 0, -1)] + [0]
 
 
 def run(copies):
@@ -62,13 +60,9 @@
 
 
 def stack(*refs):
-    *pieces, out_ref, sems = refs
-    run(
-        [
-            pltpu.make_async_copy(ref.at[pl.ds(1, 2)], out_ref.at[number], sems.at[number])
-            for number, ref in enumerate(pieces)
-        ]
-    )
+    *pieces, out_ref = refs
+    for number, ref in enumerate(pieces):
+        out_ref[number] = ref[1:3]
 
 
 def unpack(held_ref, out_ref, sems):
@@ -180,7 +174,6 @@
         out_shape=jax.ShapeDtypeStruct((devices, 2, rows, width), queries.dtype),
         in_specs=[VMEM] * devices,
         out_specs=VMEM,
-        scratch_shapes=[pltpu.SemaphoreType.DMA((devices,))],
         compiler_params=PARAMS,
     )(*pieces)
     stacks = [

time: 32.2 us -> 32.5 us (level)
  starting transfers between devices: 12.5 us -> 13.7 us
  waiting for transfers between devices: 5.08 us -> 4.19 us
  Pallas kernels: 2.96 us -> 2.58 us
    ppermute x7, starting transfers between devices: 12.4 us -> 13.7 us  [whole_heads(): lax.ppermute(piece, 'seq', [(one, one ^ away) for one in range(devices)])]
    ppermute x7, waiting for transfers between devices: 3.56 us -> 2.67 us  [whole_heads(): lax.ppermute(piece, 'seq', [(one, one ^ away) for one in range(devices)])]
    pallas_call x1, Pallas kernels: 0.39 us -> 0.02 us  [whole_heads(): pl.pallas_call(stack, out_shape=jax.ShapeDtypeStruct((devices, 2, rows, w...]
where the time goes in v19:
time: 32.5 us; the launch traced here: 32.2 us
  starting transfers between devices  13.7 us (42%)
  blocking collectives  11.7 us (36%)
  waiting for transfers between devices  4.19 us (13%)
  Pallas kernels  2.58 us (8%)
    ppermute x7, starting transfers between devices, whole_heads(): lax.ppermute(piece, 'seq', [(one, one ^ away) for one in range(devices)])  13.7 us
    all_to_all x1, blocking collectives, whole_heads(): lax.all_to_all(answer, 'seq', split_axis=0, concat_axis=0, tiled=True)  11.7 us
    ppermute x7, waiting for transfers between devices, whole_heads(): lax.ppermute(piece, 'seq', [(one, one ^ away) for one in range(devices)])  2.67 us
    ppermute x1, waiting for transfers between devices, whole_heads(): lax.ppermute(stacked, 'frame', [(one, (one - away) % groups) for one in r...  1.52 us
    pallas_call x1, Pallas kernels, whole_heads(): pl.pallas_call(pack, out_shape=[jax.ShapeDtypeStruct((3, rows, width), qu...  1.2 us
    pallas_call x1, Pallas kernels, whole_heads(): pl.pallas_call(functools.partial(attend, tokens=tokens), out_shape=jax.Sh...  0.69 us
    pallas_call x1, Pallas kernels, whole_heads(): pl.pallas_call(unpack, out_shape=jax.ShapeDtypeStruct((local_frames, devi...  0.68 us
  transfers between devices with their start and end apart: 8, of which 5 were waited for; matrix products, arithmetic and copies ran while one was open for 0% of the time, Pallas kernels for 0%

profile of v19, /device:TPU:0, one launch (start us, length us, event | category | flops | bytes accessed | tf_op | source)
XLA Modules:
  0.0 32.2 jit_solution(5364428719391660422)
XLA Ops:
  0.0 1.2 %shard_map.64 = (bf16[3,32,256]{2,1,0:T(8,128)(2,1)S(1)}, bf16[3,32,256]{2,1,0:T(8,128)(2,1)S(1)}, bf16[3,32,256]{2,1,0:T(8,128)(2,1)S(1)}, bf16[3,32,256]{2,1,0...) custom-call(bf16[32,2048]{1,0:T(8,128)(2,1)} %bitcast.8, ...), custom_call_target="tpu_custom_call" | custom-call | tf_op jit(solution)/shard_map/pallas_call | solution.py:149
  1.2 5.1 %collective-permute-start = (bf16[3,32,256]{2,1,0:T(8,128)(2,1)S(1)}, bf16[3,32,256]{2,1,0:T(8,128)(2,1)S(1)}, u32[]{:S(2)}, u32[]{:S(2)}) collective-permute-start(bf16[3,32,256]{2,1,0:T(8,128)(2,1)S(1)} %get-tuple-element.19), channel_id=1, source_target_pairs={{0,6},{1,7},{2,4},{3,5},{4,2},{5,3},{6,0},{7,1},{8,14},{9,15},{10,... | collective-permute-start | bytes 147464 | tf_op jit(solution)/shard_map/ppermute | solution.py:166
  6.3 0.4 %collective-permute-start.1 = (bf16[3,32,256]{2,1,0:T(8,128)(2,1)S(1)}, bf16[3,32,256]{2,1,0:T(8,128)(2,1)S(1)}, u32[]{:S(2)}, u32[]{:S(2)}) collective-permute-start(bf16[3,32,256]{2,1,0:T(8,128)(2,1)S(1)} %get-tuple-element.20), channel_id=1, source_target_pairs={{0,5},{1,4},{2,7},{3,6},{4,1},{5,0},{6,3},{7,2},{8,13},{9,12},{10,... | collective-permute-start | bytes 147464 | tf_op jit(solution)/shard_map/ppermute | solution.py:166
  6.7 2.4 %collective-permute-start.2 = (bf16[3,32,256]{2,1,0:T(8,128)(2,1)S(1)}, bf16[3,32,256]{2,1,0:T(8,128)(2,1)S(1)}, u32[]{:S(2)}, u32[]{:S(2)}) collective-permute-start(bf16[3,32,256]{2,1,0:T(8,128)(2,1)S(1)} %get-tuple-element.21), channel_id=1, source_target_pairs={{0,7},{1,6},{2,5},{3,4},{4,3},{5,2},{6,1},{7,0},{8,15},{9,14},{10,... | collective-permute-start | bytes 147464 | tf_op jit(solution)/shard_map/ppermute | solution.py:166
  9.1 1.0 %collective-permute-start.3 = (bf16[3,32,256]{2,1,0:T(8,128)(2,1)S(1)}, bf16[3,32,256]{2,1,0:T(8,128)(2,1)S(1)}, u32[]{:S(2)}, u32[]{:S(2)}) collective-permute-start(bf16[3,32,256]{2,1,0:T(8,128)(2,1)S(1)} %get-tuple-element.22), channel_id=1, source_target_pairs={{0,4},{1,5},{2,6},{3,7},{4,0},{5,1},{6,2},{7,3},{8,12},{9,13},{10,... | collective-permute-start | bytes 147464 | tf_op jit(solution)/shard_map/ppermute | solution.py:166
  10.2 1.8 %collective-permute-start.4 = (bf16[3,32,256]{2,1,0:T(8,128)(2,1)S(1)}, bf16[3,32,256]{2,1,0:T(8,128)(2,1)S(1)}, u32[]{:S(2)}, u32[]{:S(2)}) collective-permute-start(bf16[3,32,256]{2,1,0:T(8,128)(2,1)S(1)} %get-tuple-element.23), channel_id=1, source_target_pairs={{0,3},{1,2},{2,1},{3,0},{4,7},{5,6},{6,5},{7,4},{8,11},{9,10},{10,... | collective-permute-start | bytes 147464 | tf_op jit(solution)/shard_map/ppermute | solution.py:166
  12.0 0.0 collective-permute-done.refs_0_
  12.0 0.5 %collective-permute-start.5 = (bf16[3,32,256]{2,1,0:T(8,128)(2,1)S(1)}, bf16[3,32,256]{2,1,0:T(8,128)(2,1)S(1)}, u32[]{:S(2)}, u32[]{:S(2)}) collective-permute-start(bf16[3,32,256]{2,1,0:T(8,128)(2,1)S(1)} %get-tuple-element.24), channel_id=1, source_target_pairs={{0,2},{1,3},{2,0},{3,1},{4,6},{5,7},{6,4},{7,5},{8,10},{9,11},{10,... | collective-permute-start | bytes 147464 | tf_op jit(solution)/shard_map/ppermute | solution.py:166
  12.4 0.6 %collective-permute-done.1.refs_1_ = bf16[3,32,256]{2,1,0:T(8,128)(2,1)S(1)} collective-permute-done((bf16[3,32,256]{2,1,0:T(8,128)(2,1)S(1)}, bf16[3,32,256]{2,1,0:T(8,128)(2,1)S(1)}, u32[]{:S(2)}, u32[]{:S(2)}) %collective-permute-start.1) | collective-permute-done | bytes 49184 | tf_op jit(solution)/shard_map/ppermute | solution.py:166
  13.0 2.5 %collective-permute-start.6 = (bf16[3,32,256]{2,1,0:T(8,128)(2,1)S(1)}, bf16[3,32,256]{2,1,0:T(8,128)(2,1)S(1)}, u32[]{:S(2)}, u32[]{:S(2)}) collective-permute-start(bf16[3,32,256]{2,1,0:T(8,128)(2,1)S(1)} %get-tuple-element.25), channel_id=1, source_target_pairs={{0,1},{1,0},{2,3},{3,2},{4,5},{5,4},{6,7},{7,6},{8,9},{9,8},{10,11... | collective-permute-start | bytes 147464 | tf_op jit(solution)/shard_map/ppermute | solution.py:166
  15.5 0.0 collective-permute-done.2.refs_2_
  15.5 0.7 %collective-permute-done.3.refs_3_ = bf16[3,32,256]{2,1,0:T(8,128)(2,1)S(1)} collective-permute-done((bf16[3,32,256]{2,1,0:T(8,128)(2,1)S(1)}, bf16[3,32,256]{2,1,0:T(8,128)(2,1)S(1)}, u32[]{:S(2)}, u32[]{:S(2)}) %collective-permute-start.3) | collective-permute-done | bytes 49184 | tf_op jit(solution)/shard_map/ppermute | solution.py:166
  16.1 0.0 collective-permute-done.4.refs_4_
  16.1 0.4 %collective-permute-done.5.refs_5_ = bf16[3,32,256]{2,1,0:T(8,128)(2,1)S(1)} collective-permute-done((bf16[3,32,256]{2,1,0:T(8,128)(2,1)S(1)}, bf16[3,32,256]{2,1,0:T(8,128)(2,1)S(1)}, u32[]{:S(2)}, u32[]{:S(2)}) %collective-permute-start.5) | collective-permute-done | bytes 49184 | tf_op jit(solution)/shard_map/ppermute | solution.py:166
  16.6 1.0 %collective-permute-done.6.refs_6_ = bf16[3,32,256]{2,1,0:T(8,128)(2,1)S(1)} collective-permute-done((bf16[3,32,256]{2,1,0:T(8,128)(2,1)S(1)}, bf16[3,32,256]{2,1,0:T(8,128)(2,1)S(1)}, u32[]{:S(2)}, u32[]{:S(2)}) %collective-permute-start.6) | collective-permute-done | bytes 49184 | tf_op jit(solution)/shard_map/ppermute | solution.py:166
  17.6 0.1 collective-permute-start.7
  17.6 1.5 %collective-permute-done.7.refs_8_ = bf16[8,2,32,256]{3,2,1,0:T(8,128)(2,1)S(1)} collective-permute-done((bf16[8,2,32,256]{3,2,1,0:T(8,128)(2,1)S(1)}, bf16[8,2,32,256]{3,2,1,0:T(8,128)(2,1)S(1)}, u32[]{:S(2)}, u32[]{:S(2)}) %collective-permute-start.7) | collective-permute-done | bytes 262176 | tf_op jit(solution)/shard_map/ppermute | solution.py:180
  19.2 0.7 %shard_map.66 = bf16[8,32,256]{2,1,0:T(8,128)(2,1)S(1)} custom-call(s32[2,4]{1,0:T(2,128)S(1)} %get-tuple-element.16.slot_ref, s32[2,4]{1,0:T(2,128)S(1)} %get-tuple-element.17.level_ref, f32[8,256]{1,0:T(8,128)S(1)} %get-tuple-element.18.gate_ref, bf16[3,32,256]{2,1,0:T(8,128)(2,1)S(1)} %collective-permute-done.refs_0_, ...), custom_call_target="tpu_custom_call" | custom-call | tf_op jit(solution)/shard_map/pallas_call | solution.py:183
  19.9 11.7 %all_to_all.5.held_ref = bf16[8,4,8,256]{3,2,1,0:T(8,128)(2,1)S(1)} all-to-all(bf16[8,4,8,256]{3,2,1,0:T(8,128)(2,1)S(1)} %bitcast.7), channel_id=1, replica_groups=mesh['rollout'=2,'frame'=2,'seq'=8] {'seq'}, dimensions={0} | all-to-all | bytes 262144 | tf_op jit(solution)/shard_map/all_to_all | solution.py:191
  31.6 0.7 %shard_map.67 = bf16[4,8,8,256]{3,2,1,0:T(8,128)(2,1)} custom-call(bf16[8,4,8,256]{3,2,1,0:T(8,128)(2,1)S(1)} %all_to_all.5.held_ref), custom_call_target="tpu_custom_call" | custom-call | tf_op jit(solution)/shard_map/pallas_call | solution.py:192
  (1 shorter events, 0.0 us)
Async XLA Ops:
  1.2 10.8 %collective-permute-start = (bf16[3,32,256]{2,1,0:T(8,128)(2,1)S(1)}, bf16[3,32,256]{2,1,0:T(8,128)(2,1)S(1)}, u32[]{:S(2)}, u32[]{:S(2)}) collective-permute-start(bf16[3,32,256]{2,1,0:T(8,128)(2,1)S(1)} %get-tuple-element.19), channel_id=1, source_target_pairs={{0,6},{1,7},{2,4},{3,5},{4,2},{5,3},{6,0},{7,1},{8,14},{9,15},{10,... | collective-permute-start | bytes 147464 | tf_op jit(solution)/shard_map/ppermute | solution.py:166
  6.3 6.7 %collective-permute-start.1 = (bf16[3,32,256]{2,1,0:T(8,128)(2,1)S(1)}, bf16[3,32,256]{2,1,0:T(8,128)(2,1)S(1)}, u32[]{:S(2)}, u32[]{:S(2)}) collective-permute-start(bf16[3,32,256]{2,1,0:T(8,128)(2,1)S(1)} %get-tuple-element.20), channel_id=1, source_target_pairs={{0,5},{1,4},{2,7},{3,6},{4,1},{5,0},{6,3},{7,2},{8,13},{9,12},{10,... | collective-permute-start | bytes 147464 | tf_op jit(solution)/shard_map/ppermute | solution.py:166
  6.7 8.8 %collective-permute-start.2 = (bf16[3,32,256]{2,1,0:T(8,128)(2,1)S(1)}, bf16[3,32,256]{2,1,0:T(8,128)(2,1)S(1)}, u32[]{:S(2)}, u32[]{:S(2)}) collective-permute-start(bf16[3,32,256]{2,1,0:T(8,128)(2,1)S(1)} %get-tuple-element.21), channel_id=1, source_target_pairs={{0,7},{1,6},{2,5},{3,4},{4,3},{5,2},{6,1},{7,0},{8,15},{9,14},{10,... | collective-permute-start | bytes 147464 | tf_op jit(solution)/shard_map/ppermute | solution.py:166
  9.1 7.0 %collective-permute-start.3 = (bf16[3,32,256]{2,1,0:T(8,128)(2,1)S(1)}, bf16[3,32,256]{2,1,0:T(8,128)(2,1)S(1)}, u32[]{:S(2)}, u32[]{:S(2)}) collective-permute-start(bf16[3,32,256]{2,1,0:T(8,128)(2,1)S(1)} %get-tuple-element.22), channel_id=1, source_target_pairs={{0,4},{1,5},{2,6},{3,7},{4,0},{5,1},{6,2},{7,3},{8,12},{9,13},{10,... | collective-permute-start | bytes 147464 | tf_op jit(solution)/shard_map/ppermute | solution.py:166
  10.2 6.0 %collective-permute-start.4 = (bf16[3,32,256]{2,1,0:T(8,128)(2,1)S(1)}, bf16[3,32,256]{2,1,0:T(8,128)(2,1)S(1)}, u32[]{:S(2)}, u32[]{:S(2)}) collective-permute-start(bf16[3,32,256]{2,1,0:T(8,128)(2,1)S(1)} %get-tuple-element.23), channel_id=1, source_target_pairs={{0,3},{1,2},{2,1},{3,0},{4,7},{5,6},{6,5},{7,4},{8,11},{9,10},{10,... | collective-permute-start | bytes 147464 | tf_op jit(solution)/shard_map/ppermute | solution.py:166
  12.0 4.6 %collective-permute-start.5 = (bf16[3,32,256]{2,1,0:T(8,128)(2,1)S(1)}, bf16[3,32,256]{2,1,0:T(8,128)(2,1)S(1)}, u32[]{:S(2)}, u32[]{:S(2)}) collective-permute-start(bf16[3,32,256]{2,1,0:T(8,128)(2,1)S(1)} %get-tuple-element.24), channel_id=1, source_target_pairs={{0,2},{1,3},{2,0},{3,1},{4,6},{5,7},{6,4},{7,5},{8,10},{9,11},{10,... | collective-permute-start | bytes 147464 | tf_op jit(solution)/shard_map/ppermute | solution.py:166
  13.0 4.5 %collective-permute-start.6 = (bf16[3,32,256]{2,1,0:T(8,128)(2,1)S(1)}, bf16[3,32,256]{2,1,0:T(8,128)(2,1)S(1)}, u32[]{:S(2)}, u32[]{:S(2)}) collective-permute-start(bf16[3,32,256]{2,1,0:T(8,128)(2,1)S(1)} %get-tuple-element.25), channel_id=1, source_target_pairs={{0,1},{1,0},{2,3},{3,2},{4,5},{5,4},{6,7},{7,6},{8,9},{9,8},{10,11... | collective-permute-start | bytes 147464 | tf_op jit(solution)/shard_map/ppermute | solution.py:166
  17.6 1.6 %collective-permute-start.7 = (bf16[8,2,32,256]{3,2,1,0:T(8,128)(2,1)S(1)}, bf16[8,2,32,256]{3,2,1,0:T(8,128)(2,1)S(1)}, u32[]{:S(2)}, u32[]{:S(2)}) collective-permute-start(bf16[8,2,32,256]{3,2,1,0:T(8,128)(2,1)S(1)} %shard_map.65), channel_id=1, source_target_pairs={{0,8},{8,0},{1,9},{9,1},{2,10},{10,2},{3,11},{11,3},{4,12},{12,4},... | collective-permute-start | bytes 786440 | tf_op jit(solution)/shard_map/ppermute | solution.py:180

commit v20 on v19

--- a/solution.py
+++ b/solution.py
@@ -19,8 +19,10 @@
 def send_order(devices):
     half = devices // 2
     far = [*range(half + 1, devices), half][:half]
-    far[:2] = far[1::-1]
-    return far + [*range(half - 1, 0, -1)] + [0]
+    order = far[:1]
+    for pair in zip(far[1:], range(half - 1, 0, -1)):
+        order += pair
+    return order + [0]
 
 
 def run(copies):

time: 32.5 us -> 31.8 us (0.978)
  starting transfers between devices: 13.7 us -> 12.5 us
  waiting for transfers between devices: 4.19 us -> 5.08 us
    ppermute x7, starting transfers between devices: 13.7 us -> 12.4 us  [whole_heads(): lax.ppermute(piece, 'seq', [(one, one ^ away) for one in range(devices)])]
    ppermute x7, waiting for transfers between devices: 2.67 us -> 3.56 us  [whole_heads(): lax.ppermute(piece, 'seq', [(one, one ^ away) for one in range(devices)])]
where the time goes in v20:
time: 31.8 us; the launch traced here: 31.6 us
  starting transfers between devices  12.5 us (39%)
  blocking collectives  11.4 us (36%)
  waiting for transfers between devices  5.08 us (16%)
  Pallas kernels  2.58 us (8%)
    ppermute x7, starting transfers between devices, whole_heads(): lax.ppermute(piece, 'seq', [(one, one ^ away) for one in range(devices)])  12.4 us
    all_to_all x1, blocking collectives, whole_heads(): lax.all_to_all(answer, 'seq', split_axis=0, concat_axis=0, tiled=True)  11.4 us
    ppermute x7, waiting for transfers between devices, whole_heads(): lax.ppermute(piece, 'seq', [(one, one ^ away) for one in range(devices)])  3.56 us
    ppermute x1, waiting for transfers between devices, whole_heads(): lax.ppermute(stacked, 'frame', [(one, (one - away) % groups) for one in r...  1.52 us
    pallas_call x1, Pallas kernels, whole_heads(): pl.pallas_call(pack, out_shape=[jax.ShapeDtypeStruct((3, rows, width), qu...  1.2 us
    pallas_call x1, Pallas kernels, whole_heads(): pl.pallas_call(functools.partial(attend, tokens=tokens), out_shape=jax.Sh...  0.69 us
    pallas_call x1, Pallas kernels, whole_heads(): pl.pallas_call(unpack, out_shape=jax.ShapeDtypeStruct((local_frames, devi...  0.68 us
  transfers between devices with their start and end apart: 8, of which 5 were waited for; matrix products, arithmetic and copies ran while one was open for 0% of the time, Pallas kernels for 0%

profile of v20, /device:TPU:0, one launch (start us, length us, event | category | flops | bytes accessed | tf_op | source)
XLA Modules:
  0.0 31.6 jit_solution(9539332915925895133)
XLA Ops:
  0.0 1.2 %shard_map.64 = (bf16[3,32,256]{2,1,0:T(8,128)(2,1)S(1)}, bf16[3,32,256]{2,1,0:T(8,128)(2,1)S(1)}, bf16[3,32,256]{2,1,0:T(8,128)(2,1)S(1)}, bf16[3,32,256]{2,1,0...) custom-call(bf16[32,2048]{1,0:T(8,128)(2,1)} %bitcast.8, ...), custom_call_target="tpu_custom_call" | custom-call | tf_op jit(solution)/shard_map/pallas_call | solution.py:151
  1.2 5.0 %collective-permute-start = (bf16[3,32,256]{2,1,0:T(8,128)(2,1)S(1)}, bf16[3,32,256]{2,1,0:T(8,128)(2,1)S(1)}, u32[]{:S(2)}, u32[]{:S(2)}) collective-permute-start(bf16[3,32,256]{2,1,0:T(8,128)(2,1)S(1)} %get-tuple-element.19), channel_id=1, source_target_pairs={{0,5},{1,4},{2,7},{3,6},{4,1},{5,0},{6,3},{7,2},{8,13},{9,12},{10,... | collective-permute-start | bytes 147464 | tf_op jit(solution)/shard_map/ppermute | solution.py:168
  6.2 1.3 %collective-permute-start.1 = (bf16[3,32,256]{2,1,0:T(8,128)(2,1)S(1)}, bf16[3,32,256]{2,1,0:T(8,128)(2,1)S(1)}, u32[]{:S(2)}, u32[]{:S(2)}) collective-permute-start(bf16[3,32,256]{2,1,0:T(8,128)(2,1)S(1)} %get-tuple-element.20), channel_id=1, source_target_pairs={{0,6},{1,7},{2,4},{3,5},{4,2},{5,3},{6,0},{7,1},{8,14},{9,15},{10,... | collective-permute-start | bytes 147464 | tf_op jit(solution)/shard_map/ppermute | solution.py:168
  7.6 0.2 collective-permute-start.2
  7.8 3.8 %collective-permute-start.3 = (bf16[3,32,256]{2,1,0:T(8,128)(2,1)S(1)}, bf16[3,32,256]{2,1,0:T(8,128)(2,1)S(1)}, u32[]{:S(2)}, u32[]{:S(2)}) collective-permute-start(bf16[3,32,256]{2,1,0:T(8,128)(2,1)S(1)} %get-tuple-element.22), channel_id=1, source_target_pairs={{0,7},{1,6},{2,5},{3,4},{4,3},{5,2},{6,1},{7,0},{8,15},{9,14},{10,... | collective-permute-start | bytes 147464 | tf_op jit(solution)/shard_map/ppermute | solution.py:168
  11.6 0.5 %collective-permute-start.4 = (bf16[3,32,256]{2,1,0:T(8,128)(2,1)S(1)}, bf16[3,32,256]{2,1,0:T(8,128)(2,1)S(1)}, u32[]{:S(2)}, u32[]{:S(2)}) collective-permute-start(bf16[3,32,256]{2,1,0:T(8,128)(2,1)S(1)} %get-tuple-element.23), channel_id=1, source_target_pairs={{0,2},{1,3},{2,0},{3,1},{4,6},{5,7},{6,4},{7,5},{8,10},{9,11},{10,... | collective-permute-start | bytes 147464 | tf_op jit(solution)/shard_map/ppermute | solution.py:168
  12.1 0.0 collective-permute-done.refs_0_
  12.1 1.0 %collective-permute-start.5 = (bf16[3,32,256]{2,1,0:T(8,128)(2,1)S(1)}, bf16[3,32,256]{2,1,0:T(8,128)(2,1)S(1)}, u32[]{:S(2)}, u32[]{:S(2)}) collective-permute-start(bf16[3,32,256]{2,1,0:T(8,128)(2,1)S(1)} %get-tuple-element.24), channel_id=1, source_target_pairs={{0,4},{1,5},{2,6},{3,7},{4,0},{5,1},{6,2},{7,3},{8,12},{9,13},{10,... | collective-permute-start | bytes 147464 | tf_op jit(solution)/shard_map/ppermute | solution.py:168
  13.1 0.0 collective-permute-done.1.refs_1_
  13.1 0.5 %collective-permute-start.6 = (bf16[3,32,256]{2,1,0:T(8,128)(2,1)S(1)}, bf16[3,32,256]{2,1,0:T(8,128)(2,1)S(1)}, u32[]{:S(2)}, u32[]{:S(2)}) collective-permute-start(bf16[3,32,256]{2,1,0:T(8,128)(2,1)S(1)} %get-tuple-element.25), channel_id=1, source_target_pairs={{0,1},{1,0},{2,3},{3,2},{4,5},{5,4},{6,7},{7,6},{8,9},{9,8},{10,11... | collective-permute-start | bytes 147464 | tf_op jit(solution)/shard_map/ppermute | solution.py:168
  13.6 0.0 collective-permute-done.2.refs_2_
  13.7 1.2 %collective-permute-done.3.refs_3_ = bf16[3,32,256]{2,1,0:T(8,128)(2,1)S(1)} collective-permute-done((bf16[3,32,256]{2,1,0:T(8,128)(2,1)S(1)}, bf16[3,32,256]{2,1,0:T(8,128)(2,1)S(1)}, u32[]{:S(2)}, u32[]{:S(2)}) %collective-permute-start.3) | collective-permute-done | bytes 49184 | tf_op jit(solution)/shard_map/ppermute | solution.py:168
  14.8 0.9 %collective-permute-done.4.refs_4_ = bf16[3,32,256]{2,1,0:T(8,128)(2,1)S(1)} collective-permute-done((bf16[3,32,256]{2,1,0:T(8,128)(2,1)S(1)}, bf16[3,32,256]{2,1,0:T(8,128)(2,1)S(1)}, u32[]{:S(2)}, u32[]{:S(2)}) %collective-permute-start.4) | collective-permute-done | bytes 49184 | tf_op jit(solution)/shard_map/ppermute | solution.py:168
  15.7 1.4 %collective-permute-done.5.refs_5_ = bf16[3,32,256]{2,1,0:T(8,128)(2,1)S(1)} collective-permute-done((bf16[3,32,256]{2,1,0:T(8,128)(2,1)S(1)}, bf16[3,32,256]{2,1,0:T(8,128)(2,1)S(1)}, u32[]{:S(2)}, u32[]{:S(2)}) %collective-permute-start.5) | collective-permute-done | bytes 49184 | tf_op jit(solution)/shard_map/ppermute | solution.py:168
  17.1 0.1 collective-permute-done.6.refs_6_
  17.2 0.1 collective-permute-start.7
  17.3 1.5 %collective-permute-done.7.refs_8_ = bf16[8,2,32,256]{3,2,1,0:T(8,128)(2,1)S(1)} collective-permute-done((bf16[8,2,32,256]{3,2,1,0:T(8,128)(2,1)S(1)}, bf16[8,2,32,256]{3,2,1,0:T(8,128)(2,1)S(1)}, u32[]{:S(2)}, u32[]{:S(2)}) %collective-permute-start.7) | collective-permute-done | bytes 262176 | tf_op jit(solution)/shard_map/ppermute | solution.py:182
  18.8 0.7 %shard_map.66 = bf16[8,32,256]{2,1,0:T(8,128)(2,1)S(1)} custom-call(s32[2,4]{1,0:T(2,128)S(1)} %get-tuple-element.16.slot_ref, s32[2,4]{1,0:T(2,128)S(1)} %get-tuple-element.17.level_ref, f32[8,256]{1,0:T(8,128)S(1)} %get-tuple-element.18.gate_ref, bf16[3,32,256]{2,1,0:T(8,128)(2,1)S(1)} %collective-permute-done.refs_0_, ...), custom_call_target="tpu_custom_call" | custom-call | tf_op jit(solution)/shard_map/pallas_call | solution.py:185
  19.5 11.4 %all_to_all.5.held_ref = bf16[8,4,8,256]{3,2,1,0:T(8,128)(2,1)S(1)} all-to-all(bf16[8,4,8,256]{3,2,1,0:T(8,128)(2,1)S(1)} %bitcast.7), channel_id=1, replica_groups=mesh['rollout'=2,'frame'=2,'seq'=8] {'seq'}, dimensions={0} | all-to-all | bytes 262144 | tf_op jit(solution)/shard_map/all_to_all | solution.py:193
  30.9 0.7 %shard_map.67 = bf16[4,8,8,256]{3,2,1,0:T(8,128)(2,1)} custom-call(bf16[8,4,8,256]{3,2,1,0:T(8,128)(2,1)S(1)} %all_to_all.5.held_ref), custom_call_target="tpu_custom_call" | custom-call | tf_op jit(solution)/shard_map/pallas_call | solution.py:194
  (1 shorter events, 0.0 us)
Async XLA Ops:
  1.2 10.9 %collective-permute-start = (bf16[3,32,256]{2,1,0:T(8,128)(2,1)S(1)}, bf16[3,32,256]{2,1,0:T(8,128)(2,1)S(1)}, u32[]{:S(2)}, u32[]{:S(2)}) collective-permute-start(bf16[3,32,256]{2,1,0:T(8,128)(2,1)S(1)} %get-tuple-element.19), channel_id=1, source_target_pairs={{0,5},{1,4},{2,7},{3,6},{4,1},{5,0},{6,3},{7,2},{8,13},{9,12},{10,... | collective-permute-start | bytes 147464 | tf_op jit(solution)/shard_map/ppermute | solution.py:168
  6.2 6.9 %collective-permute-start.1 = (bf16[3,32,256]{2,1,0:T(8,128)(2,1)S(1)}, bf16[3,32,256]{2,1,0:T(8,128)(2,1)S(1)}, u32[]{:S(2)}, u32[]{:S(2)}) collective-permute-start(bf16[3,32,256]{2,1,0:T(8,128)(2,1)S(1)} %get-tuple-element.20), channel_id=1, source_target_pairs={{0,6},{1,7},{2,4},{3,5},{4,2},{5,3},{6,0},{7,1},{8,14},{9,15},{10,... | collective-permute-start | bytes 147464 | tf_op jit(solution)/shard_map/ppermute | solution.py:168
  7.6 6.1 %collective-permute-start.2 = (bf16[3,32,256]{2,1,0:T(8,128)(2,1)S(1)}, bf16[3,32,256]{2,1,0:T(8,128)(2,1)S(1)}, u32[]{:S(2)}, u32[]{:S(2)}) collective-permute-start(bf16[3,32,256]{2,1,0:T(8,128)(2,1)S(1)} %get-tuple-element.21), channel_id=1, source_target_pairs={{0,3},{1,2},{2,1},{3,0},{4,7},{5,6},{6,5},{7,4},{8,11},{9,10},{10,... | collective-permute-start | bytes 147464 | tf_op jit(solution)/shard_map/ppermute | solution.py:168
  7.8 7.1 %collective-permute-start.3 = (bf16[3,32,256]{2,1,0:T(8,128)(2,1)S(1)}, bf16[3,32,256]{2,1,0:T(8,128)(2,1)S(1)}, u32[]{:S(2)}, u32[]{:S(2)}) collective-permute-start(bf16[3,32,256]{2,1,0:T(8,128)(2,1)S(1)} %get-tuple-element.22), channel_id=1, source_target_pairs={{0,7},{1,6},{2,5},{3,4},{4,3},{5,2},{6,1},{7,0},{8,15},{9,14},{10,... | collective-permute-start | bytes 147464 | tf_op jit(solution)/shard_map/ppermute | solution.py:168
  11.6 4.1 %collective-permute-start.4 = (bf16[3,32,256]{2,1,0:T(8,128)(2,1)S(1)}, bf16[3,32,256]{2,1,0:T(8,128)(2,1)S(1)}, u32[]{:S(2)}, u32[]{:S(2)}) collective-permute-start(bf16[3,32,256]{2,1,0:T(8,128)(2,1)S(1)} %get-tuple-element.23), channel_id=1, source_target_pairs={{0,2},{1,3},{2,0},{3,1},{4,6},{5,7},{6,4},{7,5},{8,10},{9,11},{10,... | collective-permute-start | bytes 147464 | tf_op jit(solution)/shard_map/ppermute | solution.py:168
  12.1 5.0 %collective-permute-start.5 = (bf16[3,32,256]{2,1,0:T(8,128)(2,1)S(1)}, bf16[3,32,256]{2,1,0:T(8,128)(2,1)S(1)}, u32[]{:S(2)}, u32[]{:S(2)}) collective-permute-start(bf16[3,32,256]{2,1,0:T(8,128)(2,1)S(1)} %get-tuple-element.24), channel_id=1, source_target_pairs={{0,4},{1,5},{2,6},{3,7},{4,0},{5,1},{6,2},{7,3},{8,12},{9,13},{10,... | collective-permute-start | bytes 147464 | tf_op jit(solution)/shard_map/ppermute | solution.py:168
  13.1 4.1 %collective-permute-start.6 = (bf16[3,32,256]{2,1,0:T(8,128)(2,1)S(1)}, bf16[3,32,256]{2,1,0:T(8,128)(2,1)S(1)}, u32[]{:S(2)}, u32[]{:S(2)}) collective-permute-start(bf16[3,32,256]{2,1,0:T(8,128)(2,1)S(1)} %get-tuple-element.25), channel_id=1, source_target_pairs={{0,1},{1,0},{2,3},{3,2},{4,5},{5,4},{6,7},{7,6},{8,9},{9,8},{10,11... | collective-permute-start | bytes 147464 | tf_op jit(solution)/shard_map/ppermute | solution.py:168
  17.2 1.6 %collective-permute-start.7 = (bf16[8,2,32,256]{3,2,1,0:T(8,128)(2,1)S(1)}, bf16[8,2,32,256]{3,2,1,0:T(8,128)(2,1)S(1)}, u32[]{:S(2)}, u32[]{:S(2)}) collective-permute-start(bf16[8,2,32,256]{3,2,1,0:T(8,128)(2,1)S(1)} %shard_map.65), channel_id=1, source_target_pairs={{0,8},{8,0},{1,9},{9,1},{2,10},{10,2},{3,11},{11,3},{4,12},{12,4},... | collective-permute-start | bytes 786440 | tf_op jit(solution)/shard_map/ppermute | solution.py:182

commit v21 on v20

--- a/solution.py
+++ b/solution.py
@@ -33,32 +33,16 @@
 
 
 def pack(*refs):
-    *operands, slot_ref, level_ref, gate_ref = refs[:6]
-    *outs, slot_out, level_out, gate_out, sems, table_sems = refs[6:]
-    width = gate_out.shape[-1]
-    place = lax.axis_index("seq")
-
-    def columns(place):
-        return pl.ds(pl.multiple_of(place * width, width), width)
-
-    tables = (
-        (slot_ref, slot_out),
-        (level_ref, level_out),
-        (gate_ref.at[:, columns(place)], gate_out),
-    )
-    run(
-        [
-            pltpu.make_async_copy(
-                ref.at[:, columns(place ^ away)], out_ref.at[kind], sems.at[away, kind]
-            )
-            for away, out_ref in zip(send_order(len(outs)), outs)
+    operands, outs, sems = refs[:3], refs[3:-1], refs[-1]
+    place, width = lax.axis_index("seq"), outs[0].shape[-1]
+    copies = []
+    for away, out_ref in zip(send_order(len(outs)), outs):
+        columns = pl.ds(pl.multiple_of((place ^ away) * width, width), width)
+        copies += [
+            pltpu.make_async_copy(ref.at[:, columns], out_ref.at[kind], sems.at[away, kind])
             for kind, ref in enumerate(operands)
         ]
-        + [
-            pltpu.make_async_copy(ref, out_ref, table_sems.at[kind])
-            for kind, (ref, out_ref) in enumerate(tables)
-        ]
-    )
+    run(copies)
 
 
 def stack(*refs):
@@ -95,7 +79,8 @@
         key_slots = jnp.where(
             frame == one, entry(slot_ref, one // local_frames, one % local_frames), key_slots
         )
-    gate_blocks = gate_ref[...]
+    place = lax.axis_index("seq")
+    gate_blocks = gate_ref[:, pl.ds(pl.multiple_of(place * width, width), width)]
     level_rows = lax.broadcasted_iota(jnp.int32, gate_blocks.shape, 0)
     shown, gate_rows = [], []
     for local in range(local_frames):
@@ -137,7 +122,7 @@
             mixed = mixed.reshape(step, local_frames, tokens, HEAD) * gates
             mixed = mixed.reshape(step, rows, HEAD).astype(out_ref.dtype)
             for number, away in enumerate(send_order(devices)[start : start + step]):
-                out_ref[lax.axis_index("seq") ^ away, :, part] = mixed[number]
+                out_ref[place ^ away, :, part] = mixed[number]
 
 
 def whole_heads(queries, keys, values, slot_of, level_of, gate_table):
@@ -145,24 +130,18 @@
     _, local_frames, tokens, all_width = queries.shape
     rows, width = local_frames * tokens, all_width // devices
 
-    def in_hbm(taken):
-        return pltpu.with_memory_space_constraint(taken, pltpu.HBM)
-
-    *pieces, slots, levels, gates = pl.pallas_call(
+    pieces = pl.pallas_call(
         pack,
-        out_shape=[jax.ShapeDtypeStruct((3, rows, width), queries.dtype)] * devices
-        + [
-            jax.ShapeDtypeStruct(slot_of.shape, slot_of.dtype),
-            jax.ShapeDtypeStruct(level_of.shape, level_of.dtype),
-            jax.ShapeDtypeStruct((gate_table.shape[0], width), gate_table.dtype),
-        ],
-        in_specs=[HBM] * 6,
-        out_specs=[VMEM] * (devices + 3),
-        scratch_shapes=[pltpu.SemaphoreType.DMA((devices, 3)), pltpu.SemaphoreType.DMA((3,))],
+        out_shape=[jax.ShapeDtypeStruct((3, rows, width), queries.dtype)] * devices,
+        in_specs=[HBM] * 3,
+        out_specs=[VMEM] * devices,
+        scratch_shapes=[pltpu.SemaphoreType.DMA((devices, 3))],
         compiler_params=PARAMS,
     )(
-        *(in_hbm(taken.reshape(rows, all_width)) for taken in (queries, keys, values)),
-        *(in_hbm(taken) for taken in (slot_of, level_of, gate_table)),
+        *(
+            pltpu.with_memory_space_constraint(taken.reshape(rows, all_width), pltpu.HBM)
+            for taken in (queries, keys, values)
+        )
     )
     pieces = [
         lax.ppermute(piece, "seq", [(one, one ^ away) for one in range(devices)])
@@ -188,7 +167,7 @@
         in_specs=[VMEM] * (3 + devices + len(stacks)),
         out_specs=VMEM,
         compiler_params=PARAMS,
-    )(slots, levels, gates, *pieces, *stacks)
+    )(slot_of, level_of, gate_table, *pieces, *stacks)
     answer = answer.reshape(devices, local_frames, tokens, width)
     answer = lax.all_to_all(answer, "seq", split_axis=0, concat_axis=0, tiled=True)
     answer = pl.pallas_call(

time: 31.8 us -> 31.8 us (level)
  no operation moved by 1% of the time
where the time goes in v21:
time: 31.8 us; the launch traced here: 31.6 us
  starting transfers between devices  12.5 us (39%)
  blocking collectives  11.4 us (36%)
  waiting for transfers between devices  5.08 us (16%)
  Pallas kernels  2.55 us (8%)
    ppermute x7, starting transfers between devices, whole_heads(): lax.ppermute(piece, 'seq', [(one, one ^ away) for one in range(devices)])  12.4 us
    all_to_all x1, blocking collectives, whole_heads(): lax.all_to_all(answer, 'seq', split_axis=0, concat_axis=0, tiled=True)  11.4 us
    ppermute x7, waiting for transfers between devices, whole_heads(): lax.ppermute(piece, 'seq', [(one, one ^ away) for one in range(devices)])  3.56 us
    ppermute x1, waiting for transfers between devices, whole_heads(): lax.ppermute(stacked, 'frame', [(one, (one - away) % groups) for one in r...  1.52 us
    pallas_call x1, Pallas kernels, whole_heads(): pl.pallas_call(pack, out_shape=[jax.ShapeDtypeStruct((3, rows, width), qu...  1.16 us
    pallas_call x1, Pallas kernels, whole_heads(): pl.pallas_call(functools.partial(attend, tokens=tokens), out_shape=jax.Sh...  0.7 us
    pallas_call x1, Pallas kernels, whole_heads(): pl.pallas_call(unpack, out_shape=jax.ShapeDtypeStruct((local_frames, devi...  0.68 us
  transfers between devices with their start and end apart: 8, of which 5 were waited for; matrix products, arithmetic and copies ran while one was open for 0% of the time, Pallas kernels for 0%

profile of v21, /device:TPU:0, one launch (start us, length us, event | category | flops | bytes accessed | tf_op | source)
XLA Modules:
  0.0 31.6 jit_solution(4491191181972507587)
XLA Ops:
  0.0 1.2 %shard_map.64 = (bf16[3,32,256]{2,1,0:T(8,128)(2,1)S(1)}, bf16[3,32,256]{2,1,0:T(8,128)(2,1)S(1)}, bf16[3,32,256]{2,1,0:T(8,128)(2,1)S(1)}, bf16[3,32,256]{2,1,0...) custom-call(bf16[32,2048]{1,0:T(8,128)(2,1)} %bitcast.8, ...), custom_call_target="tpu_custom_call" | custom-call | tf_op jit(solution)/shard_map/pallas_call | solution.py:133
  1.2 5.0 %collective-permute-start = (bf16[3,32,256]{2,1,0:T(8,128)(2,1)S(1)}, bf16[3,32,256]{2,1,0:T(8,128)(2,1)S(1)}, u32[]{:S(2)}, u32[]{:S(2)}) collective-permute-start(bf16[3,32,256]{2,1,0:T(8,128)(2,1)S(1)} %get-tuple-element.13), channel_id=1, source_target_pairs={{0,5},{1,4},{2,7},{3,6},{4,1},{5,0},{6,3},{7,2},{8,13},{9,12},{10,... | collective-permute-start | bytes 147464 | tf_op jit(solution)/shard_map/ppermute | solution.py:147
  6.2 1.3 %collective-permute-start.1 = (bf16[3,32,256]{2,1,0:T(8,128)(2,1)S(1)}, bf16[3,32,256]{2,1,0:T(8,128)(2,1)S(1)}, u32[]{:S(2)}, u32[]{:S(2)}) collective-permute-start(bf16[3,32,256]{2,1,0:T(8,128)(2,1)S(1)} %get-tuple-element.14), channel_id=1, source_target_pairs={{0,6},{1,7},{2,4},{3,5},{4,2},{5,3},{6,0},{7,1},{8,14},{9,15},{10,... | collective-permute-start | bytes 147464 | tf_op jit(solution)/shard_map/ppermute | solution.py:147
  7.5 0.2 collective-permute-start.2
  7.7 3.8 %collective-permute-start.3 = (bf16[3,32,256]{2,1,0:T(8,128)(2,1)S(1)}, bf16[3,32,256]{2,1,0:T(8,128)(2,1)S(1)}, u32[]{:S(2)}, u32[]{:S(2)}) collective-permute-start(bf16[3,32,256]{2,1,0:T(8,128)(2,1)S(1)} %get-tuple-element.16), channel_id=1, source_target_pairs={{0,7},{1,6},{2,5},{3,4},{4,3},{5,2},{6,1},{7,0},{8,15},{9,14},{10,... | collective-permute-start | bytes 147464 | tf_op jit(solution)/shard_map/ppermute | solution.py:147
  11.6 0.5 %collective-permute-start.4 = (bf16[3,32,256]{2,1,0:T(8,128)(2,1)S(1)}, bf16[3,32,256]{2,1,0:T(8,128)(2,1)S(1)}, u32[]{:S(2)}, u32[]{:S(2)}) collective-permute-start(bf16[3,32,256]{2,1,0:T(8,128)(2,1)S(1)} %get-tuple-element.17), channel_id=1, source_target_pairs={{0,2},{1,3},{2,0},{3,1},{4,6},{5,7},{6,4},{7,5},{8,10},{9,11},{10,... | collective-permute-start | bytes 147464 | tf_op jit(solution)/shard_map/ppermute | solution.py:147
  12.0 0.0 collective-permute-done.refs_0_
  12.1 1.0 %collective-permute-start.5 = (bf16[3,32,256]{2,1,0:T(8,128)(2,1)S(1)}, bf16[3,32,256]{2,1,0:T(8,128)(2,1)S(1)}, u32[]{:S(2)}, u32[]{:S(2)}) collective-permute-start(bf16[3,32,256]{2,1,0:T(8,128)(2,1)S(1)} %get-tuple-element.18), channel_id=1, source_target_pairs={{0,4},{1,5},{2,6},{3,7},{4,0},{5,1},{6,2},{7,3},{8,12},{9,13},{10,... | collective-permute-start | bytes 147464 | tf_op jit(solution)/shard_map/ppermute | solution.py:147
  13.1 0.0 collective-permute-done.1.refs_1_
  13.1 0.5 %collective-permute-start.6 = (bf16[3,32,256]{2,1,0:T(8,128)(2,1)S(1)}, bf16[3,32,256]{2,1,0:T(8,128)(2,1)S(1)}, u32[]{:S(2)}, u32[]{:S(2)}) collective-permute-start(bf16[3,32,256]{2,1,0:T(8,128)(2,1)S(1)} %get-tuple-element.19), channel_id=1, source_target_pairs={{0,1},{1,0},{2,3},{3,2},{4,5},{5,4},{6,7},{7,6},{8,9},{9,8},{10,11... | collective-permute-start | bytes 147464 | tf_op jit(solution)/shard_map/ppermute | solution.py:147
  13.6 0.0 collective-permute-done.2.refs_2_
  13.6 1.2 %collective-permute-done.3.refs_3_ = bf16[3,32,256]{2,1,0:T(8,128)(2,1)S(1)} collective-permute-done((bf16[3,32,256]{2,1,0:T(8,128)(2,1)S(1)}, bf16[3,32,256]{2,1,0:T(8,128)(2,1)S(1)}, u32[]{:S(2)}, u32[]{:S(2)}) %collective-permute-start.3) | collective-permute-done | bytes 49184 | tf_op jit(solution)/shard_map/ppermute | solution.py:147
  14.8 0.9 %collective-permute-done.4.refs_4_ = bf16[3,32,256]{2,1,0:T(8,128)(2,1)S(1)} collective-permute-done((bf16[3,32,256]{2,1,0:T(8,128)(2,1)S(1)}, bf16[3,32,256]{2,1,0:T(8,128)(2,1)S(1)}, u32[]{:S(2)}, u32[]{:S(2)}) %collective-permute-start.4) | collective-permute-done | bytes 49184 | tf_op jit(solution)/shard_map/ppermute | solution.py:147
  15.7 1.4 %collective-permute-done.5.refs_5_ = bf16[3,32,256]{2,1,0:T(8,128)(2,1)S(1)} collective-permute-done((bf16[3,32,256]{2,1,0:T(8,128)(2,1)S(1)}, bf16[3,32,256]{2,1,0:T(8,128)(2,1)S(1)}, u32[]{:S(2)}, u32[]{:S(2)}) %collective-permute-start.5) | collective-permute-done | bytes 49184 | tf_op jit(solution)/shard_map/ppermute | solution.py:147
  17.0 0.1 collective-permute-done.6.refs_6_
  17.2 0.0 copy-start
  17.2 0.0 copy-start.1
  17.2 0.0 copy-start.2
  17.2 0.1 collective-permute-start.7
  17.3 1.5 %collective-permute-done.7.refs_8_ = bf16[8,2,32,256]{3,2,1,0:T(8,128)(2,1)S(1)} collective-permute-done((bf16[8,2,32,256]{3,2,1,0:T(8,128)(2,1)S(1)}, bf16[8,2,32,256]{3,2,1,0:T(8,128)(2,1)S(1)}, u32[]{:S(2)}, u32[]{:S(2)}) %collective-permute-start.7) | collective-permute-done | bytes 262176 | tf_op jit(solution)/shard_map/ppermute | solution.py:161
  18.8 0.0 copy-done
  18.8 0.0 copy-done.1
  18.8 0.0 copy-done.2
  18.8 0.7 %shard_map.66 = bf16[8,32,256]{2,1,0:T(8,128)(2,1)S(1)} custom-call(s32[2,4]{1,0:T(2,128)S(1)} %copy-done.1, s32[2,4]{1,0:T(2,128)S(1)} %copy-done.2, f32[8,2048]{1,0:T(8,128)S(1)} %copy-done, bf16[3,32,256]{2,1,0:T(8,128)(2,1)S(1)} %collective-permute-done.refs_0_, bf16[3,32,256]{2,1,0:T(8,128)(2,1)S(1)} %collective-permute-done.1.refs_1_, ...), custom_call_target="tpu_custom_call" | custom-call | tf_op jit(solution)/shard_map/pallas_call | solution.py:164
  19.5 11.4 %all_to_all.5.held_ref = bf16[8,4,8,256]{3,2,1,0:T(8,128)(2,1)S(1)} all-to-all(bf16[8,4,8,256]{3,2,1,0:T(8,128)(2,1)S(1)} %bitcast.7), channel_id=1, replica_groups=mesh['rollout'=2,'frame'=2,'seq'=8] {'seq'}, dimensions={0} | all-to-all | bytes 262144 | tf_op jit(solution)/shard_map/all_to_all | solution.py:172
  30.9 0.7 %shard_map.67 = bf16[4,8,8,256]{3,2,1,0:T(8,128)(2,1)} custom-call(bf16[8,4,8,256]{3,2,1,0:T(8,128)(2,1)S(1)} %all_to_all.5.held_ref), custom_call_target="tpu_custom_call" | custom-call | tf_op jit(solution)/shard_map/pallas_call | solution.py:173
  (1 shorter events, 0.0 us)
Async XLA Ops:
  1.2 10.9 %collective-permute-start = (bf16[3,32,256]{2,1,0:T(8,128)(2,1)S(1)}, bf16[3,32,256]{2,1,0:T(8,128)(2,1)S(1)}, u32[]{:S(2)}, u32[]{:S(2)}) collective-permute-start(bf16[3,32,256]{2,1,0:T(8,128)(2,1)S(1)} %get-tuple-element.13), channel_id=1, source_target_pairs={{0,5},{1,4},{2,7},{3,6},{4,1},{5,0},{6,3},{7,2},{8,13},{9,12},{10,... | collective-permute-start | bytes 147464 | tf_op jit(solution)/shard_map/ppermute | solution.py:147
  6.2 6.9 %collective-permute-start.1 = (bf16[3,32,256]{2,1,0:T(8,128)(2,1)S(1)}, bf16[3,32,256]{2,1,0:T(8,128)(2,1)S(1)}, u32[]{:S(2)}, u32[]{:S(2)}) collective-permute-start(bf16[3,32,256]{2,1,0:T(8,128)(2,1)S(1)} %get-tuple-element.14), channel_id=1, source_target_pairs={{0,6},{1,7},{2,4},{3,5},{4,2},{5,3},{6,0},{7,1},{8,14},{9,15},{10,... | collective-permute-start | bytes 147464 | tf_op jit(solution)/shard_map/ppermute | solution.py:147
  7.5 6.1 %collective-permute-start.2 = (bf16[3,32,256]{2,1,0:T(8,128)(2,1)S(1)}, bf16[3,32,256]{2,1,0:T(8,128)(2,1)S(1)}, u32[]{:S(2)}, u32[]{:S(2)}) collective-permute-start(bf16[3,32,256]{2,1,0:T(8,128)(2,1)S(1)} %get-tuple-element.15), channel_id=1, source_target_pairs={{0,3},{1,2},{2,1},{3,0},{4,7},{5,6},{6,5},{7,4},{8,11},{9,10},{10,... | collective-permute-start | bytes 147464 | tf_op jit(solution)/shard_map/ppermute | solution.py:147
  7.7 7.1 %collective-permute-start.3 = (bf16[3,32,256]{2,1,0:T(8,128)(2,1)S(1)}, bf16[3,32,256]{2,1,0:T(8,128)(2,1)S(1)}, u32[]{:S(2)}, u32[]{:S(2)}) collective-permute-start(bf16[3,32,256]{2,1,0:T(8,128)(2,1)S(1)} %get-tuple-element.16), channel_id=1, source_target_pairs={{0,7},{1,6},{2,5},{3,4},{4,3},{5,2},{6,1},{7,0},{8,15},{9,14},{10,... | collective-permute-start | bytes 147464 | tf_op jit(solution)/shard_map/ppermute | solution.py:147
  11.6 4.1 %collective-permute-start.4 = (bf16[3,32,256]{2,1,0:T(8,128)(2,1)S(1)}, bf16[3,32,256]{2,1,0:T(8,128)(2,1)S(1)}, u32[]{:S(2)}, u32[]{:S(2)}) collective-permute-start(bf16[3,32,256]{2,1,0:T(8,128)(2,1)S(1)} %get-tuple-element.17), channel_id=1, source_target_pairs={{0,2},{1,3},{2,0},{3,1},{4,6},{5,7},{6,4},{7,5},{8,10},{9,11},{10,... | collective-permute-start | bytes 147464 | tf_op jit(solution)/shard_map/ppermute | solution.py:147
  12.1 5.0 %collective-permute-start.5 = (bf16[3,32,256]{2,1,0:T(8,128)(2,1)S(1)}, bf16[3,32,256]{2,1,0:T(8,128)(2,1)S(1)}, u32[]{:S(2)}, u32[]{:S(2)}) collective-permute-start(bf16[3,32,256]{2,1,0:T(8,128)(2,1)S(1)} %get-tuple-element.18), channel_id=1, source_target_pairs={{0,4},{1,5},{2,6},{3,7},{4,0},{5,1},{6,2},{7,3},{8,12},{9,13},{10,... | collective-permute-start | bytes 147464 | tf_op jit(solution)/shard_map/ppermute | solution.py:147
  13.1 4.1 %collective-permute-start.6 = (bf16[3,32,256]{2,1,0:T(8,128)(2,1)S(1)}, bf16[3,32,256]{2,1,0:T(8,128)(2,1)S(1)}, u32[]{:S(2)}, u32[]{:S(2)}) collective-permute-start(bf16[3,32,256]{2,1,0:T(8,128)(2,1)S(1)} %get-tuple-element.19), channel_id=1, source_target_pairs={{0,1},{1,0},{2,3},{3,2},{4,5},{5,4},{6,7},{7,6},{8,9},{9,8},{10,11... | collective-permute-start | bytes 147464 | tf_op jit(solution)/shard_map/ppermute | solution.py:147
  17.2 1.6 %copy-start = (f32[8,2048]{1,0:T(8,128)S(1)}, f32[8,2048]{1,0:T(8,128)}, u32[]{:S(2)}) copy-start(f32[8,2048]{1,0:T(8,128)} %gate_ref.1) | copy-start | bytes 196612
  17.2 1.6 %copy-start.1 = (s32[2,4]{1,0:T(2,128)S(1)}, s32[2,4]{1,0:T(2,128)}, u32[]{:S(2)}) copy-start(s32[2,4]{1,0:T(2,128)} %slot_ref.1) | copy-start | bytes 100
  17.2 1.6 %copy-start.2 = (s32[2,4]{1,0:T(2,128)S(1)}, s32[2,4]{1,0:T(2,128)}, u32[]{:S(2)}) copy-start(s32[2,4]{1,0:T(2,128)} %level_ref.1) | copy-start | bytes 100
  17.2 1.6 %collective-permute-start.7 = (bf16[8,2,32,256]{3,2,1,0:T(8,128)(2,1)S(1)}, bf16[8,2,32,256]{3,2,1,0:T(8,128)(2,1)S(1)}, u32[]{:S(2)}, u32[]{:S(2)}) collective-permute-start(bf16[8,2,32,256]{3,2,1,0:T(8,128)(2,1)S(1)} %shard_map.65), channel_id=1, source_target_pairs={{0,8},{8,0},{1,9},{9,1},{2,10},{10,2},{3,11},{11,3},{4,12},{12,4},... | collective-permute-start | bytes 786440 | tf_op jit(solution)/shard_map/ppermute | solution.py:161

commit v22 on v21

--- a/solution.py
+++ b/solution.py
@@ -25,39 +25,53 @@
     return order + [0]
 
 
-def run(copies):
+BLOCKS = 4
+
+
+def blocks_of(width):
+    return [pl.ds(start, width // BLOCKS) for start in range(0, width, width // BLOCKS)]
+
+
+def pack(*refs):
+    operands, outs, held_ref, sems = refs[:3], refs[3:-2], refs[-2], refs[-1]
+    place, width = lax.axis_index("seq"), outs[0].shape[-1]
+    copies = [
+        [
+            pltpu.make_async_copy(
+                ref.at[:, block], held_ref.at[kind, :, block], sems.at[kind, number]
+            )
+            for number, block in enumerate(blocks_of(ref.shape[-1]))
+        ]
+        for kind, ref in enumerate(operands)
+    ]
+    for copy in sum(copies, []):
+        copy.start()
+    for kind, parts in enumerate(copies):
+        for copy in parts:
+            copy.wait()
+        for away, out_ref in zip(send_order(len(outs)), outs):
+            columns = pl.ds(pl.multiple_of((place ^ away) * width, width), width)
+            out_ref[kind] = held_ref[kind, :, columns]
+
+
+def stack(*refs):
+    *pieces, out_ref = refs
+    for number, ref in enumerate(pieces):
+        out_ref[number] = ref[1:3]
+
+
+def unpack(held_ref, out_ref, joined_ref, sems):
+    width = held_ref.shape[-1]
+    for device in range(held_ref.shape[0]):
+        joined_ref[:, device * width : (device + 1) * width] = held_ref[device]
+    copies = [
+        pltpu.make_async_copy(joined_ref.at[:, block], out_ref.at[:, block], sems.at[number])
+        for number, block in enumerate(blocks_of(out_ref.shape[-1]))
+    ]
     for copy in copies:
         copy.start()
     for copy in copies:
         copy.wait()
-
-
-def pack(*refs):
-    operands, outs, sems = refs[:3], refs[3:-1], refs[-1]
-    place, width = lax.axis_index("seq"), outs[0].shape[-1]
-    copies = []
-    for away, out_ref in zip(send_order(len(outs)), outs):
-        columns = pl.ds(pl.multiple_of((place ^ away) * width, width), width)
-        copies += [
-            pltpu.make_async_copy(ref.at[:, columns], out_ref.at[kind], sems.at[away, kind])
-            for kind, ref in enumerate(operands)
-        ]
-    run(copies)
-
-
-def stack(*refs):
-    *pieces, out_ref = refs
-    for number, ref in enumerate(pieces):
-        out_ref[number] = ref[1:3]
-
-
-def unpack(held_ref, out_ref, sems):
-    run(
-        [
-            pltpu.make_async_copy(held_ref.at[:, frame], out_ref.at[frame], sems.at[frame])
-            for frame in range(out_ref.shape[0])
-        ]
-    )
 
 
 def entry(ref, row, column):
@@ -135,7 +149,10 @@
         out_shape=[jax.ShapeDtypeStruct((3, rows, width), queries.dtype)] * devices,
         in_specs=[HBM] * 3,
         out_specs=[VMEM] * devices,
-        scratch_shapes=[pltpu.SemaphoreType.DMA((devices, 3))],
+        scratch_shapes=[
+            pltpu.VMEM((3, rows, all_width), queries.dtype),
+            pltpu.SemaphoreType.DMA((3, BLOCKS)),
+        ],
         compiler_params=PARAMS,
     )(
         *(
@@ -168,17 +185,19 @@
         out_specs=VMEM,
         compiler_params=PARAMS,
     )(slot_of, level_of, gate_table, *pieces, *stacks)
-    answer = answer.reshape(devices, local_frames, tokens, width)
     answer = lax.all_to_all(answer, "seq", split_axis=0, concat_axis=0, tiled=True)
     answer = pl.pallas_call(
         unpack,
-        out_shape=jax.ShapeDtypeStruct((local_frames, devices, tokens, width), queries.dtype),
+        out_shape=jax.ShapeDtypeStruct((rows, all_width), queries.dtype),
         in_specs=[VMEM],
         out_specs=HBM,
-        scratch_shapes=[pltpu.SemaphoreType.DMA((local_frames,))],
+        scratch_shapes=[
+            pltpu.VMEM((rows, all_width), queries.dtype),
+            pltpu.SemaphoreType.DMA((BLOCKS,)),
+        ],
         compiler_params=PARAMS,
     )(answer)
-    return answer.transpose(0, 2, 1, 3).reshape(queries.shape)
+    return answer.reshape(queries.shape)
 
 
 def shared_heads(queries, keys, values, slot_of, level_of, gate_table):

time: 31.8 us -> 31.7 us (level)
  no operation moved by 1% of the time
where the time goes in v22:
time: 31.7 us; the launch traced here: 31.5 us
  starting transfers between devices  12.5 us (39%)
  blocking collectives  11.4 us (36%)
  waiting for transfers between devices  5.08 us (16%)
  Pallas kernels  2.46 us (8%)
    ppermute x7, starting transfers between devices, whole_heads(): lax.ppermute(piece, 'seq', [(one, one ^ away) for one in range(devices)])  12.4 us
    all_to_all x1, blocking collectives, whole_heads(): lax.all_to_all(answer, 'seq', split_axis=0, concat_axis=0, tiled=True)  11.4 us
    ppermute x7, waiting for transfers between devices, whole_heads(): lax.ppermute(piece, 'seq', [(one, one ^ away) for one in range(devices)])  3.56 us
    ppermute x1, waiting for transfers between devices, whole_heads(): lax.ppermute(stacked, 'frame', [(one, (one - away) % groups) for one in r...  1.52 us
    pallas_call x1, Pallas kernels, whole_heads(): pl.pallas_call(pack, out_shape=[jax.ShapeDtypeStruct((3, rows, width), qu...  1.06 us
    pallas_call x1, Pallas kernels, whole_heads(): pl.pallas_call(functools.partial(attend, tokens=tokens), out_shape=jax.Sh...  0.7 us
    pallas_call x1, Pallas kernels, whole_heads(): pl.pallas_call(unpack, out_shape=jax.ShapeDtypeStruct((rows, all_width),...  0.69 us
  transfers between devices with their start and end apart: 8, of which 5 were waited for; matrix products, arithmetic and copies ran while one was open for 0% of the time, Pallas kernels for 0%

profile of v22, /device:TPU:0, one launch (start us, length us, event | category | flops | bytes accessed | tf_op | source)
XLA Modules:
  0.0 31.5 jit_solution(1700632803334365920)
XLA Ops:
  0.0 1.1 %shard_map.64 = (bf16[3,32,256]{2,1,0:T(8,128)(2,1)S(1)}, bf16[3,32,256]{2,1,0:T(8,128)(2,1)S(1)}, bf16[3,32,256]{2,1,0:T(8,128)(2,1)S(1)}, bf16[3,32,256]{2,1,0...) custom-call(bf16[32,2048]{1,0:T(8,128)(2,1)} %bitcast.4, ...), custom_call_target="tpu_custom_call" | custom-call | tf_op jit(solution)/shard_map/pallas_call | solution.py:147
  1.1 5.0 %collective-permute-start = (bf16[3,32,256]{2,1,0:T(8,128)(2,1)S(1)}, bf16[3,32,256]{2,1,0:T(8,128)(2,1)S(1)}, u32[]{:S(2)}, u32[]{:S(2)}) collective-permute-start(bf16[3,32,256]{2,1,0:T(8,128)(2,1)S(1)} %get-tuple-element.13), channel_id=1, source_target_pairs={{0,5},{1,4},{2,7},{3,6},{4,1},{5,0},{6,3},{7,2},{8,13},{9,12},{10,... | collective-permute-start | bytes 147464 | tf_op jit(solution)/shard_map/ppermute | solution.py:164
  6.1 1.3 %collective-permute-start.1 = (bf16[3,32,256]{2,1,0:T(8,128)(2,1)S(1)}, bf16[3,32,256]{2,1,0:T(8,128)(2,1)S(1)}, u32[]{:S(2)}, u32[]{:S(2)}) collective-permute-start(bf16[3,32,256]{2,1,0:T(8,128)(2,1)S(1)} %get-tuple-element.14), channel_id=1, source_target_pairs={{0,6},{1,7},{2,4},{3,5},{4,2},{5,3},{6,0},{7,1},{8,14},{9,15},{10,... | collective-permute-start | bytes 147464 | tf_op jit(solution)/shard_map/ppermute | solution.py:164
  7.4 0.2 collective-permute-start.2
  7.6 3.8 %collective-permute-start.3 = (bf16[3,32,256]{2,1,0:T(8,128)(2,1)S(1)}, bf16[3,32,256]{2,1,0:T(8,128)(2,1)S(1)}, u32[]{:S(2)}, u32[]{:S(2)}) collective-permute-start(bf16[3,32,256]{2,1,0:T(8,128)(2,1)S(1)} %get-tuple-element.16), channel_id=1, source_target_pairs={{0,7},{1,6},{2,5},{3,4},{4,3},{5,2},{6,1},{7,0},{8,15},{9,14},{10,... | collective-permute-start | bytes 147464 | tf_op jit(solution)/shard_map/ppermute | solution.py:164
  11.5 0.5 %collective-permute-start.4 = (bf16[3,32,256]{2,1,0:T(8,128)(2,1)S(1)}, bf16[3,32,256]{2,1,0:T(8,128)(2,1)S(1)}, u32[]{:S(2)}, u32[]{:S(2)}) collective-permute-start(bf16[3,32,256]{2,1,0:T(8,128)(2,1)S(1)} %get-tuple-element.17), channel_id=1, source_target_pairs={{0,2},{1,3},{2,0},{3,1},{4,6},{5,7},{6,4},{7,5},{8,10},{9,11},{10,... | collective-permute-start | bytes 147464 | tf_op jit(solution)/shard_map/ppermute | solution.py:164
  11.9 0.0 collective-permute-done.refs_0_
  11.9 1.0 %collective-permute-start.5 = (bf16[3,32,256]{2,1,0:T(8,128)(2,1)S(1)}, bf16[3,32,256]{2,1,0:T(8,128)(2,1)S(1)}, u32[]{:S(2)}, u32[]{:S(2)}) collective-permute-start(bf16[3,32,256]{2,1,0:T(8,128)(2,1)S(1)} %get-tuple-element.18), channel_id=1, source_target_pairs={{0,4},{1,5},{2,6},{3,7},{4,0},{5,1},{6,2},{7,3},{8,12},{9,13},{10,... | collective-permute-start | bytes 147464 | tf_op jit(solution)/shard_map/ppermute | solution.py:164
  13.0 0.0 collective-permute-done.1.refs_1_
  13.0 0.5 %collective-permute-start.6 = (bf16[3,32,256]{2,1,0:T(8,128)(2,1)S(1)}, bf16[3,32,256]{2,1,0:T(8,128)(2,1)S(1)}, u32[]{:S(2)}, u32[]{:S(2)}) collective-permute-start(bf16[3,32,256]{2,1,0:T(8,128)(2,1)S(1)} %get-tuple-element.19), channel_id=1, source_target_pairs={{0,1},{1,0},{2,3},{3,2},{4,5},{5,4},{6,7},{7,6},{8,9},{9,8},{10,11... | collective-permute-start | bytes 147464 | tf_op jit(solution)/shard_map/ppermute | solution.py:164
  13.5 0.0 collective-permute-done.2.refs_2_
  13.5 1.2 %collective-permute-done.3.refs_3_ = bf16[3,32,256]{2,1,0:T(8,128)(2,1)S(1)} collective-permute-done((bf16[3,32,256]{2,1,0:T(8,128)(2,1)S(1)}, bf16[3,32,256]{2,1,0:T(8,128)(2,1)S(1)}, u32[]{:S(2)}, u32[]{:S(2)}) %collective-permute-start.3) | collective-permute-done | bytes 49184 | tf_op jit(solution)/shard_map/ppermute | solution.py:164
  14.7 0.9 %collective-permute-done.4.refs_4_ = bf16[3,32,256]{2,1,0:T(8,128)(2,1)S(1)} collective-permute-done((bf16[3,32,256]{2,1,0:T(8,128)(2,1)S(1)}, bf16[3,32,256]{2,1,0:T(8,128)(2,1)S(1)}, u32[]{:S(2)}, u32[]{:S(2)}) %collective-permute-start.4) | collective-permute-done | bytes 49184 | tf_op jit(solution)/shard_map/ppermute | solution.py:164
  15.6 1.4 %collective-permute-done.5.refs_5_ = bf16[3,32,256]{2,1,0:T(8,128)(2,1)S(1)} collective-permute-done((bf16[3,32,256]{2,1,0:T(8,128)(2,1)S(1)}, bf16[3,32,256]{2,1,0:T(8,128)(2,1)S(1)}, u32[]{:S(2)}, u32[]{:S(2)}) %collective-permute-start.5) | collective-permute-done | bytes 49184 | tf_op jit(solution)/shard_map/ppermute | solution.py:164
  16.9 0.1 collective-permute-done.6.refs_6_
  17.1 0.0 copy-start
  17.1 0.0 copy-start.1
  17.1 0.0 copy-start.2
  17.1 0.1 collective-permute-start.7
  17.2 1.5 %collective-permute-done.7.refs_8_ = bf16[8,2,32,256]{3,2,1,0:T(8,128)(2,1)S(1)} collective-permute-done((bf16[8,2,32,256]{3,2,1,0:T(8,128)(2,1)S(1)}, bf16[8,2,32,256]{3,2,1,0:T(8,128)(2,1)S(1)}, u32[]{:S(2)}, u32[]{:S(2)}) %collective-permute-start.7) | collective-permute-done | bytes 262176 | tf_op jit(solution)/shard_map/ppermute | solution.py:178
  18.7 0.0 copy-done
  18.7 0.0 copy-done.1
  18.7 0.0 copy-done.2
  18.7 0.7 %shard_map.66 = bf16[8,32,256]{2,1,0:T(8,128)(2,1)S(1)} custom-call(s32[2,4]{1,0:T(2,128)S(1)} %copy-done.1, s32[2,4]{1,0:T(2,128)S(1)} %copy-done.2, f32[8,2048]{1,0:T(8,128)S(1)} %copy-done, bf16[3,32,256]{2,1,0:T(8,128)(2,1)S(1)} %collective-permute-done.refs_0_, bf16[3,32,256]{2,1,0:T(8,128)(2,1)S(1)} %collective-permute-done.1.refs_1_, ...), custom_call_target="tpu_custom_call" | custom-call | tf_op jit(solution)/shard_map/pallas_call | solution.py:181
  19.4 11.4 %all_to_all.5.held_ref = bf16[8,32,256]{2,1,0:T(8,128)(2,1)S(1)} all-to-all(bf16[8,32,256]{2,1,0:T(8,128)(2,1)S(1)} %shard_map.66), channel_id=1, replica_groups=mesh['rollout'=2,'frame'=2,'seq'=8] {'seq'}, dimensions={0} | all-to-all | bytes 262144 | tf_op jit(solution)/shard_map/all_to_all | solution.py:188
  30.8 0.7 %shard_map.67 = bf16[32,2048]{1,0:T(8,128)(2,1)} custom-call(bf16[8,32,256]{2,1,0:T(8,128)(2,1)S(1)} %all_to_all.5.held_ref), custom_call_target="tpu_custom_call" | custom-call | tf_op jit(solution)/shard_map/pallas_call | solution.py:189
  (1 shorter events, 0.0 us)
Async XLA Ops:
  1.1 10.9 %collective-permute-start = (bf16[3,32,256]{2,1,0:T(8,128)(2,1)S(1)}, bf16[3,32,256]{2,1,0:T(8,128)(2,1)S(1)}, u32[]{:S(2)}, u32[]{:S(2)}) collective-permute-start(bf16[3,32,256]{2,1,0:T(8,128)(2,1)S(1)} %get-tuple-element.13), channel_id=1, source_target_pairs={{0,5},{1,4},{2,7},{3,6},{4,1},{5,0},{6,3},{7,2},{8,13},{9,12},{10,... | collective-permute-start | bytes 147464 | tf_op jit(solution)/shard_map/ppermute | solution.py:164
  6.1 6.9 %collective-permute-start.1 = (bf16[3,32,256]{2,1,0:T(8,128)(2,1)S(1)}, bf16[3,32,256]{2,1,0:T(8,128)(2,1)S(1)}, u32[]{:S(2)}, u32[]{:S(2)}) collective-permute-start(bf16[3,32,256]{2,1,0:T(8,128)(2,1)S(1)} %get-tuple-element.14), channel_id=1, source_target_pairs={{0,6},{1,7},{2,4},{3,5},{4,2},{5,3},{6,0},{7,1},{8,14},{9,15},{10,... | collective-permute-start | bytes 147464 | tf_op jit(solution)/shard_map/ppermute | solution.py:164
  7.4 6.1 %collective-permute-start.2 = (bf16[3,32,256]{2,1,0:T(8,128)(2,1)S(1)}, bf16[3,32,256]{2,1,0:T(8,128)(2,1)S(1)}, u32[]{:S(2)}, u32[]{:S(2)}) collective-permute-start(bf16[3,32,256]{2,1,0:T(8,128)(2,1)S(1)} %get-tuple-element.15), channel_id=1, source_target_pairs={{0,3},{1,2},{2,1},{3,0},{4,7},{5,6},{6,5},{7,4},{8,11},{9,10},{10,... | collective-permute-start | bytes 147464 | tf_op jit(solution)/shard_map/ppermute | solution.py:164
  7.6 7.1 %collective-permute-start.3 = (bf16[3,32,256]{2,1,0:T(8,128)(2,1)S(1)}, bf16[3,32,256]{2,1,0:T(8,128)(2,1)S(1)}, u32[]{:S(2)}, u32[]{:S(2)}) collective-permute-start(bf16[3,32,256]{2,1,0:T(8,128)(2,1)S(1)} %get-tuple-element.16), channel_id=1, source_target_pairs={{0,7},{1,6},{2,5},{3,4},{4,3},{5,2},{6,1},{7,0},{8,15},{9,14},{10,... | collective-permute-start | bytes 147464 | tf_op jit(solution)/shard_map/ppermute | solution.py:164
  11.5 4.1 %collective-permute-start.4 = (bf16[3,32,256]{2,1,0:T(8,128)(2,1)S(1)}, bf16[3,32,256]{2,1,0:T(8,128)(2,1)S(1)}, u32[]{:S(2)}, u32[]{:S(2)}) collective-permute-start(bf16[3,32,256]{2,1,0:T(8,128)(2,1)S(1)} %get-tuple-element.17), channel_id=1, source_target_pairs={{0,2},{1,3},{2,0},{3,1},{4,6},{5,7},{6,4},{7,5},{8,10},{9,11},{10,... | collective-permute-start | bytes 147464 | tf_op jit(solution)/shard_map/ppermute | solution.py:164
  11.9 5.0 %collective-permute-start.5 = (bf16[3,32,256]{2,1,0:T(8,128)(2,1)S(1)}, bf16[3,32,256]{2,1,0:T(8,128)(2,1)S(1)}, u32[]{:S(2)}, u32[]{:S(2)}) collective-permute-start(bf16[3,32,256]{2,1,0:T(8,128)(2,1)S(1)} %get-tuple-element.18), channel_id=1, source_target_pairs={{0,4},{1,5},{2,6},{3,7},{4,0},{5,1},{6,2},{7,3},{8,12},{9,13},{10,... | collective-permute-start | bytes 147464 | tf_op jit(solution)/shard_map/ppermute | solution.py:164
  13.0 4.1 %collective-permute-start.6 = (bf16[3,32,256]{2,1,0:T(8,128)(2,1)S(1)}, bf16[3,32,256]{2,1,0:T(8,128)(2,1)S(1)}, u32[]{:S(2)}, u32[]{:S(2)}) collective-permute-start(bf16[3,32,256]{2,1,0:T(8,128)(2,1)S(1)} %get-tuple-element.19), channel_id=1, source_target_pairs={{0,1},{1,0},{2,3},{3,2},{4,5},{5,4},{6,7},{7,6},{8,9},{9,8},{10,11... | collective-permute-start | bytes 147464 | tf_op jit(solution)/shard_map/ppermute | solution.py:164
  17.1 1.6 %copy-start = (f32[8,2048]{1,0:T(8,128)S(1)}, f32[8,2048]{1,0:T(8,128)}, u32[]{:S(2)}) copy-start(f32[8,2048]{1,0:T(8,128)} %gate_ref.1) | copy-start | bytes 196612
  17.1 1.6 %copy-start.1 = (s32[2,4]{1,0:T(2,128)S(1)}, s32[2,4]{1,0:T(2,128)}, u32[]{:S(2)}) copy-start(s32[2,4]{1,0:T(2,128)} %slot_ref.1) | copy-start | bytes 100
  17.1 1.6 %copy-start.2 = (s32[2,4]{1,0:T(2,128)S(1)}, s32[2,4]{1,0:T(2,128)}, u32[]{:S(2)}) copy-start(s32[2,4]{1,0:T(2,128)} %level_ref.1) | copy-start | bytes 100
  17.1 1.6 %collective-permute-start.7 = (bf16[8,2,32,256]{3,2,1,0:T(8,128)(2,1)S(1)}, bf16[8,2,32,256]{3,2,1,0:T(8,128)(2,1)S(1)}, u32[]{:S(2)}, u32[]{:S(2)}) collective-permute-start(bf16[8,2,32,256]{3,2,1,0:T(8,128)(2,1)S(1)} %shard_map.65), channel_id=1, source_target_pairs={{0,8},{8,0},{1,9},{9,1},{2,10},{10,2},{3,11},{11,3},{4,12},{12,4},... | collective-permute-start | bytes 786440 | tf_op jit(solution)/shard_map/ppermute | solution.py:178

commit v23 on v22

--- a/solution.py
+++ b/solution.py
@@ -108,7 +108,7 @@
     shown = jnp.concatenate(shown, axis=1)
     ones = jnp.ones((key_count, HEAD), jnp.bfloat16)
     scale = math.log2(math.e) / math.sqrt(HEAD)
-    step = max(1, min(devices, 128 // rows))
+    step = max(1, min(devices, 256 // rows))
     for column in range(0, width, HEAD):
         part = slice(column, column + HEAD)
         gates = [row[:, part].reshape(1, 1, 1, HEAD) for row in gate_rows]

time: 31.7 us -> 31.7 us (level)
  no operation moved by 1% of the time
where the time goes in v23:
time: 31.7 us; the launch traced here: 31.5 us
  starting transfers between devices  12.5 us (39%)
  blocking collectives  11.4 us (36%)
  waiting for transfers between devices  5.08 us (16%)
  Pallas kernels  2.49 us (8%)
    ppermute x7, starting transfers between devices, whole_heads(): lax.ppermute(piece, 'seq', [(one, one ^ away) for one in range(devices)])  12.4 us
    all_to_all x1, blocking collectives, whole_heads(): lax.all_to_all(answer, 'seq', split_axis=0, concat_axis=0, tiled=True)  11.4 us
    ppermute x7, waiting for transfers between devices, whole_heads(): lax.ppermute(piece, 'seq', [(one, one ^ away) for one in range(devices)])  3.56 us
    ppermute x1, waiting for transfers between devices, whole_heads(): lax.ppermute(stacked, 'frame', [(one, (one - away) % groups) for one in r...  1.52 us
    pallas_call x1, Pallas kernels, whole_heads(): pl.pallas_call(pack, out_shape=[jax.ShapeDtypeStruct((3, rows, width), qu...  1.06 us
    pallas_call x1, Pallas kernels, whole_heads(): pl.pallas_call(functools.partial(attend, tokens=tokens), out_shape=jax.Sh...  0.73 us
    pallas_call x1, Pallas kernels, whole_heads(): pl.pallas_call(unpack, out_shape=jax.ShapeDtypeStruct((rows, all_width),...  0.69 us
  transfers between devices with their start and end apart: 8, of which 5 were waited for; matrix products, arithmetic and copies ran while one was open for 0% of the time, Pallas kernels for 0%

profile of v23, /device:TPU:0, one launch (start us, length us, event | category | flops | bytes accessed | tf_op | source)
XLA Modules:
  0.0 31.5 jit_solution(15905214589504382372)
XLA Ops:
  0.0 1.1 %shard_map.64 = (bf16[3,32,256]{2,1,0:T(8,128)(2,1)S(1)}, bf16[3,32,256]{2,1,0:T(8,128)(2,1)S(1)}, bf16[3,32,256]{2,1,0:T(8,128)(2,1)S(1)}, bf16[3,32,256]{2,1,0...) custom-call(bf16[32,2048]{1,0:T(8,128)(2,1)} %bitcast.4, ...), custom_call_target="tpu_custom_call" | custom-call | tf_op jit(solution)/shard_map/pallas_call | solution.py:147
  1.1 5.0 %collective-permute-start = (bf16[3,32,256]{2,1,0:T(8,128)(2,1)S(1)}, bf16[3,32,256]{2,1,0:T(8,128)(2,1)S(1)}, u32[]{:S(2)}, u32[]{:S(2)}) collective-permute-start(bf16[3,32,256]{2,1,0:T(8,128)(2,1)S(1)} %get-tuple-element.13), channel_id=1, source_target_pairs={{0,5},{1,4},{2,7},{3,6},{4,1},{5,0},{6,3},{7,2},{8,13},{9,12},{10,... | collective-permute-start | bytes 147464 | tf_op jit(solution)/shard_map/ppermute | solution.py:164
  6.1 1.3 %collective-permute-start.1 = (bf16[3,32,256]{2,1,0:T(8,128)(2,1)S(1)}, bf16[3,32,256]{2,1,0:T(8,128)(2,1)S(1)}, u32[]{:S(2)}, u32[]{:S(2)}) collective-permute-start(bf16[3,32,256]{2,1,0:T(8,128)(2,1)S(1)} %get-tuple-element.14), channel_id=1, source_target_pairs={{0,6},{1,7},{2,4},{3,5},{4,2},{5,3},{6,0},{7,1},{8,14},{9,15},{10,... | collective-permute-start | bytes 147464 | tf_op jit(solution)/shard_map/ppermute | solution.py:164
  7.4 0.2 collective-permute-start.2
  7.6 3.8 %collective-permute-start.3 = (bf16[3,32,256]{2,1,0:T(8,128)(2,1)S(1)}, bf16[3,32,256]{2,1,0:T(8,128)(2,1)S(1)}, u32[]{:S(2)}, u32[]{:S(2)}) collective-permute-start(bf16[3,32,256]{2,1,0:T(8,128)(2,1)S(1)} %get-tuple-element.16), channel_id=1, source_target_pairs={{0,7},{1,6},{2,5},{3,4},{4,3},{5,2},{6,1},{7,0},{8,15},{9,14},{10,... | collective-permute-start | bytes 147464 | tf_op jit(solution)/shard_map/ppermute | solution.py:164
  11.5 0.5 %collective-permute-start.4 = (bf16[3,32,256]{2,1,0:T(8,128)(2,1)S(1)}, bf16[3,32,256]{2,1,0:T(8,128)(2,1)S(1)}, u32[]{:S(2)}, u32[]{:S(2)}) collective-permute-start(bf16[3,32,256]{2,1,0:T(8,128)(2,1)S(1)} %get-tuple-element.17), channel_id=1, source_target_pairs={{0,2},{1,3},{2,0},{3,1},{4,6},{5,7},{6,4},{7,5},{8,10},{9,11},{10,... | collective-permute-start | bytes 147464 | tf_op jit(solution)/shard_map/ppermute | solution.py:164
  11.9 0.0 collective-permute-done.refs_0_
  11.9 1.0 %collective-permute-start.5 = (bf16[3,32,256]{2,1,0:T(8,128)(2,1)S(1)}, bf16[3,32,256]{2,1,0:T(8,128)(2,1)S(1)}, u32[]{:S(2)}, u32[]{:S(2)}) collective-permute-start(bf16[3,32,256]{2,1,0:T(8,128)(2,1)S(1)} %get-tuple-element.18), channel_id=1, source_target_pairs={{0,4},{1,5},{2,6},{3,7},{4,0},{5,1},{6,2},{7,3},{8,12},{9,13},{10,... | collective-permute-start | bytes 147464 | tf_op jit(solution)/shard_map/ppermute | solution.py:164
  13.0 0.0 collective-permute-done.1.refs_1_
  13.0 0.5 %collective-permute-start.6 = (bf16[3,32,256]{2,1,0:T(8,128)(2,1)S(1)}, bf16[3,32,256]{2,1,0:T(8,128)(2,1)S(1)}, u32[]{:S(2)}, u32[]{:S(2)}) collective-permute-start(bf16[3,32,256]{2,1,0:T(8,128)(2,1)S(1)} %get-tuple-element.19), channel_id=1, source_target_pairs={{0,1},{1,0},{2,3},{3,2},{4,5},{5,4},{6,7},{7,6},{8,9},{9,8},{10,11... | collective-permute-start | bytes 147464 | tf_op jit(solution)/shard_map/ppermute | solution.py:164
  13.5 0.0 collective-permute-done.2.refs_2_
  13.5 1.2 %collective-permute-done.3.refs_3_ = bf16[3,32,256]{2,1,0:T(8,128)(2,1)S(1)} collective-permute-done((bf16[3,32,256]{2,1,0:T(8,128)(2,1)S(1)}, bf16[3,32,256]{2,1,0:T(8,128)(2,1)S(1)}, u32[]{:S(2)}, u32[]{:S(2)}) %collective-permute-start.3) | collective-permute-done | bytes 49184 | tf_op jit(solution)/shard_map/ppermute | solution.py:164
  14.7 0.9 %collective-permute-done.4.refs_4_ = bf16[3,32,256]{2,1,0:T(8,128)(2,1)S(1)} collective-permute-done((bf16[3,32,256]{2,1,0:T(8,128)(2,1)S(1)}, bf16[3,32,256]{2,1,0:T(8,128)(2,1)S(1)}, u32[]{:S(2)}, u32[]{:S(2)}) %collective-permute-start.4) | collective-permute-done | bytes 49184 | tf_op jit(solution)/shard_map/ppermute | solution.py:164
  15.6 1.4 %collective-permute-done.5.refs_5_ = bf16[3,32,256]{2,1,0:T(8,128)(2,1)S(1)} collective-permute-done((bf16[3,32,256]{2,1,0:T(8,128)(2,1)S(1)}, bf16[3,32,256]{2,1,0:T(8,128)(2,1)S(1)}, u32[]{:S(2)}, u32[]{:S(2)}) %collective-permute-start.5) | collective-permute-done | bytes 49184 | tf_op jit(solution)/shard_map/ppermute | solution.py:164
  16.9 0.1 collective-permute-done.6.refs_6_
  17.1 0.0 copy-start
  17.1 0.0 copy-start.1
  17.1 0.0 copy-start.2
  17.1 0.1 collective-permute-start.7
  17.2 1.5 %collective-permute-done.7.refs_8_ = bf16[8,2,32,256]{3,2,1,0:T(8,128)(2,1)S(1)} collective-permute-done((bf16[8,2,32,256]{3,2,1,0:T(8,128)(2,1)S(1)}, bf16[8,2,32,256]{3,2,1,0:T(8,128)(2,1)S(1)}, u32[]{:S(2)}, u32[]{:S(2)}) %collective-permute-start.7) | collective-permute-done | bytes 262176 | tf_op jit(solution)/shard_map/ppermute | solution.py:178
  18.7 0.0 copy-done
  18.7 0.0 copy-done.1
  18.7 0.0 copy-done.2
  18.7 0.7 %shard_map.66 = bf16[8,32,256]{2,1,0:T(8,128)(2,1)S(1)} custom-call(s32[2,4]{1,0:T(2,128)S(1)} %copy-done.1, s32[2,4]{1,0:T(2,128)S(1)} %copy-done.2, f32[8,2048]{1,0:T(8,128)S(1)} %copy-done, bf16[3,32,256]{2,1,0:T(8,128)(2,1)S(1)} %collective-permute-done.refs_0_, bf16[3,32,256]{2,1,0:T(8,128)(2,1)S(1)} %collective-permute-done.1.refs_1_, ...), custom_call_target="tpu_custom_call" | custom-call | tf_op jit(solution)/shard_map/pallas_call | solution.py:181
  19.4 11.4 %all_to_all.5.held_ref = bf16[8,32,256]{2,1,0:T(8,128)(2,1)S(1)} all-to-all(bf16[8,32,256]{2,1,0:T(8,128)(2,1)S(1)} %shard_map.66), channel_id=1, replica_groups=mesh['rollout'=2,'frame'=2,'seq'=8] {'seq'}, dimensions={0} | all-to-all | bytes 262144 | tf_op jit(solution)/shard_map/all_to_all | solution.py:188
  30.8 0.7 %shard_map.67 = bf16[32,2048]{1,0:T(8,128)(2,1)} custom-call(bf16[8,32,256]{2,1,0:T(8,128)(2,1)S(1)} %all_to_all.5.held_ref), custom_call_target="tpu_custom_call" | custom-call | tf_op jit(solution)/shard_map/pallas_call | solution.py:189
  (1 shorter events, 0.0 us)
Async XLA Ops:
  1.1 10.9 %collective-permute-start = (bf16[3,32,256]{2,1,0:T(8,128)(2,1)S(1)}, bf16[3,32,256]{2,1,0:T(8,128)(2,1)S(1)}, u32[]{:S(2)}, u32[]{:S(2)}) collective-permute-start(bf16[3,32,256]{2,1,0:T(8,128)(2,1)S(1)} %get-tuple-element.13), channel_id=1, source_target_pairs={{0,5},{1,4},{2,7},{3,6},{4,1},{5,0},{6,3},{7,2},{8,13},{9,12},{10,... | collective-permute-start | bytes 147464 | tf_op jit(solution)/shard_map/ppermute | solution.py:164
  6.1 6.9 %collective-permute-start.1 = (bf16[3,32,256]{2,1,0:T(8,128)(2,1)S(1)}, bf16[3,32,256]{2,1,0:T(8,128)(2,1)S(1)}, u32[]{:S(2)}, u32[]{:S(2)}) collective-permute-start(bf16[3,32,256]{2,1,0:T(8,128)(2,1)S(1)} %get-tuple-element.14), channel_id=1, source_target_pairs={{0,6},{1,7},{2,4},{3,5},{4,2},{5,3},{6,0},{7,1},{8,14},{9,15},{10,... | collective-permute-start | bytes 147464 | tf_op jit(solution)/shard_map/ppermute | solution.py:164
  7.4 6.1 %collective-permute-start.2 = (bf16[3,32,256]{2,1,0:T(8,128)(2,1)S(1)}, bf16[3,32,256]{2,1,0:T(8,128)(2,1)S(1)}, u32[]{:S(2)}, u32[]{:S(2)}) collective-permute-start(bf16[3,32,256]{2,1,0:T(8,128)(2,1)S(1)} %get-tuple-element.15), channel_id=1, source_target_pairs={{0,3},{1,2},{2,1},{3,0},{4,7},{5,6},{6,5},{7,4},{8,11},{9,10},{10,... | collective-permute-start | bytes 147464 | tf_op jit(solution)/shard_map/ppermute | solution.py:164
  7.6 7.1 %collective-permute-start.3 = (bf16[3,32,256]{2,1,0:T(8,128)(2,1)S(1)}, bf16[3,32,256]{2,1,0:T(8,128)(2,1)S(1)}, u32[]{:S(2)}, u32[]{:S(2)}) collective-permute-start(bf16[3,32,256]{2,1,0:T(8,128)(2,1)S(1)} %get-tuple-element.16), channel_id=1, source_target_pairs={{0,7},{1,6},{2,5},{3,4},{4,3},{5,2},{6,1},{7,0},{8,15},{9,14},{10,... | collective-permute-start | bytes 147464 | tf_op jit(solution)/shard_map/ppermute | solution.py:164
  11.5 4.1 %collective-permute-start.4 = (bf16[3,32,256]{2,1,0:T(8,128)(2,1)S(1)}, bf16[3,32,256]{2,1,0:T(8,128)(2,1)S(1)}, u32[]{:S(2)}, u32[]{:S(2)}) collective-permute-start(bf16[3,32,256]{2,1,0:T(8,128)(2,1)S(1)} %get-tuple-element.17), channel_id=1, source_target_pairs={{0,2},{1,3},{2,0},{3,1},{4,6},{5,7},{6,4},{7,5},{8,10},{9,11},{10,... | collective-permute-start | bytes 147464 | tf_op jit(solution)/shard_map/ppermute | solution.py:164
  11.9 5.0 %collective-permute-start.5 = (bf16[3,32,256]{2,1,0:T(8,128)(2,1)S(1)}, bf16[3,32,256]{2,1,0:T(8,128)(2,1)S(1)}, u32[]{:S(2)}, u32[]{:S(2)}) collective-permute-start(bf16[3,32,256]{2,1,0:T(8,128)(2,1)S(1)} %get-tuple-element.18), channel_id=1, source_target_pairs={{0,4},{1,5},{2,6},{3,7},{4,0},{5,1},{6,2},{7,3},{8,12},{9,13},{10,... | collective-permute-start | bytes 147464 | tf_op jit(solution)/shard_map/ppermute | solution.py:164
  13.0 4.1 %collective-permute-start.6 = (bf16[3,32,256]{2,1,0:T(8,128)(2,1)S(1)}, bf16[3,32,256]{2,1,0:T(8,128)(2,1)S(1)}, u32[]{:S(2)}, u32[]{:S(2)}) collective-permute-start(bf16[3,32,256]{2,1,0:T(8,128)(2,1)S(1)} %get-tuple-element.19), channel_id=1, source_target_pairs={{0,1},{1,0},{2,3},{3,2},{4,5},{5,4},{6,7},{7,6},{8,9},{9,8},{10,11... | collective-permute-start | bytes 147464 | tf_op jit(solution)/shard_map/ppermute | solution.py:164
  17.1 1.6 %copy-start = (f32[8,2048]{1,0:T(8,128)S(1)}, f32[8,2048]{1,0:T(8,128)}, u32[]{:S(2)}) copy-start(f32[8,2048]{1,0:T(8,128)} %gate_ref.1) | copy-start | bytes 196612
  17.1 1.6 %copy-start.1 = (s32[2,4]{1,0:T(2,128)S(1)}, s32[2,4]{1,0:T(2,128)}, u32[]{:S(2)}) copy-start(s32[2,4]{1,0:T(2,128)} %slot_ref.1) | copy-start | bytes 100
  17.1 1.6 %copy-start.2 = (s32[2,4]{1,0:T(2,128)S(1)}, s32[2,4]{1,0:T(2,128)}, u32[]{:S(2)}) copy-start(s32[2,4]{1,0:T(2,128)} %level_ref.1) | copy-start | bytes 100
  17.1 1.6 %collective-permute-start.7 = (bf16[8,2,32,256]{3,2,1,0:T(8,128)(2,1)S(1)}, bf16[8,2,32,256]{3,2,1,0:T(8,128)(2,1)S(1)}, u32[]{:S(2)}, u32[]{:S(2)}) collective-permute-start(bf16[8,2,32,256]{3,2,1,0:T(8,128)(2,1)S(1)} %shard_map.65), channel_id=1, source_target_pairs={{0,8},{8,0},{1,9},{9,1},{2,10},{10,2},{3,11},{11,3},{4,12},{12,4},... | collective-permute-start | bytes 786440 | tf_op jit(solution)/shard_map/ppermute | solution.py:178

commit v24 on v23

--- a/solution.py
+++ b/solution.py
@@ -78,65 +78,94 @@
     return ref[row : row + 1, column : column + 1]
 
 
-def attend(slot_ref, level_ref, gate_ref, *refs, tokens):
-    out_ref = refs[-1]
-    devices, rows, width = out_ref.shape
-    own_refs, pair_refs = refs[:devices], refs[devices:-1]
+def shown_keys(slot_ref, first, last, group_keys, tokens):
     groups, local_frames = slot_ref.shape
-    group_keys = devices * rows
-    key_count = groups * group_keys
     group = lax.axis_index("frame")
+    key_count = (last - first) * group_keys
     index = lax.broadcasted_iota(jnp.int32, (1, key_count), 1)
-    frame = (index // group_keys + group) % groups * local_frames + index // tokens % local_frames
+    frame = (index // group_keys + first + group) % groups * local_frames
+    frame = frame + index // tokens % local_frames
     key_slots = jnp.zeros((1, key_count), jnp.int32)
     for one in range(groups * local_frames):
         key_slots = jnp.where(
             frame == one, entry(slot_ref, one // local_frames, one % local_frames), key_slots
         )
-    place = lax.axis_index("seq")
+    shown = []
+    for local in range(local_frames):
+        slot = entry(slot_ref, 0, local)
+        for other in range(1, groups):
+            slot = jnp.where(group == other, entry(slot_ref, other, local), slot)
+        shown.append(jnp.where(key_slots <= slot, 0.0, -jnp.inf).reshape(1, 1, 1, key_count))
+    return jnp.concatenate(shown, axis=1)
+
+
+def scores_of(queries, keys, shown, tokens):
+    count, local_frames = keys.shape[0], shown.shape[1]
+    scores = lax.dot_general(
+        queries, keys, (((1,), (1,)), ((), ())), preferred_element_type=jnp.float32
+    )
+    scores = scores.reshape(-1, local_frames, tokens, count)
+    scores = scores * (math.log2(math.e) / math.sqrt(HEAD)) + shown
+    return scores.reshape(-1, count)
+
+
+def weigh(scores, values):
+    values = jnp.concatenate([values, jnp.ones(values.shape, values.dtype)], axis=1)
+    return jnp.dot(scores.astype(jnp.bfloat16), values, preferred_element_type=jnp.float32)
+
+
+def attend_own(slot_ref, *refs, tokens):
+    *own_refs, sum_ref, top_ref = refs
+    devices, (_, rows, width) = len(own_refs), own_refs[0].shape
+    shown = shown_keys(slot_ref, 0, 1, devices * rows, tokens)
+    for number, column in enumerate(range(0, width, HEAD)):
+        part = slice(column, column + HEAD)
+        queries, keys, values = (
+            jnp.concatenate([ref[kind, :, part] for ref in own_refs]) for kind in range(3)
+        )
+        scores = scores_of(queries, keys, shown, tokens)
+        top = jnp.max(scores, axis=1, keepdims=True)
+        sum_ref[number] = weigh(jnp.exp2(scores - top), values)
+        top_ref[number] = jnp.broadcast_to(top, top_ref.shape[1:])
+
+
+def attend(slot_ref, level_ref, gate_ref, sum_ref, top_ref, *refs, tokens):
+    out_ref = refs[-1]
+    devices, rows, width = out_ref.shape
+    own_refs, pair_refs = refs[:devices], refs[devices:-1]
+    groups, local_frames = slot_ref.shape
+    group, place = lax.axis_index("frame"), lax.axis_index("seq")
     gate_blocks = gate_ref[:, pl.ds(pl.multiple_of(place * width, width), width)]
     level_rows = lax.broadcasted_iota(jnp.int32, gate_blocks.shape, 0)
-    shown, gate_rows = [], []
+    gate_rows = []
     for local in range(local_frames):
-        slot, level = entry(slot_ref, 0, local), entry(level_ref, 0, local)
+        level = entry(level_ref, 0, local)
         for other in range(1, groups):
-            slot = jnp.where(group == other, entry(slot_ref, other, local), slot)
             level = jnp.where(group == other, entry(level_ref, other, local), level)
-        shown.append(jnp.where(key_slots <= slot, 0.0, -jnp.inf).reshape(1, 1, 1, key_count))
         gate = jnp.where(level_rows == level, gate_blocks, 0.0)
         gate_rows.append(jnp.sum(gate, axis=0, keepdims=True))
-    shown = jnp.concatenate(shown, axis=1)
-    ones = jnp.ones((key_count, HEAD), jnp.bfloat16)
-    scale = math.log2(math.e) / math.sqrt(HEAD)
-    step = max(1, min(devices, 256 // rows))
-    for column in range(0, width, HEAD):
+    if pair_refs:
+        shown = shown_keys(slot_ref, 1, groups, devices * rows, tokens)
+    for number, column in enumerate(range(0, width, HEAD)):
         part = slice(column, column + HEAD)
         gates = [row[:, part].reshape(1, 1, 1, HEAD) for row in gate_rows]
         gates = jnp.concatenate(gates, axis=1)
-        keys, values = (
-            jnp.concatenate(
-                [ref[1 + kind, :, part] for ref in own_refs]
-                + [ref[:, kind, :, part].reshape(ref.shape[0] * rows, HEAD) for ref in pair_refs]
+        mixed = sum_ref[number]
+        if pair_refs:
+            keys, values = (
+                jnp.concatenate([ref[:, kind, :, part].reshape(-1, HEAD) for ref in pair_refs])
+                for kind in range(2)
             )
-            for kind in range(2)
-        )
-        values = jnp.concatenate([values, ones], axis=1)
-        for start in range(0, devices, step):
-            queries = jnp.concatenate([ref[0, :, part] for ref in own_refs[start : start + step]])
-            scores = lax.dot_general(
-                queries, keys, (((1,), (1,)), ((), ())), preferred_element_type=jnp.float32
-            )
-            scores = scores.reshape(step, local_frames, tokens, key_count) * scale + shown
-            scores = scores.reshape(step * rows, key_count)
-            weights = jnp.exp2(scores - jnp.max(scores, axis=1, keepdims=True))
-            mixed = jnp.dot(
-                weights.astype(jnp.bfloat16), values, preferred_element_type=jnp.float32
-            )
-            mixed = mixed[:, :HEAD] / mixed[:, HEAD:]
-            mixed = mixed.reshape(step, local_frames, tokens, HEAD) * gates
-            mixed = mixed.reshape(step, rows, HEAD).astype(out_ref.dtype)
-            for number, away in enumerate(send_order(devices)[start : start + step]):
-                out_ref[place ^ away, :, part] = mixed[number]
+            queries = jnp.concatenate([ref[0, :, part] for ref in own_refs])
+            scores = scores_of(queries, keys, shown, tokens)
+            own_top = top_ref[number][:, :1]
+            top = jnp.maximum(own_top, jnp.max(scores, axis=1, keepdims=True))
+            mixed = mixed * jnp.exp2(own_top - top) + weigh(jnp.exp2(scores - top), values)
+        mixed = mixed[:, :HEAD] / mixed[:, HEAD:]
+        mixed = mixed.reshape(devices, local_frames, tokens, HEAD) * gates
+        mixed = mixed.reshape(devices, rows, HEAD).astype(out_ref.dtype)
+        for at, away in enumerate(send_order(devices)):
+            out_ref[place ^ away, :, part] = mixed[at]
 
 
 def whole_heads(queries, keys, values, slot_of, level_of, gate_table):
@@ -178,13 +207,29 @@
         lax.ppermute(stacked, "frame", [(one, (one - away) % groups) for one in range(groups)])
         for away in range(1, groups)
     ]
+    heads, own_rows = width // HEAD, devices * rows
+    sums, tops = pl.pallas_call(
+        functools.partial(attend_own, tokens=tokens),
+        out_shape=[
+            jax.ShapeDtypeStruct((heads, own_rows, 2 * HEAD), jnp.float32),
+            jax.ShapeDtypeStruct((heads, own_rows, HEAD), jnp.float32),
+        ],
+        in_specs=[VMEM] * (1 + devices),
+        out_specs=[VMEM] * 2,
+        compiler_params=PARAMS,
+        cost_estimate=pl.CostEstimate(
+            flops=6 * heads * own_rows * own_rows * HEAD,
+            bytes_accessed=2 * 4 * heads * own_rows * HEAD,
+            transcendentals=heads * own_rows * own_rows,
+        ),
+    )(slot_of, *pieces)
     answer = pl.pallas_call(
         functools.partial(attend, tokens=tokens),
         out_shape=jax.ShapeDtypeStruct((devices, rows, width), queries.dtype),
-        in_specs=[VMEM] * (3 + devices + len(stacks)),
+        in_specs=[VMEM] * (5 + devices + len(stacks)),
         out_specs=VMEM,
         compiler_params=PARAMS,
-    )(slot_of, level_of, gate_table, *pieces, *stacks)
+    )(slot_of, level_of, gate_table, sums, tops, *pieces, *stacks)
     answer = lax.all_to_all(answer, "seq", split_axis=0, concat_axis=0, tiled=True)
     answer = pl.pallas_call(
         unpack,

time: 31.7 us -> 32.5 us (1.025)
  local copies, waits for them, and re-layouts: 0.01 us -> 1.25 us
  waiting for transfers between devices: 5.08 us -> 4.02 us
  Pallas kernels: 2.49 us -> 3.02 us
    unnamed x6, local copies, waits for them, and re-layouts: 0.01 us -> 1.25 us
    ppermute x1, waiting for transfers between devices: 1.52 us -> 0.47 us  [whole_heads(): lax.ppermute(stacked, 'frame', [(one, (one - away) % groups) for one in r...]
    pallas_call x0 -> x1, Pallas kernels: none -> 0.49 us  [whole_heads(): pl.pallas_call(functools.partial(attend_own, tokens=tokens), out_shape=[j...]
  transfers between devices with their start and end apart: 8 -> 8, of which waited for: 5 -> 5; matrix products, arithmetic and copies ran while one was open for 0% -> 0% of each run, Pallas kernels for 0% -> 2%
where the time goes in v24:
time: 32.5 us; the launch traced here: 32.2 us
  starting transfers between devices  12.5 us (38%)
  blocking collectives  11.4 us (35%)
  waiting for transfers between devices  4.02 us (12%)
  Pallas kernels  3.02 us (9%)
  local copies, waits for them, and re-layouts  1.25 us (4%)
    ppermute x7, starting transfers between devices, whole_heads(): lax.ppermute(piece, 'seq', [(one, one ^ away) for one in range(devices)])  12.4 us
    all_to_all x1, blocking collectives, whole_heads(): lax.all_to_all(answer, 'seq', split_axis=0, concat_axis=0, tiled=True)  11.4 us
    ppermute x7, waiting for transfers between devices, whole_heads(): lax.ppermute(piece, 'seq', [(one, one ^ away) for one in range(devices)])  3.56 us
    unnamed x6, local copies, waits for them, and re-layouts  1.25 us
    pallas_call x1, Pallas kernels, whole_heads(): pl.pallas_call(pack, out_shape=[jax.ShapeDtypeStruct((3, rows, width), qu...  1.06 us
    pallas_call x1, Pallas kernels, whole_heads(): pl.pallas_call(functools.partial(attend, tokens=tokens), out_shape=jax.Sh...  0.76 us
    pallas_call x1, Pallas kernels, whole_heads(): pl.pallas_call(unpack, out_shape=jax.ShapeDtypeStruct((rows, all_width),...  0.69 us
  transfers between devices with their start and end apart: 8, of which 5 were waited for; matrix products, arithmetic and copies ran while one was open for 0% of the time, Pallas kernels for 2%

profile of v24, /device:TPU:0, one launch (start us, length us, event | category | flops | bytes accessed | tf_op | source)
XLA Modules:
  0.0 32.2 jit_solution(3244882916672626758)
XLA Ops:
  0.0 1.1 %shard_map.64 = (bf16[3,32,256]{2,1,0:T(8,128)(2,1)S(1)}, bf16[3,32,256]{2,1,0:T(8,128)(2,1)S(1)}, bf16[3,32,256]{2,1,0:T(8,128)(2,1)S(1)}, bf16[3,32,256]{2,1,0...) custom-call(bf16[32,2048]{1,0:T(8,128)(2,1)} %bitcast.4, ...), custom_call_target="tpu_custom_call" | custom-call | tf_op jit(solution)/shard_map/pallas_call | solution.py:176
  1.1 5.0 %collective-permute-start = (bf16[3,32,256]{2,1,0:T(8,128)(2,1)S(1)}, bf16[3,32,256]{2,1,0:T(8,128)(2,1)S(1)}, u32[]{:S(2)}, u32[]{:S(2)}) collective-permute-start(bf16[3,32,256]{2,1,0:T(8,128)(2,1)S(1)} %get-tuple-element.15), channel_id=1, source_target_pairs={{0,5},{1,4},{2,7},{3,6},{4,1},{5,0},{6,3},{7,2},{8,13},{9,12},{10,... | collective-permute-start | bytes 147464 | tf_op jit(solution)/shard_map/ppermute | solution.py:193
  6.1 1.3 %collective-permute-start.1 = (bf16[3,32,256]{2,1,0:T(8,128)(2,1)S(1)}, bf16[3,32,256]{2,1,0:T(8,128)(2,1)S(1)}, u32[]{:S(2)}, u32[]{:S(2)}) collective-permute-start(bf16[3,32,256]{2,1,0:T(8,128)(2,1)S(1)} %get-tuple-element.16), channel_id=1, source_target_pairs={{0,6},{1,7},{2,4},{3,5},{4,2},{5,3},{6,0},{7,1},{8,14},{9,15},{10,... | collective-permute-start | bytes 147464 | tf_op jit(solution)/shard_map/ppermute | solution.py:193
  7.4 0.2 collective-permute-start.2
  7.6 3.8 %collective-permute-start.3 = (bf16[3,32,256]{2,1,0:T(8,128)(2,1)S(1)}, bf16[3,32,256]{2,1,0:T(8,128)(2,1)S(1)}, u32[]{:S(2)}, u32[]{:S(2)}) collective-permute-start(bf16[3,32,256]{2,1,0:T(8,128)(2,1)S(1)} %get-tuple-element.18), channel_id=1, source_target_pairs={{0,7},{1,6},{2,5},{3,4},{4,3},{5,2},{6,1},{7,0},{8,15},{9,14},{10,... | collective-permute-start | bytes 147464 | tf_op jit(solution)/shard_map/ppermute | solution.py:193
  11.5 0.5 %collective-permute-start.4 = (bf16[3,32,256]{2,1,0:T(8,128)(2,1)S(1)}, bf16[3,32,256]{2,1,0:T(8,128)(2,1)S(1)}, u32[]{:S(2)}, u32[]{:S(2)}) collective-permute-start(bf16[3,32,256]{2,1,0:T(8,128)(2,1)S(1)} %get-tuple-element.19), channel_id=1, source_target_pairs={{0,2},{1,3},{2,0},{3,1},{4,6},{5,7},{6,4},{7,5},{8,10},{9,11},{10,... | collective-permute-start | bytes 147464 | tf_op jit(solution)/shard_map/ppermute | solution.py:193
  11.9 0.0 collective-permute-done.refs_0_
  11.9 1.0 %collective-permute-start.5 = (bf16[3,32,256]{2,1,0:T(8,128)(2,1)S(1)}, bf16[3,32,256]{2,1,0:T(8,128)(2,1)S(1)}, u32[]{:S(2)}, u32[]{:S(2)}) collective-permute-start(bf16[3,32,256]{2,1,0:T(8,128)(2,1)S(1)} %get-tuple-element.20), channel_id=1, source_target_pairs={{0,4},{1,5},{2,6},{3,7},{4,0},{5,1},{6,2},{7,3},{8,12},{9,13},{10,... | collective-permute-start | bytes 147464 | tf_op jit(solution)/shard_map/ppermute | solution.py:193
  13.0 0.0 collective-permute-done.1.refs_1_
  13.0 0.5 %collective-permute-start.6 = (bf16[3,32,256]{2,1,0:T(8,128)(2,1)S(1)}, bf16[3,32,256]{2,1,0:T(8,128)(2,1)S(1)}, u32[]{:S(2)}, u32[]{:S(2)}) collective-permute-start(bf16[3,32,256]{2,1,0:T(8,128)(2,1)S(1)} %get-tuple-element.21), channel_id=1, source_target_pairs={{0,1},{1,0},{2,3},{3,2},{4,5},{5,4},{6,7},{7,6},{8,9},{9,8},{10,11... | collective-permute-start | bytes 147464 | tf_op jit(solution)/shard_map/ppermute | solution.py:193
  13.5 0.0 collective-permute-done.2.refs_2_
  13.5 1.2 %collective-permute-done.3.refs_3_ = bf16[3,32,256]{2,1,0:T(8,128)(2,1)S(1)} collective-permute-done((bf16[3,32,256]{2,1,0:T(8,128)(2,1)S(1)}, bf16[3,32,256]{2,1,0:T(8,128)(2,1)S(1)}, u32[]{:S(2)}, u32[]{:S(2)}) %collective-permute-start.3) | collective-permute-done | bytes 49184 | tf_op jit(solution)/shard_map/ppermute | solution.py:193
  14.7 0.9 %collective-permute-done.4.refs_4_ = bf16[3,32,256]{2,1,0:T(8,128)(2,1)S(1)} collective-permute-done((bf16[3,32,256]{2,1,0:T(8,128)(2,1)S(1)}, bf16[3,32,256]{2,1,0:T(8,128)(2,1)S(1)}, u32[]{:S(2)}, u32[]{:S(2)}) %collective-permute-start.4) | collective-permute-done | bytes 49184 | tf_op jit(solution)/shard_map/ppermute | solution.py:193
  15.6 1.4 %collective-permute-done.5.refs_5_ = bf16[3,32,256]{2,1,0:T(8,128)(2,1)S(1)} collective-permute-done((bf16[3,32,256]{2,1,0:T(8,128)(2,1)S(1)}, bf16[3,32,256]{2,1,0:T(8,128)(2,1)S(1)}, u32[]{:S(2)}, u32[]{:S(2)}) %collective-permute-start.5) | collective-permute-done | bytes 49184 | tf_op jit(solution)/shard_map/ppermute | solution.py:193
  16.9 0.1 collective-permute-done.6.refs_6_
  17.1 0.0 copy-start.1
  17.1 0.0 copy-start
  17.1 0.1 collective-permute-start.7
  17.2 0.6 %copy-done.1 = s32[2,4]{1,0:T(2,128)S(1)} copy-done((s32[2,4]{1,0:T(2,128)S(1)}, s32[2,4]{1,0:T(2,128)}, u32[]{:S(2)}) %copy-start.1) | copy-done | bytes 56
  17.7 0.5 %shard_map.65 = (f32[2,256,256]{2,1,0:T(8,128)S(1)}, f32[2,256,128]{2,1,0:T(8,128)S(1)}) custom-call(s32[2,4]{1,0:T(2,128)S(1)} %copy-done.1, bf16[3,32,256]{2,1,0:T(8,128)(2,1)S(1)} %collective-permute-done.refs_0_, bf16[3,32,256]{2,1,0:T(8,128)(2,1)S(1)} %collective-permute-done.1.refs_1_, bf16[3,32,256]{2,1,0:T(8,128)(2,1)S(1)} %collective-permute-done.2.refs_2_, ...), custom_call_target="tpu_custom_call" | custom-call | flops 100663296 | bytes 524288 | tf_op jit(solution)/shard_map/pallas_call | solution.py:211
  18.2 0.5 %collective-permute-done.7.refs_8_ = bf16[8,2,32,256]{3,2,1,0:T(8,128)(2,1)S(1)} collective-permute-done((bf16[8,2,32,256]{3,2,1,0:T(8,128)(2,1)S(1)}, bf16[8,2,32,256]{3,2,1,0:T(8,128)(2,1)S(1)}, u32[]{:S(2)}, u32[]{:S(2)}) %collective-permute-start.7) | collective-permute-done | bytes 262176 | tf_op jit(solution)/shard_map/ppermute | solution.py:207
  18.7 0.0 copy-start.2
  18.7 0.0 copy-done
  18.7 0.7 %copy-done.2 = s32[2,4]{1,0:T(2,128)S(1)} copy-done((s32[2,4]{1,0:T(2,128)S(1)}, s32[2,4]{1,0:T(2,128)}, u32[]{:S(2)}) %copy-start.2) | copy-done | bytes 56
  19.4 0.8 %shard_map.67 = bf16[8,32,256]{2,1,0:T(8,128)(2,1)S(1)} custom-call(s32[2,4]{1,0:T(2,128)S(1)} %copy-done.1, s32[2,4]{1,0:T(2,128)S(1)} %copy-done.2, f32[8,2048]{1,0:T(8,128)S(1)} %copy-done, f32[2,256,256]{2,1,0:T(8,128)S(1)} %get-tuple-element.23.sum_ref, f32[2,256,128]{2,1,0:T(8,128)S(1)} %get-tuple-element.24.top_ref, ...), custom_call_target="tpu_custom_call" | custom-call | tf_op jit(solution)/shard_map/pallas_call | solution.py:226
  20.1 11.4 %all_to_all.5.held_ref = bf16[8,32,256]{2,1,0:T(8,128)(2,1)S(1)} all-to-all(bf16[8,32,256]{2,1,0:T(8,128)(2,1)S(1)} %shard_map.67), channel_id=1, replica_groups=mesh['rollout'=2,'frame'=2,'seq'=8] {'seq'}, dimensions={0} | all-to-all | bytes 262144 | tf_op jit(solution)/shard_map/all_to_all | solution.py:233
  31.5 0.7 %shard_map.68 = bf16[32,2048]{1,0:T(8,128)(2,1)} custom-call(bf16[8,32,256]{2,1,0:T(8,128)(2,1)S(1)} %all_to_all.5.held_ref), custom_call_target="tpu_custom_call" | custom-call | tf_op jit(solution)/shard_map/pallas_call | solution.py:234
  (1 shorter events, 0.0 us)
Async XLA Ops:
  1.1 10.9 %collective-permute-start = (bf16[3,32,256]{2,1,0:T(8,128)(2,1)S(1)}, bf16[3,32,256]{2,1,0:T(8,128)(2,1)S(1)}, u32[]{:S(2)}, u32[]{:S(2)}) collective-permute-start(bf16[3,32,256]{2,1,0:T(8,128)(2,1)S(1)} %get-tuple-element.15), channel_id=1, source_target_pairs={{0,5},{1,4},{2,7},{3,6},{4,1},{5,0},{6,3},{7,2},{8,13},{9,12},{10,... | collective-permute-start | bytes 147464 | tf_op jit(solution)/shard_map/ppermute | solution.py:193
  6.1 6.9 %collective-permute-start.1 = (bf16[3,32,256]{2,1,0:T(8,128)(2,1)S(1)}, bf16[3,32,256]{2,1,0:T(8,128)(2,1)S(1)}, u32[]{:S(2)}, u32[]{:S(2)}) collective-permute-start(bf16[3,32,256]{2,1,0:T(8,128)(2,1)S(1)} %get-tuple-element.16), channel_id=1, source_target_pairs={{0,6},{1,7},{2,4},{3,5},{4,2},{5,3},{6,0},{7,1},{8,14},{9,15},{10,... | collective-permute-start | bytes 147464 | tf_op jit(solution)/shard_map/ppermute | solution.py:193
  7.4 6.1 %collective-permute-start.2 = (bf16[3,32,256]{2,1,0:T(8,128)(2,1)S(1)}, bf16[3,32,256]{2,1,0:T(8,128)(2,1)S(1)}, u32[]{:S(2)}, u32[]{:S(2)}) collective-permute-start(bf16[3,32,256]{2,1,0:T(8,128)(2,1)S(1)} %get-tuple-element.17), channel_id=1, source_target_pairs={{0,3},{1,2},{2,1},{3,0},{4,7},{5,6},{6,5},{7,4},{8,11},{9,10},{10,... | collective-permute-start | bytes 147464 | tf_op jit(solution)/shard_map/ppermute | solution.py:193
  7.6 7.1 %collective-permute-start.3 = (bf16[3,32,256]{2,1,0:T(8,128)(2,1)S(1)}, bf16[3,32,256]{2,1,0:T(8,128)(2,1)S(1)}, u32[]{:S(2)}, u32[]{:S(2)}) collective-permute-start(bf16[3,32,256]{2,1,0:T(8,128)(2,1)S(1)} %get-tuple-element.18), channel_id=1, source_target_pairs={{0,7},{1,6},{2,5},{3,4},{4,3},{5,2},{6,1},{7,0},{8,15},{9,14},{10,... | collective-permute-start | bytes 147464 | tf_op jit(solution)/shard_map/ppermute | solution.py:193
  11.5 4.1 %collective-permute-start.4 = (bf16[3,32,256]{2,1,0:T(8,128)(2,1)S(1)}, bf16[3,32,256]{2,1,0:T(8,128)(2,1)S(1)}, u32[]{:S(2)}, u32[]{:S(2)}) collective-permute-start(bf16[3,32,256]{2,1,0:T(8,128)(2,1)S(1)} %get-tuple-element.19), channel_id=1, source_target_pairs={{0,2},{1,3},{2,0},{3,1},{4,6},{5,7},{6,4},{7,5},{8,10},{9,11},{10,... | collective-permute-start | bytes 147464 | tf_op jit(solution)/shard_map/ppermute | solution.py:193
  11.9 5.0 %collective-permute-start.5 = (bf16[3,32,256]{2,1,0:T(8,128)(2,1)S(1)}, bf16[3,32,256]{2,1,0:T(8,128)(2,1)S(1)}, u32[]{:S(2)}, u32[]{:S(2)}) collective-permute-start(bf16[3,32,256]{2,1,0:T(8,128)(2,1)S(1)} %get-tuple-element.20), channel_id=1, source_target_pairs={{0,4},{1,5},{2,6},{3,7},{4,0},{5,1},{6,2},{7,3},{8,12},{9,13},{10,... | collective-permute-start | bytes 147464 | tf_op jit(solution)/shard_map/ppermute | solution.py:193
  13.0 4.1 %collective-permute-start.6 = (bf16[3,32,256]{2,1,0:T(8,128)(2,1)S(1)}, bf16[3,32,256]{2,1,0:T(8,128)(2,1)S(1)}, u32[]{:S(2)}, u32[]{:S(2)}) collective-permute-start(bf16[3,32,256]{2,1,0:T(8,128)(2,1)S(1)} %get-tuple-element.21), channel_id=1, source_target_pairs={{0,1},{1,0},{2,3},{3,2},{4,5},{5,4},{6,7},{7,6},{8,9},{9,8},{10,11... | collective-permute-start | bytes 147464 | tf_op jit(solution)/shard_map/ppermute | solution.py:193
  17.1 0.7 %copy-start.1 = (s32[2,4]{1,0:T(2,128)S(1)}, s32[2,4]{1,0:T(2,128)}, u32[]{:S(2)}) copy-start(s32[2,4]{1,0:T(2,128)} %slot_ref.3) | copy-start | bytes 100
  17.1 1.6 %copy-start = (f32[8,2048]{1,0:T(8,128)S(1)}, f32[8,2048]{1,0:T(8,128)}, u32[]{:S(2)}) copy-start(f32[8,2048]{1,0:T(8,128)} %gate_ref.1) | copy-start | bytes 196612
  17.1 1.6 %collective-permute-start.7 = (bf16[8,2,32,256]{3,2,1,0:T(8,128)(2,1)S(1)}, bf16[8,2,32,256]{3,2,1,0:T(8,128)(2,1)S(1)}, u32[]{:S(2)}, u32[]{:S(2)}) collective-permute-start(bf16[8,2,32,256]{3,2,1,0:T(8,128)(2,1)S(1)} %shard_map.66), channel_id=1, source_target_pairs={{0,8},{8,0},{1,9},{9,1},{2,10},{10,2},{3,11},{11,3},{4,12},{12,4},... | collective-permute-start | bytes 786440 | tf_op jit(solution)/shard_map/ppermute | solution.py:207
  18.7 0.7 %copy-start.2 = (s32[2,4]{1,0:T(2,128)S(1)}, s32[2,4]{1,0:T(2,128)}, u32[]{:S(2)}) copy-start(s32[2,4]{1,0:T(2,128)} %level_ref.1) | copy-start | bytes 100

commit v25 on v22

--- a/solution.py
+++ b/solution.py
@@ -25,7 +25,7 @@
     return order + [0]
 
 
-BLOCKS = 4
+BLOCKS = 8
 
 
 def blocks_of(width):
@@ -61,15 +61,20 @@
 
 
 def unpack(held_ref, out_ref, joined_ref, sems):
-    width = held_ref.shape[-1]
-    for device in range(held_ref.shape[0]):
-        joined_ref[:, device * width : (device + 1) * width] = held_ref[device]
-    copies = [
-        pltpu.make_async_copy(joined_ref.at[:, block], out_ref.at[:, block], sems.at[number])
-        for number, block in enumerate(blocks_of(out_ref.shape[-1]))
-    ]
-    for copy in copies:
-        copy.start()
+    devices, _, width = held_ref.shape
+    blocks = blocks_of(out_ref.shape[-1])
+    copies = []
+    for number, block in enumerate(blocks):
+        for device in range(devices):
+            start = max(device * width, block.start)
+            stop = min((device + 1) * width, block.start + block.size)
+            if start < stop:
+                own = slice(start - device * width, stop - device * width)
+                joined_ref[:, start:stop] = held_ref[device, :, own]
+        copies.append(
+            pltpu.make_async_copy(joined_ref.at[:, block], out_ref.at[:, block], sems.at[number])
+        )
+        copies[-1].start()
     for copy in copies:
         copy.wait()
 

time: 31.7 us -> 31.8 us (level)
  no operation moved by 1% of the time
where the time goes in v25:
time: 31.8 us; the launch traced here: 31.6 us
  starting transfers between devices  12.5 us (39%)
  blocking collectives  11.4 us (36%)
  waiting for transfers between devices  5.08 us (16%)
  Pallas kernels  2.6 us (8%)
    ppermute x7, starting transfers between devices, whole_heads(): lax.ppermute(piece, 'seq', [(one, one ^ away) for one in range(devices)])  12.4 us
    all_to_all x1, blocking collectives, whole_heads(): lax.all_to_all(answer, 'seq', split_axis=0, concat_axis=0, tiled=True)  11.4 us
    ppermute x7, waiting for transfers between devices, whole_heads(): lax.ppermute(piece, 'seq', [(one, one ^ away) for one in range(devices)])  3.56 us
    ppermute x1, waiting for transfers between devices, whole_heads(): lax.ppermute(stacked, 'frame', [(one, (one - away) % groups) for one in r...  1.52 us
    pallas_call x1, Pallas kernels, whole_heads(): pl.pallas_call(pack, out_shape=[jax.ShapeDtypeStruct((3, rows, width), qu...  1.18 us
    pallas_call x1, Pallas kernels, whole_heads(): pl.pallas_call(unpack, out_shape=jax.ShapeDtypeStruct((rows, all_width),...  0.71 us
    pallas_call x1, Pallas kernels, whole_heads(): pl.pallas_call(functools.partial(attend, tokens=tokens), out_shape=jax.Sh...  0.7 us
  transfers between devices with their start and end apart: 8, of which 5 were waited for; matrix products, arithmetic and copies ran while one was open for 0% of the time, Pallas kernels for 0%

profile of v25, /device:TPU:0, one launch (start us, length us, event | category | flops | bytes accessed | tf_op | source)
XLA Modules:
  0.0 31.6 jit_solution(9118304020314455852)
XLA Ops:
  0.0 1.2 %shard_map.64 = (bf16[3,32,256]{2,1,0:T(8,128)(2,1)S(1)}, bf16[3,32,256]{2,1,0:T(8,128)(2,1)S(1)}, bf16[3,32,256]{2,1,0:T(8,128)(2,1)S(1)}, bf16[3,32,256]{2,1,0...) custom-call(bf16[32,2048]{1,0:T(8,128)(2,1)} %bitcast.4, ...), custom_call_target="tpu_custom_call" | custom-call | tf_op jit(solution)/shard_map/pallas_call | solution.py:152
  1.2 5.0 %collective-permute-start = (bf16[3,32,256]{2,1,0:T(8,128)(2,1)S(1)}, bf16[3,32,256]{2,1,0:T(8,128)(2,1)S(1)}, u32[]{:S(2)}, u32[]{:S(2)}) collective-permute-start(bf16[3,32,256]{2,1,0:T(8,128)(2,1)S(1)} %get-tuple-element.13), channel_id=1, source_target_pairs={{0,5},{1,4},{2,7},{3,6},{4,1},{5,0},{6,3},{7,2},{8,13},{9,12},{10,... | collective-permute-start | bytes 147464 | tf_op jit(solution)/shard_map/ppermute | solution.py:169
  6.2 1.3 %collective-permute-start.1 = (bf16[3,32,256]{2,1,0:T(8,128)(2,1)S(1)}, bf16[3,32,256]{2,1,0:T(8,128)(2,1)S(1)}, u32[]{:S(2)}, u32[]{:S(2)}) collective-permute-start(bf16[3,32,256]{2,1,0:T(8,128)(2,1)S(1)} %get-tuple-element.14), channel_id=1, source_target_pairs={{0,6},{1,7},{2,4},{3,5},{4,2},{5,3},{6,0},{7,1},{8,14},{9,15},{10,... | collective-permute-start | bytes 147464 | tf_op jit(solution)/shard_map/ppermute | solution.py:169
  7.6 0.2 collective-permute-start.2
  7.8 3.8 %collective-permute-start.3 = (bf16[3,32,256]{2,1,0:T(8,128)(2,1)S(1)}, bf16[3,32,256]{2,1,0:T(8,128)(2,1)S(1)}, u32[]{:S(2)}, u32[]{:S(2)}) collective-permute-start(bf16[3,32,256]{2,1,0:T(8,128)(2,1)S(1)} %get-tuple-element.16), channel_id=1, source_target_pairs={{0,7},{1,6},{2,5},{3,4},{4,3},{5,2},{6,1},{7,0},{8,15},{9,14},{10,... | collective-permute-start | bytes 147464 | tf_op jit(solution)/shard_map/ppermute | solution.py:169
  11.6 0.5 %collective-permute-start.4 = (bf16[3,32,256]{2,1,0:T(8,128)(2,1)S(1)}, bf16[3,32,256]{2,1,0:T(8,128)(2,1)S(1)}, u32[]{:S(2)}, u32[]{:S(2)}) collective-permute-start(bf16[3,32,256]{2,1,0:T(8,128)(2,1)S(1)} %get-tuple-element.17), channel_id=1, source_target_pairs={{0,2},{1,3},{2,0},{3,1},{4,6},{5,7},{6,4},{7,5},{8,10},{9,11},{10,... | collective-permute-start | bytes 147464 | tf_op jit(solution)/shard_map/ppermute | solution.py:169
  12.1 0.0 collective-permute-done.refs_0_
  12.1 1.0 %collective-permute-start.5 = (bf16[3,32,256]{2,1,0:T(8,128)(2,1)S(1)}, bf16[3,32,256]{2,1,0:T(8,128)(2,1)S(1)}, u32[]{:S(2)}, u32[]{:S(2)}) collective-permute-start(bf16[3,32,256]{2,1,0:T(8,128)(2,1)S(1)} %get-tuple-element.18), channel_id=1, source_target_pairs={{0,4},{1,5},{2,6},{3,7},{4,0},{5,1},{6,2},{7,3},{8,12},{9,13},{10,... | collective-permute-start | bytes 147464 | tf_op jit(solution)/shard_map/ppermute | solution.py:169
  13.1 0.0 collective-permute-done.1.refs_1_
  13.1 0.5 %collective-permute-start.6 = (bf16[3,32,256]{2,1,0:T(8,128)(2,1)S(1)}, bf16[3,32,256]{2,1,0:T(8,128)(2,1)S(1)}, u32[]{:S(2)}, u32[]{:S(2)}) collective-permute-start(bf16[3,32,256]{2,1,0:T(8,128)(2,1)S(1)} %get-tuple-element.19), channel_id=1, source_target_pairs={{0,1},{1,0},{2,3},{3,2},{4,5},{5,4},{6,7},{7,6},{8,9},{9,8},{10,11... | collective-permute-start | bytes 147464 | tf_op jit(solution)/shard_map/ppermute | solution.py:169
  13.6 0.0 collective-permute-done.2.refs_2_
  13.6 1.2 %collective-permute-done.3.refs_3_ = bf16[3,32,256]{2,1,0:T(8,128)(2,1)S(1)} collective-permute-done((bf16[3,32,256]{2,1,0:T(8,128)(2,1)S(1)}, bf16[3,32,256]{2,1,0:T(8,128)(2,1)S(1)}, u32[]{:S(2)}, u32[]{:S(2)}) %collective-permute-start.3) | collective-permute-done | bytes 49184 | tf_op jit(solution)/shard_map/ppermute | solution.py:169
  14.8 0.9 %collective-permute-done.4.refs_4_ = bf16[3,32,256]{2,1,0:T(8,128)(2,1)S(1)} collective-permute-done((bf16[3,32,256]{2,1,0:T(8,128)(2,1)S(1)}, bf16[3,32,256]{2,1,0:T(8,128)(2,1)S(1)}, u32[]{:S(2)}, u32[]{:S(2)}) %collective-permute-start.4) | collective-permute-done | bytes 49184 | tf_op jit(solution)/shard_map/ppermute | solution.py:169
  15.7 1.4 %collective-permute-done.5.refs_5_ = bf16[3,32,256]{2,1,0:T(8,128)(2,1)S(1)} collective-permute-done((bf16[3,32,256]{2,1,0:T(8,128)(2,1)S(1)}, bf16[3,32,256]{2,1,0:T(8,128)(2,1)S(1)}, u32[]{:S(2)}, u32[]{:S(2)}) %collective-permute-start.5) | collective-permute-done | bytes 49184 | tf_op jit(solution)/shard_map/ppermute | solution.py:169
  17.1 0.1 collective-permute-done.6.refs_6_
  17.2 0.0 copy-start
  17.2 0.0 copy-start.1
  17.2 0.0 copy-start.2
  17.2 0.1 collective-permute-start.7
  17.3 1.5 %collective-permute-done.7.refs_8_ = bf16[8,2,32,256]{3,2,1,0:T(8,128)(2,1)S(1)} collective-permute-done((bf16[8,2,32,256]{3,2,1,0:T(8,128)(2,1)S(1)}, bf16[8,2,32,256]{3,2,1,0:T(8,128)(2,1)S(1)}, u32[]{:S(2)}, u32[]{:S(2)}) %collective-permute-start.7) | collective-permute-done | bytes 262176 | tf_op jit(solution)/shard_map/ppermute | solution.py:183
  18.8 0.0 copy-done
  18.8 0.0 copy-done.1
  18.8 0.0 copy-done.2
  18.8 0.7 %shard_map.66 = bf16[8,32,256]{2,1,0:T(8,128)(2,1)S(1)} custom-call(s32[2,4]{1,0:T(2,128)S(1)} %copy-done.1, s32[2,4]{1,0:T(2,128)S(1)} %copy-done.2, f32[8,2048]{1,0:T(8,128)S(1)} %copy-done, bf16[3,32,256]{2,1,0:T(8,128)(2,1)S(1)} %collective-permute-done.refs_0_, bf16[3,32,256]{2,1,0:T(8,128)(2,1)S(1)} %collective-permute-done.1.refs_1_, ...), custom_call_target="tpu_custom_call" | custom-call | tf_op jit(solution)/shard_map/pallas_call | solution.py:186
  19.5 11.4 %all_to_all.5.held_ref = bf16[8,32,256]{2,1,0:T(8,128)(2,1)S(1)} all-to-all(bf16[8,32,256]{2,1,0:T(8,128)(2,1)S(1)} %shard_map.66), channel_id=1, replica_groups=mesh['rollout'=2,'frame'=2,'seq'=8] {'seq'}, dimensions={0} | all-to-all | bytes 262144 | tf_op jit(solution)/shard_map/all_to_all | solution.py:193
  30.9 0.7 %shard_map.67 = bf16[32,2048]{1,0:T(8,128)(2,1)} custom-call(bf16[8,32,256]{2,1,0:T(8,128)(2,1)S(1)} %all_to_all.5.held_ref), custom_call_target="tpu_custom_call" | custom-call | tf_op jit(solution)/shard_map/pallas_call | solution.py:194
  (1 shorter events, 0.0 us)
Async XLA Ops:
  1.2 10.9 %collective-permute-start = (bf16[3,32,256]{2,1,0:T(8,128)(2,1)S(1)}, bf16[3,32,256]{2,1,0:T(8,128)(2,1)S(1)}, u32[]{:S(2)}, u32[]{:S(2)}) collective-permute-start(bf16[3,32,256]{2,1,0:T(8,128)(2,1)S(1)} %get-tuple-element.13), channel_id=1, source_target_pairs={{0,5},{1,4},{2,7},{3,6},{4,1},{5,0},{6,3},{7,2},{8,13},{9,12},{10,... | collective-permute-start | bytes 147464 | tf_op jit(solution)/shard_map/ppermute | solution.py:169
  6.2 6.9 %collective-permute-start.1 = (bf16[3,32,256]{2,1,0:T(8,128)(2,1)S(1)}, bf16[3,32,256]{2,1,0:T(8,128)(2,1)S(1)}, u32[]{:S(2)}, u32[]{:S(2)}) collective-permute-start(bf16[3,32,256]{2,1,0:T(8,128)(2,1)S(1)} %get-tuple-element.14), channel_id=1, source_target_pairs={{0,6},{1,7},{2,4},{3,5},{4,2},{5,3},{6,0},{7,1},{8,14},{9,15},{10,... | collective-permute-start | bytes 147464 | tf_op jit(solution)/shard_map/ppermute | solution.py:169
  7.6 6.1 %collective-permute-start.2 = (bf16[3,32,256]{2,1,0:T(8,128)(2,1)S(1)}, bf16[3,32,256]{2,1,0:T(8,128)(2,1)S(1)}, u32[]{:S(2)}, u32[]{:S(2)}) collective-permute-start(bf16[3,32,256]{2,1,0:T(8,128)(2,1)S(1)} %get-tuple-element.15), channel_id=1, source_target_pairs={{0,3},{1,2},{2,1},{3,0},{4,7},{5,6},{6,5},{7,4},{8,11},{9,10},{10,... | collective-permute-start | bytes 147464 | tf_op jit(solution)/shard_map/ppermute | solution.py:169
  7.8 7.1 %collective-permute-start.3 = (bf16[3,32,256]{2,1,0:T(8,128)(2,1)S(1)}, bf16[3,32,256]{2,1,0:T(8,128)(2,1)S(1)}, u32[]{:S(2)}, u32[]{:S(2)}) collective-permute-start(bf16[3,32,256]{2,1,0:T(8,128)(2,1)S(1)} %get-tuple-element.16), channel_id=1, source_target_pairs={{0,7},{1,6},{2,5},{3,4},{4,3},{5,2},{6,1},{7,0},{8,15},{9,14},{10,... | collective-permute-start | bytes 147464 | tf_op jit(solution)/shard_map/ppermute | solution.py:169
  11.6 4.1 %collective-permute-start.4 = (bf16[3,32,256]{2,1,0:T(8,128)(2,1)S(1)}, bf16[3,32,256]{2,1,0:T(8,128)(2,1)S(1)}, u32[]{:S(2)}, u32[]{:S(2)}) collective-permute-start(bf16[3,32,256]{2,1,0:T(8,128)(2,1)S(1)} %get-tuple-element.17), channel_id=1, source_target_pairs={{0,2},{1,3},{2,0},{3,1},{4,6},{5,7},{6,4},{7,5},{8,10},{9,11},{10,... | collective-permute-start | bytes 147464 | tf_op jit(solution)/shard_map/ppermute | solution.py:169
  12.1 5.0 %collective-permute-start.5 = (bf16[3,32,256]{2,1,0:T(8,128)(2,1)S(1)}, bf16[3,32,256]{2,1,0:T(8,128)(2,1)S(1)}, u32[]{:S(2)}, u32[]{:S(2)}) collective-permute-start(bf16[3,32,256]{2,1,0:T(8,128)(2,1)S(1)} %get-tuple-element.18), channel_id=1, source_target_pairs={{0,4},{1,5},{2,6},{3,7},{4,0},{5,1},{6,2},{7,3},{8,12},{9,13},{10,... | collective-permute-start | bytes 147464 | tf_op jit(solution)/shard_map/ppermute | solution.py:169
  13.1 4.1 %collective-permute-start.6 = (bf16[3,32,256]{2,1,0:T(8,128)(2,1)S(1)}, bf16[3,32,256]{2,1,0:T(8,128)(2,1)S(1)}, u32[]{:S(2)}, u32[]{:S(2)}) collective-permute-start(bf16[3,32,256]{2,1,0:T(8,128)(2,1)S(1)} %get-tuple-element.19), channel_id=1, source_target_pairs={{0,1},{1,0},{2,3},{3,2},{4,5},{5,4},{6,7},{7,6},{8,9},{9,8},{10,11... | collective-permute-start | bytes 147464 | tf_op jit(solution)/shard_map/ppermute | solution.py:169
  17.2 1.6 %copy-start = (f32[8,2048]{1,0:T(8,128)S(1)}, f32[8,2048]{1,0:T(8,128)}, u32[]{:S(2)}) copy-start(f32[8,2048]{1,0:T(8,128)} %gate_ref.1) | copy-start | bytes 196612
  17.2 1.6 %copy-start.1 = (s32[2,4]{1,0:T(2,128)S(1)}, s32[2,4]{1,0:T(2,128)}, u32[]{:S(2)}) copy-start(s32[2,4]{1,0:T(2,128)} %slot_ref.1) | copy-start | bytes 100
  17.2 1.6 %copy-start.2 = (s32[2,4]{1,0:T(2,128)S(1)}, s32[2,4]{1,0:T(2,128)}, u32[]{:S(2)}) copy-start(s32[2,4]{1,0:T(2,128)} %level_ref.1) | copy-start | bytes 100
  17.2 1.6 %collective-permute-start.7 = (bf16[8,2,32,256]{3,2,1,0:T(8,128)(2,1)S(1)}, bf16[8,2,32,256]{3,2,1,0:T(8,128)(2,1)S(1)}, u32[]{:S(2)}, u32[]{:S(2)}) collective-permute-start(bf16[8,2,32,256]{3,2,1,0:T(8,128)(2,1)S(1)} %shard_map.65), channel_id=1, source_target_pairs={{0,8},{8,0},{1,9},{9,1},{2,10},{10,2},{3,11},{11,3},{4,12},{12,4},... | collective-permute-start | bytes 786440 | tf_op jit(solution)/shard_map/ppermute | solution.py:183
